TPU v7x, 32 devices: a whole 2x2x4 slice. The times are simulated.
32 devices in a mesh: dp: 8 (over z, y), tensor: 4 (over x, core).
Axes of the slice: x: 2, y: 2, z: 4, core: 2. Of those that a mesh axis runs over, the one named last changes fastest.
Arguments:
- queries: bfloat16 [4096, 4096], P('dp', 'tensor'), may hold values from -20 to 20
- cotangent: bfloat16 [4096, 4096], P('dp', 'tensor'), may hold values from -6 to 6
- table: bfloat16 [128, 128, 896], P('dp'), may hold values from -6 to 6
- key_weight: bfloat16 [896, 4096], P(None, 'tensor'), may hold values from -0.1875 to 0.1875
- value_weight: bfloat16 [896, 4096], P(None, 'tensor'), may hold values from -0.1875 to 0.1875
- owners: int32 [64, 2], P('dp'), may hold values from 0 to 7, all different within a row; in each aligned block of 8 rows (0 to 7, 8 to 15, ...) at most 4 rows name the same one
- slots: int32 [64, 2], P('dp'), may hold values from 0 to 15
Outputs:
- attended: bfloat16 [4096, 4096], P('dp', 'tensor')
- d_query: bfloat16 [4096, 4096], P('dp', 'tensor')
- d_table: float32 [128, 128, 896], P('dp', 'tensor')
Inputs may be any that keep to these rules, and one draw needn't show every extreme that they name: `owners`: in each aligned block of 8 rows (the spans of one dp index) no value occurs more than 4 times, and in some block one value occurs exactly 4 times; the two entries of a row differ.
All inputs are finite; a program needn't handle non-finite values.
Results may differ from a plain program's by a relative error of at most 0.0055.
The roundings to bfloat16 on the way count: a program that leaves them out, or rounds other values in their place, can miss the bound.
Values may be sent and summed in bfloat16 or wider, within the bound.
No kernel may reach another device: no remote copies, remote signals or barrier semaphores. Data moves between devices by JAX's collectives and lax.ppermute only.
A program may use at most 128 MiB of HBM per device.

v0:
```python
import math

import jax
import jax.numpy as jnp
from jax import lax
from jax.sharding import PartitionSpec as P

HD = 128
SPAN = 64


def on_device(queries, cotangent, table, key_weight, value_weight, owners, slots):
    n_dp = lax.axis_size("dp")
    n_tp = lax.axis_size("tensor")
    spans = owners.shape[0]
    n_requests = 2 * spans
    n_slabs, n_tokens, enc_width = table.shape
    kv_width = key_weight.shape[1]
    n_heads = kv_width // HD
    capacity = max(2, (4 * spans + n_dp - 1) // n_dp)
    tok_share = n_tokens // n_tp
    score_scale = 1.0 / math.sqrt(HD)
    owner_flat = owners.reshape(n_requests)
    slot_flat = slots.reshape(n_requests)
    onehot = (owner_flat[:, None] == jnp.arange(n_dp, dtype=jnp.int32)[None, :]).astype(jnp.int32)
    within = jnp.sum((jnp.cumsum(onehot, axis=0) - onehot) * onehot, axis=1)
    position = owner_flat * capacity + within
    request_buffer = jnp.full((n_dp * capacity,), -1, jnp.int32).at[position].set(slot_flat)
    asked = lax.all_to_all(
        request_buffer.reshape(n_dp, capacity), "dp", split_axis=0, concat_axis=0, tiled=True
    )
    safe_slot = jnp.maximum(asked, 0)
    w_kv = jnp.concatenate([key_weight, value_weight], axis=1)
    sent_rows = table[safe_slot]
    arrived = lax.all_to_all(sent_rows, "dp", split_axis=0, concat_axis=0, tiled=True)
    own_rows = arrived.reshape(n_dp * capacity, n_tokens, enc_width)[position]
    key_value = jnp.dot(own_rows.reshape(-1, enc_width), w_kv, preferred_element_type=jnp.float32)
    key_value = key_value.astype(jnp.bfloat16).reshape(n_requests, n_tokens, 2 * kv_width)
    key_value = key_value.reshape(spans, 2 * n_tokens, 2 * kv_width)
    keys = key_value[:, :, :kv_width].reshape(spans, 2 * n_tokens, n_heads, HD)
    values = key_value[:, :, kv_width:].reshape(spans, 2 * n_tokens, n_heads, HD)
    query_heads = queries.reshape(spans, SPAN, n_heads, HD)
    grad_heads = cotangent.reshape(spans, SPAN, n_heads, HD)
    scores = (
        jnp.einsum("cqhd,ckhd->chqk", query_heads, keys, preferred_element_type=jnp.float32)
        * score_scale
    )
    attn_probs = jax.nn.softmax(scores, axis=-1)
    weights = attn_probs.astype(jnp.bfloat16)
    attended = jnp.einsum("chqk,ckhd->cqhd", weights, values, preferred_element_type=jnp.float32)
    attended = attended.astype(jnp.bfloat16).reshape(spans * SPAN, kv_width)
    d_weights = jnp.einsum(
        "cqhd,ckhd->chqk", grad_heads, values, preferred_element_type=jnp.float32
    )
    row_sums = jnp.sum(d_weights * attn_probs, axis=-1, keepdims=True)
    dscores = (attn_probs * (d_weights - row_sums) * score_scale).astype(jnp.bfloat16)
    d_query = jnp.einsum("chqk,ckhd->cqhd", dscores, keys, preferred_element_type=jnp.float32)
    d_query = d_query.astype(jnp.bfloat16).reshape(spans * SPAN, kv_width)
    d_keys = jnp.einsum(
        "chqk,cqhd->ckhd", dscores, query_heads, preferred_element_type=jnp.float32
    ).astype(jnp.bfloat16)
    d_values = jnp.einsum(
        "chqk,cqhd->ckhd", weights, grad_heads, preferred_element_type=jnp.float32
    ).astype(jnp.bfloat16)
    d_kv = jnp.concatenate(
        [
            d_keys.reshape(spans, 2 * n_tokens, kv_width),
            d_values.reshape(spans, 2 * n_tokens, kv_width),
        ],
        axis=2,
    )
    d_kv_tokens = d_kv.reshape(n_requests, n_tokens, 2 * kv_width).transpose(1, 0, 2)
    summed = jnp.dot(
        d_kv_tokens.reshape(-1, 2 * kv_width), w_kv.T, preferred_element_type=jnp.float32
    )
    share_grad = lax.psum_scatter(
        summed.reshape(tok_share * lax.axis_size("tensor"), n_requests, enc_width),
        "tensor",
        scatter_dimension=0,
        tiled=True,
    )
    back_buffer = jnp.zeros((n_dp * capacity, tok_share, enc_width), jnp.float32)
    back_buffer = back_buffer.at[position].set(share_grad.transpose(1, 0, 2))
    returned = lax.all_to_all(
        back_buffer.reshape(n_dp, capacity, tok_share, enc_width),
        "dp",
        split_axis=0,
        concat_axis=0,
        tiled=True,
    )
    matches = (asked[:, :, None] == jnp.arange(n_slabs, dtype=jnp.int32)[None, None, :]).astype(
        jnp.float32
    )
    d_table = jnp.einsum("pcs,pcte->ste", matches, returned, precision=lax.Precision.HIGHEST)
    return (attended, d_query, d_table)


def solution(mesh):
    in_specs = (
        P("dp", "tensor"),
        P("dp", "tensor"),
        P("dp", None, None),
        P(None, "tensor"),
        P(None, "tensor"),
        P("dp", None),
        P("dp", None),
    )
    out_specs = (P("dp", "tensor"), P("dp", "tensor"), P("dp", "tensor", None))
    return jax.shard_map(
        on_device, mesh=mesh, in_specs=in_specs, out_specs=out_specs, check_vma=False
    )
```

profile of v0, /device:TPU:0, one launch (start us, length us, event | category | flops | bytes accessed | tf_op | source)
XLA Modules:
  0.0 506.6 jit_solution(397254410545300409)
XLA Ops:
  10.7 13.5 %all_to_all.19 = s32[8,1,4]{2,1,0:T(1,128)S(1)} all-to-all(s32[8,1,4]{2,1,0:T(1,128)S(1)} %bitcast.132), channel_id=1, replica_groups=mesh['dp'=8,'tensor'=4] {'dp'}, dimensions={0} | all-to-all | bytes 256 | tf_op jit(solution)/shard_map/all_to_all | solution.py:29
  24.3 6.5 %gather_fusion = bf16[32,128,896]{2,1,0:T(8,128)(2,1)} fusion(bf16[16,128,896]{2,1,0:T(8,128)(2,1)} %param.9, s32[1024]{0:T(1024)S(1)} %pad_clamp_fusion.1), kind=kCustom, calls=%fused_computation | custom fusion | bytes 14680192 | tf_op jit(solution)/shard_map/gather | solution.py:34
  30.8 5.0 all-to-all-start.1
  40.3 154.9 %all-to-all-done.1 = bf16[8,4,128,896]{3,2,1,0:T(8,128)(2,1)} async-done(((bf16[8,4,128,896]{3,2,1,0:T(8,128)(2,1)}), bf16[8,4,128,896]{3,2,1,0:T(8,128)(2,1)}, u32[]{:S(2)}, u32[]{:S(2)}) %all-to-all-start.1) | async-done | bytes 7340064 | tf_op jit(solution)/shard_map/all_to_all | solution.py:35
  195.2 6.0 %gather_fusion.1 = bf16[16,128,896]{2,1,0:T(8,128)(2,1)} fusion(bf16[32,128,896]{2,1,0:T(8,128)(2,1)} %bitcast.4, s32[1024]{0:T(1024)S(1)} %pad_clamp_fusion), kind=kCustom, calls=%fused_computation.1 | custom fusion | bytes 7340096 | tf_op jit(solution)/shard_map/gather | solution.py:36
  201.2 11.7 %convolution_convert_fusion = bf16[2048,2048]{1,0:T(8,128)(2,1)S(1)} fusion(bf16[2048,896]{1,0:T(8,128)(2,1)} %bitcast.128, bf16[896,2048]{1,0:T(8,128)(2,1)} %constant_dynamic-update-slice_fusion), kind=kOutput, calls=%fused_computation.10 | convolution fusion | flops 7520387072 | bytes 15728640 | tf_op jit(solution)/shard_map/dot_general | solution.py:37
  212.9 3.7 fusion.54
  216.5 6.4 %copy.67 = bf16[8,256,1024]{1,2,0:T(8,128)(2,1)} copy(bf16[8,256,1024]{2,1,0:T(8,128)(2,1)} %get-tuple-element.12) | data formatting | bytes 8388608
  223.0 6.4 %copy.66 = bf16[8,256,1024]{1,2,0:T(8,128)(2,1)} copy(bf16[8,256,1024]{2,1,0:T(8,128)(2,1)} %get-tuple-element.13) | data formatting | bytes 8388608
  240.2 13.3 %convert_bitcast_fusion = bf16[8,256,8,128]{3,1,2,0:T(8,128)(2,1)} fusion(bf16[8,64,8,128]{3,2,1,0:T(8,128)(2,1)S(1)} %bitcast.125, f32[8,8,64]{2,1,0:T(8,128)S(1)} %get-tuple-element.14, f32[8,8,256,64]{2,3,1,0:T(8,128)} %copy-done.1), kind=kOutput, calls=%fused_computation.20 | convolution fusion | flops 275779840 | bytes 9453568 | tf_op jit(solution)/shard_map/chqk,cqhd->ckhd/dot_general | solution.py:62
  253.4 6.8 %copy.57 = bf16[8,256,8,128]{3,2,1,0:T(8,128)(2,1)} copy(bf16[8,256,8,128]{3,1,2,0:T(8,128)(2,1)} %convert_bitcast_fusion) | data formatting | bytes 8388608 | tf_op jit(solution)/shard_map/convert_element_type | solution.py:64
  260.3 7.3 %concatenate.13 = bf16[16,128,1024]{2,1,0:T(8,128)(2,1)} reshape(bf16[8,256,8,128]{3,2,1,0:T(8,128)(2,1)} %copy.57) | data formatting | bytes 8388608 | tf_op jit(solution)/shard_map/concatenate | solution.py:65
  267.6 31.8 %convert_bitcast_fusion.1 = bf16[8,256,8,128]{3,1,2,0:T(8,128)(2,1)} fusion(f32[8,8,256,64]{2,3,1,0:T(8,128)} %fusion.28, bf16[8,64,8,128]{3,2,1,0:T(8,128)(2,1)S(1)} %bitcast.123, f32[8,8,64,256]{3,2,1,0:T(8,128)} %get-tuple-element.15, f32[8,8,64]{2,1,0:T(8,128)S(1)} %get-tuple-element.14), kind=kOutput, calls=%fused_computation.21 | convolution fusion | flops 277876992 | bytes 13647872 | tf_op jit(solution)/shard_map/chqk,cqhd->ckhd/dot_general | solution.py:59
  299.4 6.8 %copy.55 = bf16[8,256,8,128]{3,2,1,0:T(8,128)(2,1)} copy(bf16[8,256,8,128]{3,1,2,0:T(8,128)(2,1)} %convert_bitcast_fusion.1) | data formatting | bytes 8388608 | tf_op jit(solution)/shard_map/convert_element_type | solution.py:61
  306.2 7.3 %concatenate.12 = bf16[16,128,1024]{2,1,0:T(8,128)(2,1)} reshape(bf16[8,256,8,128]{3,2,1,0:T(8,128)(2,1)} %copy.55) | data formatting | bytes 8388608 | tf_op jit(solution)/shard_map/concatenate | solution.py:65
  313.5 14.4 %fusion.2 = f32[128,16,896]{2,0,1:T(8,128)} fusion(bf16[16,128,1024]{2,1,0:T(8,128)(2,1)} %concatenate.13, bf16[16,128,1024]{2,1,0:T(8,128)(2,1)} %concatenate.12, bf16[896,2048]{1,0:T(8,128)(2,1)} %constant_dynamic-update-slice_fusion), kind=kOutput, calls=%fused_computation.7 | convolution fusion | flops 7532969984 | bytes 19398656 | tf_op jit(solution)/shard_map/dot_general | solution.py:73
  327.9 64.7 %reduce-scatter.2.cloned.1.call-done = f32[32,16,896]{2,0,1:T(8,128)} async-done(((f32[128,16,896]{2,0,1:T(8,128)}), f32[32,16,896]{2,0,1:T(8,128)}) %reduce-scatter.2.cloned.1.call-update) | async-done | bytes 1835024 | tf_op jit(solution)/shard_map/reduce_scatter | solution.py:76
  394.8 3.6 scatter_fusion
  398.4 6.2 %copy.58 = f32[8,4,32,896]{3,1,2,0:T(4,128)} copy(f32[8,4,32,896]{3,2,1,0:T(8,128)} %bitcast.120) | data formatting | bytes 7340032 | tf_op jit(solution)/shard_map/reshape | solution.py:85
  404.6 5.5 %all-to-all-start.2 = ((f32[8,4,32,896]{3,1,2,0:T(4,128)}), f32[8,4,32,896]{3,1,2,0:T(4,128)}, u32[]{:S(2)}, u32[]{:S(2)}) async-start(f32[8,4,32,896]{3,1,2,0:T(4,128)} %copy.58), calls=%async_computation.3 | async-start | bytes 7340032 | tf_op jit(solution)/shard_map/all_to_all | solution.py:84
  410.3 29.7 %fusion.24 = bf16[8,64,8,128]{3,1,2,0:T(8,128)(2,1)S(1)} fusion(bf16[8,256,8,128]{1,3,2,0:T(8,128)(2,1)} %bitcast.118, f32[8,8,256,64]{2,3,1,0:T(8,128)} %fusion.28, f32[8,8,64,256]{3,2,1,0:T(8,128)} %get-tuple-element.15, f32[8,8,64]{2,1,0:T(8,128)S(1)} %get-tuple-element.14), kind=kOutput, calls=%fused_computation.34 | convolution fusion | flops 276304128 | bytes 13647872 | tf_op jit(solution)/shard_map/chqk,ckhd->cqhd/dot_general | solution.py:57
  440.7 11.9 %fusion.23 = bf16[8,64,8,128]{3,1,2,0:T(8,128)(2,1)S(1)} fusion(bf16[8,256,8,128]{1,3,2,0:T(8,128)(2,1)} %bitcast.115, f32[8,8,64]{2,1,0:T(8,128)S(1)} %get-tuple-element.14, f32[8,8,256,64]{2,3,1,0:T(8,128)} %copy-done.1), kind=kOutput, calls=%fused_computation.33 | convolution fusion | flops 274206976 | bytes 9453568 | tf_op jit(solution)/shard_map/chqk,ckhd->cqhd/dot_general | solution.py:50
  455.1 37.1 %all-to-all-done.2 = f32[8,4,32,896]{3,1,2,0:T(4,128)} async-done(((f32[8,4,32,896]{3,1,2,0:T(4,128)}), f32[8,4,32,896]{3,1,2,0:T(4,128)}, u32[]{:S(2)}, u32[]{:S(2)}) %all-to-all-start.2) | async-done | bytes 3670048 | tf_op jit(solution)/shard_map/all_to_all | solution.py:84
  492.2 5.3 %fusion.19 = f32[16,32,896]{2,0,1:T(8,128)S(1)} fusion(f32[8,4,32,896]{3,1,2,0:T(4,128)} %all-to-all-done.2, s32[8,4]{0,1:T(4,128)S(1)} %bitcast.133), kind=kOutput, calls=%fused_computation.30 | convolution fusion | flops 176161280 | bytes 5505152 | tf_op jit(solution)/shard_map/pcs,pcte->ste/dot_general | solution.py:94
  (46 shorter events, 26.2 us)
Async XLA Ops:
  30.8 5.1 copy-start.5
  30.8 5.3 %copy-start.6 = (bf16[512,1024]{1,0:T(8,128)(2,1)S(1)}, bf16[512,1024]{1,0:T(8,128)(2,1)}, u32[]{:S(2)}) copy-start(bf16[512,1024]{1,0:T(8,128)(2,1)} %param.7) | copy-start | bytes 3145732
  30.8 164.4 %all-to-all-start.1 = ((bf16[8,4,128,896]{3,2,1,0:T(8,128)(2,1)}), bf16[8,4,128,896]{3,2,1,0:T(8,128)(2,1)}, u32[]{:S(2)}, u32[]{:S(2)}) async-start(bf16[8,4,128,896]{3,2,1,0:T(8,128)(2,1)} %bitcast.119), calls=%async_computation.1 | async-start | bytes 14680064 | tf_op jit(solution)/shard_map/all_to_all | solution.py:35
  35.8 356.8 %reduce-scatter.2.cloned.1.call-start = ((), (), s32[]{:S(2)}) async-start(), calls=%async_computation.4 | async-start | bytes 9175040 | tf_op jit(solution)/shard_map/reduce_scatter | solution.py:76
  35.8 1.5 copy-start.2
  35.8 2.9 copy-start.3
  232.3 4.1 copy-start.1
  232.3 5.1 %copy-start = (bf16[8,256,1024]{1,2,0:T(8,128)(2,1)S(1)}, bf16[8,256,1024]{1,2,0:T(8,128)(2,1)}, u32[]{:S(2)}) copy-start(bf16[8,256,1024]{1,2,0:T(8,128)(2,1)} %copy.66) | copy-start | bytes 12582916
  392.6 2.3 copy-start.4
  404.6 87.6 %all-to-all-start.2 = ((f32[8,4,32,896]{3,1,2,0:T(4,128)}), f32[8,4,32,896]{3,1,2,0:T(4,128)}, u32[]{:S(2)}, u32[]{:S(2)}) async-start(f32[8,4,32,896]{3,1,2,0:T(4,128)} %copy.58), calls=%async_computation.3 | async-start | bytes 7340032 | tf_op jit(solution)/shard_map/all_to_all | solution.py:84
Sparse Core Ops, SparseCore 0:
  328.0 64.5 reduce-scatter.1
where the time goes:
time: 517 us; the launch traced here: 507 us
  waiting for transfers between devices  257 us (50%)
  matrix products  124 us (24%)
  local copies, waits for them, and re-layouts  83.5 us (16%)
  between operations  14.6 us (3%)
  blocking collectives  13.5 us (3%)
  starting transfers between devices  10.5 us (2%)
    all_to_all x1, waiting for transfers between devices, on_device(): lax.all_to_all(sent_rows, 'dp', split_axis=0, concat_axis=0, tiled=True)  155 us
    reduce_scatter x1, waiting for transfers between devices, on_device(): lax.psum_scatter(summed.reshape(tok_share * lax.axis_size('tensor'), n_re...  64.7 us
    all_to_all x1, waiting for transfers between devices, on_device(): lax.all_to_all(back_buffer.reshape(n_dp, capacity, tok_share, enc_width),...  37.1 us
    dot_general x1, matrix products, on_device(): jnp.einsum('chqk,cqhd->ckhd', dscores, query_heads, preferred_element_typ...  31.8 us
    dot_general x1, matrix products, on_device(): jnp.einsum('chqk,ckhd->cqhd', dscores, keys, preferred_element_type=jnp.f...  29.7 us
    unnamed x22, local copies, waits for them, and re-layouts  21.2 us
    concatenate x2, local copies, waits for them, and re-layouts, on_device(): jnp.concatenate([d_keys.reshape(spans, 2 * n_tokens, kv_width), d_values....  14.6 us
    dot_general x1, matrix products, on_device(): jnp.dot(d_kv_tokens.reshape(-1, 2 * kv_width), w_kv.T, preferred_element_...  14.4 us
  transfers between devices with their start and end apart: 3, of which 3 were waited for; matrix products, arithmetic and copies ran while one was open for 10% of the time, Pallas kernels for 0%

commit v1 on v0

v1 whole, which is shorter than its diff:
```python
import functools
import math

import jax
import jax.numpy as jnp
from jax import lax
from jax.experimental import pallas as pl
from jax.experimental.pallas import tpu as pltpu
from jax.sharding import PartitionSpec as P

HD = 128
SPAN = 64
SUB = 16
LANES = 128
VMEM_LIMIT = 56 * 1024 * 1024
F32 = jnp.float32
BF16 = jnp.bfloat16

ANY = pl.BlockSpec(memory_space=pl.ANY)
SMEM = pl.BlockSpec(memory_space=pltpu.SMEM)
VMEM = pl.BlockSpec(memory_space=pltpu.VMEM)


def params():
    return pltpu.CompilerParams(vmem_limit_bytes=VMEM_LIMIT)


def cost(flops, nbytes):
    return pl.CostEstimate(flops=int(flops), bytes_accessed=int(nbytes), transcendentals=0)


def pack_body(n_chunks, share, asked, first, table, *rest):
    outs, sem = rest[:n_chunks], rest[n_chunks]
    n = asked.shape[0]
    base = first[0]

    def each(act):
        for s in range(n):
            slab = asked[s]

            @pl.when(slab >= 0)
            def _():
                for c in range(n_chunks):
                    row = pl.multiple_of(base + c * SUB, SUB)
                    act(
                        pltpu.make_async_copy(
                            table.at[slab, pl.ds(row, SUB)], outs[c].at[s], sem.at[c, s]
                        )
                    )

    each(lambda copy: copy.start())
    each(lambda copy: copy.wait())


def pack(asked, first, table, n_chunks):
    n = asked.shape[0]
    enc = table.shape[2]
    return pl.pallas_call(
        functools.partial(pack_body, n_chunks, None),
        out_shape=[jax.ShapeDtypeStruct((n, SUB, enc), table.dtype)] * n_chunks,
        in_specs=[SMEM, SMEM, ANY],
        out_specs=[ANY] * n_chunks,
        scratch_shapes=[pltpu.SemaphoreType.DMA((n_chunks, n))],
        compiler_params=params(),
        cost_estimate=cost(0, 4 * n_chunks * n * SUB * enc),
        name="pack_rows",
    )(asked, first, table)


def compact_body(position, arrived, out, sem):
    n = position.shape[0]
    copies = [
        pltpu.make_async_copy(arrived.at[position[r]], out.at[r], sem.at[r]) for r in range(n)
    ]
    for copy in copies:
        copy.start()
    for copy in copies:
        copy.wait()


def compact(position, arrived):
    n = position.shape[0]
    shape = (n,) + arrived.shape[1:]
    return pl.pallas_call(
        compact_body,
        out_shape=jax.ShapeDtypeStruct(shape, arrived.dtype),
        in_specs=[SMEM, ANY],
        out_specs=ANY,
        scratch_shapes=[pltpu.SemaphoreType.DMA((n,))],
        compiler_params=params(),
        cost_estimate=cost(0, 4 * math.prod(shape)),
        name="compact_rows",
    )(position, arrived)


def project_body(n_in, *refs):
    w, out = refs[n_in], refs[n_in + 1]
    for i in range(n_in):
        n, sub, enc = refs[i].shape
        rows = refs[i][...].reshape(n * sub, enc)
        res = jnp.dot(rows, w[...], preferred_element_type=F32)
        out[i] = res.astype(BF16).reshape(n, sub, res.shape[1])


def project(pieces, w_kv):
    n_in = len(pieces)
    n, sub, enc = pieces[0].shape
    width = w_kv.shape[1]
    step = width // 4
    return pl.pallas_call(
        functools.partial(project_body, n_in),
        out_shape=jax.ShapeDtypeStruct((n_in, n, sub, width), BF16),
        grid=(4,),
        in_specs=[pl.BlockSpec((n, sub, enc), lambda i: (0, 0, 0))] * n_in
        + [pl.BlockSpec((enc, step), lambda i: (0, i))],
        out_specs=pl.BlockSpec((n_in, n, sub, step), lambda i: (0, 0, 0, i)),
        compiler_params=params(),
        cost_estimate=cost(
            2 * n_in * n * sub * enc * width, 2 * (n_in * n * sub * (enc + width) + enc * width)
        ),
        name="project",
    )(*pieces, w_kv)


def attend_body(groups, n_x, n_chunks, *refs):
    n_kv = n_chunks * len(groups)
    kvs = refs[:n_kv]
    q_ref, g_ref = refs[n_kv : n_kv + 2]
    att_ref, dq_ref = refs[n_kv + 2 : n_kv + 4]
    own_refs = refs[n_kv + 4 : n_kv + 4 + n_chunks]
    core_refs = refs[n_kv + 4 + n_chunks :]
    width = q_ref.shape[1]
    scale = 1.0 / math.sqrt(HD)

    def keys_of(col):
        cols = pl.ds(col, HD)
        parts = []
        for ref in kvs:
            block = ref[:, :, :, cols]
            parts.append(block.reshape(-1, HD))
        return jnp.concatenate(parts, axis=0)

    def put(col, grad):
        at = 0
        for c in range(n_chunks):
            for group in groups:
                for kind, d in group:
                    ref = (own_refs if kind == 0 else core_refs)[c]
                    ref[d, :, :, pl.ds(col, HD)] = grad[at : at + 2 * SUB].reshape(2, SUB, HD)
                    at += 2 * SUB

    last = (((1,), (1,)), ((), ()))
    first = (((0,), (0,)), ((), ()))
    for h in range(width // HD):
        cols = pl.ds(h * HD, HD)
        q, g = q_ref[:, cols], g_ref[:, cols]
        k, v = keys_of(h * HD), keys_of(width + h * HD)
        s = lax.dot_general(q, k, last, preferred_element_type=F32) * scale
        e = jnp.exp(s - jnp.max(s, axis=1, keepdims=True))
        p = e / jnp.sum(e, axis=1, keepdims=True)
        w = p.astype(BF16)
        att_ref[:, cols] = jnp.dot(w, v, preferred_element_type=F32).astype(BF16)
        dw = lax.dot_general(g, v, last, preferred_element_type=F32)
        rs = jnp.sum(dw * p, axis=1, keepdims=True)
        ds = (p * (dw - rs) * scale).astype(BF16)
        dq_ref[:, cols] = jnp.dot(ds, k, preferred_element_type=F32).astype(BF16)
        put(h * HD, lax.dot_general(ds, q, first, preferred_element_type=F32).astype(BF16))
        put(width + h * HD, lax.dot_general(w, g, first, preferred_element_type=F32).astype(BF16))


def attend(kvs, groups, n_x, n_chunks, queries, cotangent):
    tokens, width = queries.shape
    spans = tokens // SPAN
    n = kvs[0].shape[1]
    rows = pl.BlockSpec((SPAN, width), lambda i: (i, 0))

    def kv_block(pieces):
        return pl.BlockSpec((pieces, 2, SUB, 2 * width), lambda i: (0, i, 0, 0))

    keys = n_chunks * 2 * n_x * 2 * SUB
    out = pl.pallas_call(
        functools.partial(attend_body, groups, n_x, n_chunks),
        out_shape=[jax.ShapeDtypeStruct((tokens, width), BF16)] * 2
        + [jax.ShapeDtypeStruct((n_x, n, SUB, 2 * width), BF16)] * (2 * n_chunks),
        grid=(spans,),
        in_specs=[kv_block(kv.shape[0]) for kv in kvs] + [rows, rows],
        out_specs=[rows, rows] + [kv_block(n_x)] * (2 * n_chunks),
        compiler_params=params(),
        cost_estimate=cost(12 * tokens * width * keys, 8 * tokens * width + 8 * spans * keys * 2 * width),
        name="attend",
    )(*kvs, queries, cotangent)
    return out[0], out[1], out[2 : 2 + n_chunks], out[2 + n_chunks :]


def encode(x, axes):
    top = jnp.maximum(jnp.max(jnp.abs(x), axis=axes, keepdims=True), 1e-30)
    power = jnp.floor(jnp.log2(top)) + 1.0
    code = jnp.clip(jnp.round(x * jnp.exp2(15.0 - power)), -32767.0, 32767.0)
    return code.astype(jnp.int32).astype(jnp.int16), power


def partial_grad(d_ref, w_ref, acc):
    k = pl.program_id(0)
    n_x, n, sub, step = d_ref.shape
    part = lax.dot_general(
        d_ref[...].reshape(n_x * n * sub, step),
        w_ref[...],
        (((1,), (1,)), ((), ())),
        preferred_element_type=F32,
    )

    @pl.when(k == 0)
    def _():
        acc[...] = part

    @pl.when(k > 0)
    def _():
        acc[...] += part


def core_grad_body(d_ref, w_ref, out, acc):
    partial_grad(d_ref, w_ref, acc)

    @pl.when(pl.program_id(0) == pl.num_programs(0) - 1)
    def _():
        out[...] = acc[...].reshape(out.shape)


def own_grad_body(n_x, d_ref, w_ref, got, own, *rest):
    codes, acc = rest[:-1], rest[-1]
    partial_grad(d_ref, w_ref, acc)
    n, sub, enc = own.shape
    rows = n * sub

    @pl.when(pl.program_id(0) == pl.num_programs(0) - 1)
    def _():
        own[...] = acc[:rows].reshape(own.shape) + got[0]
        for d in range(1, n_x):
            full = acc[d * rows : (d + 1) * rows].reshape(n, sub, enc) + got[d]
            code, power = encode(full, (1, 2))
            out = codes[d - 1]
            for e in range(enc // LANES):
                out[e] = code[:, :, e * LANES : (e + 1) * LANES]
            note = jnp.broadcast_to(power.reshape(n, 1, 1), (n, sub, LANES))
            out[enc // LANES] = note.astype(jnp.int32).astype(jnp.int16)


def core_grad(d_kv, w_kv):
    n_x, n, sub, width = d_kv.shape
    enc = w_kv.shape[0]
    step = width // 4
    return pl.pallas_call(
        core_grad_body,
        out_shape=jax.ShapeDtypeStruct((n_x, n, sub, enc), F32),
        grid=(4,),
        in_specs=[
            pl.BlockSpec((n_x, n, sub, step), lambda i: (0, 0, 0, i)),
            pl.BlockSpec((enc, step), lambda i: (0, i)),
        ],
        out_specs=pl.BlockSpec((n_x, n, sub, enc), lambda i: (0, 0, 0, 0)),
        scratch_shapes=[pltpu.VMEM((n_x * n * sub, enc), F32)],
        compiler_params=params(),
        cost_estimate=cost(2 * n_x * n * sub * enc * width, 2 * (enc + n_x * n * sub) * width),
        name="core_grad",
    )(d_kv, w_kv)


def own_grad(d_kv, w_kv, got):
    n_x, n, sub, width = d_kv.shape
    enc = w_kv.shape[0]
    step = width // 4
    code = (enc // LANES + 1, n, sub, LANES)
    out = pl.pallas_call(
        functools.partial(own_grad_body, n_x),
        out_shape=[jax.ShapeDtypeStruct((n, sub, enc), F32)]
        + [jax.ShapeDtypeStruct(code, jnp.int16)] * (n_x - 1),
        grid=(4,),
        in_specs=[
            pl.BlockSpec((n_x, n, sub, step), lambda i: (0, 0, 0, i)),
            pl.BlockSpec((enc, step), lambda i: (0, i)),
            pl.BlockSpec((n_x, n, sub, enc), lambda i: (0, 0, 0, 0)),
        ],
        out_specs=[pl.BlockSpec((n, sub, enc), lambda i: (0, 0, 0))]
        + [pl.BlockSpec(code, lambda i: (0, 0, 0, 0))] * (n_x - 1),
        scratch_shapes=[pltpu.VMEM((n_x * n * sub, enc), F32)],
        compiler_params=params(),
        cost_estimate=cost(2 * n_x * n * sub * enc * width, 2 * (enc + n_x * n * sub) * width),
        name="own_grad",
    )(d_kv, w_kv, got)
    return out[0], out[1:]


def send_body(cap, position, own, *rest):
    codes, out, notes = rest[:-2], rest[-2], rest[-1]
    n, sub, enc = own.shape
    tiles = enc // LANES
    row = lax.broadcasted_iota(jnp.int32, (SUB, LANES), 0) // (SUB // cap)
    notes[...] = jnp.zeros_like(notes)
    for r in range(n):
        total = own[r]
        for code in codes:
            power = code[tiles, r].astype(F32)
            unit = jnp.exp2(power - 15.0)
            total = total + jnp.concatenate(
                [code[e, r].astype(F32) * unit for e in range(tiles)], axis=1
            )
        coded, power = encode(total, (0, 1))
        p = position[r]
        dest, slot = p // cap, p % cap
        for e in range(tiles):
            out[dest, slot * tiles + e] = coded[:, e * LANES : (e + 1) * LANES]
        mark = jnp.broadcast_to(power, (SUB, LANES)).astype(jnp.int32)
        notes[dest] = jnp.where(row == slot, mark, notes[dest])
    for d in range(out.shape[0]):
        out[d, cap * tiles] = notes[d].astype(jnp.int16)


def send_codes(position, own, codes, n_dp, cap):
    n, sub, enc = own.shape
    shape = (n_dp, cap * (enc // LANES) + 1, SUB, LANES)
    return pl.pallas_call(
        functools.partial(send_body, cap),
        out_shape=jax.ShapeDtypeStruct(shape, jnp.int16),
        in_specs=[SMEM, VMEM] + [VMEM] * len(codes),
        out_specs=VMEM,
        scratch_shapes=[pltpu.VMEM((n_dp, SUB, LANES), jnp.int32)],
        compiler_params=params(),
        cost_estimate=cost(10 * n * sub * enc, 6 * n * sub * enc + 2 * math.prod(shape)),
        name="send_codes",
    )(position, own, *codes)


def gather_body(cap, n_chunks, asked, *rest):
    arrived, out = rest[:n_chunks], rest[n_chunks]
    tiles = out.shape[2] // LANES
    out[...] = jnp.zeros_like(out)
    n_dp = arrived[0].shape[0]
    for d in range(n_dp):
        for s in range(cap):
            slab = asked[d * cap + s]

            @pl.when(slab >= 0)
            def _():
                for c in range(n_chunks):
                    ref = arrived[c]
                    note = ref[d, cap * tiles].astype(F32)
                    at = s * (SUB // cap)
                    unit = jnp.exp2(note[at : at + 1] - 15.0)
                    for e in range(tiles):
                        value = ref[d, s * tiles + e].astype(F32) * unit
                        out[slab, pl.ds(c * SUB, SUB), pl.ds(e * LANES, LANES)] += value


def gather_grads(asked, arrived, n_slabs, enc, cap):
    n_chunks = len(arrived)
    shape = (n_slabs, n_chunks * SUB, enc)
    return pl.pallas_call(
        functools.partial(gather_body, cap, n_chunks),
        out_shape=jax.ShapeDtypeStruct(shape, F32),
        in_specs=[SMEM] + [VMEM] * n_chunks,
        out_specs=VMEM,
        compiler_params=params(),
        cost_estimate=cost(0, 8 * math.prod(shape)),
        name="gather_grads",
    )(asked, *arrived)


def on_device(queries, cotangent, table, key_weight, value_weight, owners, slots):
    n_dp = lax.axis_size("dp")
    n_tp = lax.axis_size("tensor")
    n_x = n_tp // 2
    spans = owners.shape[0]
    n_requests = 2 * spans
    n_slabs, n_tokens, enc = table.shape
    cap = max(2, (4 * spans + n_dp - 1) // n_dp)
    share = n_tokens // n_tp
    n_chunks = share // SUB

    def over_core(x):
        return lax.ppermute(x, "tensor", [(t, t ^ 1) for t in range(n_tp)])

    def over_x(x, d):
        return lax.ppermute(x, "tensor", [(t, (t + 2 * d) % n_tp) for t in range(n_tp)])

    def over_dp(x):
        return lax.all_to_all(x, "dp", split_axis=0, concat_axis=0, tiled=True)

    owner_flat = owners.reshape(n_requests)
    slot_flat = slots.reshape(n_requests)
    onehot = (owner_flat[:, None] == jnp.arange(n_dp, dtype=jnp.int32)[None, :]).astype(jnp.int32)
    within = jnp.sum((jnp.cumsum(onehot, axis=0) - onehot) * onehot, axis=1)
    position = owner_flat * cap + within
    wanted = jnp.full((n_dp * cap,), -1, jnp.int32).at[position].set(slot_flat)
    asked = over_dp(wanted.reshape(n_dp, cap)).reshape(-1)

    first = (lax.axis_index("tensor") * share).astype(jnp.int32).reshape(1)
    w_kv = jnp.concatenate([key_weight, value_weight], axis=1)
    groups = [[(0, 0), (1, 0)], [(0, d) for d in range(1, n_x)] + [(1, d) for d in range(1, n_x)]]

    kvs = []
    for sent in pack(asked, first, table, n_chunks):
        mine = compact(position, over_dp(sent))
        near = [mine, over_core(mine)]
        far = [over_x(mine, d) for d in range(1, n_x)]
        far = far + [over_core(x) for x in far]
        kvs += [project(near, w_kv), project(far, w_kv)]

    attended, d_query, d_own, d_core = attend(kvs, groups, n_x, n_chunks, queries, cotangent)

    got = [over_core(core_grad(d, w_kv)) for d in d_core]
    arrived = []
    for c in range(n_chunks):
        own, codes = own_grad(d_own[c], w_kv, got[c])
        codes = [over_x(code, n_x - d) for d, code in enumerate(codes, 1)]
        arrived.append(over_dp(send_codes(position, own, codes, n_dp, cap)))
    d_table = gather_grads(asked, arrived, n_slabs, enc, cap)
    return (attended, d_query, d_table)


def solution(mesh):
    in_specs = (
        P("dp", "tensor"),
        P("dp", "tensor"),
        P("dp", None, None),
        P(None, "tensor"),
        P(None, "tensor"),
        P("dp", None),
        P("dp", None),
    )
    out_specs = (P("dp", "tensor"), P("dp", "tensor"), P("dp", "tensor", None))
    return jax.shard_map(
        on_device, mesh=mesh, in_specs=in_specs, out_specs=out_specs, check_vma=False
    )
```

time: 517 us -> 322 us (0.62)
  the two profiles are of different devices: /device:TPU:0 before, /device:TPU:13 now
where the time goes in v1:
time: 322 us; the launch traced here: 316 us
  Pallas kernels  158 us (49%)
  blocking collectives  77.5 us (24%)
  waiting for transfers between devices  38.3 us (12%)
  starting transfers between devices  26.4 us (8%)
  local copies, waits for them, and re-layouts  12.8 us (4%)
    all_to_all x2, blocking collectives, over_dp(): return lax.all_to_all(x, 'dp', split_axis=0, concat_axis=0, tiled=True)  77.5 us
    pallas_call x1, Pallas kernels, attend(): pl.pallas_call(functools.partial(attend_body, groups, n_x, n_chunks), out...  35.2 us
    ppermute x4, waiting for transfers between devices, over_x(): lax.ppermute(x, 'tensor', [(t, (t + 2 * d) % n_tp) for t in range(n_tp)])  32.4 us
    pallas_call x2, Pallas kernels, compact(): pl.pallas_call(compact_body, out_shape=jax.ShapeDtypeStruct(shape, arrive...  31.6 us
    pallas_call x1, Pallas kernels, pack(): pl.pallas_call(functools.partial(pack_body, n_chunks, None), out_shape=[j...  30.1 us
    pallas_call x4, Pallas kernels, project(): pl.pallas_call(functools.partial(project_body, n_in), out_shape=jax.Shape...  23.6 us
    all_to_all x3, starting transfers between devices, over_dp(): return lax.all_to_all(x, 'dp', split_axis=0, concat_axis=0, tiled=True)  18.2 us
    pallas_call x2, Pallas kernels, own_grad(): pl.pallas_call(functools.partial(own_grad_body, n_x), out_shape=[jax.Shap...  15.2 us
  transfers between devices with their start and end apart: 13, of which 5 were waited for; matrix products, arithmetic and copies ran while one was open for 0% of the time, Pallas kernels for 24%

profile of v1, /device:TPU:13, one launch (start us, length us, event | category | flops | bytes accessed | tf_op | source)
XLA Modules:
  0.0 316.0 jit_solution(15688885810928283612)
XLA Ops:
  4.8 5.7 %all-to-all-start = ((s32[8,1,4]{2,1,0:T(1,128)}), s32[8,1,4]{2,1,0:T(1,128)S(1)}, u32[]{:S(2)}, u32[]{:S(2)}) async-start(s32[8,1,4]{2,1,0:T(1,128)} %bitcast.2), calls=%async_computation | async-start | bytes 8192 | tf_op jit(solution)/shard_map/all_to_all | solution.py:386
  10.4 3.2 %all-to-all-done = s32[8,1,4]{2,1,0:T(1,128)S(1)} async-done(((s32[8,1,4]{2,1,0:T(1,128)}), s32[8,1,4]{2,1,0:T(1,128)S(1)}, u32[]{:S(2)}, u32[]{:S(2)}) %all-to-all-start) | async-done | bytes 160 | tf_op jit(solution)/shard_map/all_to_all | solution.py:386
  15.4 30.1 %pack_rows.1 = (bf16[32,16,896]{2,1,0:T(8,128)(2,1)}, bf16[32,16,896]{2,1,0:T(8,128)(2,1)}) custom-call(s32[32]{0:T(128)} %reshape.54.asked, s32[1]{0:T(128)} %bitcast.3.first, bf16[16,128,896]{2,1,0:T(8,128)(2,1)} %table.1), custom_call_target="tpu_custom_call" | custom-call | bytes 3670016 | tf_op jit(solution)/shard_map/pack_rows/pallas_call | solution.py:58
  45.6 51.5 %all_to_all.29.arrived = bf16[32,16,896]{2,1,0:T(8,128)(2,1)} all-to-all(bf16[32,16,896]{2,1,0:T(8,128)(2,1)} %get-tuple-element.16), channel_id=1, replica_groups=mesh['dp'=8,'tensor'=4] {'dp'}, dimensions={0} | all-to-all | bytes 1835008 | tf_op jit(solution)/shard_map/all_to_all | solution.py:386
  97.1 6.2 %all-to-all-start.1 = ((bf16[32,16,896]{2,1,0:T(8,128)(2,1)}), bf16[32,16,896]{2,1,0:T(8,128)(2,1)S(1)}, u32[]{:S(2)}, u32[]{:S(2)}) async-start(bf16[32,16,896]{2,1,0:T(8,128)(2,1)} %get-tuple-element.15), calls=%async_computation.1 | async-start | bytes 1835008 | tf_op jit(solution)/shard_map/all_to_all | solution.py:386
  103.9 15.8 %compact_rows.3.refs_0_ = bf16[16,16,896]{2,1,0:T(8,128)(2,1)} custom-call(s32[16]{0:T(128)} %multiply_add_fusion.position, bf16[32,16,896]{2,1,0:T(8,128)(2,1)} %all_to_all.29.arrived), custom_call_target="tpu_custom_call" | custom-call | bytes 917504 | tf_op jit(solution)/shard_map/compact_rows/pallas_call | solution.py:84
  121.0 2.8 all-to-all-done.1.arrived
  124.6 15.8 %compact_rows.2.refs_0_ = bf16[16,16,896]{2,1,0:T(8,128)(2,1)} custom-call(s32[16]{0:T(128)} %multiply_add_fusion.position, bf16[32,16,896]{2,1,0:T(8,128)(2,1)} %copy-done.2), custom_call_target="tpu_custom_call" | custom-call | bytes 917504 | tf_op jit(solution)/shard_map/compact_rows/pallas_call | solution.py:84
  143.5 8.9 %collective-permute-done.1.refs_0_ = bf16[16,16,896]{2,1,0:T(8,128)(2,1)S(1)} collective-permute-done((bf16[16,16,896]{2,1,0:T(8,128)(2,1)}, bf16[16,16,896]{2,1,0:T(8,128)(2,1)S(1)}, u32[]{:S(2)}, u32[]{:S(2)}) %collective-permute-start.1) | collective-permute-done | bytes 458784 | tf_op jit(solution)/shard_map/ppermute | solution.py:383
  154.5 5.9 %project.6.refs_2_ = bf16[2,16,16,2048]{3,2,1,0:T(8,128)(2,1)} custom-call(bf16[16,16,896]{2,1,0:T(8,128)(2,1)} %compact_rows.3.refs_0_, bf16[16,16,896]{2,1,0:T(8,128)(2,1)} %copy-done.12, bf16[896,2048]{1,0:T(8,128)(2,1)} %copy-done), custom_call_target="tpu_custom_call" | custom-call | flops 1879048192 | bytes 6684672 | tf_op jit(solution)/shard_map/project/pallas_call | solution.py:110
  161.1 5.9 %project.4.refs_0_ = bf16[2,16,16,2048]{3,2,1,0:T(8,128)(2,1)} custom-call(bf16[16,16,896]{2,1,0:T(8,128)(2,1)} %compact_rows.2.refs_0_, bf16[16,16,896]{2,1,0:T(8,128)(2,1)} %copy-done.11, bf16[896,2048]{1,0:T(8,128)(2,1)} %copy-done), custom_call_target="tpu_custom_call" | custom-call | flops 1879048192 | bytes 6684672 | tf_op jit(solution)/shard_map/project/pallas_call | solution.py:110
  167.8 5.9 %project.7.refs_3_ = bf16[2,16,16,2048]{3,2,1,0:T(8,128)(2,1)} custom-call(bf16[16,16,896]{2,1,0:T(8,128)(2,1)} %copy-done.9, bf16[16,16,896]{2,1,0:T(8,128)(2,1)} %copy-done.13, bf16[896,2048]{1,0:T(8,128)(2,1)} %copy-done), custom_call_target="tpu_custom_call" | custom-call | flops 1879048192 | bytes 6684672 | tf_op jit(solution)/shard_map/project/pallas_call | solution.py:110
  174.4 5.9 %project.5.refs_1_ = bf16[2,16,16,2048]{3,2,1,0:T(8,128)(2,1)} custom-call(bf16[16,16,896]{2,1,0:T(8,128)(2,1)} %copy-done.10, bf16[16,16,896]{2,1,0:T(8,128)(2,1)} %copy-done.14, bf16[896,2048]{1,0:T(8,128)(2,1)} %copy-done), custom_call_target="tpu_custom_call" | custom-call | flops 1879048192 | bytes 6684672 | tf_op jit(solution)/shard_map/project/pallas_call | solution.py:110
  180.4 35.2 %attend.1 = (bf16[512,1024]{1,0:T(8,128)(2,1)}, bf16[512,1024]{1,0:T(8,128)(2,1)}, bf16[2,16,16,2048]{3,2,1,0:T(8,128)(2,1)}, bf16[2,16,16,2048]{3,2,1,0:T(8,128...) custom-call(bf16[2,16,16,2048]{3,2,1,0:T(8,128)(2,1)} %project.4.refs_0_, ...), custom_call_target="tpu_custom_call" | custom-call | flops 1610612736 | bytes 37748736 | tf_op jit(solution)/shard_map/attend/pallas_call | solution.py:181
  215.5 6.9 %core_grad.3 = f32[2,16,16,896]{3,2,1,0:T(8,128)} custom-call(bf16[2,16,16,2048]{3,2,1,0:T(8,128)(2,1)} %get-tuple-element.24.d_ref, bf16[896,2048]{1,0:T(8,128)(2,1)} %copy-done), custom_call_target="tpu_custom_call" | custom-call | flops 1879048192 | bytes 5767168 | tf_op jit(solution)/shard_map/core_grad/pallas_call | solution.py:252
  222.5 6.8 %core_grad.2 = f32[2,16,16,896]{3,2,1,0:T(8,128)} custom-call(bf16[2,16,16,2048]{3,2,1,0:T(8,128)(2,1)} %get-tuple-element.20.d_ref, bf16[896,2048]{1,0:T(8,128)(2,1)} %copy-done), custom_call_target="tpu_custom_call" | custom-call | flops 1879048192 | bytes 5767168 | tf_op jit(solution)/shard_map/core_grad/pallas_call | solution.py:252
  231.0 7.6 %own_grad.3 = (f32[16,16,896]{2,1,0:T(8,128)}, s16[8,16,16,128]{3,2,1,0:T(8,128)(2,1)}) custom-call(bf16[2,16,16,2048]{3,2,1,0:T(8,128)(2,1)} %get-tuple-element.23.d_ref, bf16[896,2048]{1,0:T(8,128)(2,1)} %copy-done, f32[2,16,16,896]{3,2,1,0:T(8,128)} %copy-done.6), custom_call_target="tpu_custom_call" | custom-call | flops 1879048192 | bytes 5767168 | tf_op jit(solution)/shard_map/own_grad/pallas_call | solution.py:273
  239.8 12.5 %collective-permute-done.9.rest_0_ = s16[8,16,16,128]{3,2,1,0:T(8,128)(2,1)S(1)} collective-permute-done((s16[8,16,16,128]{3,2,1,0:T(8,128)(2,1)}, s16[8,16,16,128]{3,2,1,0:T(8,128)(2,1)S(1)}, u32[]{:S(2)}, u32[]{:S(2)}) %collective-permute-start.9) | collective-permute-done | bytes 524320 | tf_op jit(solution)/shard_map/ppermute | solution.py:383
  253.1 2.7 send_codes.3
  255.8 6.3 %all-to-all-start.4 = ((s16[8,29,16,128]{3,2,1,0:T(8,128)(2,1)}), s16[8,29,16,128]{3,2,1,0:T(8,128)(2,1)S(1)}, u32[]{:S(2)}, u32[]{:S(2)}) async-start(s16[8,29,16,128]{3,2,1,0:T(8,128)(2,1)} %send_codes.3), calls=%async_computation.4 | async-start | bytes 1900544 | tf_op jit(solution)/shard_map/all_to_all | solution.py:386
  263.4 7.6 %own_grad.2 = (f32[16,16,896]{2,1,0:T(8,128)}, s16[8,16,16,128]{3,2,1,0:T(8,128)(2,1)}) custom-call(bf16[2,16,16,2048]{3,2,1,0:T(8,128)(2,1)} %get-tuple-element.19.d_ref, bf16[896,2048]{1,0:T(8,128)(2,1)} %copy-done, f32[2,16,16,896]{3,2,1,0:T(8,128)} %copy-done.5), custom_call_target="tpu_custom_call" | custom-call | flops 1879048192 | bytes 5767168 | tf_op jit(solution)/shard_map/own_grad/pallas_call | solution.py:273
  272.2 11.0 %collective-permute-done.7.rest_0_ = s16[8,16,16,128]{3,2,1,0:T(8,128)(2,1)S(1)} collective-permute-done((s16[8,16,16,128]{3,2,1,0:T(8,128)(2,1)}, s16[8,16,16,128]{3,2,1,0:T(8,128)(2,1)S(1)}, u32[]{:S(2)}, u32[]{:S(2)}) %collective-permute-start.7) | collective-permute-done | bytes 524320 | tf_op jit(solution)/shard_map/ppermute | solution.py:383
  286.6 26.0 %all_to_all.30.rest_0_ = s16[8,29,16,128]{3,2,1,0:T(8,128)(2,1)} all-to-all(s16[8,29,16,128]{3,2,1,0:T(8,128)(2,1)} %send_codes.2), channel_id=1, replica_groups=mesh['dp'=8,'tensor'=4] {'dp'}, dimensions={0} | all-to-all | bytes 1900544 | tf_op jit(solution)/shard_map/all_to_all | solution.py:386
  312.7 3.4 %gather_grads.1 = f32[16,32,896]{2,1,0:T(8,128)} custom-call(s32[32]{0:T(128)} %reshape.54.asked, s16[8,29,16,128]{3,2,1,0:T(8,128)(2,1)} %all_to_all.30.rest_0_, s16[8,29,16,128]{3,2,1,0:T(8,128)(2,1)} %copy-done.1), custom_call_target="tpu_custom_call" | custom-call | bytes 3670016 | tf_op jit(solution)/shard_map/gather_grads/pallas_call | solution.py:357
  (68 shorter events, 25.8 us)
Async XLA Ops:
  4.8 8.8 %all-to-all-start = ((s32[8,1,4]{2,1,0:T(1,128)}), s32[8,1,4]{2,1,0:T(1,128)S(1)}, u32[]{:S(2)}, u32[]{:S(2)}) async-start(s32[8,1,4]{2,1,0:T(1,128)} %bitcast.2), calls=%async_computation | async-start | bytes 8192 | tf_op jit(solution)/shard_map/all_to_all | solution.py:386
  97.1 45.4 %copy-start.3 = (bf16[896,1024]{1,0:T(8,128)(2,1)S(1)}, bf16[896,1024]{1,0:T(8,128)(2,1)}, u32[]{:S(2)}) copy-start(bf16[896,1024]{1,0:T(8,128)(2,1)} %param.10) | copy-start | bytes 5505028
  97.1 26.6 %all-to-all-start.1 = ((bf16[32,16,896]{2,1,0:T(8,128)(2,1)}), bf16[32,16,896]{2,1,0:T(8,128)(2,1)S(1)}, u32[]{:S(2)}, u32[]{:S(2)}) async-start(bf16[32,16,896]{2,1,0:T(8,128)(2,1)} %get-tuple-element.15), calls=%async_computation.1 | async-start | bytes 1835008 | tf_op jit(solution)/shard_map/all_to_all | solution.py:386
  119.7 23.1 %collective-permute-start.4 = (bf16[16,16,896]{2,1,0:T(8,128)(2,1)}, bf16[16,16,896]{2,1,0:T(8,128)(2,1)S(1)}, u32[]{:S(2)}, u32[]{:S(2)}) collective-permute-start(bf16[16,16,896]{2,1,0:T(8,128)(2,1)} %compact_rows.3.refs_0_), channel_id=1, source_target_pairs={{0,2},{1,3},{2,0},{3,1},{4,6},{5,7},{6,4},{7,5},{8,10},{9,11},{10,... | collective-permute-start | bytes 1376264 | tf_op jit(solution)/shard_map/ppermute | solution.py:383
  123.7 0.9 copy-start.2
  140.5 2.9 copy-start.4
  140.5 11.9 %collective-permute-start.1 = (bf16[16,16,896]{2,1,0:T(8,128)(2,1)}, bf16[16,16,896]{2,1,0:T(8,128)(2,1)S(1)}, u32[]{:S(2)}, u32[]{:S(2)}) collective-permute-start(bf16[16,16,896]{2,1,0:T(8,128)(2,1)} %compact_rows.2.refs_0_), channel_id=1, source_target_pairs={{0,2},{1,3},{2,0},{3,1},{4,6},{5,7},{6,4},{7,5},{8,10},{9,11},{10,... | collective-permute-start | bytes 1376264 | tf_op jit(solution)/shard_map/ppermute | solution.py:383
  141.8 11.9 %collective-permute-start.3 = (bf16[16,16,896]{2,1,0:T(8,128)(2,1)}, bf16[16,16,896]{2,1,0:T(8,128)(2,1)S(1)}, u32[]{:S(2)}, u32[]{:S(2)}) collective-permute-start(bf16[16,16,896]{2,1,0:T(8,128)(2,1)} %compact_rows.3.refs_0_), channel_id=1, source_target_pairs={{0,1},{1,0},{2,3},{3,2},{4,5},{5,4},{6,7},{7,6},{8,9},{9,8},{10,11... | collective-permute-start | bytes 1376264 | tf_op jit(solution)/shard_map/ppermute | solution.py:380
  142.5 17.8 %collective-permute-start = (bf16[16,16,896]{2,1,0:T(8,128)(2,1)}, bf16[16,16,896]{2,1,0:T(8,128)(2,1)S(1)}, u32[]{:S(2)}, u32[]{:S(2)}) collective-permute-start(bf16[16,16,896]{2,1,0:T(8,128)(2,1)} %compact_rows.2.refs_0_), channel_id=1, source_target_pairs={{0,1},{1,0},{2,3},{3,2},{4,5},{5,4},{6,7},{7,6},{8,9},{9,8},{10,11... | collective-permute-start | bytes 1376264 | tf_op jit(solution)/shard_map/ppermute | solution.py:380
  142.8 17.6 %copy-start.9 = (bf16[16,16,896]{2,1,0:T(8,128)(2,1)}, bf16[16,16,896]{2,1,0:T(8,128)(2,1)S(1)}, u32[]{:S(2)}) copy-start(bf16[16,16,896]{2,1,0:T(8,128)(2,1)S(1)} %collective-permute-done.4.refs_0_) | copy-start | bytes 1376260
  142.8 24.3 %collective-permute-start.5 = (bf16[16,16,896]{2,1,0:T(8,128)(2,1)S(1)}, bf16[16,16,896]{2,1,0:T(8,128)(2,1)S(1)}, u32[]{:S(2)}, u32[]{:S(2)}) collective-permute-start(bf16[16,16,896]{2,1,0:T(8,128)(2,1)S(1)} %collective-permute-done.4.refs_0_), channel_id=1, source_target_pairs={{0,1},{1,0},{2,3},{3,2},{4,5},{5,4},{6,7},{7,6},{8,9},{9,8},{10,11... | collective-permute-start | bytes 1376264 | tf_op jit(solution)/shard_map/ppermute | solution.py:380
  143.5 10.2 %copy-start = (bf16[896,2048]{1,0:T(8,128)(2,1)}, bf16[896,2048]{1,0:T(8,128)(2,1)S(1)}, u32[]{:S(2)}) copy-start(bf16[896,2048]{1,0:T(8,128)(2,1)S(1)} %constant_dynamic-update-slice_fusion.refs_2_.w_ref) | copy-start | bytes 11010052
  152.4 8.0 %copy-start.10 = (bf16[16,16,896]{2,1,0:T(8,128)(2,1)}, bf16[16,16,896]{2,1,0:T(8,128)(2,1)S(1)}, u32[]{:S(2)}) copy-start(bf16[16,16,896]{2,1,0:T(8,128)(2,1)S(1)} %collective-permute-done.1.refs_0_) | copy-start | bytes 1376260
  152.4 21.3 %collective-permute-start.2 = (bf16[16,16,896]{2,1,0:T(8,128)(2,1)S(1)}, bf16[16,16,896]{2,1,0:T(8,128)(2,1)S(1)}, u32[]{:S(2)}, u32[]{:S(2)}) collective-permute-start(bf16[16,16,896]{2,1,0:T(8,128)(2,1)S(1)} %collective-permute-done.1.refs_0_), channel_id=1, source_target_pairs={{0,1},{1,0},{2,3},{3,2},{4,5},{5,4},{6,7},{7,6},{8,9},{9,8},{10,11... | collective-permute-start | bytes 1376264 | tf_op jit(solution)/shard_map/ppermute | solution.py:380
  222.4 7.3 %collective-permute-start.8 = (f32[2,16,16,896]{3,2,1,0:T(8,128)}, f32[2,16,16,896]{3,2,1,0:T(8,128)S(1)}, u32[]{:S(2)}, u32[]{:S(2)}) collective-permute-start(f32[2,16,16,896]{3,2,1,0:T(8,128)} %core_grad.3), channel_id=1, source_target_pairs={{0,1},{1,0},{2,3},{3,2},{4,5},{5,4},{6,7},{7,6},{8,9},{9,8},{10,11... | collective-permute-start | bytes 5505032 | tf_op jit(solution)/shard_map/ppermute | solution.py:380
  229.3 32.9 %collective-permute-start.6 = (f32[2,16,16,896]{3,2,1,0:T(8,128)}, f32[2,16,16,896]{3,2,1,0:T(8,128)S(1)}, u32[]{:S(2)}, u32[]{:S(2)}) collective-permute-start(f32[2,16,16,896]{3,2,1,0:T(8,128)} %core_grad.2), channel_id=1, source_target_pairs={{0,1},{1,0},{2,3},{3,2},{4,5},{5,4},{6,7},{7,6},{8,9},{9,8},{10,11... | collective-permute-start | bytes 5505032 | tf_op jit(solution)/shard_map/ppermute | solution.py:380
  229.7 1.3 copy-start.6
  238.6 13.7 %collective-permute-start.9 = (s16[8,16,16,128]{3,2,1,0:T(8,128)(2,1)}, s16[8,16,16,128]{3,2,1,0:T(8,128)(2,1)S(1)}, u32[]{:S(2)}, u32[]{:S(2)}) collective-permute-start(s16[8,16,16,128]{3,2,1,0:T(8,128)(2,1)} %get-tuple-element.26), channel_id=1, source_target_pairs={{0,2},{1,3},{2,0},{3,1},{4,6},{5,7},{6,4},{7,5},{8,10},{9,11},{10,... | collective-permute-start | bytes 1572872 | tf_op jit(solution)/shard_map/ppermute | solution.py:383
  252.3 0.8 copy-start.8
  255.8 30.9 %all-to-all-start.4 = ((s16[8,29,16,128]{3,2,1,0:T(8,128)(2,1)}), s16[8,29,16,128]{3,2,1,0:T(8,128)(2,1)S(1)}, u32[]{:S(2)}, u32[]{:S(2)}) async-start(s16[8,29,16,128]{3,2,1,0:T(8,128)(2,1)} %send_codes.3), calls=%async_computation.4 | async-start | bytes 1900544 | tf_op jit(solution)/shard_map/all_to_all | solution.py:386
  262.1 1.2 copy-start.5
  271.0 12.2 %collective-permute-start.7 = (s16[8,16,16,128]{3,2,1,0:T(8,128)(2,1)}, s16[8,16,16,128]{3,2,1,0:T(8,128)(2,1)S(1)}, u32[]{:S(2)}, u32[]{:S(2)}) collective-permute-start(s16[8,16,16,128]{3,2,1,0:T(8,128)(2,1)} %get-tuple-element.22), channel_id=1, source_target_pairs={{0,2},{1,3},{2,0},{3,1},{4,6},{5,7},{6,4},{7,5},{8,10},{9,11},{10,... | collective-permute-start | bytes 1572872 | tf_op jit(solution)/shard_map/ppermute | solution.py:383
  283.2 0.8 copy-start.7
  286.6 26.0 %copy-start.1 = (s16[8,29,16,128]{3,2,1,0:T(8,128)(2,1)}, s16[8,29,16,128]{3,2,1,0:T(8,128)(2,1)S(1)}, u32[]{:S(2)}) copy-start(s16[8,29,16,128]{3,2,1,0:T(8,128)(2,1)S(1)} %all-to-all-done.4.rest_1_) | copy-start | bytes 2850820
  (4 other events, 3.1 us)

commit v2 on v1

v2 whole, which is shorter than its diff:
```python
import functools
import math

import jax
import jax.numpy as jnp
from jax import lax
from jax.experimental import pallas as pl
from jax.experimental.pallas import tpu as pltpu
from jax.sharding import PartitionSpec as P

HD = 128
SPAN = 64
SUB = 16
LANES = 128
VMEM_LIMIT = 56 * 1024 * 1024
F32 = jnp.float32
BF16 = jnp.bfloat16

ANY = pl.BlockSpec(memory_space=pl.ANY)
SMEM = pl.BlockSpec(memory_space=pltpu.SMEM)
VMEM = pl.BlockSpec(memory_space=pltpu.VMEM)


def params():
    return pltpu.CompilerParams(vmem_limit_bytes=VMEM_LIMIT)


def cost(flops, nbytes):
    return pl.CostEstimate(flops=int(flops), bytes_accessed=int(nbytes), transcendentals=0)


def pack_body(n_chunks, asked, first, table, *rest):
    outs, sem = rest[:n_chunks], rest[n_chunks]
    n = asked.shape[0]
    base = first[0]

    def each(act):
        for c in range(n_chunks):
            row = pl.multiple_of(base + c * SUB, SUB)
            for s in range(n):
                slab = asked[s]

                @pl.when(slab >= 0)
                def _():
                    act(
                        pltpu.make_async_copy(
                            table.at[slab, pl.ds(row, SUB)], outs[c].at[s], sem.at[c, s]
                        )
                    )

    each(lambda copy: copy.start())
    each(lambda copy: copy.wait())


def pack(asked, first, table, n_chunks):
    n = asked.shape[0]
    enc = table.shape[2]
    return pl.pallas_call(
        functools.partial(pack_body, n_chunks),
        out_shape=[jax.ShapeDtypeStruct((n, SUB, enc), table.dtype)] * n_chunks,
        in_specs=[SMEM, SMEM, ANY],
        out_specs=[VMEM] * n_chunks,
        scratch_shapes=[pltpu.SemaphoreType.DMA((n_chunks, n))],
        compiler_params=params(),
        cost_estimate=cost(0, 4 * n_chunks * n * SUB * enc),
        name="pack_rows",
    )(asked, first, table)


def compact_body(position, arrived, out, sem):
    n = position.shape[0]
    copies = [
        pltpu.make_async_copy(arrived.at[position[r]], out.at[r], sem.at[r]) for r in range(n)
    ]
    for copy in copies:
        copy.start()
    for copy in copies:
        copy.wait()


def compact(position, arrived):
    n = position.shape[0]
    shape = (n,) + arrived.shape[1:]
    return pl.pallas_call(
        compact_body,
        out_shape=jax.ShapeDtypeStruct(shape, arrived.dtype),
        in_specs=[SMEM, ANY],
        out_specs=VMEM,
        scratch_shapes=[pltpu.SemaphoreType.DMA((n,))],
        compiler_params=params(),
        cost_estimate=cost(0, 4 * math.prod(shape)),
        name="compact_rows",
    )(position, arrived)


def project_body(n_in, *refs):
    w, out = refs[n_in], refs[n_in + 1]
    n, sub, enc = refs[0].shape
    rows = jnp.concatenate([ref[...].reshape(n * sub, enc) for ref in refs[:n_in]], axis=0)
    res = jnp.dot(rows, w[...], preferred_element_type=F32)
    out[...] = res.astype(BF16).reshape(out.shape)


def project(pieces, w_kv):
    n_in = len(pieces)
    n, sub, enc = pieces[0].shape
    width = w_kv.shape[1]
    step = width // 4
    return pl.pallas_call(
        functools.partial(project_body, n_in),
        out_shape=jax.ShapeDtypeStruct((n_in, n, sub, width), BF16),
        grid=(4,),
        in_specs=[pl.BlockSpec((n, sub, enc), lambda i: (0, 0, 0))] * n_in
        + [pl.BlockSpec((enc, step), lambda i: (0, i))],
        out_specs=pl.BlockSpec((n_in, n, sub, step), lambda i: (0, 0, 0, i)),
        compiler_params=params(),
        cost_estimate=cost(
            2 * n_in * n * sub * enc * width, 2 * (n_in * n * sub * (enc + width) + enc * width)
        ),
        name="project",
    )(*pieces, w_kv)


def attend_body(places, n_kv, *refs):
    kvs = refs[:n_kv]
    q_ref, g_ref, att_ref, dq_ref = refs[n_kv : n_kv + 4]
    grads = refs[n_kv + 4 :]
    width = q_ref.shape[1]
    scale = 1.0 / math.sqrt(HD)
    heads = width // HD
    group = min(4, heads)

    def keys_of(col):
        parts = [ref[:, :, :, pl.ds(col, HD)].reshape(-1, HD) for ref in kvs]
        return jnp.concatenate(parts, axis=0)

    def put(col, grad):
        for at, (ref, i) in enumerate(places):
            block = grad[at * 2 * SUB : (at + 1) * 2 * SUB]
            grads[ref][i, :, :, pl.ds(col, HD)] = block.reshape(2, SUB, HD)

    last = (((1,), (1,)), ((), ()))
    first = (((0,), (0,)), ((), ()))

    def dot(a, b, dims=(((1,), (0,)), ((), ()))):
        return lax.dot_general(a, b, dims, preferred_element_type=F32)

    for h0 in range(0, heads, group):
        hs = range(h0, h0 + group)
        q = [q_ref[:, pl.ds(h * HD, HD)] for h in hs]
        g = [g_ref[:, pl.ds(h * HD, HD)] for h in hs]
        k = [keys_of(h * HD) for h in hs]
        v = [keys_of(width + h * HD) for h in hs]
        s = jnp.concatenate([dot(a, b, last) for a, b in zip(q, k)], axis=0) * scale
        dw = jnp.concatenate([dot(a, b, last) for a, b in zip(g, v)], axis=0)
        e = jnp.exp(s - jnp.max(s, axis=1, keepdims=True))
        p = e * (1.0 / jnp.sum(e, axis=1, keepdims=True))
        rs = jnp.sum(dw * p, axis=1, keepdims=True)
        w = p.astype(BF16)
        ds = (p * (dw - rs) * scale).astype(BF16)
        ws = [w[i * SPAN : (i + 1) * SPAN] for i in range(group)]
        dss = [ds[i * SPAN : (i + 1) * SPAN] for i in range(group)]
        att = [dot(a, b).astype(BF16) for a, b in zip(ws, v)]
        dq = [dot(a, b).astype(BF16) for a, b in zip(dss, k)]
        dk = [dot(a, b, first).astype(BF16) for a, b in zip(dss, q)]
        dv = [dot(a, b, first).astype(BF16) for a, b in zip(ws, g)]
        for i, h in enumerate(hs):
            att_ref[:, pl.ds(h * HD, HD)] = att[i]
            dq_ref[:, pl.ds(h * HD, HD)] = dq[i]
            put(h * HD, dk[i])
            put(width + h * HD, dv[i])


def attend(kvs, places, sizes, queries, cotangent):
    tokens, width = queries.shape
    spans = tokens // SPAN
    n = kvs[0].shape[1]
    rows = pl.BlockSpec((SPAN, width), lambda i: (i, 0))

    def kv_block(pieces):
        return pl.BlockSpec((pieces, 2, SUB, 2 * width), lambda i: (0, i, 0, 0))

    keys = len(places) * 2 * SUB
    out = pl.pallas_call(
        functools.partial(attend_body, places, len(kvs)),
        out_shape=[jax.ShapeDtypeStruct((tokens, width), BF16)] * 2
        + [jax.ShapeDtypeStruct((size, n, SUB, 2 * width), BF16) for size in sizes],
        grid=(spans,),
        in_specs=[kv_block(kv.shape[0]) for kv in kvs] + [rows, rows],
        out_specs=[rows, rows] + [kv_block(size) for size in sizes],
        compiler_params=params(),
        cost_estimate=cost(12 * tokens * width * keys, 8 * tokens * width + 8 * spans * keys * 2 * width),
        name="attend",
    )(*kvs, queries, cotangent)
    return out[0], out[1], out[2:]


def encode(x, axes):
    top = jnp.maximum(jnp.max(jnp.abs(x), axis=axes, keepdims=True), 1e-30)
    power = jnp.floor(jnp.log2(top)) + 1.0
    code = jnp.clip(jnp.round(x * jnp.exp2(15.0 - power)), -32767.0, 32767.0)
    return code.astype(jnp.int32).astype(jnp.int16), power


def grad_body(kind, *refs):
    d_ref, w_ref = refs[:2]
    acc = refs[-1]
    k = pl.program_id(0)
    pieces, n, sub, step = d_ref.shape
    rows = d_ref[...].reshape(pieces * n * sub, step)
    part = jnp.dot(rows, w_ref[...], preferred_element_type=F32)

    @pl.when(k == 0)
    def _():
        acc[...] = part

    @pl.when(k > 0)
    def _():
        acc[...] += part

    @pl.when(k == pl.num_programs(0) - 1)
    def _():
        full = acc[...].reshape(pieces, n, sub, acc.shape[1])
        if kind == "plain":
            refs[2][...] = full
        elif kind == "add":
            refs[3][...] = full + refs[2][...]
        else:
            for i in range(pieces):
                code, power = encode(full[i] + refs[2][i], (1, 2))
                out = refs[3 + i]
                tiles = out.shape[0] - 1
                for e in range(tiles):
                    out[e] = code[:, :, e * LANES : (e + 1) * LANES]
                note = jnp.broadcast_to(power.reshape(n, 1, 1), (n, sub, LANES))
                out[tiles] = note.astype(jnp.int32).astype(jnp.int16)


def grad(kind, d_kv, w_t, got=None):
    pieces, n, sub, width = d_kv.shape
    enc = w_t.shape[1]
    step = width // 4
    full = (pieces, n, sub, enc)
    whole = pl.BlockSpec(full, lambda i: (0, 0, 0, 0))
    if kind == "code":
        code = (enc // LANES + 1, n, sub, LANES)
        out_shape = [jax.ShapeDtypeStruct(code, jnp.int16)] * pieces
        out_specs = [pl.BlockSpec(code, lambda i: (0, 0, 0, 0))] * pieces
    else:
        out_shape, out_specs = jax.ShapeDtypeStruct(full, F32), whole
    return pl.pallas_call(
        functools.partial(grad_body, kind),
        out_shape=out_shape,
        grid=(4,),
        in_specs=[
            pl.BlockSpec((pieces, n, sub, step), lambda i: (0, 0, 0, i)),
            pl.BlockSpec((step, enc), lambda i: (i, 0)),
        ]
        + [whole] * (got is not None),
        out_specs=out_specs,
        scratch_shapes=[pltpu.VMEM((pieces * n * sub, enc), F32)],
        compiler_params=params(),
        cost_estimate=cost(2 * pieces * n * sub * enc * width, 2 * (enc + pieces * n * sub) * width),
        name="grad_" + kind,
    )(d_kv, w_t, *([] if got is None else [got]))


def send_body(cap, chunk, position, own, *rest):
    codes, out, notes = rest[:-2], rest[-2], rest[-1]
    n, sub, enc = own.shape[1:]
    tiles = enc // LANES
    row = lax.broadcasted_iota(jnp.int32, (SUB, LANES), 0) // (SUB // cap)
    notes[...] = jnp.zeros_like(notes)
    for r in range(n):
        total = own[chunk, r]
        for code in codes:
            power = code[tiles, r].astype(F32)
            unit = jnp.exp2(power - 15.0)
            total = total + jnp.concatenate(
                [code[e, r].astype(F32) * unit for e in range(tiles)], axis=1
            )
        coded, power = encode(total, (0, 1))
        p = position[r]
        dest, slot = p // cap, p % cap
        for e in range(tiles):
            out[dest, slot * tiles + e] = coded[:, e * LANES : (e + 1) * LANES]
        mark = jnp.broadcast_to(power, (SUB, LANES)).astype(jnp.int32)
        notes[dest] = jnp.where(row == slot, mark, notes[dest])
    for d in range(out.shape[0]):
        out[d, cap * tiles] = notes[d].astype(jnp.int16)


def send_codes(chunk, position, own, codes, n_dp, cap):
    n, sub, enc = own.shape[1:]
    shape = (n_dp, cap * (enc // LANES) + 1, SUB, LANES)
    return pl.pallas_call(
        functools.partial(send_body, cap, chunk),
        out_shape=jax.ShapeDtypeStruct(shape, jnp.int16),
        in_specs=[SMEM, VMEM] + [VMEM] * len(codes),
        out_specs=VMEM,
        scratch_shapes=[pltpu.VMEM((n_dp, SUB, LANES), jnp.int32)],
        compiler_params=params(),
        cost_estimate=cost(10 * n * sub * enc, 6 * n * sub * enc + 2 * math.prod(shape)),
        name="send_codes",
    )(position, own, *codes)


def gather_body(cap, n_chunks, asked, *rest):
    arrived, out = rest[:n_chunks], rest[n_chunks]
    tiles = out.shape[2] // LANES
    out[...] = jnp.zeros_like(out)
    n_dp = arrived[0].shape[0]
    for d in range(n_dp):
        for s in range(cap):
            slab = asked[d * cap + s]

            @pl.when(slab >= 0)
            def _():
                for c in range(n_chunks):
                    ref = arrived[c]
                    note = ref[d, cap * tiles].astype(F32)
                    at = s * (SUB // cap)
                    unit = jnp.exp2(note[at : at + 1] - 15.0)
                    for e in range(tiles):
                        value = ref[d, s * tiles + e].astype(F32) * unit
                        out[slab, pl.ds(c * SUB, SUB), pl.ds(e * LANES, LANES)] += value


def gather_grads(asked, arrived, n_slabs, enc, cap):
    n_chunks = len(arrived)
    shape = (n_slabs, n_chunks * SUB, enc)
    return pl.pallas_call(
        functools.partial(gather_body, cap, n_chunks),
        out_shape=jax.ShapeDtypeStruct(shape, F32),
        in_specs=[SMEM] + [VMEM] * n_chunks,
        out_specs=VMEM,
        compiler_params=params(),
        cost_estimate=cost(0, 8 * math.prod(shape)),
        name="gather_grads",
    )(asked, *arrived)


def on_device(queries, cotangent, table, key_weight, value_weight, owners, slots):
    n_dp = lax.axis_size("dp")
    n_tp = lax.axis_size("tensor")
    n_x = n_tp // 2
    spans = owners.shape[0]
    n_requests = 2 * spans
    n_slabs, n_tokens, enc = table.shape
    cap = max(2, (4 * spans + n_dp - 1) // n_dp)
    share = n_tokens // n_tp
    n_chunks = share // SUB

    def over_core(x):
        return lax.ppermute(x, "tensor", [(t, t ^ 1) for t in range(n_tp)])

    def over_x(x, d):
        return lax.ppermute(x, "tensor", [(t, (t + 2 * d) % n_tp) for t in range(n_tp)])

    def over_dp(x):
        return lax.all_to_all(x, "dp", split_axis=0, concat_axis=0, tiled=True)

    owner_flat = owners.reshape(n_requests)
    slot_flat = slots.reshape(n_requests)
    onehot = (owner_flat[:, None] == jnp.arange(n_dp, dtype=jnp.int32)[None, :]).astype(jnp.int32)
    within = jnp.sum((jnp.cumsum(onehot, axis=0) - onehot) * onehot, axis=1)
    position = owner_flat * cap + within
    wanted = jnp.full((n_dp * cap,), -1, jnp.int32).at[position].set(slot_flat)
    asked = over_dp(wanted.reshape(n_dp, cap)).reshape(-1)

    first = (lax.axis_index("tensor") * share).astype(jnp.int32).reshape(1)
    w_kv = jnp.concatenate([key_weight, value_weight], axis=1)
    w_t = w_kv.T

    def place(c, kind, d):
        return (kind, c) if d == 0 else (2 + kind, c * (n_x - 1) + d - 1)

    kvs, places = [], []
    for c, sent in enumerate(pack(asked, first, table, n_chunks)):
        mine = compact(position, over_dp(sent))
        near = [mine, over_core(mine)]
        far = [over_x(mine, d) for d in range(1, n_x)]
        far = far + [over_core(x) for x in far]
        near_at = [place(c, kind, 0) for kind in range(2)]
        far_at = [place(c, kind, d) for kind in range(2) for d in range(1, n_x)]
        if c < n_chunks - 1:
            kvs.append(project(near + far, w_kv))
        else:
            kvs += [project(near, w_kv), project(far, w_kv)]
        places += near_at + far_at

    sizes = [n_chunks, n_chunks, n_chunks * (n_x - 1), n_chunks * (n_x - 1)]
    attended, d_query, grads = attend(kvs, places, sizes, queries, cotangent)
    own_near, core_near, own_far, core_far = grads

    far_got = over_core(grad("plain", core_far, w_t))
    near_got = over_core(grad("plain", core_near, w_t))
    codes = grad("code", own_far, w_t, far_got)
    own = grad("add", own_near, w_t, near_got)
    arrived = []
    for c in range(n_chunks):
        got = [over_x(codes[c * (n_x - 1) + d - 1], n_x - d) for d in range(1, n_x)]
        arrived.append(over_dp(send_codes(c, position, own, got, n_dp, cap)))
    d_table = gather_grads(asked, arrived, n_slabs, enc, cap)
    return (attended, d_query, d_table)


def solution(mesh):
    in_specs = (
        P("dp", "tensor"),
        P("dp", "tensor"),
        P("dp", None, None),
        P(None, "tensor"),
        P(None, "tensor"),
        P("dp", None),
        P("dp", None),
    )
    out_specs = (P("dp", "tensor"), P("dp", "tensor"), P("dp", "tensor", None))
    return jax.shard_map(
        on_device, mesh=mesh, in_specs=in_specs, out_specs=out_specs, check_vma=False
    )
```

time: 322 us -> 239 us (0.74)
  the two profiles are of different devices: /device:TPU:13 before, /device:TPU:0 now
where the time goes in v2:
time: 239 us; the launch traced here: 237 us
  Pallas kernels  80.7 us (34%)
  blocking collectives  53.9 us (23%)
  waiting for transfers between devices  48 us (20%)
  starting transfers between devices  23.7 us (10%)
  local copies, waits for them, and re-layouts  22.3 us (9%)
  other arithmetic  7.32 us (3%)
    all_to_all x2, blocking collectives, over_dp(): return lax.all_to_all(x, 'dp', split_axis=0, concat_axis=0, tiled=True)  53.9 us
    all_to_all x3, waiting for transfers between devices, over_dp(): return lax.all_to_all(x, 'dp', split_axis=0, concat_axis=0, tiled=True)  30.7 us
    pallas_call x4, Pallas kernels, grad(): pl.pallas_call(functools.partial(grad_body, kind), out_shape=out_shape, g...  28.4 us
    pallas_call x3, Pallas kernels, project(): pl.pallas_call(functools.partial(project_body, n_in), out_shape=jax.Shape...  20 us
    ppermute x4, waiting for transfers between devices, over_x(): lax.ppermute(x, 'tensor', [(t, (t + 2 * d) % n_tp) for t in range(n_tp)])  17.3 us
    all_to_all x3, starting transfers between devices, over_dp(): return lax.all_to_all(x, 'dp', split_axis=0, concat_axis=0, tiled=True)  16.4 us
    pallas_call x1, Pallas kernels, attend(): pl.pallas_call(functools.partial(attend_body, places, len(kvs)), out_shap...  14.4 us
    unnamed x24, local copies, waits for them, and re-layouts  13.4 us
  transfers between devices with their start and end apart: 13, of which 6 were waited for; matrix products, arithmetic and copies ran while one was open for 8% of the time, Pallas kernels for 18%

profile of v2, /device:TPU:0, one launch (start us, length us, event | category | flops | bytes accessed | tf_op | source)
XLA Modules:
  0.0 236.7 jit_solution(13528131565387561567)
XLA Ops:
  4.8 7.3 %all-to-all-start = ((s32[8,1,4]{2,1,0:T(1,128)}), s32[8,1,4]{2,1,0:T(1,128)S(1)}, u32[]{:S(2)}, u32[]{:S(2)}) async-start(s32[8,1,4]{2,1,0:T(1,128)} %bitcast.2), calls=%async_computation | async-start | bytes 8192 | tf_op jit(solution)/shard_map/all_to_all | solution.py:361
  12.0 6.4 %all-to-all-done = s32[8,1,4]{2,1,0:T(1,128)S(1)} async-done(((s32[8,1,4]{2,1,0:T(1,128)}), s32[8,1,4]{2,1,0:T(1,128)S(1)}, u32[]{:S(2)}, u32[]{:S(2)}) %all-to-all-start) | async-done | bytes 160 | tf_op jit(solution)/shard_map/all_to_all | solution.py:361
  20.2 3.7 %pack_rows.1 = (bf16[32,16,896]{2,1,0:T(8,128)(2,1)}, bf16[32,16,896]{2,1,0:T(8,128)(2,1)}) custom-call(s32[32]{0:T(128)} %reshape.54.asked, s32[1]{0:T(128)} %bitcast.3.first, bf16[16,128,896]{2,1,0:T(8,128)(2,1)} %table.1), custom_call_target="tpu_custom_call" | custom-call | bytes 3670016 | tf_op jit(solution)/shard_map/pack_rows/pallas_call | solution.py:58
  23.9 26.4 %all_to_all.29.arrived = bf16[32,16,896]{2,1,0:T(8,128)(2,1)} all-to-all(bf16[32,16,896]{2,1,0:T(8,128)(2,1)} %get-tuple-element.14), channel_id=1, replica_groups=mesh['dp'=8,'tensor'=4] {'dp'}, dimensions={0} | all-to-all | bytes 1835008 | tf_op jit(solution)/shard_map/all_to_all | solution.py:361
  50.3 3.6 %all-to-all-start.1 = ((bf16[32,16,896]{2,1,0:T(8,128)(2,1)}), bf16[32,16,896]{2,1,0:T(8,128)(2,1)S(1)}, u32[]{:S(2)}, u32[]{:S(2)}) async-start(bf16[32,16,896]{2,1,0:T(8,128)(2,1)} %get-tuple-element.13), calls=%async_computation.1 | async-start | bytes 1835008 | tf_op jit(solution)/shard_map/all_to_all | solution.py:361
  58.5 17.6 %all-to-all-done.1.arrived = bf16[32,16,896]{2,1,0:T(8,128)(2,1)S(1)} async-done(((bf16[32,16,896]{2,1,0:T(8,128)(2,1)}), bf16[32,16,896]{2,1,0:T(8,128)(2,1)S(1)}, u32[]{:S(2)}, u32[]{:S(2)}) %all-to-all-start.1) | async-done | bytes 917536 | tf_op jit(solution)/shard_map/all_to_all | solution.py:361
  81.2 3.1 %copy.30 = bf16[896,1024]{0,1:T(8,128)(2,1)S(1)} copy(bf16[896,1024]{1,0:T(8,128)(2,1)} %param.10) | data formatting | bytes 3670016 | tf_op args[3]
  84.3 3.9 %copy.31 = bf16[896,1024]{0,1:T(8,128)(2,1)} copy(bf16[896,1024]{1,0:T(8,128)(2,1)} %param.11) | data formatting | bytes 3670016 | tf_op args[4]
  90.2 5.1 %fusion.4 = (bf16[2048,896]{1,0:T(8,128)(2,1)}, bf16[896,2048]{0,1:T(8,128)(2,1)}) fusion(bf16[896,1024]{0,1:T(8,128)(2,1)} %copy.31, bf16[896,1024]{0,1:T(8,128)(2,1)S(1)} %copy.30), kind=kLoop, calls=%fused_computation.12 | loop fusion | flops 7340032 | bytes 11010048 | tf_op jit(solution)/shard_map/transpose | solution.py:373
  95.3 6.1 %copy.32.refs_4_.refs_2_ = bf16[896,2048]{1,0:T(8,128)(2,1)} copy(bf16[896,2048]{0,1:T(8,128)(2,1)} %get-tuple-element.24) | data formatting | bytes 7340032 | tf_op jit(solution)/shard_map/concatenate | solution.py:372
  101.4 5.9 %project.4.refs_1_ = bf16[2,16,16,2048]{3,2,1,0:T(8,128)(2,1)} custom-call(bf16[16,16,896]{2,1,0:T(8,128)(2,1)} %compact_rows.3.refs_0_, bf16[16,16,896]{2,1,0:T(8,128)(2,1)} %collective-permute-done.3.refs_1_, bf16[896,2048]{1,0:T(8,128)(2,1)} %copy.32.refs_4_.refs_2_), custom_call_target="tpu_custom_call" | custom-call | flops 1879048192 | bytes 6684672 | tf_op jit(solution)/shard_map/project/pallas_call | solution.py:109
  107.3 5.9 %project.5.refs_2_ = bf16[2,16,16,2048]{3,2,1,0:T(8,128)(2,1)} custom-call(bf16[16,16,896]{2,1,0:T(8,128)(2,1)} %copy-done.8, bf16[16,16,896]{2,1,0:T(8,128)(2,1)} %collective-permute-done.5.refs_1_, bf16[896,2048]{1,0:T(8,128)(2,1)} %copy.32.refs_4_.refs_2_), custom_call_target="tpu_custom_call" | custom-call | flops 1879048192 | bytes 6684672 | tf_op jit(solution)/shard_map/project/pallas_call | solution.py:109
  113.2 8.2 %project.3.refs_0_ = bf16[4,16,16,2048]{3,2,1,0:T(8,128)(2,1)} custom-call(bf16[16,16,896]{2,1,0:T(8,128)(2,1)} %compact_rows.2.refs_0_, bf16[16,16,896]{2,1,0:T(8,128)(2,1)} %collective-permute-done.refs_1_, bf16[16,16,896]{2,1,0:T(8,128)(2,1)} %copy-done.9, bf16[16,16,896]{2,1,0:T(8,128)(2,1)} %collective-permute-done.2.refs_3_, ...), custom_call_target="tpu_custom_call" | custom-call | flops 3758096384 | bytes 9699328 | tf_op jit(solution)/shard_map/project/pallas_call | solution.py:109
  121.4 14.4 %attend.1 = (bf16[512,1024]{1,0:T(8,128)(2,1)}, bf16[512,1024]{1,0:T(8,128)(2,1)}, bf16[2,16,16,2048]{3,2,1,0:T(8,128)(2,1)}, bf16[2,16,16,2048]{3,2,1,0:T(8,128...) custom-call(bf16[4,16,16,2048]{3,2,1,0:T(8,128)(2,1)} %project.3.refs_0_, ...), custom_call_target="tpu_custom_call" | custom-call | flops 1610612736 | bytes 37748736 | tf_op jit(solution)/shard_map/attend/pallas_call | solution.py:184
  135.8 6.8 %grad_plain.3 = f32[2,16,16,896]{3,2,1,0:T(8,128)} custom-call(bf16[2,16,16,2048]{3,2,1,0:T(8,128)(2,1)} %get-tuple-element.20.refs_0_, bf16[2048,896]{1,0:T(8,128)(2,1)} %get-tuple-element.23.refs_1_), custom_call_target="tpu_custom_call" | custom-call | flops 1879048192 | bytes 5767168 | tf_op jit(solution)/shard_map/grad_plain/pallas_call | solution.py:251
  142.9 6.7 %grad_plain.2 = f32[2,16,16,896]{3,2,1,0:T(8,128)} custom-call(bf16[2,16,16,2048]{3,2,1,0:T(8,128)(2,1)} %get-tuple-element.18.refs_0_, bf16[2048,896]{1,0:T(8,128)(2,1)} %get-tuple-element.23.refs_1_), custom_call_target="tpu_custom_call" | custom-call | flops 1879048192 | bytes 5767168 | tf_op jit(solution)/shard_map/grad_plain/pallas_call | solution.py:251
  151.0 7.5 %grad_code.1 = (s16[8,16,16,128]{3,2,1,0:T(8,128)(2,1)}, s16[8,16,16,128]{3,2,1,0:T(8,128)(2,1)}) custom-call(bf16[2,16,16,2048]{3,2,1,0:T(8,128)(2,1)} %get-tuple-element.19.refs_0_, bf16[2048,896]{1,0:T(8,128)(2,1)} %get-tuple-element.23.refs_1_, f32[2,16,16,896]{3,2,1,0:T(8,128)} %copy-done.3), custom_call_target="tpu_custom_call" | custom-call | flops 1879048192 | bytes 5767168 | tf_op jit(solution)/shard_map/grad_code/pallas_call | solution.py:251
  161.3 7.4 %grad_add.1.own = f32[2,16,16,896]{3,2,1,0:T(8,128)} custom-call(bf16[2,16,16,2048]{3,2,1,0:T(8,128)(2,1)} %get-tuple-element.17.refs_0_, bf16[2048,896]{1,0:T(8,128)(2,1)} %get-tuple-element.23.refs_1_, f32[2,16,16,896]{3,2,1,0:T(8,128)} %copy-done.2), custom_call_target="tpu_custom_call" | custom-call | flops 1879048192 | bytes 5767168 | tf_op jit(solution)/shard_map/grad_add/pallas_call | solution.py:251
  168.7 4.2 %collective-permute-done.8.rest_0_ = s16[8,16,16,128]{3,2,1,0:T(8,128)(2,1)S(1)} collective-permute-done((s16[8,16,16,128]{3,2,1,0:T(8,128)(2,1)}, s16[8,16,16,128]{3,2,1,0:T(8,128)(2,1)S(1)}, u32[]{:S(2)}, u32[]{:S(2)}) %collective-permute-start.8) | collective-permute-done | bytes 524320 | tf_op jit(solution)/shard_map/ppermute | solution.py:358
  176.6 5.6 %all-to-all-start.3 = ((s16[8,29,16,128]{3,2,1,0:T(8,128)(2,1)}), s16[8,29,16,128]{3,2,1,0:T(8,128)(2,1)S(1)}, u32[]{:S(2)}, u32[]{:S(2)}) async-start(s16[8,29,16,128]{3,2,1,0:T(8,128)(2,1)} %send_codes.2), calls=%async_computation.3 | async-start | bytes 1900544 | tf_op jit(solution)/shard_map/all_to_all | solution.py:361
  183.8 11.6 %collective-permute-done.9.rest_0_ = s16[8,16,16,128]{3,2,1,0:T(8,128)(2,1)S(1)} collective-permute-done((s16[8,16,16,128]{3,2,1,0:T(8,128)(2,1)S(1)}, s16[8,16,16,128]{3,2,1,0:T(8,128)(2,1)S(1)}, u32[]{:S(2)}, u32[]{:S(2)}) %collective-permute-start.9) | collective-permute-done | bytes 524320 | tf_op jit(solution)/shard_map/ppermute | solution.py:358
  199.1 6.7 %all-to-all-done.3.rest_0_ = s16[8,29,16,128]{3,2,1,0:T(8,128)(2,1)S(1)} async-done(((s16[8,29,16,128]{3,2,1,0:T(8,128)(2,1)}), s16[8,29,16,128]{3,2,1,0:T(8,128)(2,1)S(1)}, u32[]{:S(2)}, u32[]{:S(2)}) %all-to-all-start.3) | async-done | bytes 950304 | tf_op jit(solution)/shard_map/all_to_all | solution.py:361
  205.8 27.6 %all_to_all.30.rest_1_ = s16[8,29,16,128]{3,2,1,0:T(8,128)(2,1)} all-to-all(s16[8,29,16,128]{3,2,1,0:T(8,128)(2,1)} %send_codes.3), channel_id=1, replica_groups=mesh['dp'=8,'tensor'=4] {'dp'}, dimensions={0} | all-to-all | bytes 1900544 | tf_op jit(solution)/shard_map/all_to_all | solution.py:361
  233.4 3.4 %gather_grads.1 = f32[16,32,896]{2,1,0:T(8,128)} custom-call(s32[32]{0:T(128)} %reshape.54.asked, s16[8,29,16,128]{3,2,1,0:T(8,128)(2,1)} %copy-done, s16[8,29,16,128]{3,2,1,0:T(8,128)(2,1)} %all_to_all.30.rest_1_), custom_call_target="tpu_custom_call" | custom-call | bytes 3670016 | tf_op jit(solution)/shard_map/gather_grads/pallas_call | solution.py:332
  (59 shorter events, 31.2 us)
Async XLA Ops:
  4.8 13.7 %all-to-all-start = ((s32[8,1,4]{2,1,0:T(1,128)}), s32[8,1,4]{2,1,0:T(1,128)S(1)}, u32[]{:S(2)}, u32[]{:S(2)}) async-start(s32[8,1,4]{2,1,0:T(1,128)} %bitcast.2), calls=%async_computation | async-start | bytes 8192 | tf_op jit(solution)/shard_map/all_to_all | solution.py:361
  50.3 25.9 %all-to-all-start.1 = ((bf16[32,16,896]{2,1,0:T(8,128)(2,1)}), bf16[32,16,896]{2,1,0:T(8,128)(2,1)S(1)}, u32[]{:S(2)}, u32[]{:S(2)}) async-start(bf16[32,16,896]{2,1,0:T(8,128)(2,1)} %get-tuple-element.13), calls=%async_computation.1 | async-start | bytes 1835008 | tf_op jit(solution)/shard_map/all_to_all | solution.py:361
  57.0 31.7 %collective-permute-start.4 = (bf16[16,16,896]{2,1,0:T(8,128)(2,1)}, bf16[16,16,896]{2,1,0:T(8,128)(2,1)S(1)}, u32[]{:S(2)}, u32[]{:S(2)}) collective-permute-start(bf16[16,16,896]{2,1,0:T(8,128)(2,1)} %compact_rows.3.refs_0_), channel_id=1, source_target_pairs={{0,2},{1,3},{2,0},{3,1},{4,6},{5,7},{6,4},{7,5},{8,10},{9,11},{10,... | collective-permute-start | bytes 1376264 | tf_op jit(solution)/shard_map/ppermute | solution.py:358
  76.2 0.9 copy-start.1
  79.6 10.5 %collective-permute-start.1 = (bf16[16,16,896]{2,1,0:T(8,128)(2,1)}, bf16[16,16,896]{2,1,0:T(8,128)(2,1)S(1)}, u32[]{:S(2)}, u32[]{:S(2)}) collective-permute-start(bf16[16,16,896]{2,1,0:T(8,128)(2,1)} %compact_rows.2.refs_0_), channel_id=1, source_target_pairs={{0,2},{1,3},{2,0},{3,1},{4,6},{5,7},{6,4},{7,5},{8,10},{9,11},{10,... | collective-permute-start | bytes 1376264 | tf_op jit(solution)/shard_map/ppermute | solution.py:358
  81.2 20.2 %collective-permute-start.3 = (bf16[16,16,896]{2,1,0:T(8,128)(2,1)}, bf16[16,16,896]{2,1,0:T(8,128)(2,1)}, u32[]{:S(2)}, u32[]{:S(2)}) collective-permute-start(bf16[16,16,896]{2,1,0:T(8,128)(2,1)} %compact_rows.3.refs_0_), channel_id=1, source_target_pairs={{0,1},{1,0},{2,3},{3,2},{4,5},{5,4},{6,7},{7,6},{8,9},{9,8},{10,11... | collective-permute-start | bytes 1376264 | tf_op jit(solution)/shard_map/ppermute | solution.py:355
  84.3 3.9 %copy-start.6 = (bf16[16,16,896]{2,1,0:T(8,128)(2,1)S(1)}, bf16[16,16,896]{2,1,0:T(8,128)(2,1)}, u32[]{:S(2)}) copy-start(bf16[16,16,896]{2,1,0:T(8,128)(2,1)} %compact_rows.2.refs_0_) | copy-start | bytes 1376260
  88.1 25.1 %collective-permute-start = (bf16[16,16,896]{2,1,0:T(8,128)(2,1)S(1)}, bf16[16,16,896]{2,1,0:T(8,128)(2,1)}, u32[]{:S(2)}, u32[]{:S(2)}) collective-permute-start(bf16[16,16,896]{2,1,0:T(8,128)(2,1)S(1)} %copy-done.6), channel_id=1, source_target_pairs={{0,1},{1,0},{2,3},{3,2},{4,5},{5,4},{6,7},{7,6},{8,9},{9,8},{10,11... | collective-permute-start | bytes 1376264 | tf_op jit(solution)/shard_map/ppermute | solution.py:355
  88.6 6.6 %copy-start.8 = (bf16[16,16,896]{2,1,0:T(8,128)(2,1)}, bf16[16,16,896]{2,1,0:T(8,128)(2,1)S(1)}, u32[]{:S(2)}) copy-start(bf16[16,16,896]{2,1,0:T(8,128)(2,1)S(1)} %collective-permute-done.4.refs_0_) | copy-start | bytes 1376260
  88.6 18.7 %collective-permute-start.5 = (bf16[16,16,896]{2,1,0:T(8,128)(2,1)S(1)}, bf16[16,16,896]{2,1,0:T(8,128)(2,1)}, u32[]{:S(2)}, u32[]{:S(2)}) collective-permute-start(bf16[16,16,896]{2,1,0:T(8,128)(2,1)S(1)} %collective-permute-done.4.refs_0_), channel_id=1, source_target_pairs={{0,1},{1,0},{2,3},{3,2},{4,5},{5,4},{6,7},{7,6},{8,9},{9,8},{10,11... | collective-permute-start | bytes 1376264 | tf_op jit(solution)/shard_map/ppermute | solution.py:355
  90.2 5.1 %copy-start.9 = (bf16[16,16,896]{2,1,0:T(8,128)(2,1)}, bf16[16,16,896]{2,1,0:T(8,128)(2,1)S(1)}, u32[]{:S(2)}) copy-start(bf16[16,16,896]{2,1,0:T(8,128)(2,1)S(1)} %collective-permute-done.1.refs_2_) | copy-start | bytes 1376260
  90.2 23.0 %collective-permute-start.2 = (bf16[16,16,896]{2,1,0:T(8,128)(2,1)S(1)}, bf16[16,16,896]{2,1,0:T(8,128)(2,1)}, u32[]{:S(2)}, u32[]{:S(2)}) collective-permute-start(bf16[16,16,896]{2,1,0:T(8,128)(2,1)S(1)} %collective-permute-done.1.refs_2_), channel_id=1, source_target_pairs={{0,1},{1,0},{2,3},{3,2},{4,5},{5,4},{6,7},{7,6},{8,9},{9,8},{10,11... | collective-permute-start | bytes 1376264 | tf_op jit(solution)/shard_map/ppermute | solution.py:355
  142.5 7.2 %collective-permute-start.7 = (f32[2,16,16,896]{3,2,1,0:T(8,128)}, f32[2,16,16,896]{3,2,1,0:T(8,128)S(1)}, u32[]{:S(2)}, u32[]{:S(2)}) collective-permute-start(f32[2,16,16,896]{3,2,1,0:T(8,128)} %grad_plain.3), channel_id=1, source_target_pairs={{0,1},{1,0},{2,3},{3,2},{4,5},{5,4},{6,7},{7,6},{8,9},{9,8},{10,11... | collective-permute-start | bytes 5505032 | tf_op jit(solution)/shard_map/ppermute | solution.py:355
  149.6 10.4 %collective-permute-start.6 = (f32[2,16,16,896]{3,2,1,0:T(8,128)}, f32[2,16,16,896]{3,2,1,0:T(8,128)S(1)}, u32[]{:S(2)}, u32[]{:S(2)}) collective-permute-start(f32[2,16,16,896]{3,2,1,0:T(8,128)} %grad_plain.2), channel_id=1, source_target_pairs={{0,1},{1,0},{2,3},{3,2},{4,5},{5,4},{6,7},{7,6},{8,9},{9,8},{10,11... | collective-permute-start | bytes 5505032 | tf_op jit(solution)/shard_map/ppermute | solution.py:355
  149.8 1.3 copy-start.3
  158.5 14.4 %collective-permute-start.8 = (s16[8,16,16,128]{3,2,1,0:T(8,128)(2,1)}, s16[8,16,16,128]{3,2,1,0:T(8,128)(2,1)S(1)}, u32[]{:S(2)}, u32[]{:S(2)}) collective-permute-start(s16[8,16,16,128]{3,2,1,0:T(8,128)(2,1)} %get-tuple-element.21), channel_id=1, source_target_pairs={{0,2},{1,3},{2,0},{3,1},{4,6},{5,7},{6,4},{7,5},{8,10},{9,11},{10,... | collective-permute-start | bytes 1572872 | tf_op jit(solution)/shard_map/ppermute | solution.py:358
  160.0 1.2 copy-start.2
  168.7 13.5 %copy-start.7 = (s16[8,16,16,128]{3,2,1,0:T(8,128)(2,1)S(1)}, s16[8,16,16,128]{3,2,1,0:T(8,128)(2,1)}, u32[]{:S(2)}) copy-start(s16[8,16,16,128]{3,2,1,0:T(8,128)(2,1)} %get-tuple-element.22) | copy-start | bytes 1572868
  172.9 0.8 copy-start.4
  176.6 29.1 %all-to-all-start.3 = ((s16[8,29,16,128]{3,2,1,0:T(8,128)(2,1)}), s16[8,29,16,128]{3,2,1,0:T(8,128)(2,1)S(1)}, u32[]{:S(2)}, u32[]{:S(2)}) async-start(s16[8,29,16,128]{3,2,1,0:T(8,128)(2,1)} %send_codes.2), calls=%async_computation.3 | async-start | bytes 1900544 | tf_op jit(solution)/shard_map/all_to_all | solution.py:361
  182.2 13.2 %collective-permute-start.9 = (s16[8,16,16,128]{3,2,1,0:T(8,128)(2,1)S(1)}, s16[8,16,16,128]{3,2,1,0:T(8,128)(2,1)S(1)}, u32[]{:S(2)}, u32[]{:S(2)}) collective-permute-start(s16[8,16,16,128]{3,2,1,0:T(8,128)(2,1)S(1)} %copy-done.7), channel_id=1, source_target_pairs={{0,2},{1,3},{2,0},{3,1},{4,6},{5,7},{6,4},{7,5},{8,10},{9,11},{10,... | collective-permute-start | bytes 1572872 | tf_op jit(solution)/shard_map/ppermute | solution.py:358
  195.4 0.8 copy-start.5
  205.8 27.6 %copy-start = (s16[8,29,16,128]{3,2,1,0:T(8,128)(2,1)}, s16[8,29,16,128]{3,2,1,0:T(8,128)(2,1)S(1)}, u32[]{:S(2)}) copy-start(s16[8,29,16,128]{3,2,1,0:T(8,128)(2,1)S(1)} %all-to-all-done.3.rest_0_) | copy-start | bytes 2850820

commit v3 on v2

--- a/solution.py
+++ b/solution.py
@@ -27,6 +27,34 @@
 
 def cost(flops, nbytes):
     return pl.CostEstimate(flops=int(flops), bytes_accessed=int(nbytes), transcendentals=0)
+
+
+def ask_body(cap, owners, slots, position, wanted, count):
+    spans, two = owners.shape
+    for i in range(wanted.shape[0]):
+        wanted[i] = -1
+    for i in range(wanted.shape[0] // cap):
+        count[i] = 0
+    for r in range(spans * two):
+        owner = owners[r // two, r % two]
+        at = owner * cap + count[owner]
+        count[owner] = count[owner] + 1
+        position[r] = at
+        wanted[at] = slots[r // two, r % two]
+
+
+def ask(owners, slots, n_dp, cap):
+    return pl.pallas_call(
+        functools.partial(ask_body, cap),
+        out_shape=[
+            jax.ShapeDtypeStruct((owners.size,), jnp.int32),
+            jax.ShapeDtypeStruct((n_dp * cap,), jnp.int32),
+        ],
+        in_specs=[SMEM, SMEM],
+        out_specs=[SMEM, SMEM],
+        scratch_shapes=[pltpu.SMEM((n_dp,), jnp.int32)],
+        name="ask",
+    )(owners, slots)
 
 
 def pack_body(n_chunks, asked, first, table, *rest):
@@ -93,32 +121,40 @@
     )(position, arrived)
 
 
+def weight_specs(rows, step, first=0):
+    return [
+        pl.BlockSpec((rows, step), lambda i: (first, jnp.minimum(i, 1))),
+        pl.BlockSpec((rows, step), lambda i: (first, jnp.maximum(i - 2, 0))),
+    ]
+
+
 def project_body(n_in, *refs):
-    w, out = refs[n_in], refs[n_in + 1]
+    wk, wv, out = refs[n_in : n_in + 3]
     n, sub, enc = refs[0].shape
+    w = jnp.where(pl.program_id(0) < 2, wk[...], wv[...])
     rows = jnp.concatenate([ref[...].reshape(n * sub, enc) for ref in refs[:n_in]], axis=0)
-    res = jnp.dot(rows, w[...], preferred_element_type=F32)
+    res = jnp.dot(rows, w, preferred_element_type=F32)
     out[...] = res.astype(BF16).reshape(out.shape)
 
 
-def project(pieces, w_kv):
+def project(pieces, wk, wv):
     n_in = len(pieces)
     n, sub, enc = pieces[0].shape
-    width = w_kv.shape[1]
+    width = 2 * wk.shape[1]
     step = width // 4
     return pl.pallas_call(
         functools.partial(project_body, n_in),
         out_shape=jax.ShapeDtypeStruct((n_in, n, sub, width), BF16),
         grid=(4,),
         in_specs=[pl.BlockSpec((n, sub, enc), lambda i: (0, 0, 0))] * n_in
-        + [pl.BlockSpec((enc, step), lambda i: (0, i))],
+        + weight_specs(enc, step),
         out_specs=pl.BlockSpec((n_in, n, sub, step), lambda i: (0, 0, 0, i)),
         compiler_params=params(),
         cost_estimate=cost(
             2 * n_in * n * sub * enc * width, 2 * (n_in * n * sub * (enc + width) + enc * width)
         ),
         name="project",
-    )(*pieces, w_kv)
+    )(*pieces, wk, wv)
 
 
 def attend_body(places, n_kv, *refs):
@@ -202,142 +238,166 @@
     return code.astype(jnp.int32).astype(jnp.int16), power
 
 
-def grad_body(kind, *refs):
-    d_ref, w_ref = refs[:2]
-    acc = refs[-1]
-    k = pl.program_id(0)
+def grad_step(d_ref, wk, wv, acc):
+    i = pl.program_id(0)
     pieces, n, sub, step = d_ref.shape
+    w = jnp.where(i < 2, wk[...], wv[...])
     rows = d_ref[...].reshape(pieces * n * sub, step)
-    part = jnp.dot(rows, w_ref[...], preferred_element_type=F32)
-
-    @pl.when(k == 0)
+    part = lax.dot_general(rows, w, (((1,), (1,)), ((), ())), preferred_element_type=F32)
+
+    @pl.when(i == 0)
     def _():
         acc[...] = part
 
-    @pl.when(k > 0)
+    @pl.when(i > 0)
     def _():
         acc[...] += part
 
-    @pl.when(k == pl.num_programs(0) - 1)
+
+def core_grad_body(near, d_ref, wk, wv, near_out, far_out, acc):
+    grad_step(d_ref, wk, wv, acc)
+
+    @pl.when(pl.program_id(0) == pl.num_programs(0) - 1)
     def _():
-        full = acc[...].reshape(pieces, n, sub, acc.shape[1])
-        if kind == "plain":
-            refs[2][...] = full
-        elif kind == "add":
-            refs[3][...] = full + refs[2][...]
-        else:
-            for i in range(pieces):
-                code, power = encode(full[i] + refs[2][i], (1, 2))
-                out = refs[3 + i]
-                tiles = out.shape[0] - 1
-                for e in range(tiles):
-                    out[e] = code[:, :, e * LANES : (e + 1) * LANES]
-                note = jnp.broadcast_to(power.reshape(n, 1, 1), (n, sub, LANES))
-                out[tiles] = note.astype(jnp.int32).astype(jnp.int16)
-
-
-def grad(kind, d_kv, w_t, got=None):
+        full = acc[...].reshape(d_ref.shape[:3] + acc.shape[1:])
+        near_out[...] = full[:near]
+        far_out[...] = full[near:]
+
+
+def own_grad_body(near, d_ref, wk, wv, near_got, far_got, near_out, *rest):
+    codes, acc = rest[:-1], rest[-1]
+    grad_step(d_ref, wk, wv, acc)
+
+    @pl.when(pl.program_id(0) == pl.num_programs(0) - 1)
+    def _():
+        full = acc[...].reshape(d_ref.shape[:3] + acc.shape[1:])
+        near_out[...] = full[:near] + near_got[...]
+        for i in range(far_got.shape[0]):
+            out, c = codes[i // near], i % near
+            tiles, n = out.shape[1] - 1, out.shape[2]
+            code, power = encode(full[near + i] + far_got[i], (1, 2))
+            for e in range(tiles):
+                out[c, e] = code[:, :, e * LANES : (e + 1) * LANES]
+            note = jnp.broadcast_to(power.reshape(n, 1, 1), out.shape[2:])
+            out[c, tiles] = note.astype(jnp.int32).astype(jnp.int16)
+
+
+def grads_of(d_kv, wk, wv, near, cols, got=None):
     pieces, n, sub, width = d_kv.shape
-    enc = w_t.shape[1]
+    far = pieces - near
+    first, count = cols
     step = width // 4
-    full = (pieces, n, sub, enc)
-    whole = pl.BlockSpec(full, lambda i: (0, 0, 0, 0))
-    if kind == "code":
-        code = (enc // LANES + 1, n, sub, LANES)
-        out_shape = [jax.ShapeDtypeStruct(code, jnp.int16)] * pieces
-        out_specs = [pl.BlockSpec(code, lambda i: (0, 0, 0, 0))] * pieces
+    tiles = count // LANES
+    near_shape, far_shape = (near, n, sub, count), (far, n, sub, count)
+
+    def whole(shape):
+        return pl.BlockSpec(shape, lambda i: (0,) * len(shape))
+
+    if got is None:
+        body, outs = core_grad_body, [(near_shape, F32), (far_shape, F32)]
     else:
-        out_shape, out_specs = jax.ShapeDtypeStruct(full, F32), whole
-    return pl.pallas_call(
-        functools.partial(grad_body, kind),
-        out_shape=out_shape,
+        body = own_grad_body
+        outs = [(near_shape, F32)] + [((near, tiles + 1, n, sub, LANES), jnp.int16)] * (far // near)
+    out = pl.pallas_call(
+        functools.partial(body, near),
+        out_shape=[jax.ShapeDtypeStruct(*o) for o in outs],
         grid=(4,),
-        in_specs=[
-            pl.BlockSpec((pieces, n, sub, step), lambda i: (0, 0, 0, i)),
-            pl.BlockSpec((step, enc), lambda i: (i, 0)),
-        ]
-        + [whole] * (got is not None),
-        out_specs=out_specs,
-        scratch_shapes=[pltpu.VMEM((pieces * n * sub, enc), F32)],
-        compiler_params=params(),
-        cost_estimate=cost(2 * pieces * n * sub * enc * width, 2 * (enc + pieces * n * sub) * width),
-        name="grad_" + kind,
-    )(d_kv, w_t, *([] if got is None else [got]))
-
-
-def send_body(cap, chunk, position, own, *rest):
+        in_specs=[pl.BlockSpec((pieces, n, sub, step), lambda i: (0, 0, 0, i))]
+        + weight_specs(count, step)
+        + ([] if got is None else [whole(near_shape), whole(far_shape)]),
+        out_specs=[whole(shape) for shape, _ in outs],
+        scratch_shapes=[pltpu.VMEM((pieces * n * sub, count), F32)],
+        compiler_params=params(),
+        cost_estimate=cost(2 * pieces * n * sub * count * width, 2 * (count + pieces * n * sub) * width),
+        name="core_grads" if got is None else "own_grads",
+    )(
+        d_kv,
+        wk[first : first + count],
+        wv[first : first + count],
+        *([] if got is None else got),
+    )
+    return out[0], out[1:]
+
+
+def send_body(cap, position, own, *rest):
     codes, out, notes = rest[:-2], rest[-2], rest[-1]
-    n, sub, enc = own.shape[1:]
-    tiles = enc // LANES
-    row = lax.broadcasted_iota(jnp.int32, (SUB, LANES), 0) // (SUB // cap)
+    n_chunks, n, sub, count = own.shape
+    tiles = count // LANES
+    row = lax.broadcasted_iota(jnp.int32, (SUB, LANES), 0)
     notes[...] = jnp.zeros_like(notes)
     for r in range(n):
-        total = own[chunk, r]
-        for code in codes:
-            power = code[tiles, r].astype(F32)
-            unit = jnp.exp2(power - 15.0)
-            total = total + jnp.concatenate(
-                [code[e, r].astype(F32) * unit for e in range(tiles)], axis=1
-            )
-        coded, power = encode(total, (0, 1))
         p = position[r]
         dest, slot = p // cap, p % cap
-        for e in range(tiles):
-            out[dest, slot * tiles + e] = coded[:, e * LANES : (e + 1) * LANES]
-        mark = jnp.broadcast_to(power, (SUB, LANES)).astype(jnp.int32)
-        notes[dest] = jnp.where(row == slot, mark, notes[dest])
+        for c in range(n_chunks):
+            total = own[c, r]
+            for code in codes:
+                unit = jnp.exp2(code[c, tiles, r].astype(F32) - 15.0)
+                total = total + jnp.concatenate(
+                    [code[c, e, r].astype(F32) * unit for e in range(tiles)], axis=1
+                )
+            coded, power = encode(total, (0, 1))
+            mine = slot * n_chunks + c
+            for e in range(tiles):
+                out[dest, mine * tiles + e] = coded[:, e * LANES : (e + 1) * LANES]
+            mark = jnp.broadcast_to(power, (SUB, LANES)).astype(jnp.int32)
+            notes[dest] = jnp.where(row == mine, mark, notes[dest])
     for d in range(out.shape[0]):
-        out[d, cap * tiles] = notes[d].astype(jnp.int16)
-
-
-def send_codes(chunk, position, own, codes, n_dp, cap):
-    n, sub, enc = own.shape[1:]
-    shape = (n_dp, cap * (enc // LANES) + 1, SUB, LANES)
-    return pl.pallas_call(
-        functools.partial(send_body, cap, chunk),
+        out[d, cap * n_chunks * tiles] = notes[d].astype(jnp.int16)
+
+
+def send_codes(position, own, codes, n_dp, cap):
+    n_chunks, n, sub, count = own.shape
+    shape = (n_dp, cap * n_chunks * (count // LANES) + 1, SUB, LANES)
+    return pl.pallas_call(
+        functools.partial(send_body, cap),
         out_shape=jax.ShapeDtypeStruct(shape, jnp.int16),
         in_specs=[SMEM, VMEM] + [VMEM] * len(codes),
         out_specs=VMEM,
         scratch_shapes=[pltpu.VMEM((n_dp, SUB, LANES), jnp.int32)],
         compiler_params=params(),
-        cost_estimate=cost(10 * n * sub * enc, 6 * n * sub * enc + 2 * math.prod(shape)),
+        cost_estimate=cost(10 * own.size, 6 * own.size + 2 * math.prod(shape)),
         name="send_codes",
     )(position, own, *codes)
 
 
-def gather_body(cap, n_chunks, asked, *rest):
-    arrived, out = rest[:n_chunks], rest[n_chunks]
-    tiles = out.shape[2] // LANES
-    out[...] = jnp.zeros_like(out)
-    n_dp = arrived[0].shape[0]
-    for d in range(n_dp):
+def gather_body(cap, n_chunks, first, asked, arrived, *rest):
+    out, total, sem = rest[-3:]
+    count = total.shape[2]
+    tiles = count // LANES
+    total[...] = jnp.zeros_like(total)
+    for d in range(arrived.shape[0]):
         for s in range(cap):
             slab = asked[d * cap + s]
 
             @pl.when(slab >= 0)
             def _():
+                note = arrived[d, cap * n_chunks * tiles].astype(F32)
                 for c in range(n_chunks):
-                    ref = arrived[c]
-                    note = ref[d, cap * tiles].astype(F32)
-                    at = s * (SUB // cap)
+                    at = s * n_chunks + c
                     unit = jnp.exp2(note[at : at + 1] - 15.0)
                     for e in range(tiles):
-                        value = ref[d, s * tiles + e].astype(F32) * unit
-                        out[slab, pl.ds(c * SUB, SUB), pl.ds(e * LANES, LANES)] += value
-
-
-def gather_grads(asked, arrived, n_slabs, enc, cap):
-    n_chunks = len(arrived)
-    shape = (n_slabs, n_chunks * SUB, enc)
-    return pl.pallas_call(
-        functools.partial(gather_body, cap, n_chunks),
-        out_shape=jax.ShapeDtypeStruct(shape, F32),
-        in_specs=[SMEM] + [VMEM] * n_chunks,
-        out_specs=VMEM,
-        compiler_params=params(),
-        cost_estimate=cost(0, 8 * math.prod(shape)),
+                        value = arrived[d, at * tiles + e].astype(F32) * unit
+                        total[slab, pl.ds(c * SUB, SUB), pl.ds(e * LANES, LANES)] += value
+
+    copy = pltpu.make_async_copy(total, out.at[:, :, pl.ds(first, count)], sem)
+    copy.start()
+    copy.wait()
+
+
+def gather_grads(asked, arrived, n_slabs, n_chunks, enc, cap, cols, before):
+    first, count = cols
+    rows = n_chunks * SUB
+    return pl.pallas_call(
+        functools.partial(gather_body, cap, n_chunks, first),
+        out_shape=jax.ShapeDtypeStruct((n_slabs, rows, enc), F32),
+        in_specs=[SMEM, VMEM] + [ANY] * (before is not None),
+        out_specs=ANY,
+        scratch_shapes=[pltpu.VMEM((n_slabs, rows, count), F32), pltpu.SemaphoreType.DMA],
+        input_output_aliases={} if before is None else {2: 0},
+        compiler_params=params(),
+        cost_estimate=cost(0, 8 * n_slabs * rows * count),
         name="gather_grads",
-    )(asked, *arrived)
+    )(asked, arrived, *([] if before is None else [before]))
 
 
 def on_device(queries, cotangent, table, key_weight, value_weight, owners, slots):
@@ -360,48 +420,43 @@
     def over_dp(x):
         return lax.all_to_all(x, "dp", split_axis=0, concat_axis=0, tiled=True)
 
-    owner_flat = owners.reshape(n_requests)
-    slot_flat = slots.reshape(n_requests)
-    onehot = (owner_flat[:, None] == jnp.arange(n_dp, dtype=jnp.int32)[None, :]).astype(jnp.int32)
-    within = jnp.sum((jnp.cumsum(onehot, axis=0) - onehot) * onehot, axis=1)
-    position = owner_flat * cap + within
-    wanted = jnp.full((n_dp * cap,), -1, jnp.int32).at[position].set(slot_flat)
+    position, wanted = ask(owners, slots, n_dp, cap)
     asked = over_dp(wanted.reshape(n_dp, cap)).reshape(-1)
 
     first = (lax.axis_index("tensor") * share).astype(jnp.int32).reshape(1)
-    w_kv = jnp.concatenate([key_weight, value_weight], axis=1)
-    w_t = w_kv.T
 
     def place(c, kind, d):
-        return (kind, c) if d == 0 else (2 + kind, c * (n_x - 1) + d - 1)
+        return (kind, c if d == 0 else n_chunks * d + c)
 
     kvs, places = [], []
     for c, sent in enumerate(pack(asked, first, table, n_chunks)):
-        mine = compact(position, over_dp(sent))
+        got = over_dp(sent)
+        if kvs:
+            got, kvs = lax.optimization_barrier((got, kvs))
+        mine = compact(position, got)
         near = [mine, over_core(mine)]
         far = [over_x(mine, d) for d in range(1, n_x)]
         far = far + [over_core(x) for x in far]
         near_at = [place(c, kind, 0) for kind in range(2)]
         far_at = [place(c, kind, d) for kind in range(2) for d in range(1, n_x)]
         if c < n_chunks - 1:
-            kvs.append(project(near + far, w_kv))
+            kvs = kvs + [project(near + far, key_weight, value_weight)]
         else:
-            kvs += [project(near, w_kv), project(far, w_kv)]
+            kvs = kvs + [project(x, key_weight, value_weight) for x in (near, far)]
         places += near_at + far_at
 
-    sizes = [n_chunks, n_chunks, n_chunks * (n_x - 1), n_chunks * (n_x - 1)]
-    attended, d_query, grads = attend(kvs, places, sizes, queries, cotangent)
-    own_near, core_near, own_far, core_far = grads
-
-    far_got = over_core(grad("plain", core_far, w_t))
-    near_got = over_core(grad("plain", core_near, w_t))
-    codes = grad("code", own_far, w_t, far_got)
-    own = grad("add", own_near, w_t, near_got)
-    arrived = []
-    for c in range(n_chunks):
-        got = [over_x(codes[c * (n_x - 1) + d - 1], n_x - d) for d in range(1, n_x)]
-        arrived.append(over_dp(send_codes(c, position, own, got, n_dp, cap)))
-    d_table = gather_grads(asked, arrived, n_slabs, enc, cap)
+    sizes = [n_chunks * n_x, n_chunks * n_x]
+    attended, d_query, (d_own, d_core) = attend(kvs, places, sizes, queries, cotangent)
+
+    lead = 2 * LANES
+    d_table = None
+    for cols in ((0, lead), (lead, enc - lead)):
+        grads = grads_of(d_core, key_weight, value_weight, n_chunks, cols)
+        got = over_core(grads[0]), over_core(grads[1][0])
+        own, codes = grads_of(d_own, key_weight, value_weight, n_chunks, cols, got)
+        codes = [over_x(code, n_x - d) for d, code in enumerate(codes, 1)]
+        arrived = over_dp(send_codes(position, own, codes, n_dp, cap))
+        d_table = gather_grads(asked, arrived, n_slabs, n_chunks, enc, cap, cols, d_table)
     return (attended, d_query, d_table)
 
 

time: 239 us -> 252 us (1.054)
  waiting for transfers between devices: 48 us -> 87.6 us
  blocking collectives: 53.9 us -> 26.4 us
  other arithmetic: 7.32 us -> 0.66 us
  starting transfers between devices: 23.7 us -> 29.4 us
  Pallas kernels: 80.7 us -> 85.6 us
    ppermute x4, waiting for transfers between devices: 17.3 us -> 48.7 us  [over_x(): lax.ppermute(x, 'tensor', [(t, (t + 2 * d) % n_tp) for t in range(n_tp)])]
    all_to_all x2 -> x1, blocking collectives: 53.9 us -> 26.4 us  [over_dp(): return lax.all_to_all(x, 'dp', split_axis=0, concat_axis=0, tiled=True)]
    concatenate x1 -> x0, local copies, waits for them, and re-layouts: 6.14 us -> none  [on_device(): w_kv = jnp.concatenate([key_weight, value_weight], axis=1)]
    slice x0 -> x4, local copies, waits for them, and re-layouts: none -> 6.12 us  [the longest x2 3.06 us: grads_of(): wk[first:first + count]]
    all_to_all x3 -> x4, starting transfers between devices: 16.4 us -> 22.3 us  [over_dp(): return lax.all_to_all(x, 'dp', split_axis=0, concat_axis=0, tiled=True)]
    transpose x1 -> x0, other arithmetic: 5.08 us -> none  [on_device(): w_t = w_kv.T]
    ppermute x6 -> x8, waiting for transfers between devices: 0.02 us -> 4.24 us  [over_core(): return lax.ppermute(x, 'tensor', [(t, t ^ 1) for t in range(n_tp)])]
    pallas_call x7 -> x9, Pallas kernels: 37.6 us -> 41.8 us  [the longest x4 29.8 us: grads_of(): pl.pallas_call(functools.partial(body, near), out_shape=[jax.ShapeDtypeSt...]
  transfers between devices with their start and end apart: 13 -> 16, of which waited for: 6 -> 9; matrix products, arithmetic and copies ran while one was open for 8% -> 2% of each run, Pallas kernels for 18% -> 18%
where the time goes in v3:
time: 252 us; the launch traced here: 251 us
  waiting for transfers between devices  87.6 us (35%)
  Pallas kernels  85.6 us (34%)
  starting transfers between devices  29.4 us (12%)
  blocking collectives  26.4 us (10%)
  local copies, waits for them, and re-layouts  20.3 us (8%)
    ppermute x4, waiting for transfers between devices, over_x(): lax.ppermute(x, 'tensor', [(t, (t + 2 * d) % n_tp) for t in range(n_tp)])  48.7 us
    all_to_all x4, waiting for transfers between devices, over_dp(): return lax.all_to_all(x, 'dp', split_axis=0, concat_axis=0, tiled=True)  34.7 us
    pallas_call x4, Pallas kernels, grads_of(): pl.pallas_call(functools.partial(body, near), out_shape=[jax.ShapeDtypeSt...  29.8 us
    all_to_all x1, blocking collectives, over_dp(): return lax.all_to_all(x, 'dp', split_axis=0, concat_axis=0, tiled=True)  26.4 us
    all_to_all x4, starting transfers between devices, over_dp(): return lax.all_to_all(x, 'dp', split_axis=0, concat_axis=0, tiled=True)  22.3 us
    pallas_call x3, Pallas kernels, project(): pl.pallas_call(functools.partial(project_body, n_in), out_shape=jax.Shape...  20.7 us
    pallas_call x1, Pallas kernels, attend(): pl.pallas_call(functools.partial(attend_body, places, len(kvs)), out_shap...  14.4 us
    unnamed x36, local copies, waits for them, and re-layouts  11.7 us
  transfers between devices with their start and end apart: 16, of which 9 were waited for; matrix products, arithmetic and copies ran while one was open for 2% of the time, Pallas kernels for 18%

profile of v3, /device:TPU:0, one launch (start us, length us, event | category | flops | bytes accessed | tf_op | source)
XLA Modules:
  0.0 250.8 jit_solution(18440497901388145803)
XLA Ops:
  6.1 7.3 %all-to-all-start = ((s32[8,1,4]{2,1,0:T(1,128)}), s32[8,1,4]{2,1,0:T(1,128)S(1)}, u32[]{:S(2)}, u32[]{:S(2)}) async-start(s32[8,1,4]{2,1,0:T(1,128)} %bitcast), calls=%async_computation | async-start | bytes 8192 | tf_op jit(solution)/shard_map/all_to_all | solution.py:421
  13.4 6.4 %all-to-all-done = s32[8,1,4]{2,1,0:T(1,128)S(1)} async-done(((s32[8,1,4]{2,1,0:T(1,128)}), s32[8,1,4]{2,1,0:T(1,128)S(1)}, u32[]{:S(2)}, u32[]{:S(2)}) %all-to-all-start) | async-done | bytes 160 | tf_op jit(solution)/shard_map/all_to_all | solution.py:421
  21.6 3.5 %pack_rows.1 = (bf16[32,16,896]{2,1,0:T(8,128)(2,1)}, bf16[32,16,896]{2,1,0:T(8,128)(2,1)}) custom-call(s32[32]{0:T(128)} %reshape.17.asked, s32[1]{0:T(128)} %bitcast.1.first, bf16[16,128,896]{2,1,0:T(8,128)(2,1)} %table.1), custom_call_target="tpu_custom_call" | custom-call | bytes 3670016 | tf_op jit(solution)/shard_map/pack_rows/pallas_call | solution.py:86
  25.1 26.4 %all_to_all.29.arrived = bf16[32,16,896]{2,1,0:T(8,128)(2,1)} all-to-all(bf16[32,16,896]{2,1,0:T(8,128)(2,1)} %get-tuple-element.24), channel_id=1, replica_groups=mesh['dp'=8,'tensor'=4] {'dp'}, dimensions={0} | all-to-all | bytes 1835008 | tf_op jit(solution)/shard_map/all_to_all | solution.py:421
  51.5 3.6 %all-to-all-start.1 = ((bf16[32,16,896]{2,1,0:T(8,128)(2,1)}), bf16[32,16,896]{2,1,0:T(8,128)(2,1)S(1)}, u32[]{:S(2)}, u32[]{:S(2)}) async-start(bf16[32,16,896]{2,1,0:T(8,128)(2,1)} %get-tuple-element.22), calls=%async_computation.1 | async-start | bytes 1835008 | tf_op jit(solution)/shard_map/all_to_all | solution.py:421
  55.0 2.6 %compact_rows.2.refs_0_ = bf16[16,16,896]{2,1,0:T(8,128)(2,1)} custom-call(s32[16]{0:T(128)} %get-tuple-element.23.position, bf16[32,16,896]{2,1,0:T(8,128)(2,1)} %all_to_all.29.arrived), custom_call_target="tpu_custom_call" | custom-call | bytes 917504 | tf_op jit(solution)/shard_map/compact_rows/pallas_call | solution.py:112
  59.1 9.9 %collective-permute-done.1.refs_2_ = bf16[16,16,896]{2,1,0:T(8,128)(2,1)S(1)} collective-permute-done((bf16[16,16,896]{2,1,0:T(8,128)(2,1)}, bf16[16,16,896]{2,1,0:T(8,128)(2,1)S(1)}, u32[]{:S(2)}, u32[]{:S(2)}) %collective-permute-start.1) | collective-permute-done | bytes 458784 | tf_op jit(solution)/shard_map/ppermute | solution.py:418
  71.6 8.5 %project.3.refs_0_ = bf16[4,16,16,2048]{3,2,1,0:T(8,128)(2,1)} custom-call(bf16[16,16,896]{2,1,0:T(8,128)(2,1)} %compact_rows.2.refs_0_, bf16[16,16,896]{2,1,0:T(8,128)(2,1)} %copy-done.13, bf16[16,16,896]{2,1,0:T(8,128)(2,1)} %copy-done.12, bf16[16,16,896]{2,1,0:T(8,128)(2,1)} %copy-done.16, bf16[896,1024]{1,0:T(8,128)(2,1)} %refs_2_.3, ...), custom_call_target="tpu_custom_call" | custom-call | flops 3758096384 | bytes 9699328 | tf_op jit(solution)/shard_map/project/pallas_call | solution.py:145
  81.0 2.7 %compact_rows.3.refs_0_ = bf16[16,16,896]{2,1,0:T(8,128)(2,1)} custom-call(s32[16]{0:T(128)} %get-tuple-element.23.position, bf16[32,16,896]{2,1,0:T(8,128)(2,1)} %copy-done.1), custom_call_target="tpu_custom_call" | custom-call | bytes 917504 | tf_op jit(solution)/shard_map/compact_rows/pallas_call | solution.py:112
  85.3 11.3 %collective-permute-done.4.refs_0_ = bf16[16,16,896]{2,1,0:T(8,128)(2,1)S(1)} collective-permute-done((bf16[16,16,896]{2,1,0:T(8,128)(2,1)}, bf16[16,16,896]{2,1,0:T(8,128)(2,1)S(1)}, u32[]{:S(2)}, u32[]{:S(2)}) %collective-permute-start.4) | collective-permute-done | bytes 458784 | tf_op jit(solution)/shard_map/ppermute | solution.py:418
  99.7 6.1 %project.4.refs_1_ = bf16[2,16,16,2048]{3,2,1,0:T(8,128)(2,1)} custom-call(bf16[16,16,896]{2,1,0:T(8,128)(2,1)} %compact_rows.3.refs_0_, bf16[16,16,896]{2,1,0:T(8,128)(2,1)} %copy-done.14, bf16[896,1024]{1,0:T(8,128)(2,1)} %refs_2_.3, bf16[896,1024]{1,0:T(8,128)(2,1)} %refs_3_.4), custom_call_target="tpu_custom_call" | custom-call | flops 1879048192 | bytes 6684672 | tf_op jit(solution)/shard_map/project/pallas_call | solution.py:145
  106.6 6.1 %project.5.refs_2_ = bf16[2,16,16,2048]{3,2,1,0:T(8,128)(2,1)} custom-call(bf16[16,16,896]{2,1,0:T(8,128)(2,1)} %copy-done.11, bf16[16,16,896]{2,1,0:T(8,128)(2,1)} %copy-done.15, bf16[896,1024]{1,0:T(8,128)(2,1)} %refs_2_.3, bf16[896,1024]{1,0:T(8,128)(2,1)} %refs_3_.4), custom_call_target="tpu_custom_call" | custom-call | flops 1879048192 | bytes 6684672 | tf_op jit(solution)/shard_map/project/pallas_call | solution.py:145
  112.8 14.4 %attend.1 = (bf16[512,1024]{1,0:T(8,128)(2,1)}, bf16[512,1024]{1,0:T(8,128)(2,1)}, bf16[4,16,16,2048]{3,2,1,0:T(8,128)(2,1)}, bf16[4,16,16,2048]{3,2,1,0:T(8,128)(2,1)}) custom-call(bf16[4,16,16,2048]{3,2,1,0:T(8,128)(2,1)} %project.3.refs_0_, bf16[2,16,16,2048]{3,2,1,0:T(8,128)(2,1)} %project.4.refs_1_, bf16[2,16,16,2048]{3,2,1,0:T(8,128)(2,1)} %project.5.refs_2_, ...), custom_call_target="tpu_custom_call" | custom-call | flops 1610612736 | bytes 37748736 | tf_op jit(solution)/shard_map/attend/pallas_call | solution.py:220
  127.2 8.5 %core_grads.2 = (f32[2,16,16,640]{3,2,1,0:T(8,128)}, f32[2,16,16,640]{3,2,1,0:T(8,128)}) custom-call(bf16[4,16,16,2048]{3,2,1,0:T(8,128)(2,1)} %get-tuple-element.30.d_ref, bf16[640,1024]{1,0:T(8,128)(2,1)} %slice.16.wk, bf16[640,1024]{1,0:T(8,128)(2,1)} %slice.17.wv), custom_call_target="tpu_custom_call" | custom-call | flops 2684354560 | bytes 6815744 | tf_op jit(solution)/shard_map/core_grads/pallas_call | solution.py:301
  139.9 5.5 %core_grads.3 = (f32[2,16,16,256]{3,2,1,0:T(8,128)}, f32[2,16,16,256]{3,2,1,0:T(8,128)}) custom-call(bf16[4,16,16,2048]{3,2,1,0:T(8,128)(2,1)} %get-tuple-element.30.d_ref, bf16[256,1024]{1,0:T(8,128)(2,1)} %slice.18.wk, bf16[256,1024]{1,0:T(8,128)(2,1)} %slice.19.wv), custom_call_target="tpu_custom_call" | custom-call | flops 1073741824 | bytes 5242880 | tf_op jit(solution)/shard_map/core_grads/pallas_call | solution.py:301
  149.2 6.1 %own_grads.3 = (f32[2,16,16,256]{3,2,1,0:T(8,128)}, s16[2,3,16,16,128]{4,3,2,1,0:T(8,128)(2,1)}) custom-call(bf16[4,16,16,2048]{3,2,1,0:T(8,128)(2,1)} %get-tuple-element.29.d_ref, bf16[256,1024]{1,0:T(8,128)(2,1)} %slice.18.wk, bf16[256,1024]{1,0:T(8,128)(2,1)} %slice.19.wv, f32[2,16,16,256]{3,2,1,0:T(8,128)} %copy-done.7, f32[2,16,16,256]{3,2,1,0:T(8,128)} %copy-done.6), custom_call_target="tpu_custom_call" | custom-call | flops 1073741824 | bytes 5242880 | tf_op jit(solution)/shard_map/own_grads/pallas_call | solution.py:301
  156.8 10.1 %collective-permute-done.11.rest_0_ = s16[2,3,16,16,128]{4,3,2,1,0:T(8,128)(2,1)S(1)} collective-permute-done((s16[2,3,16,16,128]{4,3,2,1,0:T(8,128)(2,1)}, s16[2,3,16,16,128]{4,3,2,1,0:T(8,128)(2,1)S(1)}, u32[]{:S(2)}, u32[]{:S(2)}) %collective-permute-start.11) | collective-permute-done | bytes 393248 | tf_op jit(solution)/shard_map/ppermute | solution.py:418
  169.9 5.7 %all-to-all-start.4 = ((s16[8,17,16,128]{3,2,1,0:T(8,128)(2,1)}), s16[8,17,16,128]{3,2,1,0:T(8,128)(2,1)S(1)}, u32[]{:S(2)}, u32[]{:S(2)}) async-start(s16[8,17,16,128]{3,2,1,0:T(8,128)(2,1)} %send_codes.3), calls=%async_computation.4 | async-start | bytes 1114112 | tf_op jit(solution)/shard_map/all_to_all | solution.py:421
  177.9 9.7 %own_grads.2 = (f32[2,16,16,640]{3,2,1,0:T(8,128)}, s16[2,6,16,16,128]{4,3,2,1,0:T(8,128)(2,1)}) custom-call(bf16[4,16,16,2048]{3,2,1,0:T(8,128)(2,1)} %get-tuple-element.29.d_ref, bf16[640,1024]{1,0:T(8,128)(2,1)} %slice.16.wk, bf16[640,1024]{1,0:T(8,128)(2,1)} %slice.17.wv, f32[2,16,16,640]{3,2,1,0:T(8,128)} %copy-done.9, f32[2,16,16,640]{3,2,1,0:T(8,128)} %copy-done.10), custom_call_target="tpu_custom_call" | custom-call | flops 2684354560 | bytes 6815744 | tf_op jit(solution)/shard_map/own_grads/pallas_call | solution.py:301
  189.1 17.4 %collective-permute-done.8.rest_0_ = s16[2,6,16,16,128]{4,3,2,1,0:T(8,128)(2,1)S(1)} collective-permute-done((s16[2,6,16,16,128]{4,3,2,1,0:T(8,128)(2,1)}, s16[2,6,16,16,128]{4,3,2,1,0:T(8,128)(2,1)S(1)}, u32[]{:S(2)}, u32[]{:S(2)}) %collective-permute-start.8) | collective-permute-done | bytes 786464 | tf_op jit(solution)/shard_map/ppermute | solution.py:418
  207.4 3.2 %send_codes.2 = s16[8,41,16,128]{3,2,1,0:T(8,128)(2,1)} custom-call(s32[16]{0:T(128)} %get-tuple-element.23.position, f32[2,16,16,640]{3,2,1,0:T(8,128)} %get-tuple-element.33.own, s16[2,6,16,16,128]{4,3,2,1,0:T(8,128)(2,1)} %copy-done.5), custom_call_target="tpu_custom_call" | custom-call | flops 3276800 | bytes 3309568 | tf_op jit(solution)/shard_map/send_codes/pallas_call | solution.py:351
  210.6 5.7 %all-to-all-start.3 = ((s16[8,41,16,128]{3,2,1,0:T(8,128)(2,1)}), s16[8,41,16,128]{3,2,1,0:T(8,128)(2,1)S(1)}, u32[]{:S(2)}, u32[]{:S(2)}) async-start(s16[8,41,16,128]{3,2,1,0:T(8,128)(2,1)} %send_codes.2), calls=%async_computation.3 | async-start | bytes 2686976 | tf_op jit(solution)/shard_map/all_to_all | solution.py:421
  218.5 28.3 %all-to-all-done.3.arrived = s16[8,41,16,128]{3,2,1,0:T(8,128)(2,1)S(1)} async-done(((s16[8,41,16,128]{3,2,1,0:T(8,128)(2,1)}), s16[8,41,16,128]{3,2,1,0:T(8,128)(2,1)S(1)}, u32[]{:S(2)}, u32[]{:S(2)}) %all-to-all-start.3) | async-done | bytes 1343520 | tf_op jit(solution)/shard_map/all_to_all | solution.py:421
  248.0 2.8 %gather_grads.3 = f32[16,32,896]{2,1,0:T(8,128)} custom-call(s32[32]{0:T(128)} %reshape.17.asked, s16[8,41,16,128]{3,2,1,0:T(8,128)(2,1)} %copy-done, f32[16,32,896]{2,1,0:T(8,128)} %gather_grads.2.rest_0_), custom_call_target="tpu_custom_call", output_to_operand_aliasing={{}: (2, {})} | custom-call | bytes 2621440 | tf_op jit(solution)/shard_map/gather_grads/pallas_call | solution.py:390
  (69 shorter events, 38.3 us)
Async XLA Ops:
  6.1 13.7 %all-to-all-start = ((s32[8,1,4]{2,1,0:T(1,128)}), s32[8,1,4]{2,1,0:T(1,128)S(1)}, u32[]{:S(2)}, u32[]{:S(2)}) async-start(s32[8,1,4]{2,1,0:T(1,128)} %bitcast), calls=%async_computation | async-start | bytes 8192 | tf_op jit(solution)/shard_map/all_to_all | solution.py:421
  51.5 28.6 %all-to-all-start.1 = ((bf16[32,16,896]{2,1,0:T(8,128)(2,1)}), bf16[32,16,896]{2,1,0:T(8,128)(2,1)S(1)}, u32[]{:S(2)}, u32[]{:S(2)}) async-start(bf16[32,16,896]{2,1,0:T(8,128)(2,1)} %get-tuple-element.22), calls=%async_computation.1 | async-start | bytes 1835008 | tf_op jit(solution)/shard_map/all_to_all | solution.py:421
  57.6 11.4 %collective-permute-start.1 = (bf16[16,16,896]{2,1,0:T(8,128)(2,1)}, bf16[16,16,896]{2,1,0:T(8,128)(2,1)S(1)}, u32[]{:S(2)}, u32[]{:S(2)}) collective-permute-start(bf16[16,16,896]{2,1,0:T(8,128)(2,1)} %compact_rows.2.refs_0_), channel_id=1, source_target_pairs={{0,2},{1,3},{2,0},{3,1},{4,6},{5,7},{6,4},{7,5},{8,10},{9,11},{10,... | collective-permute-start | bytes 1376264 | tf_op jit(solution)/shard_map/ppermute | solution.py:418
  59.1 9.9 %collective-permute-start = (bf16[16,16,896]{2,1,0:T(8,128)(2,1)}, bf16[16,16,896]{2,1,0:T(8,128)(2,1)S(1)}, u32[]{:S(2)}, u32[]{:S(2)}) collective-permute-start(bf16[16,16,896]{2,1,0:T(8,128)(2,1)} %compact_rows.2.refs_0_), channel_id=1, source_target_pairs={{0,1},{1,0},{2,3},{3,2},{4,5},{5,4},{6,7},{7,6},{8,9},{9,8},{10,11... | collective-permute-start | bytes 1376264 | tf_op jit(solution)/shard_map/ppermute | solution.py:415
  69.0 1.8 copy-start.12
  69.0 1.8 collective-permute-start.2
  69.0 1.8 copy-start.13
  71.6 25.0 %copy-start.3 = (bf16[896,1024]{1,0:T(8,128)(2,1)S(1)}, bf16[896,1024]{1,0:T(8,128)(2,1)}, u32[]{:S(2)}) copy-start(bf16[896,1024]{1,0:T(8,128)(2,1)} %refs_2_.3) | copy-start | bytes 5505028
  81.0 16.7 %copy-start.4 = (bf16[896,1024]{1,0:T(8,128)(2,1)S(1)}, bf16[896,1024]{1,0:T(8,128)(2,1)}, u32[]{:S(2)}) copy-start(bf16[896,1024]{1,0:T(8,128)(2,1)} %refs_3_.4) | copy-start | bytes 5505028
  83.7 12.8 %collective-permute-start.4 = (bf16[16,16,896]{2,1,0:T(8,128)(2,1)}, bf16[16,16,896]{2,1,0:T(8,128)(2,1)S(1)}, u32[]{:S(2)}, u32[]{:S(2)}) collective-permute-start(bf16[16,16,896]{2,1,0:T(8,128)(2,1)} %compact_rows.3.refs_0_), channel_id=1, source_target_pairs={{0,2},{1,3},{2,0},{3,1},{4,6},{5,7},{6,4},{7,5},{8,10},{9,11},{10,... | collective-permute-start | bytes 1376264 | tf_op jit(solution)/shard_map/ppermute | solution.py:418
  85.3 13.7 %collective-permute-start.3 = (bf16[16,16,896]{2,1,0:T(8,128)(2,1)}, bf16[16,16,896]{2,1,0:T(8,128)(2,1)S(1)}, u32[]{:S(2)}, u32[]{:S(2)}) collective-permute-start(bf16[16,16,896]{2,1,0:T(8,128)(2,1)} %compact_rows.3.refs_0_), channel_id=1, source_target_pairs={{0,1},{1,0},{2,3},{3,2},{4,5},{5,4},{6,7},{7,6},{8,9},{9,8},{10,11... | collective-permute-start | bytes 1376264 | tf_op jit(solution)/shard_map/ppermute | solution.py:415
  96.6 2.4 copy-start.11
  96.6 9.3 %collective-permute-start.5 = (bf16[16,16,896]{2,1,0:T(8,128)(2,1)S(1)}, bf16[16,16,896]{2,1,0:T(8,128)(2,1)S(1)}, u32[]{:S(2)}, u32[]{:S(2)}) collective-permute-start(bf16[16,16,896]{2,1,0:T(8,128)(2,1)S(1)} %collective-permute-done.4.refs_0_), channel_id=1, source_target_pairs={{0,1},{1,0},{2,3},{3,2},{4,5},{5,4},{6,7},{7,6},{8,9},{9,8},{10,11... | collective-permute-start | bytes 1376264 | tf_op jit(solution)/shard_map/ppermute | solution.py:415
  135.7 40.0 %collective-permute-start.6 = (f32[2,16,16,640]{3,2,1,0:T(8,128)}, f32[2,16,16,640]{3,2,1,0:T(8,128)S(1)}, u32[]{:S(2)}, u32[]{:S(2)}) collective-permute-start(f32[2,16,16,640]{3,2,1,0:T(8,128)} %get-tuple-element.31), channel_id=1, source_target_pairs={{0,1},{1,0},{2,3},{3,2},{4,5},{5,4},{6,7},{7,6},{8,9},{9,8},{10,11... | collective-permute-start | bytes 3932168 | tf_op jit(solution)/shard_map/ppermute | solution.py:415
  136.1 39.6 %collective-permute-start.7 = (f32[2,16,16,640]{3,2,1,0:T(8,128)}, f32[2,16,16,640]{3,2,1,0:T(8,128)S(1)}, u32[]{:S(2)}, u32[]{:S(2)}) collective-permute-start(f32[2,16,16,640]{3,2,1,0:T(8,128)} %get-tuple-element.32), channel_id=1, source_target_pairs={{0,1},{1,0},{2,3},{3,2},{4,5},{5,4},{6,7},{7,6},{8,9},{9,8},{10,11... | collective-permute-start | bytes 3932168 | tf_op jit(solution)/shard_map/ppermute | solution.py:415
  145.4 2.2 collective-permute-start.10
  145.9 2.5 collective-permute-start.9
  155.3 11.6 %collective-permute-start.11 = (s16[2,3,16,16,128]{4,3,2,1,0:T(8,128)(2,1)}, s16[2,3,16,16,128]{4,3,2,1,0:T(8,128)(2,1)S(1)}, u32[]{:S(2)}, u32[]{:S(2)}) collective-permute-start(s16[2,3,16,16,128]{4,3,2,1,0:T(8,128)(2,1)} %get-tuple-element.38), channel_id=1, source_target_pairs={{0,2},{1,3},{2,0},{3,1},{4,6},{5,7},{6,4},{7,5},{8,10},{9,11},{10,... | collective-permute-start | bytes 1179656 | tf_op jit(solution)/shard_map/ppermute | solution.py:418
  169.9 40.7 %all-to-all-start.4 = ((s16[8,17,16,128]{3,2,1,0:T(8,128)(2,1)}), s16[8,17,16,128]{3,2,1,0:T(8,128)(2,1)S(1)}, u32[]{:S(2)}, u32[]{:S(2)}) async-start(s16[8,17,16,128]{3,2,1,0:T(8,128)(2,1)} %send_codes.3), calls=%async_computation.4 | async-start | bytes 1114112 | tf_op jit(solution)/shard_map/all_to_all | solution.py:421
  176.7 1.1 copy-start.10
  187.6 18.9 %collective-permute-start.8 = (s16[2,6,16,16,128]{4,3,2,1,0:T(8,128)(2,1)}, s16[2,6,16,16,128]{4,3,2,1,0:T(8,128)(2,1)S(1)}, u32[]{:S(2)}, u32[]{:S(2)}) collective-permute-start(s16[2,6,16,16,128]{4,3,2,1,0:T(8,128)(2,1)} %get-tuple-element.34), channel_id=1, source_target_pairs={{0,2},{1,3},{2,0},{3,1},{4,6},{5,7},{6,4},{7,5},{8,10},{9,11},{10,... | collective-permute-start | bytes 2359304 | tf_op jit(solution)/shard_map/ppermute | solution.py:418
  210.6 5.7 %copy-start.2 = (s16[8,17,16,128]{3,2,1,0:T(8,128)(2,1)}, s16[8,17,16,128]{3,2,1,0:T(8,128)(2,1)S(1)}, u32[]{:S(2)}) copy-start(s16[8,17,16,128]{3,2,1,0:T(8,128)(2,1)S(1)} %all-to-all-done.4.arrived) | copy-start | bytes 1671172
  210.6 36.2 %all-to-all-start.3 = ((s16[8,41,16,128]{3,2,1,0:T(8,128)(2,1)}), s16[8,41,16,128]{3,2,1,0:T(8,128)(2,1)S(1)}, u32[]{:S(2)}, u32[]{:S(2)}) async-start(s16[8,41,16,128]{3,2,1,0:T(8,128)(2,1)} %send_codes.2), calls=%async_computation.3 | async-start | bytes 2686976 | tf_op jit(solution)/shard_map/all_to_all | solution.py:421
  246.9 1.1 copy-start
  (9 other events, 7.6 us)

commit v4 on v3

v4 whole, which is shorter than its diff:
```python
import functools
import math

import jax
import jax.numpy as jnp
from jax import lax
from jax.experimental import pallas as pl
from jax.experimental.pallas import tpu as pltpu
from jax.sharding import PartitionSpec as P

HD = 128
SPAN = 64
SUB = 16
LANES = 128
VMEM_LIMIT = 28 * 1024 * 1024
F32 = jnp.float32
BF16 = jnp.bfloat16

ANY = pl.BlockSpec(memory_space=pl.ANY)
SMEM = pl.BlockSpec(memory_space=pltpu.SMEM)
VMEM = pl.BlockSpec(memory_space=pltpu.VMEM)


def params():
    return pltpu.CompilerParams(vmem_limit_bytes=VMEM_LIMIT)


def cost(flops, nbytes):
    return pl.CostEstimate(flops=int(flops), bytes_accessed=int(nbytes), transcendentals=0)


def ask_body(cap, me, owners, slots, wanted, request, count):
    n_dp = wanted.shape[0] // cap
    for i in range(n_dp * cap):
        wanted[i] = -1
        request[i] = -1
    for d in range(n_dp):
        count[d] = 0
    for r in range(owners.size):
        d = owners[r % 2, r // 2] - me[0]
        d = jnp.where(d < 0, d + n_dp, d)
        j = count[d]
        count[d] = j + 1
        wanted[d * cap + j] = slots[r % 2, r // 2]
        request[d * cap + j] = r


def ask(me, owners, slots, n_dp, cap):
    shape = jax.ShapeDtypeStruct((n_dp * cap,), jnp.int32)
    return pl.pallas_call(
        functools.partial(ask_body, cap),
        out_shape=[shape, shape],
        in_specs=[SMEM, SMEM, SMEM],
        out_specs=[SMEM, SMEM],
        scratch_shapes=[pltpu.SMEM((n_dp,), jnp.int32)],
        name="ask",
    )(me, owners.T, slots.T)


def pack_body(n_dp, n_chunks, *refs):
    asked, (first, table), rest = refs[:n_dp], refs[n_dp : n_dp + 2], refs[n_dp + 2 :]
    outs, sem = rest[:-1], rest[-1]
    cap = outs[0].shape[0]

    def each(act):
        for c in range(n_chunks):
            row = pl.multiple_of(first[0] + c * SUB, SUB)
            for d in range(n_dp):
                for j in range(cap):
                    slab = asked[d][d * cap + j]

                    @pl.when(slab >= 0)
                    def _():
                        act(
                            pltpu.make_async_copy(
                                table.at[slab, pl.ds(row, SUB)],
                                outs[c * n_dp + d].at[j],
                                sem.at[c, d * cap + j],
                            )
                        )

    each(lambda copy: copy.start())
    each(lambda copy: copy.wait())


def pack(asked, first, table, n_chunks, cap):
    n_dp = len(asked)
    enc = table.shape[2]
    return pl.pallas_call(
        functools.partial(pack_body, n_dp, n_chunks),
        out_shape=[jax.ShapeDtypeStruct((cap, SUB, enc), table.dtype)] * (n_chunks * n_dp),
        in_specs=[SMEM] * n_dp + [SMEM, ANY],
        out_specs=[VMEM] * (n_chunks * n_dp),
        scratch_shapes=[pltpu.SemaphoreType.DMA((n_chunks, n_dp * cap))],
        compiler_params=params(),
        cost_estimate=cost(0, 4 * n_chunks * n_dp * cap * SUB * enc),
        name="pack_rows",
    )(*asked, first, table)


def compact_body(n_dp, request, *refs):
    arrived, out, sem = refs[:n_dp], refs[n_dp], refs[n_dp + 1]
    cap = arrived[0].shape[0]

    def each(act):
        for d in range(n_dp):
            for j in range(cap):
                r = request[d * cap + j]

                @pl.when(r >= 0)
                def _():
                    act(pltpu.make_async_copy(arrived[d].at[j], out.at[r], sem.at[d * cap + j]))

    each(lambda copy: copy.start())
    each(lambda copy: copy.wait())


def compact(request, arrived, n):
    shape = (n,) + arrived[0].shape[1:]
    return pl.pallas_call(
        functools.partial(compact_body, len(arrived)),
        out_shape=jax.ShapeDtypeStruct(shape, arrived[0].dtype),
        in_specs=[SMEM] + [ANY] * len(arrived),
        out_specs=VMEM,
        scratch_shapes=[pltpu.SemaphoreType.DMA((request.shape[0],))],
        compiler_params=params(),
        cost_estimate=cost(0, 4 * math.prod(shape)),
        name="compact_rows",
    )(request, *arrived)


def weight_specs(rows, step):
    return [
        pl.BlockSpec((rows, step), lambda i: (0, jnp.minimum(i, 1))),
        pl.BlockSpec((rows, step), lambda i: (0, jnp.maximum(i - 2, 0))),
    ]


def with_weight(wk, wv, act):
    @pl.when(pl.program_id(0) < 2)
    def _():
        act(wk)

    @pl.when(pl.program_id(0) >= 2)
    def _():
        act(wv)


def project_body(n_in, *refs):
    wk, wv, out = refs[n_in : n_in + 3]
    n, sub, enc = refs[0].shape
    rows = jnp.concatenate([ref[...].reshape(n * sub, enc) for ref in refs[:n_in]], axis=0)

    def act(w):
        res = jnp.dot(rows, w[...], preferred_element_type=F32)
        out[...] = res.astype(BF16).reshape(out.shape)

    with_weight(wk, wv, act)


def project(pieces, wk, wv):
    n_in = len(pieces)
    n, sub, enc = pieces[0].shape
    width = 2 * wk.shape[1]
    step = width // 4
    return pl.pallas_call(
        functools.partial(project_body, n_in),
        out_shape=jax.ShapeDtypeStruct((n_in, n, sub, width), BF16),
        grid=(4,),
        in_specs=[pl.BlockSpec((n, sub, enc), lambda i: (0, 0, 0))] * n_in
        + weight_specs(enc, step),
        out_specs=pl.BlockSpec((n_in, n, sub, step), lambda i: (0, 0, 0, i)),
        compiler_params=params(),
        cost_estimate=cost(
            2 * n_in * n * sub * enc * width, 2 * (n_in * n * sub * (enc + width) + enc * width)
        ),
        name="project",
    )(*pieces, wk, wv)


def attend_body(places, n_kv, *refs):
    kvs = refs[:n_kv]
    q_ref, g_ref, att_ref, dq_ref = refs[n_kv : n_kv + 4]
    grads = refs[n_kv + 4 :]
    width = q_ref.shape[1]
    scale = 1.0 / math.sqrt(HD)
    heads = width // HD
    group = min(4, heads)

    def keys_of(col):
        parts = [ref[:, :, :, pl.ds(col, HD)].reshape(-1, HD) for ref in kvs]
        return jnp.concatenate(parts, axis=0)

    def put(col, grad):
        for at, (ref, i) in enumerate(places):
            block = grad[at * 2 * SUB : (at + 1) * 2 * SUB]
            grads[ref][i, :, :, pl.ds(col, HD)] = block.reshape(2, SUB, HD)

    last = (((1,), (1,)), ((), ()))
    first = (((0,), (0,)), ((), ()))

    def dot(a, b, dims=(((1,), (0,)), ((), ()))):
        return lax.dot_general(a, b, dims, preferred_element_type=F32)

    for h0 in range(0, heads, group):
        hs = range(h0, h0 + group)
        q = [q_ref[:, pl.ds(h * HD, HD)] for h in hs]
        g = [g_ref[:, pl.ds(h * HD, HD)] for h in hs]
        k = [keys_of(h * HD) for h in hs]
        v = [keys_of(width + h * HD) for h in hs]
        s = jnp.concatenate([dot(a, b, last) for a, b in zip(q, k)], axis=0) * scale
        dw = jnp.concatenate([dot(a, b, last) for a, b in zip(g, v)], axis=0)
        e = jnp.exp(s - jnp.max(s, axis=1, keepdims=True))
        p = e * (1.0 / jnp.sum(e, axis=1, keepdims=True))
        rs = jnp.sum(dw * p, axis=1, keepdims=True)
        w = p.astype(BF16)
        ds = (p * (dw - rs) * scale).astype(BF16)
        ws = [w[i * SPAN : (i + 1) * SPAN] for i in range(group)]
        dss = [ds[i * SPAN : (i + 1) * SPAN] for i in range(group)]
        att = [dot(a, b).astype(BF16) for a, b in zip(ws, v)]
        dq = [dot(a, b).astype(BF16) for a, b in zip(dss, k)]
        dk = [dot(a, b, first).astype(BF16) for a, b in zip(dss, q)]
        dv = [dot(a, b, first).astype(BF16) for a, b in zip(ws, g)]
        for i, h in enumerate(hs):
            att_ref[:, pl.ds(h * HD, HD)] = att[i]
            dq_ref[:, pl.ds(h * HD, HD)] = dq[i]
            put(h * HD, dk[i])
            put(width + h * HD, dv[i])


def attend(kvs, places, sizes, queries, cotangent):
    tokens, width = queries.shape
    spans = tokens // SPAN
    n = kvs[0].shape[1]
    rows = pl.BlockSpec((SPAN, width), lambda i: (i, 0))

    def kv_block(pieces):
        return pl.BlockSpec((pieces, 2, SUB, 2 * width), lambda i: (0, i, 0, 0))

    keys = len(places) * 2 * SUB
    out = pl.pallas_call(
        functools.partial(attend_body, places, len(kvs)),
        out_shape=[jax.ShapeDtypeStruct((tokens, width), BF16)] * 2
        + [jax.ShapeDtypeStruct((size, n, SUB, 2 * width), BF16) for size in sizes],
        grid=(spans,),
        in_specs=[kv_block(kv.shape[0]) for kv in kvs] + [rows, rows],
        out_specs=[rows, rows] + [kv_block(size) for size in sizes],
        compiler_params=params(),
        cost_estimate=cost(12 * tokens * width * keys, 8 * tokens * width + 8 * spans * keys * 2 * width),
        name="attend",
    )(*kvs, queries, cotangent)
    return out[0], out[1], out[2:]


def encode(x, axes):
    top = jnp.maximum(jnp.max(jnp.abs(x), axis=axes, keepdims=True), 1e-30)
    power = jnp.floor(jnp.log2(top)) + 1.0
    code = jnp.clip(jnp.round(x * jnp.exp2(15.0 - power)), -32767.0, 32767.0)
    return code.astype(jnp.int32).astype(jnp.int16), power


def grad_step(first, d_ref, wk, wv, acc):
    i = pl.program_id(0)
    pieces, n, sub, step = d_ref.shape
    rows = d_ref[...].reshape(pieces * n * sub, step)

    def act(w):
        w = w[first : first + acc.shape[1], :]
        part = lax.dot_general(rows, w, (((1,), (1,)), ((), ())), preferred_element_type=F32)

        @pl.when(i == 0)
        def _():
            acc[...] = part

        @pl.when(i > 0)
        def _():
            acc[...] += part

    with_weight(wk, wv, act)


def core_grad_body(near, first, d_ref, wk, wv, near_out, far_out, acc):
    grad_step(first, d_ref, wk, wv, acc)

    @pl.when(pl.program_id(0) == pl.num_programs(0) - 1)
    def _():
        full = acc[...].reshape(d_ref.shape[:3] + acc.shape[1:])
        near_out[...] = full[:near]
        far_out[...] = full[near:]


def own_grad_body(near, first, d_ref, wk, wv, near_got, far_got, near_out, *rest):
    codes, acc = rest[:-1], rest[-1]
    grad_step(first, d_ref, wk, wv, acc)

    @pl.when(pl.program_id(0) == pl.num_programs(0) - 1)
    def _():
        full = acc[...].reshape(d_ref.shape[:3] + acc.shape[1:])
        near_out[...] = full[:near] + near_got[...]
        n = d_ref.shape[1]
        tiles = acc.shape[1] // LANES
        row = lax.broadcasted_iota(jnp.int32, (SUB, LANES), 0)
        for i in range(far_got.shape[0]):
            out, c = codes[i // near], i % near
            code, power = encode(full[near + i] + far_got[i], (1, 2))
            for e in range(tiles):
                out[c, e * n : (e + 1) * n] = code[:, :, e * LANES : (e + 1) * LANES]
            note = jnp.zeros((SUB, LANES), F32)
            for r in range(n):
                note = jnp.where(row == r, power[r], note)
            out[c, tiles * n] = note.astype(jnp.int32).astype(jnp.int16)


def grads_of(d_kv, wk, wv, near, cols, got=None):
    pieces, n, sub, width = d_kv.shape
    far = pieces - near
    first, count = cols
    step = width // 4
    tiles = count // LANES
    near_shape, far_shape = (near, n, sub, count), (far, n, sub, count)

    def whole(shape):
        return pl.BlockSpec(shape, lambda i: (0,) * len(shape))

    if got is None:
        body, outs = core_grad_body, [(near_shape, F32), (far_shape, F32)]
    else:
        body = own_grad_body
        outs = [(near_shape, F32)] + [((near, tiles * n + 1, sub, LANES), jnp.int16)] * (far // near)
    out = pl.pallas_call(
        functools.partial(body, near, first),
        out_shape=[jax.ShapeDtypeStruct(*o) for o in outs],
        grid=(4,),
        in_specs=[pl.BlockSpec((pieces, n, sub, step), lambda i: (0, 0, 0, i))]
        + weight_specs(wk.shape[0], step)
        + ([] if got is None else [whole(near_shape), whole(far_shape)]),
        out_specs=[whole(shape) for shape, _ in outs],
        scratch_shapes=[pltpu.VMEM((pieces * n * sub, count), F32)],
        compiler_params=params(),
        cost_estimate=cost(2 * pieces * n * sub * count * width, 2 * (count + pieces * n * sub) * width),
        name="core_grads" if got is None else "own_grads",
    )(
        d_kv,
        wk,
        wv,
        *([] if got is None else got),
    )
    return out[0], out[1:]


def send_body(n_dp, request, own, *rest):
    codes, outs, (stage, powers) = rest[: -n_dp - 2], rest[-n_dp - 2 : -2], rest[-2:]
    n_chunks, n, sub, count = own.shape
    tiles = count // LANES
    cap = request.shape[0] // n_dp
    for c in range(n_chunks):
        for r in range(n):
            total = own[c, r]
            for code in codes:
                unit = jnp.exp2(code[c, tiles * n].astype(F32)[r : r + 1] - 15.0)
                total = total + jnp.concatenate(
                    [code[c, e * n + r].astype(F32) * unit for e in range(tiles)], axis=1
                )
            coded, power = encode(total, (0, 1))
            for e in range(tiles):
                stage[r, c * tiles + e] = coded[:, e * LANES : (e + 1) * LANES]
            powers[r, c] = jnp.broadcast_to(power, (SUB, LANES))
    row = lax.broadcasted_iota(jnp.int32, (SUB, LANES), 0)
    for d in range(n_dp):
        note = jnp.zeros((SUB, LANES), F32)
        for j in range(cap):
            r = request[d * cap + j]

            @pl.when(r >= 0)
            def _():
                outs[d][pl.ds(j * n_chunks * tiles, n_chunks * tiles)] = stage[r]

            for c in range(n_chunks):
                note = jnp.where(row == j * n_chunks + c, powers[jnp.maximum(r, 0), c], note)
        outs[d][cap * n_chunks * tiles] = note.astype(jnp.int32).astype(jnp.int16)


def send_codes(request, own, codes, n_dp):
    n_chunks, n, sub, count = own.shape
    tiles = count // LANES
    cap = request.shape[0] // n_dp
    shape = (cap * n_chunks * tiles + 1, SUB, LANES)
    return pl.pallas_call(
        functools.partial(send_body, n_dp),
        out_shape=[jax.ShapeDtypeStruct(shape, jnp.int16)] * n_dp,
        in_specs=[SMEM, VMEM] + [VMEM] * len(codes),
        out_specs=[VMEM] * n_dp,
        scratch_shapes=[
            pltpu.VMEM((n, n_chunks * tiles, SUB, LANES), jnp.int16),
            pltpu.VMEM((n, n_chunks, SUB, LANES), F32),
        ],
        compiler_params=params(),
        cost_estimate=cost(10 * own.size, 6 * own.size + 2 * n_dp * math.prod(shape)),
        name="send_codes",
    )(request, own, *codes)


def gather_body(n_dp, n_chunks, first, *refs):
    asked, arrived = refs[:n_dp], refs[n_dp : 2 * n_dp]
    out, total, sem = refs[-3:]
    count = total.shape[2]
    tiles = count // LANES
    cap = asked[0].shape[0] // n_dp
    total[...] = jnp.zeros_like(total)
    for d in range(n_dp):
        for j in range(cap):
            slab = asked[d][d * cap + j]

            @pl.when(slab >= 0)
            def _():
                note = arrived[d][cap * n_chunks * tiles].astype(F32)
                for c in range(n_chunks):
                    at = j * n_chunks + c
                    unit = jnp.exp2(note[at : at + 1] - 15.0)
                    for e in range(tiles):
                        value = arrived[d][at * tiles + e].astype(F32) * unit
                        total[slab, pl.ds(c * SUB, SUB), pl.ds(e * LANES, LANES)] += value

    copy = pltpu.make_async_copy(total, out.at[:, :, pl.ds(first, count)], sem)
    copy.start()
    copy.wait()


def gather_grads(asked, arrived, n_slabs, n_chunks, enc, cols, before):
    first, count = cols
    n_dp = len(asked)
    rows = n_chunks * SUB
    return pl.pallas_call(
        functools.partial(gather_body, n_dp, n_chunks, first),
        out_shape=jax.ShapeDtypeStruct((n_slabs, rows, enc), F32),
        in_specs=[SMEM] * n_dp + [VMEM] * n_dp + [ANY] * (before is not None),
        out_specs=ANY,
        scratch_shapes=[pltpu.VMEM((n_slabs, rows, count), F32), pltpu.SemaphoreType.DMA],
        input_output_aliases={} if before is None else {2 * n_dp: 0},
        compiler_params=params(),
        cost_estimate=cost(0, 8 * n_slabs * rows * count),
        name="gather_grads",
    )(*asked, *arrived, *([] if before is None else [before]))


def on_device(queries, cotangent, table, key_weight, value_weight, owners, slots):
    n_dp = lax.axis_size("dp")
    n_tp = lax.axis_size("tensor")
    n_x = n_tp // 2
    spans = owners.shape[0]
    n_requests = 2 * spans
    n_slabs, n_tokens, enc = table.shape
    cap = max(2, (4 * spans + n_dp - 1) // n_dp)
    share = n_tokens // n_tp
    n_chunks = share // SUB

    def over_core(x):
        return lax.ppermute(x, "tensor", [(t, t ^ 1) for t in range(n_tp)])

    def over_x(x, d):
        return lax.ppermute(x, "tensor", [(t, (t + 2 * d) % n_tp) for t in range(n_tp)])

    def over_dp(x, d):
        return lax.ppermute(x, "dp", [(i, (i + d) % n_dp) for i in range(n_dp)])

    def to_all(xs, sign):
        return [xs[0]] + [over_dp(xs[d], sign * d) for d in range(1, n_dp)]

    me = lax.axis_index("dp").astype(jnp.int32).reshape(1)
    wanted, request = ask(me, owners, slots, n_dp, cap)
    asked = to_all([wanted] * n_dp, 1)
    first = (lax.axis_index("tensor") * share).astype(jnp.int32).reshape(1)

    def place(c, kind, d):
        return (kind, c if d == 0 else n_chunks * d + c)

    kvs, places = [], []
    packed = pack(asked, first, table, n_chunks, cap)
    for c in range(n_chunks):
        arrived = to_all(packed[c * n_dp : (c + 1) * n_dp], -1)
        if kvs:
            arrived, kvs = lax.optimization_barrier((arrived, kvs))
        mine = compact(request, arrived, n_requests)
        near = [mine, over_core(mine)]
        far = [over_x(mine, d) for d in range(1, n_x)]
        near_at = [place(c, kind, 0) for kind in range(2)]
        far_at = [place(c, kind, d) for kind in range(2) for d in range(1, n_x)]
        if c < n_chunks - 1:
            far = far + [over_core(x) for x in far]
            kvs = kvs + [project(near + far, key_weight, value_weight)]
        else:
            near = project(near, key_weight, value_weight)
            near, far = lax.optimization_barrier((near, far))
            far = far + [over_core(x) for x in far]
            kvs = kvs + [near, project(far, key_weight, value_weight)]
        places += near_at + far_at

    sizes = [n_chunks * n_x, n_chunks * n_x]
    attended, d_query, (d_own, d_core) = attend(kvs, places, sizes, queries, cotangent)

    lead = 3 * LANES
    d_table = None
    for cols in ((0, lead), (lead, enc - lead)):
        grads = grads_of(d_core, key_weight, value_weight, n_chunks, cols)
        got = over_core(grads[0]), over_core(grads[1][0])
        own, codes = grads_of(d_own, key_weight, value_weight, n_chunks, cols, got)
        if d_table is None:
            codes, d_core = lax.optimization_barrier((codes, d_core))
        codes = [over_x(code, n_x - d) for d, code in enumerate(codes, 1)]
        arrived = to_all(send_codes(request, own, codes, n_dp), 1)
        d_table = gather_grads(asked, arrived, n_slabs, n_chunks, enc, cols, d_table)
    return (attended, d_query, d_table)


def solution(mesh):
    in_specs = (
        P("dp", "tensor"),
        P("dp", "tensor"),
        P("dp", None, None),
        P(None, "tensor"),
        P(None, "tensor"),
        P("dp", None),
        P("dp", None),
    )
    out_specs = (P("dp", "tensor"), P("dp", "tensor"), P("dp", "tensor", None))
    return jax.shard_map(
        on_device, mesh=mesh, in_specs=in_specs, out_specs=out_specs, check_vma=False
    )
```

time: 252 us -> 221 us (0.88)
  the two profiles are of different devices: /device:TPU:0 before, /device:TPU:13 now
where the time goes in v4:
time: 221 us; the launch traced here: 219 us
  waiting for transfers between devices  83.8 us (38%)
  starting transfers between devices  71.2 us (32%)
  Pallas kernels  60.2 us (27%)
  local copies, waits for them, and re-layouts  2.73 us (1%)
    ppermute x35, starting transfers between devices, over_dp(): return lax.ppermute(x, 'dp', [(i, (i + d) % n_dp) for i in range(n_dp)])  55.7 us
    ppermute x35, waiting for transfers between devices, over_dp(): return lax.ppermute(x, 'dp', [(i, (i + d) % n_dp) for i in range(n_dp)])  45.3 us
    ppermute x4, waiting for transfers between devices, over_x(): lax.ppermute(x, 'tensor', [(t, (t + 2 * d) % n_tp) for t in range(n_tp)])  30.3 us
    pallas_call x4, Pallas kernels, grads_of(): pl.pallas_call(functools.partial(body, near, first), out_shape=[jax.Shape...  19.2 us
    pallas_call x3, Pallas kernels, project(): pl.pallas_call(functools.partial(project_body, n_in), out_shape=jax.Shape...  13.3 us
    pallas_call x1, Pallas kernels, attend(): pl.pallas_call(functools.partial(attend_body, places, len(kvs)), out_shap...  13 us
    ppermute x8, starting transfers between devices, over_core(): return lax.ppermute(x, 'tensor', [(t, t ^ 1) for t in range(n_tp)])  11.4 us
    ppermute x8, waiting for transfers between devices, over_core(): return lax.ppermute(x, 'tensor', [(t, t ^ 1) for t in range(n_tp)])  8.21 us
  transfers between devices with their start and end apart: 47, of which 26 were waited for; matrix products, arithmetic and copies ran while one was open for 0% of the time, Pallas kernels for 7%

profile of v4, /device:TPU:13, one launch (start us, length us, event | category | flops | bytes accessed | tf_op | source)
XLA Modules:
  0.0 219.0 jit_solution(6807530326786684551)
XLA Ops:
  2.3 4.3 %collective-permute-start.4 = (s32[32]{0:T(128)}, s32[32]{0:T(128)S(1)}, u32[]{:S(2)}, u32[]{:S(2)}) collective-permute-start(s32[32]{0:T(128)} %get-tuple-element.62.refs_0_), channel_id=1, source_target_pairs={{0,20},{4,24},{8,28},{12,0},{16,4},{20,8},{24,12},{28,16},{1,21},{... | collective-permute-start | bytes 392 | tf_op jit(solution)/shard_map/ppermute | solution.py:464
  15.9 3.2 %pack_rows.1 = (bf16[4,16,896]{2,1,0:T(8,128)(2,1)S(1)}, bf16[4,16,896]{2,1,0:T(8,128)(2,1)S(1)}, bf16[4,16,896]{2,1,0:T(8,128)(2,1)S(1)}, bf16[4,16,896]{2,1,0:...) custom-call(s32[32]{0:T(128)S(1)} %copy-done.6, ...), custom_call_target="tpu_custom_call" | custom-call | bytes 3670016 | tf_op jit(solution)/shard_map/pack_rows/pallas_call | solution.py:89
  19.2 2.6 %collective-permute-start.15 = (bf16[4,16,896]{2,1,0:T(8,128)(2,1)S(1)}, bf16[4,16,896]{2,1,0:T(8,128)(2,1)S(1)}, u32[]{:S(2)}, u32[]{:S(2)}) collective-permute-start(bf16[4,16,896]{2,1,0:T(8,128)(2,1)S(1)} %get-tuple-element.74), channel_id=1, source_target_pairs={{0,24},{4,28},{8,0},{12,4},{16,8},{20,12},{24,16},{28,20},{1,25},{... | collective-permute-start | bytes 344072 | tf_op jit(solution)/shard_map/ppermute | solution.py:464
  28.5 4.0 %collective-permute-done.17.refs_4_ = bf16[4,16,896]{2,1,0:T(8,128)(2,1)S(1)} collective-permute-done((bf16[4,16,896]{2,1,0:T(8,128)(2,1)S(1)}, bf16[4,16,896]{2,1,0:T(8,128)(2,1)S(1)}, u32[]{:S(2)}, u32[]{:S(2)}) %collective-permute-start.17) | collective-permute-done | bytes 114720 | tf_op jit(solution)/shard_map/ppermute | solution.py:464
  32.5 5.0 %collective-permute-done.18.refs_5_ = bf16[4,16,896]{2,1,0:T(8,128)(2,1)S(1)} collective-permute-done((bf16[4,16,896]{2,1,0:T(8,128)(2,1)S(1)}, bf16[4,16,896]{2,1,0:T(8,128)(2,1)S(1)}, u32[]{:S(2)}, u32[]{:S(2)}) %collective-permute-start.18) | collective-permute-done | bytes 114720 | tf_op jit(solution)/shard_map/ppermute | solution.py:464
  44.1 4.1 %collective-permute-start.21 = (bf16[16,16,896]{2,1,0:T(8,128)(2,1)S(1)}, bf16[16,16,896]{2,1,0:T(8,128)(2,1)S(1)}, u32[]{:S(2)}, u32[]{:S(2)}) collective-permute-start(bf16[16,16,896]{2,1,0:T(8,128)(2,1)S(1)} %compact_rows.2.refs_0_), channel_id=1, source_target_pairs={{0,1},{1,0},{2,3},{3,2},{4,5},{5,4},{6,7},{7,6},{8,9},{9,8},{10,11... | collective-permute-start | bytes 1376264 | tf_op jit(solution)/shard_map/ppermute | solution.py:458
  48.2 2.9 %collective-permute-done.22.refs_2_ = bf16[16,16,896]{2,1,0:T(8,128)(2,1)S(1)} collective-permute-done((bf16[16,16,896]{2,1,0:T(8,128)(2,1)S(1)}, bf16[16,16,896]{2,1,0:T(8,128)(2,1)S(1)}, u32[]{:S(2)}, u32[]{:S(2)}) %collective-permute-start.22) | collective-permute-done | bytes 458784 | tf_op jit(solution)/shard_map/ppermute | solution.py:461
  51.0 4.8 %collective-permute-start.23 = (bf16[16,16,896]{2,1,0:T(8,128)(2,1)S(1)}, bf16[16,16,896]{2,1,0:T(8,128)(2,1)S(1)}, u32[]{:S(2)}, u32[]{:S(2)}) collective-permute-start(bf16[16,16,896]{2,1,0:T(8,128)(2,1)S(1)} %collective-permute-done.22.refs_2_), channel_id=1, source_target_pairs={{0,1},{1,0},{2,3},{3,2},{4,5},{5,4},{6,7},{7,6},{8,9},{9,8},{10,11... | collective-permute-start | bytes 1376264 | tf_op jit(solution)/shard_map/ppermute | solution.py:458
  66.4 6.2 %project.3.refs_0_ = bf16[4,16,16,2048]{3,2,1,0:T(8,128)(2,1)S(1)} custom-call(bf16[16,16,896]{2,1,0:T(8,128)(2,1)S(1)} %compact_rows.2.refs_0_, bf16[16,16,896]{2,1,0:T(8,128)(2,1)S(1)} %collective-permute-done.21.refs_1_, bf16[16,16,896]{2,1,0:T(8,128)(2,1)S(1)} %collective-permute-done.22.refs_2_, ...), custom_call_target="tpu_custom_call" | custom-call | flops 3758096384 | bytes 9699328 | tf_op jit(solution)/shard_map/project/pallas_call | solution.py:166
  82.1 3.6 %project.4.refs_1_ = bf16[2,16,16,2048]{3,2,1,0:T(8,128)(2,1)S(1)} custom-call(bf16[16,16,896]{2,1,0:T(8,128)(2,1)S(1)} %compact_rows.3.refs_0_, bf16[16,16,896]{2,1,0:T(8,128)(2,1)S(1)} %collective-permute-done.24.refs_1_, bf16[896,1024]{1,0:T(8,128)(2,1)S(1)} %copy-done, bf16[896,1024]{1,0:T(8,128)(2,1)S(1)} %copy-done.1), custom_call_target="tpu_custom_call" | custom-call | flops 1879048192 | bytes 6684672 | tf_op jit(solution)/shard_map/project/pallas_call | solution.py:166
  85.7 7.0 %collective-permute-done.25.refs_0_ = bf16[16,16,896]{2,1,0:T(8,128)(2,1)S(1)} collective-permute-done((bf16[16,16,896]{2,1,0:T(8,128)(2,1)S(1)}, bf16[16,16,896]{2,1,0:T(8,128)(2,1)S(1)}, u32[]{:S(2)}, u32[]{:S(2)}) %collective-permute-start.25) | collective-permute-done | bytes 458784 | tf_op jit(solution)/shard_map/ppermute | solution.py:461
  95.0 3.6 %project.5.refs_2_ = bf16[2,16,16,2048]{3,2,1,0:T(8,128)(2,1)S(1)} custom-call(bf16[16,16,896]{2,1,0:T(8,128)(2,1)S(1)} %collective-permute-done.25.refs_0_, bf16[16,16,896]{2,1,0:T(8,128)(2,1)S(1)} %collective-permute-done.26.refs_1_, bf16[896,1024]{1,0:T(8,128)(2,1)S(1)} %copy-done, bf16[896,1024]{1,0:T(8,128)(2,1)S(1)} %copy-done.1), custom_call_target="tpu_custom_call" | custom-call | flops 1879048192 | bytes 6684672 | tf_op jit(solution)/shard_map/project/pallas_call | solution.py:166
  98.7 13.0 %attend.1 = (bf16[512,1024]{1,0:T(8,128)(2,1)}, bf16[512,1024]{1,0:T(8,128)(2,1)}, bf16[4,16,16,2048]{3,2,1,0:T(8,128)(2,1)S(1)}, bf16[4,16,16,2048]{3,2,1,0:T(8,128)(2,1)S(1)}) custom-call(bf16[4,16,16,2048]{3,2,1,0:T(8,128)(2,1)S(1)} %project.3.refs_0_, bf16[2,16,16,2048]{3,2,1,0:T(8,128)(2,1)S(1)} %project.4.refs_1_, ...), custom_call_target="tpu_custom_call" | custom-call | flops 1610612736 | bytes 37748736 | tf_op jit(solution)/shard_map/attend/pallas_call | solution.py:241
  111.7 4.5 %core_grads.2 = (f32[2,16,16,384]{3,2,1,0:T(8,128)S(1)}, f32[2,16,16,384]{3,2,1,0:T(8,128)S(1)}) custom-call(bf16[4,16,16,2048]{3,2,1,0:T(8,128)(2,1)S(1)} %get-tuple-element.98.d_ref, bf16[896,1024]{1,0:T(8,128)(2,1)S(1)} %copy-done, bf16[896,1024]{1,0:T(8,128)(2,1)S(1)} %copy-done.1), custom_call_target="tpu_custom_call" | custom-call | flops 1610612736 | bytes 5767168 | tf_op jit(solution)/shard_map/core_grads/pallas_call | solution.py:330
  119.6 4.8 %own_grads.2 = (f32[2,16,16,384]{3,2,1,0:T(8,128)S(1)}, s16[2,49,16,128]{3,2,1,0:T(8,128)(2,1)S(1)}) custom-call(bf16[4,16,16,2048]{3,2,1,0:T(8,128)(2,1)S(1)} %get-tuple-element.93.d_ref, bf16[896,1024]{1,0:T(8,128)(2,1)S(1)} %copy-done, bf16[896,1024]{1,0:T(8,128)(2,1)S(1)} %copy-done.1, f32[2,16,16,384]{3,2,1,0:T(8,128)S(1)} %collective-permute-done.27.near_got, ...), custom_call_target="tpu_custom_call" | custom-call | flops 1610612736 | bytes 5767168 | tf_op jit(solution)/shard_map/own_grads/pallas_call | solution.py:330
  124.5 4.8 %core_grads.3 = (f32[2,16,16,512]{3,2,1,0:T(8,128)S(1)}, f32[2,16,16,512]{3,2,1,0:T(8,128)S(1)}) custom-call(bf16[4,16,16,2048]{3,2,1,0:T(8,128)(2,1)S(1)} %get-tuple-element.98.d_ref, bf16[896,1024]{1,0:T(8,128)(2,1)S(1)} %copy-done, bf16[896,1024]{1,0:T(8,128)(2,1)S(1)} %copy-done.1), custom_call_target="tpu_custom_call" | custom-call | flops 2147483648 | bytes 6291456 | tf_op jit(solution)/shard_map/core_grads/pallas_call | solution.py:330
  133.5 5.1 %own_grads.3 = (f32[2,16,16,512]{3,2,1,0:T(8,128)S(1)}, s16[2,65,16,128]{3,2,1,0:T(8,128)(2,1)S(1)}) custom-call(bf16[4,16,16,2048]{3,2,1,0:T(8,128)(2,1)S(1)} %get-tuple-element.93.d_ref, bf16[896,1024]{1,0:T(8,128)(2,1)S(1)} %copy-done, bf16[896,1024]{1,0:T(8,128)(2,1)S(1)} %copy-done.1, f32[2,16,16,512]{3,2,1,0:T(8,128)S(1)} %collective-permute-done.29.near_got, ...), custom_call_target="tpu_custom_call" | custom-call | flops 2147483648 | bytes 6291456 | tf_op jit(solution)/shard_map/own_grads/pallas_call | solution.py:330
  140.1 20.4 %collective-permute-done.39.rest_0_ = s16[2,49,16,128]{3,2,1,0:T(8,128)(2,1)S(1)} collective-permute-done((s16[2,49,16,128]{3,2,1,0:T(8,128)(2,1)S(1)}, s16[2,49,16,128]{3,2,1,0:T(8,128)(2,1)S(1)}, u32[]{:S(2)}, u32[]{:S(2)}) %collective-permute-start.39) | collective-permute-done | bytes 401440 | tf_op jit(solution)/shard_map/ppermute | solution.py:461
  161.9 7.3 %collective-permute-start.40 = (s16[25,16,128]{2,1,0:T(8,128)(2,1)S(1)}, s16[25,16,128]{2,1,0:T(8,128)(2,1)S(1)}, u32[]{:S(2)}, u32[]{:S(2)}) collective-permute-start(s16[25,16,128]{2,1,0:T(8,128)(2,1)S(1)} %get-tuple-element.114), channel_id=1, source_target_pairs={{0,4},{4,8},{8,12},{12,16},{16,20},{20,24},{24,28},{28,0},{1,5},{5... | collective-permute-start | bytes 307208 | tf_op jit(solution)/shard_map/ppermute | solution.py:464
  181.2 10.0 %collective-permute-start.46 = (s16[25,16,128]{2,1,0:T(8,128)(2,1)S(1)}, s16[25,16,128]{2,1,0:T(8,128)(2,1)S(1)}, u32[]{:S(2)}, u32[]{:S(2)}) collective-permute-start(s16[25,16,128]{2,1,0:T(8,128)(2,1)S(1)} %get-tuple-element.120), channel_id=1, source_target_pairs={{0,28},{4,0},{8,4},{12,8},{16,12},{20,16},{24,20},{28,24},{1,29},{... | collective-permute-start | bytes 307208 | tf_op jit(solution)/shard_map/ppermute | solution.py:464
  192.4 3.0 %collective-permute-done.45.refs_14_ = s16[25,16,128]{2,1,0:T(8,128)(2,1)S(1)} collective-permute-done((s16[25,16,128]{2,1,0:T(8,128)(2,1)S(1)}, s16[25,16,128]{2,1,0:T(8,128)(2,1)S(1)}, u32[]{:S(2)}, u32[]{:S(2)}) %collective-permute-start.45) | collective-permute-done | bytes 102432 | tf_op jit(solution)/shard_map/ppermute | solution.py:464
  201.0 6.1 %collective-permute-done.34.refs_11_ = s16[33,16,128]{2,1,0:T(8,128)(2,1)S(1)} collective-permute-done((s16[33,16,128]{2,1,0:T(8,128)(2,1)S(1)}, s16[33,16,128]{2,1,0:T(8,128)(2,1)S(1)}, u32[]{:S(2)}, u32[]{:S(2)}) %collective-permute-start.34) | collective-permute-done | bytes 135200 | tf_op jit(solution)/shard_map/ppermute | solution.py:464
  207.1 2.9 %collective-permute-done.35.refs_12_ = s16[33,16,128]{2,1,0:T(8,128)(2,1)S(1)} collective-permute-done((s16[33,16,128]{2,1,0:T(8,128)(2,1)S(1)}, s16[33,16,128]{2,1,0:T(8,128)(2,1)S(1)}, u32[]{:S(2)}, u32[]{:S(2)}) %collective-permute-start.35) | collective-permute-done | bytes 135200 | tf_op jit(solution)/shard_map/ppermute | solution.py:464
  210.3 6.4 %collective-permute-done.38.refs_15_ = s16[33,16,128]{2,1,0:T(8,128)(2,1)S(1)} collective-permute-done((s16[33,16,128]{2,1,0:T(8,128)(2,1)S(1)}, s16[33,16,128]{2,1,0:T(8,128)(2,1)S(1)}, u32[]{:S(2)}, u32[]{:S(2)}) %collective-permute-start.38) | collective-permute-done | bytes 135200 | tf_op jit(solution)/shard_map/ppermute | solution.py:464
  (102 shorter events, 78.2 us)
Async XLA Ops:
  25.1 12.5 %collective-permute-start.18 = (bf16[4,16,896]{2,1,0:T(8,128)(2,1)S(1)}, bf16[4,16,896]{2,1,0:T(8,128)(2,1)S(1)}, u32[]{:S(2)}, u32[]{:S(2)}) collective-permute-start(bf16[4,16,896]{2,1,0:T(8,128)(2,1)S(1)} %get-tuple-element.77), channel_id=1, source_target_pairs={{0,12},{4,16},{8,20},{12,24},{16,28},{20,0},{24,4},{28,8},{1,13},{... | collective-permute-start | bytes 344072 | tf_op jit(solution)/shard_map/ppermute | solution.py:464
  26.5 12.8 %collective-permute-start.19 = (bf16[4,16,896]{2,1,0:T(8,128)(2,1)S(1)}, bf16[4,16,896]{2,1,0:T(8,128)(2,1)S(1)}, u32[]{:S(2)}, u32[]{:S(2)}) collective-permute-start(bf16[4,16,896]{2,1,0:T(8,128)(2,1)S(1)} %get-tuple-element.78), channel_id=1, source_target_pairs={{0,8},{4,12},{8,16},{12,20},{16,24},{20,28},{24,0},{28,4},{1,9},{5... | collective-permute-start | bytes 344072 | tf_op jit(solution)/shard_map/ppermute | solution.py:464
  27.4 13.6 %collective-permute-start.20 = (bf16[4,16,896]{2,1,0:T(8,128)(2,1)S(1)}, bf16[4,16,896]{2,1,0:T(8,128)(2,1)S(1)}, u32[]{:S(2)}, u32[]{:S(2)}) collective-permute-start(bf16[4,16,896]{2,1,0:T(8,128)(2,1)S(1)} %get-tuple-element.79), channel_id=1, source_target_pairs={{0,4},{4,8},{8,12},{12,16},{16,20},{20,24},{24,28},{28,0},{1,5},{5... | collective-permute-start | bytes 344072 | tf_op jit(solution)/shard_map/ppermute | solution.py:464
  44.1 21.0 %collective-permute-start.21 = (bf16[16,16,896]{2,1,0:T(8,128)(2,1)S(1)}, bf16[16,16,896]{2,1,0:T(8,128)(2,1)S(1)}, u32[]{:S(2)}, u32[]{:S(2)}) collective-permute-start(bf16[16,16,896]{2,1,0:T(8,128)(2,1)S(1)} %compact_rows.2.refs_0_), channel_id=1, source_target_pairs={{0,1},{1,0},{2,3},{3,2},{4,5},{5,4},{6,7},{7,6},{8,9},{9,8},{10,11... | collective-permute-start | bytes 1376264 | tf_op jit(solution)/shard_map/ppermute | solution.py:458
  51.0 15.1 %collective-permute-start.23 = (bf16[16,16,896]{2,1,0:T(8,128)(2,1)S(1)}, bf16[16,16,896]{2,1,0:T(8,128)(2,1)S(1)}, u32[]{:S(2)}, u32[]{:S(2)}) collective-permute-start(bf16[16,16,896]{2,1,0:T(8,128)(2,1)S(1)} %collective-permute-done.22.refs_2_), channel_id=1, source_target_pairs={{0,1},{1,0},{2,3},{3,2},{4,5},{5,4},{6,7},{7,6},{8,9},{9,8},{10,11... | collective-permute-start | bytes 1376264 | tf_op jit(solution)/shard_map/ppermute | solution.py:458
  57.8 14.8 %collective-permute-start.9 = (bf16[4,16,896]{2,1,0:T(8,128)(2,1)S(1)}, bf16[4,16,896]{2,1,0:T(8,128)(2,1)S(1)}, u32[]{:S(2)}, u32[]{:S(2)}) collective-permute-start(bf16[4,16,896]{2,1,0:T(8,128)(2,1)S(1)} %get-tuple-element.66), channel_id=1, source_target_pairs={{0,20},{4,24},{8,28},{12,0},{16,4},{20,8},{24,12},{28,16},{1,21},{... | collective-permute-start | bytes 344072 | tf_op jit(solution)/shard_map/ppermute | solution.py:464
  62.1 10.5 %collective-permute-start.10 = (bf16[4,16,896]{2,1,0:T(8,128)(2,1)S(1)}, bf16[4,16,896]{2,1,0:T(8,128)(2,1)S(1)}, u32[]{:S(2)}, u32[]{:S(2)}) collective-permute-start(bf16[4,16,896]{2,1,0:T(8,128)(2,1)S(1)} %get-tuple-element.67), channel_id=1, source_target_pairs={{0,16},{4,20},{8,24},{12,28},{16,0},{20,4},{24,8},{28,12},{1,17},{... | collective-permute-start | bytes 344072 | tf_op jit(solution)/shard_map/ppermute | solution.py:464
  63.0 10.4 %collective-permute-start.11 = (bf16[4,16,896]{2,1,0:T(8,128)(2,1)S(1)}, bf16[4,16,896]{2,1,0:T(8,128)(2,1)S(1)}, u32[]{:S(2)}, u32[]{:S(2)}) collective-permute-start(bf16[4,16,896]{2,1,0:T(8,128)(2,1)S(1)} %get-tuple-element.68), channel_id=1, source_target_pairs={{0,12},{4,16},{8,20},{12,24},{16,28},{20,0},{24,4},{28,8},{1,13},{... | collective-permute-start | bytes 344072 | tf_op jit(solution)/shard_map/ppermute | solution.py:464
  65.1 10.8 %collective-permute-start.12 = (bf16[4,16,896]{2,1,0:T(8,128)(2,1)S(1)}, bf16[4,16,896]{2,1,0:T(8,128)(2,1)S(1)}, u32[]{:S(2)}, u32[]{:S(2)}) collective-permute-start(bf16[4,16,896]{2,1,0:T(8,128)(2,1)S(1)} %get-tuple-element.69), channel_id=1, source_target_pairs={{0,8},{4,12},{8,16},{12,20},{16,24},{20,28},{24,0},{28,4},{1,9},{5... | collective-permute-start | bytes 344072 | tf_op jit(solution)/shard_map/ppermute | solution.py:464
  66.2 12.1 %collective-permute-start.13 = (bf16[4,16,896]{2,1,0:T(8,128)(2,1)S(1)}, bf16[4,16,896]{2,1,0:T(8,128)(2,1)S(1)}, u32[]{:S(2)}, u32[]{:S(2)}) collective-permute-start(bf16[4,16,896]{2,1,0:T(8,128)(2,1)S(1)} %get-tuple-element.70), channel_id=1, source_target_pairs={{0,4},{4,8},{8,12},{12,16},{16,20},{20,24},{24,28},{28,0},{1,5},{5... | collective-permute-start | bytes 344072 | tf_op jit(solution)/shard_map/ppermute | solution.py:464
  80.6 12.1 %collective-permute-start.25 = (bf16[16,16,896]{2,1,0:T(8,128)(2,1)S(1)}, bf16[16,16,896]{2,1,0:T(8,128)(2,1)S(1)}, u32[]{:S(2)}, u32[]{:S(2)}) collective-permute-start(bf16[16,16,896]{2,1,0:T(8,128)(2,1)S(1)} %compact_rows.3.refs_0_), channel_id=1, source_target_pairs={{0,2},{1,3},{2,0},{3,1},{4,6},{5,7},{6,4},{7,5},{8,10},{9,11},{10,... | collective-permute-start | bytes 1376264 | tf_op jit(solution)/shard_map/ppermute | solution.py:461
  138.6 33.1 %collective-permute-start.31 = (s16[2,65,16,128]{3,2,1,0:T(8,128)(2,1)S(1)}, s16[2,65,16,128]{3,2,1,0:T(8,128)(2,1)S(1)}, u32[]{:S(2)}, u32[]{:S(2)}) collective-permute-start(s16[2,65,16,128]{3,2,1,0:T(8,128)(2,1)S(1)} %get-tuple-element.102), channel_id=1, source_target_pairs={{0,2},{1,3},{2,0},{3,1},{4,6},{5,7},{6,4},{7,5},{8,10},{9,11},{10,... | collective-permute-start | bytes 1597448 | tf_op jit(solution)/shard_map/ppermute | solution.py:461
  139.9 20.7 %collective-permute-start.39 = (s16[2,49,16,128]{3,2,1,0:T(8,128)(2,1)S(1)}, s16[2,49,16,128]{3,2,1,0:T(8,128)(2,1)S(1)}, u32[]{:S(2)}, u32[]{:S(2)}) collective-permute-start(s16[2,49,16,128]{3,2,1,0:T(8,128)(2,1)S(1)} %get-tuple-element.112), channel_id=1, source_target_pairs={{0,2},{1,3},{2,0},{3,1},{4,6},{5,7},{6,4},{7,5},{8,10},{9,11},{10,... | collective-permute-start | bytes 1204232 | tf_op jit(solution)/shard_map/ppermute | solution.py:461
  161.9 12.2 %collective-permute-start.40 = (s16[25,16,128]{2,1,0:T(8,128)(2,1)S(1)}, s16[25,16,128]{2,1,0:T(8,128)(2,1)S(1)}, u32[]{:S(2)}, u32[]{:S(2)}) collective-permute-start(s16[25,16,128]{2,1,0:T(8,128)(2,1)S(1)} %get-tuple-element.114), channel_id=1, source_target_pairs={{0,4},{4,8},{8,12},{12,16},{16,20},{20,24},{24,28},{28,0},{1,5},{5... | collective-permute-start | bytes 307208 | tf_op jit(solution)/shard_map/ppermute | solution.py:464
  172.9 23.6 %collective-permute-start.32 = (s16[33,16,128]{2,1,0:T(8,128)(2,1)S(1)}, s16[33,16,128]{2,1,0:T(8,128)(2,1)S(1)}, u32[]{:S(2)}, u32[]{:S(2)}) collective-permute-start(s16[33,16,128]{2,1,0:T(8,128)(2,1)S(1)} %get-tuple-element.104), channel_id=1, source_target_pairs={{0,4},{4,8},{8,12},{12,16},{16,20},{20,24},{24,28},{28,0},{1,5},{5... | collective-permute-start | bytes 405512 | tf_op jit(solution)/shard_map/ppermute | solution.py:464
  174.1 23.6 %collective-permute-start.33 = (s16[33,16,128]{2,1,0:T(8,128)(2,1)S(1)}, s16[33,16,128]{2,1,0:T(8,128)(2,1)S(1)}, u32[]{:S(2)}, u32[]{:S(2)}) collective-permute-start(s16[33,16,128]{2,1,0:T(8,128)(2,1)S(1)} %get-tuple-element.105), channel_id=1, source_target_pairs={{0,8},{4,12},{8,16},{12,20},{16,24},{20,28},{24,0},{28,4},{1,9},{5... | collective-permute-start | bytes 405512 | tf_op jit(solution)/shard_map/ppermute | solution.py:464
  176.0 15.2 %collective-permute-start.44 = (s16[25,16,128]{2,1,0:T(8,128)(2,1)S(1)}, s16[25,16,128]{2,1,0:T(8,128)(2,1)S(1)}, u32[]{:S(2)}, u32[]{:S(2)}) collective-permute-start(s16[25,16,128]{2,1,0:T(8,128)(2,1)S(1)} %get-tuple-element.118), channel_id=1, source_target_pairs={{0,20},{4,24},{8,28},{12,0},{16,4},{20,8},{24,12},{28,16},{1,21},{... | collective-permute-start | bytes 307208 | tf_op jit(solution)/shard_map/ppermute | solution.py:464
  178.9 16.6 %collective-permute-start.45 = (s16[25,16,128]{2,1,0:T(8,128)(2,1)S(1)}, s16[25,16,128]{2,1,0:T(8,128)(2,1)S(1)}, u32[]{:S(2)}, u32[]{:S(2)}) collective-permute-start(s16[25,16,128]{2,1,0:T(8,128)(2,1)S(1)} %get-tuple-element.119), channel_id=1, source_target_pairs={{0,24},{4,28},{8,0},{12,4},{16,8},{20,12},{24,16},{28,20},{1,25},{... | collective-permute-start | bytes 307208 | tf_op jit(solution)/shard_map/ppermute | solution.py:464
  181.2 15.3 %collective-permute-start.46 = (s16[25,16,128]{2,1,0:T(8,128)(2,1)S(1)}, s16[25,16,128]{2,1,0:T(8,128)(2,1)S(1)}, u32[]{:S(2)}, u32[]{:S(2)}) collective-permute-start(s16[25,16,128]{2,1,0:T(8,128)(2,1)S(1)} %get-tuple-element.120), channel_id=1, source_target_pairs={{0,28},{4,0},{8,4},{12,8},{16,12},{20,16},{24,20},{28,24},{1,29},{... | collective-permute-start | bytes 307208 | tf_op jit(solution)/shard_map/ppermute | solution.py:464
  191.2 15.9 %collective-permute-start.34 = (s16[33,16,128]{2,1,0:T(8,128)(2,1)S(1)}, s16[33,16,128]{2,1,0:T(8,128)(2,1)S(1)}, u32[]{:S(2)}, u32[]{:S(2)}) collective-permute-start(s16[33,16,128]{2,1,0:T(8,128)(2,1)S(1)} %get-tuple-element.106), channel_id=1, source_target_pairs={{0,12},{4,16},{8,20},{12,24},{16,28},{20,0},{24,4},{28,8},{1,13},{... | collective-permute-start | bytes 405512 | tf_op jit(solution)/shard_map/ppermute | solution.py:464
  195.4 14.6 %collective-permute-start.35 = (s16[33,16,128]{2,1,0:T(8,128)(2,1)S(1)}, s16[33,16,128]{2,1,0:T(8,128)(2,1)S(1)}, u32[]{:S(2)}, u32[]{:S(2)}) collective-permute-start(s16[33,16,128]{2,1,0:T(8,128)(2,1)S(1)} %get-tuple-element.107), channel_id=1, source_target_pairs={{0,16},{4,20},{8,24},{12,28},{16,0},{20,4},{24,8},{28,12},{1,17},{... | collective-permute-start | bytes 405512 | tf_op jit(solution)/shard_map/ppermute | solution.py:464
  196.5 13.5 %collective-permute-start.36 = (s16[33,16,128]{2,1,0:T(8,128)(2,1)S(1)}, s16[33,16,128]{2,1,0:T(8,128)(2,1)S(1)}, u32[]{:S(2)}, u32[]{:S(2)}) collective-permute-start(s16[33,16,128]{2,1,0:T(8,128)(2,1)S(1)} %get-tuple-element.108), channel_id=1, source_target_pairs={{0,20},{4,24},{8,28},{12,0},{16,4},{20,8},{24,12},{28,16},{1,21},{... | collective-permute-start | bytes 405512 | tf_op jit(solution)/shard_map/ppermute | solution.py:464
  196.5 13.8 %collective-permute-start.37 = (s16[33,16,128]{2,1,0:T(8,128)(2,1)S(1)}, s16[33,16,128]{2,1,0:T(8,128)(2,1)S(1)}, u32[]{:S(2)}, u32[]{:S(2)}) collective-permute-start(s16[33,16,128]{2,1,0:T(8,128)(2,1)S(1)} %get-tuple-element.109), channel_id=1, source_target_pairs={{0,24},{4,28},{8,0},{12,4},{16,8},{20,12},{24,16},{28,20},{1,25},{... | collective-permute-start | bytes 405512 | tf_op jit(solution)/shard_map/ppermute | solution.py:464
  197.7 19.0 %collective-permute-start.38 = (s16[33,16,128]{2,1,0:T(8,128)(2,1)S(1)}, s16[33,16,128]{2,1,0:T(8,128)(2,1)S(1)}, u32[]{:S(2)}, u32[]{:S(2)}) collective-permute-start(s16[33,16,128]{2,1,0:T(8,128)(2,1)S(1)} %get-tuple-element.110), channel_id=1, source_target_pairs={{0,28},{4,0},{8,4},{12,8},{16,12},{20,16},{24,20},{28,24},{1,29},{... | collective-permute-start | bytes 405512 | tf_op jit(solution)/shard_map/ppermute | solution.py:464
  (31 other events, 366.5 us)

commit v5 on v4

--- a/solution.py
+++ b/solution.py
@@ -57,8 +57,14 @@
     )(me, owners.T, slots.T)
 
 
-def pack_body(n_dp, n_chunks, *refs):
-    asked, (first, table), rest = refs[:n_dp], refs[n_dp : n_dp + 2], refs[n_dp + 2 :]
+def asked_of(asked, me, d, j):
+    n_dp = asked.shape[0]
+    asker = me[0] - d
+    asker = jnp.where(asker < 0, asker + n_dp, asker)
+    return asked[asker, d * (asked.shape[1] // n_dp) + j]
+
+
+def pack_body(n_dp, n_chunks, me, asked, first, table, *rest):
     outs, sem = rest[:-1], rest[-1]
     cap = outs[0].shape[0]
 
@@ -67,7 +73,7 @@
             row = pl.multiple_of(first[0] + c * SUB, SUB)
             for d in range(n_dp):
                 for j in range(cap):
-                    slab = asked[d][d * cap + j]
+                    slab = asked_of(asked, me, d, j)
 
                     @pl.when(slab >= 0)
                     def _():
@@ -83,19 +89,19 @@
     each(lambda copy: copy.wait())
 
 
-def pack(asked, first, table, n_chunks, cap):
-    n_dp = len(asked)
+def pack(me, asked, first, table, n_chunks, cap):
+    n_dp = asked.shape[0]
     enc = table.shape[2]
     return pl.pallas_call(
         functools.partial(pack_body, n_dp, n_chunks),
         out_shape=[jax.ShapeDtypeStruct((cap, SUB, enc), table.dtype)] * (n_chunks * n_dp),
-        in_specs=[SMEM] * n_dp + [SMEM, ANY],
+        in_specs=[SMEM, SMEM, SMEM, ANY],
         out_specs=[VMEM] * (n_chunks * n_dp),
         scratch_shapes=[pltpu.SemaphoreType.DMA((n_chunks, n_dp * cap))],
         compiler_params=params(),
         cost_estimate=cost(0, 4 * n_chunks * n_dp * cap * SUB * enc),
         name="pack_rows",
-    )(*asked, first, table)
+    )(me, asked, first, table)
 
 
 def compact_body(n_dp, request, *refs):
@@ -400,16 +406,16 @@
     )(request, own, *codes)
 
 
-def gather_body(n_dp, n_chunks, first, *refs):
-    asked, arrived = refs[:n_dp], refs[n_dp : 2 * n_dp]
+def gather_body(n_dp, n_chunks, first, me, asked, *refs):
+    arrived = refs[:n_dp]
     out, total, sem = refs[-3:]
     count = total.shape[2]
     tiles = count // LANES
-    cap = asked[0].shape[0] // n_dp
+    cap = asked.shape[1] // n_dp
     total[...] = jnp.zeros_like(total)
     for d in range(n_dp):
         for j in range(cap):
-            slab = asked[d][d * cap + j]
+            slab = asked_of(asked, me, d, j)
 
             @pl.when(slab >= 0)
             def _():
@@ -426,21 +432,21 @@
     copy.wait()
 
 
-def gather_grads(asked, arrived, n_slabs, n_chunks, enc, cols, before):
+def gather_grads(me, asked, arrived, n_slabs, n_chunks, enc, cols, before):
     first, count = cols
-    n_dp = len(asked)
+    n_dp = asked.shape[0]
     rows = n_chunks * SUB
     return pl.pallas_call(
         functools.partial(gather_body, n_dp, n_chunks, first),
         out_shape=jax.ShapeDtypeStruct((n_slabs, rows, enc), F32),
-        in_specs=[SMEM] * n_dp + [VMEM] * n_dp + [ANY] * (before is not None),
+        in_specs=[SMEM, SMEM] + [VMEM] * n_dp + [ANY] * (before is not None),
         out_specs=ANY,
         scratch_shapes=[pltpu.VMEM((n_slabs, rows, count), F32), pltpu.SemaphoreType.DMA],
-        input_output_aliases={} if before is None else {2 * n_dp: 0},
+        input_output_aliases={} if before is None else {2 + n_dp: 0},
         compiler_params=params(),
         cost_estimate=cost(0, 8 * n_slabs * rows * count),
         name="gather_grads",
-    )(*asked, *arrived, *([] if before is None else [before]))
+    )(me, asked, *arrived, *([] if before is None else [before]))
 
 
 def on_device(queries, cotangent, table, key_weight, value_weight, owners, slots):
@@ -463,21 +469,29 @@
     def over_dp(x, d):
         return lax.ppermute(x, "dp", [(i, (i + d) % n_dp) for i in range(n_dp)])
 
-    def to_all(xs, sign):
-        return [xs[0]] + [over_dp(xs[d], sign * d) for d in range(1, n_dp)]
+    farthest_first = sorted(range(1, n_dp), key=lambda d: -min(d, n_dp - d))
+
+    def to_all(xs, sign, distances=farthest_first):
+        got = {d: over_dp(xs[d], sign * d) for d in distances}
+        return got
 
     me = lax.axis_index("dp").astype(jnp.int32).reshape(1)
     wanted, request = ask(me, owners, slots, n_dp, cap)
-    asked = to_all([wanted] * n_dp, 1)
+    asked = lax.all_gather(wanted, "dp")
     first = (lax.axis_index("tensor") * share).astype(jnp.int32).reshape(1)
 
     def place(c, kind, d):
         return (kind, c if d == 0 else n_chunks * d + c)
 
     kvs, places = [], []
-    packed = pack(asked, first, table, n_chunks, cap)
+    packed = pack(me, asked, first, table, n_chunks, cap)
+    early = {}
     for c in range(n_chunks):
-        arrived = to_all(packed[c * n_dp : (c + 1) * n_dp], -1)
+        sent = packed[c * n_dp : (c + 1) * n_dp]
+        rest = [d for d in farthest_first if d not in early]
+        arrived = [sent[0]] + [None] * (n_dp - 1)
+        for d, x in {**early, **to_all(sent, -1, rest)}.items():
+            arrived[d] = x
         if kvs:
             arrived, kvs = lax.optimization_barrier((arrived, kvs))
         mine = compact(request, arrived, n_requests)
@@ -486,6 +500,8 @@
         near_at = [place(c, kind, 0) for kind in range(2)]
         far_at = [place(c, kind, d) for kind in range(2) for d in range(1, n_x)]
         if c < n_chunks - 1:
+            early = to_all(packed[(c + 1) * n_dp : (c + 2) * n_dp], -1, farthest_first[:3])
+            early, far = lax.optimization_barrier((early, far))
             far = far + [over_core(x) for x in far]
             kvs = kvs + [project(near + far, key_weight, value_weight)]
         else:
@@ -499,16 +515,22 @@
     attended, d_query, (d_own, d_core) = attend(kvs, places, sizes, queries, cotangent)
 
     lead = 3 * LANES
-    d_table = None
-    for cols in ((0, lead), (lead, enc - lead)):
-        grads = grads_of(d_core, key_weight, value_weight, n_chunks, cols)
-        got = over_core(grads[0]), over_core(grads[1][0])
-        own, codes = grads_of(d_own, key_weight, value_weight, n_chunks, cols, got)
-        if d_table is None:
-            codes, d_core = lax.optimization_barrier((codes, d_core))
-        codes = [over_x(code, n_x - d) for d, code in enumerate(codes, 1)]
-        arrived = to_all(send_codes(request, own, codes, n_dp), 1)
-        d_table = gather_grads(asked, arrived, n_slabs, n_chunks, enc, cols, d_table)
+    parts = ((0, lead), (lead, enc - lead))
+    d_table, got, before = None, [], None
+    for cols in parts:
+        near, (far,) = grads_of(d_core, key_weight, value_weight, n_chunks, cols)
+        if got:
+            got, near = lax.optimization_barrier((got, near))
+        got = got + [(over_core(near), over_core(far))]
+    for cols, sums in zip(parts, got):
+        own, codes = grads_of(d_own, key_weight, value_weight, n_chunks, cols, sums)
+        if before is not None:
+            codes, before = lax.optimization_barrier((codes, before))
+        codes = before = [over_x(code, n_x - d) for d, code in enumerate(codes, 1)]
+        sent = send_codes(request, own, codes, n_dp)
+        came = to_all(sent, 1)
+        arrived = [sent[0]] + [came[d] for d in range(1, n_dp)]
+        d_table = gather_grads(me, asked, arrived, n_slabs, n_chunks, enc, cols, d_table)
     return (attended, d_query, d_table)
 
 

time: 221 us -> 185 us (0.84)
  starting transfers between devices: 71.2 us -> 47.5 us
  waiting for transfers between devices: 83.8 us -> 62.4 us
  blocking collectives: 0 us -> 7.86 us
    ppermute x35 -> x28, starting transfers between devices: 55.7 us -> 35.5 us  [over_dp(): return lax.ppermute(x, 'dp', [(i, (i + d) % n_dp) for i in range(n_dp)])]
    ppermute x4, waiting for transfers between devices: 30.3 us -> 16.7 us  [over_x(): lax.ppermute(x, 'tensor', [(t, (t + 2 * d) % n_tp) for t in range(n_tp)])]
    unnamed x0 -> x1, blocking collectives: none -> 7.86 us
    ppermute x8, waiting for transfers between devices: 8.21 us -> 2.63 us  [over_core(): return lax.ppermute(x, 'tensor', [(t, t ^ 1) for t in range(n_tp)])]
    ppermute x35 -> x28, waiting for transfers between devices: 45.3 us -> 43.1 us  [over_dp(): return lax.ppermute(x, 'dp', [(i, (i + d) % n_dp) for i in range(n_dp)])]
  transfers between devices with their start and end apart: 47 -> 40, of which waited for: 26 -> 17; matrix products, arithmetic and copies ran while one was open for 0% -> 0% of each run, Pallas kernels for 7% -> 16%
where the time goes in v5:
time: 185 us
  waiting for transfers between devices  62.4 us (34%)
  Pallas kernels  61.4 us (33%)
  starting transfers between devices  47.5 us (26%)
  blocking collectives  7.86 us (4%)
  local copies, waits for them, and re-layouts  4.25 us (2%)
    ppermute x28, waiting for transfers between devices, over_dp(): return lax.ppermute(x, 'dp', [(i, (i + d) % n_dp) for i in range(n_dp)])  43.1 us
    ppermute x28, starting transfers between devices, over_dp(): return lax.ppermute(x, 'dp', [(i, (i + d) % n_dp) for i in range(n_dp)])  35.5 us
    pallas_call x4, Pallas kernels, grads_of(): pl.pallas_call(functools.partial(body, near, first), out_shape=[jax.Shape...  19.2 us
    ppermute x4, waiting for transfers between devices, over_x(): lax.ppermute(x, 'tensor', [(t, (t + 2 * d) % n_tp) for t in range(n_tp)])  16.7 us
    pallas_call x3, Pallas kernels, project(): pl.pallas_call(functools.partial(project_body, n_in), out_shape=jax.Shape...  13.4 us
    pallas_call x1, Pallas kernels, attend(): pl.pallas_call(functools.partial(attend_body, places, len(kvs)), out_shap...  13 us
    ppermute x8, starting transfers between devices, over_core(): return lax.ppermute(x, 'tensor', [(t, t ^ 1) for t in range(n_tp)])  9.89 us
    unnamed x1, blocking collectives  7.86 us
  transfers between devices with their start and end apart: 40, of which 17 were waited for; matrix products, arithmetic and copies ran while one was open for 0% of the time, Pallas kernels for 16%

profile of v5, /device:TPU:13, one launch (start us, length us, event | category | flops | bytes accessed | tf_op | source)
XLA Modules:
  0.0 185.1 jit_solution(4429019942034241994)
XLA Ops:
  4.8 7.9 %all-reduce = s32[256]{0:T(256)S(1)} all-reduce(s32[256]{0:T(256)S(1)} %dynamic-update-slice), channel_id=2, replica_groups=mesh['dp'=8,'tensor'=4] {'dp'}, use_global_device_ids=true, to_apply=%add | all-reduce | flops 256 | bytes 2048
  14.7 4.0 %pack_rows.1 = (bf16[4,16,896]{2,1,0:T(8,128)(2,1)S(1)}, bf16[4,16,896]{2,1,0:T(8,128)(2,1)S(1)}, bf16[4,16,896]{2,1,0:T(8,128)(2,1)S(1)}, bf16[4,16,896]{2,1,0:...) custom-call(s32[1]{0:T(128)} %bitcast.me, ...), custom_call_target="tpu_custom_call" | custom-call | bytes 3670016 | tf_op jit(solution)/shard_map/pack_rows/pallas_call | solution.py:95
  20.1 3.2 %collective-permute-start.7 = (bf16[4,16,896]{2,1,0:T(8,128)(2,1)S(1)}, bf16[4,16,896]{2,1,0:T(8,128)(2,1)S(1)}, u32[]{:S(2)}, u32[]{:S(2)}) collective-permute-start(bf16[4,16,896]{2,1,0:T(8,128)(2,1)S(1)} %get-tuple-element.79), channel_id=1, source_target_pairs={{0,20},{4,24},{8,28},{12,0},{16,4},{20,8},{24,12},{28,16},{1,21},{... | collective-permute-start | bytes 344072 | tf_op jit(solution)/shard_map/ppermute | solution.py:470
  26.9 6.4 %collective-permute-done.8.refs_4_ = bf16[4,16,896]{2,1,0:T(8,128)(2,1)S(1)} collective-permute-done((bf16[4,16,896]{2,1,0:T(8,128)(2,1)S(1)}, bf16[4,16,896]{2,1,0:T(8,128)(2,1)S(1)}, u32[]{:S(2)}, u32[]{:S(2)}) %collective-permute-start.8) | collective-permute-done | bytes 114720 | tf_op jit(solution)/shard_map/ppermute | solution.py:470
  33.3 3.9 %collective-permute-done.9.refs_5_ = bf16[4,16,896]{2,1,0:T(8,128)(2,1)S(1)} collective-permute-done((bf16[4,16,896]{2,1,0:T(8,128)(2,1)S(1)}, bf16[4,16,896]{2,1,0:T(8,128)(2,1)S(1)}, u32[]{:S(2)}, u32[]{:S(2)}) %collective-permute-start.9) | collective-permute-done | bytes 114720 | tf_op jit(solution)/shard_map/ppermute | solution.py:470
  47.2 4.8 %collective-permute-start.15 = (bf16[16,16,896]{2,1,0:T(8,128)(2,1)S(1)}, bf16[16,16,896]{2,1,0:T(8,128)(2,1)S(1)}, u32[]{:S(2)}, u32[]{:S(2)}) collective-permute-start(bf16[16,16,896]{2,1,0:T(8,128)(2,1)S(1)} %compact_rows.2.refs_0_), channel_id=1, source_target_pairs={{0,1},{1,0},{2,3},{3,2},{4,5},{5,4},{6,7},{7,6},{8,9},{9,8},{10,11... | collective-permute-start | bytes 1376264 | tf_op jit(solution)/shard_map/ppermute | solution.py:464
  52.0 4.9 %collective-permute-done.4.refs_5_ = bf16[4,16,896]{2,1,0:T(8,128)(2,1)S(1)} collective-permute-done((bf16[4,16,896]{2,1,0:T(8,128)(2,1)S(1)}, bf16[4,16,896]{2,1,0:T(8,128)(2,1)S(1)}, u32[]{:S(2)}, u32[]{:S(2)}) %collective-permute-start.4) | collective-permute-done | bytes 114720 | tf_op jit(solution)/shard_map/ppermute | solution.py:470
  58.7 3.6 %collective-permute-start.1 = (bf16[4,16,896]{2,1,0:T(8,128)(2,1)S(1)}, bf16[4,16,896]{2,1,0:T(8,128)(2,1)S(1)}, u32[]{:S(2)}, u32[]{:S(2)}) collective-permute-start(bf16[4,16,896]{2,1,0:T(8,128)(2,1)S(1)} %get-tuple-element.71), channel_id=1, source_target_pairs={{0,24},{4,28},{8,0},{12,4},{16,8},{20,12},{24,16},{28,20},{1,25},{... | collective-permute-start | bytes 344072 | tf_op jit(solution)/shard_map/ppermute | solution.py:470
  62.6 6.2 %project.3.refs_0_ = bf16[4,16,16,2048]{3,2,1,0:T(8,128)(2,1)S(1)} custom-call(bf16[16,16,896]{2,1,0:T(8,128)(2,1)S(1)} %compact_rows.2.refs_0_, bf16[16,16,896]{2,1,0:T(8,128)(2,1)S(1)} %collective-permute-done.15.refs_1_, bf16[16,16,896]{2,1,0:T(8,128)(2,1)S(1)} %collective-permute-done.12.refs_2_, ...), custom_call_target="tpu_custom_call" | custom-call | flops 3758096384 | bytes 9699328 | tf_op jit(solution)/shard_map/project/pallas_call | solution.py:172
  74.4 3.6 %project.4.refs_1_ = bf16[2,16,16,2048]{3,2,1,0:T(8,128)(2,1)S(1)} custom-call(bf16[16,16,896]{2,1,0:T(8,128)(2,1)S(1)} %compact_rows.3.refs_0_, bf16[16,16,896]{2,1,0:T(8,128)(2,1)S(1)} %collective-permute-done.17.refs_1_, bf16[896,1024]{1,0:T(8,128)(2,1)S(1)} %copy-done, bf16[896,1024]{1,0:T(8,128)(2,1)S(1)} %copy-done.1), custom_call_target="tpu_custom_call" | custom-call | flops 1879048192 | bytes 6684672 | tf_op jit(solution)/shard_map/project/pallas_call | solution.py:172
  78.0 7.0 %collective-permute-done.18.refs_0_ = bf16[16,16,896]{2,1,0:T(8,128)(2,1)S(1)} collective-permute-done((bf16[16,16,896]{2,1,0:T(8,128)(2,1)S(1)}, bf16[16,16,896]{2,1,0:T(8,128)(2,1)S(1)}, u32[]{:S(2)}, u32[]{:S(2)}) %collective-permute-start.18) | collective-permute-done | bytes 458784 | tf_op jit(solution)/shard_map/ppermute | solution.py:467
  87.4 3.6 %project.5.refs_2_ = bf16[2,16,16,2048]{3,2,1,0:T(8,128)(2,1)S(1)} custom-call(bf16[16,16,896]{2,1,0:T(8,128)(2,1)S(1)} %collective-permute-done.18.refs_0_, bf16[16,16,896]{2,1,0:T(8,128)(2,1)S(1)} %collective-permute-done.19.refs_1_, bf16[896,1024]{1,0:T(8,128)(2,1)S(1)} %copy-done, bf16[896,1024]{1,0:T(8,128)(2,1)S(1)} %copy-done.1), custom_call_target="tpu_custom_call" | custom-call | flops 1879048192 | bytes 6684672 | tf_op jit(solution)/shard_map/project/pallas_call | solution.py:172
  91.0 13.0 %attend.1 = (bf16[512,1024]{1,0:T(8,128)(2,1)}, bf16[512,1024]{1,0:T(8,128)(2,1)}, bf16[4,16,16,2048]{3,2,1,0:T(8,128)(2,1)S(1)}, bf16[4,16,16,2048]{3,2,1,0:T(8,128)(2,1)S(1)}) custom-call(bf16[4,16,16,2048]{3,2,1,0:T(8,128)(2,1)S(1)} %project.3.refs_0_, bf16[2,16,16,2048]{3,2,1,0:T(8,128)(2,1)S(1)} %project.4.refs_1_, ...), custom_call_target="tpu_custom_call" | custom-call | flops 1610612736 | bytes 37748736 | tf_op jit(solution)/shard_map/attend/pallas_call | solution.py:247
  104.0 4.5 %core_grads.2 = (f32[2,16,16,384]{3,2,1,0:T(8,128)S(1)}, f32[2,16,16,384]{3,2,1,0:T(8,128)S(1)}) custom-call(bf16[4,16,16,2048]{3,2,1,0:T(8,128)(2,1)S(1)} %get-tuple-element.104.d_ref, bf16[896,1024]{1,0:T(8,128)(2,1)S(1)} %copy-done, bf16[896,1024]{1,0:T(8,128)(2,1)S(1)} %copy-done.1), custom_call_target="tpu_custom_call" | custom-call | flops 1610612736 | bytes 5767168 | tf_op jit(solution)/shard_map/core_grads/pallas_call | solution.py:336
  109.1 4.8 %core_grads.3 = (f32[2,16,16,512]{3,2,1,0:T(8,128)S(1)}, f32[2,16,16,512]{3,2,1,0:T(8,128)S(1)}) custom-call(bf16[4,16,16,2048]{3,2,1,0:T(8,128)(2,1)S(1)} %get-tuple-element.104.d_ref, bf16[896,1024]{1,0:T(8,128)(2,1)S(1)} %copy-done, bf16[896,1024]{1,0:T(8,128)(2,1)S(1)} %copy-done.1), custom_call_target="tpu_custom_call" | custom-call | flops 2147483648 | bytes 6291456 | tf_op jit(solution)/shard_map/core_grads/pallas_call | solution.py:336
  114.4 4.8 %own_grads.3 = (f32[2,16,16,384]{3,2,1,0:T(8,128)S(1)}, s16[2,49,16,128]{3,2,1,0:T(8,128)(2,1)S(1)}) custom-call(bf16[4,16,16,2048]{3,2,1,0:T(8,128)(2,1)S(1)} %get-tuple-element.103.d_ref, bf16[896,1024]{1,0:T(8,128)(2,1)S(1)} %copy-done, bf16[896,1024]{1,0:T(8,128)(2,1)S(1)} %copy-done.1, f32[2,16,16,384]{3,2,1,0:T(8,128)S(1)} %collective-permute-done.20.near_got, ...), custom_call_target="tpu_custom_call" | custom-call | flops 1610612736 | bytes 5767168 | tf_op jit(solution)/shard_map/own_grads/pallas_call | solution.py:336
  119.6 5.1 %own_grads.2 = (f32[2,16,16,512]{3,2,1,0:T(8,128)S(1)}, s16[2,65,16,128]{3,2,1,0:T(8,128)(2,1)S(1)}) custom-call(bf16[4,16,16,2048]{3,2,1,0:T(8,128)(2,1)S(1)} %get-tuple-element.103.d_ref, bf16[896,1024]{1,0:T(8,128)(2,1)S(1)} %copy-done, bf16[896,1024]{1,0:T(8,128)(2,1)S(1)} %copy-done.1, f32[2,16,16,512]{3,2,1,0:T(8,128)S(1)} %collective-permute-done.22.near_got, ...), custom_call_target="tpu_custom_call" | custom-call | flops 2147483648 | bytes 6291456 | tf_op jit(solution)/shard_map/own_grads/pallas_call | solution.py:336
  124.7 5.1 %collective-permute-done.24.rest_0_ = s16[2,49,16,128]{3,2,1,0:T(8,128)(2,1)S(1)} collective-permute-done((s16[2,49,16,128]{3,2,1,0:T(8,128)(2,1)S(1)}, s16[2,49,16,128]{3,2,1,0:T(8,128)(2,1)S(1)}, u32[]{:S(2)}, u32[]{:S(2)}) %collective-permute-start.24) | collective-permute-done | bytes 401440 | tf_op jit(solution)/shard_map/ppermute | solution.py:467
  137.7 4.5 %collective-permute-done.25.rest_0_ = s16[2,65,16,128]{3,2,1,0:T(8,128)(2,1)S(1)} collective-permute-done((s16[2,65,16,128]{3,2,1,0:T(8,128)(2,1)S(1)}, s16[2,65,16,128]{3,2,1,0:T(8,128)(2,1)S(1)}, u32[]{:S(2)}, u32[]{:S(2)}) %collective-permute-start.25) | collective-permute-done | bytes 532512 | tf_op jit(solution)/shard_map/ppermute | solution.py:467
  143.4 2.6 %collective-permute-start.26 = (s16[33,16,128]{2,1,0:T(8,128)(2,1)S(1)}, s16[33,16,128]{2,1,0:T(8,128)(2,1)S(1)}, u32[]{:S(2)}, u32[]{:S(2)}) collective-permute-start(s16[33,16,128]{2,1,0:T(8,128)(2,1)S(1)} %get-tuple-element.117), channel_id=1, source_target_pairs={{0,4},{4,8},{8,12},{12,16},{16,20},{20,24},{24,28},{28,0},{1,5},{5... | collective-permute-start | bytes 405512 | tf_op jit(solution)/shard_map/ppermute | solution.py:470
  151.6 6.6 %collective-permute-done.37.refs_5_ = s16[25,16,128]{2,1,0:T(8,128)(2,1)S(1)} collective-permute-done((s16[25,16,128]{2,1,0:T(8,128)(2,1)S(1)}, s16[25,16,128]{2,1,0:T(8,128)(2,1)S(1)}, u32[]{:S(2)}, u32[]{:S(2)}) %collective-permute-start.37) | collective-permute-done | bytes 102432 | tf_op jit(solution)/shard_map/ppermute | solution.py:470
  158.3 3.3 %collective-permute-done.38.refs_6_ = s16[25,16,128]{2,1,0:T(8,128)(2,1)S(1)} collective-permute-done((s16[25,16,128]{2,1,0:T(8,128)(2,1)S(1)}, s16[25,16,128]{2,1,0:T(8,128)(2,1)S(1)}, u32[]{:S(2)}, u32[]{:S(2)}) %collective-permute-start.38) | collective-permute-done | bytes 102432 | tf_op jit(solution)/shard_map/ppermute | solution.py:470
  168.4 7.7 %collective-permute-done.29.refs_4_ = s16[33,16,128]{2,1,0:T(8,128)(2,1)S(1)} collective-permute-done((s16[33,16,128]{2,1,0:T(8,128)(2,1)S(1)}, s16[33,16,128]{2,1,0:T(8,128)(2,1)S(1)}, u32[]{:S(2)}, u32[]{:S(2)}) %collective-permute-start.29) | collective-permute-done | bytes 135200 | tf_op jit(solution)/shard_map/ppermute | solution.py:470
  176.1 5.1 %collective-permute-done.31.refs_6_ = s16[33,16,128]{2,1,0:T(8,128)(2,1)S(1)} collective-permute-done((s16[33,16,128]{2,1,0:T(8,128)(2,1)S(1)}, s16[33,16,128]{2,1,0:T(8,128)(2,1)S(1)}, u32[]{:S(2)}, u32[]{:S(2)}) %collective-permute-start.31) | collective-permute-done | bytes 135200 | tf_op jit(solution)/shard_map/ppermute | solution.py:470
  (89 shorter events, 57.4 us)
Async XLA Ops:
  23.2 13.9 %collective-permute-start.9 = (bf16[4,16,896]{2,1,0:T(8,128)(2,1)S(1)}, bf16[4,16,896]{2,1,0:T(8,128)(2,1)S(1)}, u32[]{:S(2)}, u32[]{:S(2)}) collective-permute-start(bf16[4,16,896]{2,1,0:T(8,128)(2,1)S(1)} %get-tuple-element.81), channel_id=1, source_target_pairs={{0,12},{4,16},{8,20},{12,24},{16,28},{20,0},{24,4},{28,8},{1,13},{... | collective-permute-start | bytes 344072 | tf_op jit(solution)/shard_map/ppermute | solution.py:470
  24.5 14.1 %collective-permute-start.10 = (bf16[4,16,896]{2,1,0:T(8,128)(2,1)S(1)}, bf16[4,16,896]{2,1,0:T(8,128)(2,1)S(1)}, u32[]{:S(2)}, u32[]{:S(2)}) collective-permute-start(bf16[4,16,896]{2,1,0:T(8,128)(2,1)S(1)} %get-tuple-element.82), channel_id=1, source_target_pairs={{0,8},{4,12},{8,16},{12,20},{16,24},{20,28},{24,0},{28,4},{1,9},{5... | collective-permute-start | bytes 344072 | tf_op jit(solution)/shard_map/ppermute | solution.py:470
  24.7 15.4 %collective-permute-start.11 = (bf16[4,16,896]{2,1,0:T(8,128)(2,1)S(1)}, bf16[4,16,896]{2,1,0:T(8,128)(2,1)S(1)}, u32[]{:S(2)}, u32[]{:S(2)}) collective-permute-start(bf16[4,16,896]{2,1,0:T(8,128)(2,1)S(1)} %get-tuple-element.83), channel_id=1, source_target_pairs={{0,4},{4,8},{8,12},{12,16},{16,20},{20,24},{24,28},{28,0},{1,5},{5... | collective-permute-start | bytes 344072 | tf_op jit(solution)/shard_map/ppermute | solution.py:470
  42.0 15.0 %collective-permute-start.12 = (bf16[16,16,896]{2,1,0:T(8,128)(2,1)S(1)}, bf16[16,16,896]{2,1,0:T(8,128)(2,1)S(1)}, u32[]{:S(2)}, u32[]{:S(2)}) collective-permute-start(bf16[16,16,896]{2,1,0:T(8,128)(2,1)S(1)} %compact_rows.2.refs_0_), channel_id=1, source_target_pairs={{0,2},{1,3},{2,0},{3,1},{4,6},{5,7},{6,4},{7,5},{8,10},{9,11},{10,... | collective-permute-start | bytes 1376264 | tf_op jit(solution)/shard_map/ppermute | solution.py:467
  47.2 15.0 %collective-permute-start.15 = (bf16[16,16,896]{2,1,0:T(8,128)(2,1)S(1)}, bf16[16,16,896]{2,1,0:T(8,128)(2,1)S(1)}, u32[]{:S(2)}, u32[]{:S(2)}) collective-permute-start(bf16[16,16,896]{2,1,0:T(8,128)(2,1)S(1)} %compact_rows.2.refs_0_), channel_id=1, source_target_pairs={{0,1},{1,0},{2,3},{3,2},{4,5},{5,4},{6,7},{7,6},{8,9},{9,8},{10,11... | collective-permute-start | bytes 1376264 | tf_op jit(solution)/shard_map/ppermute | solution.py:464
  58.3 10.5 %collective-permute-start = (bf16[4,16,896]{2,1,0:T(8,128)(2,1)S(1)}, bf16[4,16,896]{2,1,0:T(8,128)(2,1)S(1)}, u32[]{:S(2)}, u32[]{:S(2)}) collective-permute-start(bf16[4,16,896]{2,1,0:T(8,128)(2,1)S(1)} %get-tuple-element.70), channel_id=1, source_target_pairs={{0,28},{4,0},{8,4},{12,8},{16,12},{20,16},{24,20},{28,24},{1,29},{... | collective-permute-start | bytes 344072 | tf_op jit(solution)/shard_map/ppermute | solution.py:470
  58.7 10.2 %collective-permute-start.1 = (bf16[4,16,896]{2,1,0:T(8,128)(2,1)S(1)}, bf16[4,16,896]{2,1,0:T(8,128)(2,1)S(1)}, u32[]{:S(2)}, u32[]{:S(2)}) collective-permute-start(bf16[4,16,896]{2,1,0:T(8,128)(2,1)S(1)} %get-tuple-element.71), channel_id=1, source_target_pairs={{0,24},{4,28},{8,0},{12,4},{16,8},{20,12},{24,16},{28,20},{1,25},{... | collective-permute-start | bytes 344072 | tf_op jit(solution)/shard_map/ppermute | solution.py:470
  73.0 12.1 %collective-permute-start.18 = (bf16[16,16,896]{2,1,0:T(8,128)(2,1)S(1)}, bf16[16,16,896]{2,1,0:T(8,128)(2,1)S(1)}, u32[]{:S(2)}, u32[]{:S(2)}) collective-permute-start(bf16[16,16,896]{2,1,0:T(8,128)(2,1)S(1)} %compact_rows.3.refs_0_), channel_id=1, source_target_pairs={{0,2},{1,3},{2,0},{3,1},{4,6},{5,7},{6,4},{7,5},{8,10},{9,11},{10,... | collective-permute-start | bytes 1376264 | tf_op jit(solution)/shard_map/ppermute | solution.py:467
  119.2 10.6 %collective-permute-start.24 = (s16[2,49,16,128]{3,2,1,0:T(8,128)(2,1)S(1)}, s16[2,49,16,128]{3,2,1,0:T(8,128)(2,1)S(1)}, u32[]{:S(2)}, u32[]{:S(2)}) collective-permute-start(s16[2,49,16,128]{3,2,1,0:T(8,128)(2,1)S(1)} %get-tuple-element.114), channel_id=1, source_target_pairs={{0,2},{1,3},{2,0},{3,1},{4,6},{5,7},{6,4},{7,5},{8,10},{9,11},{10,... | collective-permute-start | bytes 1204232 | tf_op jit(solution)/shard_map/ppermute | solution.py:467
  129.8 12.4 %collective-permute-start.25 = (s16[2,65,16,128]{3,2,1,0:T(8,128)(2,1)S(1)}, s16[2,65,16,128]{3,2,1,0:T(8,128)(2,1)S(1)}, u32[]{:S(2)}, u32[]{:S(2)}) collective-permute-start(s16[2,65,16,128]{3,2,1,0:T(8,128)(2,1)S(1)} %get-tuple-element.115), channel_id=1, source_target_pairs={{0,2},{1,3},{2,0},{3,1},{4,6},{5,7},{6,4},{7,5},{8,10},{9,11},{10,... | collective-permute-start | bytes 1597448 | tf_op jit(solution)/shard_map/ppermute | solution.py:467
  131.4 14.6 %collective-permute-start.33 = (s16[25,16,128]{2,1,0:T(8,128)(2,1)S(1)}, s16[25,16,128]{2,1,0:T(8,128)(2,1)S(1)}, u32[]{:S(2)}, u32[]{:S(2)}) collective-permute-start(s16[25,16,128]{2,1,0:T(8,128)(2,1)S(1)} %get-tuple-element.126), channel_id=1, source_target_pairs={{0,4},{4,8},{8,12},{12,16},{16,20},{20,24},{24,28},{28,0},{1,5},{5... | collective-permute-start | bytes 307208 | tf_op jit(solution)/shard_map/ppermute | solution.py:470
  134.0 13.1 %collective-permute-start.34 = (s16[25,16,128]{2,1,0:T(8,128)(2,1)S(1)}, s16[25,16,128]{2,1,0:T(8,128)(2,1)S(1)}, u32[]{:S(2)}, u32[]{:S(2)}) collective-permute-start(s16[25,16,128]{2,1,0:T(8,128)(2,1)S(1)} %get-tuple-element.127), channel_id=1, source_target_pairs={{0,8},{4,12},{8,16},{12,20},{16,24},{20,28},{24,0},{28,4},{1,9},{5... | collective-permute-start | bytes 307208 | tf_op jit(solution)/shard_map/ppermute | solution.py:470
  135.1 12.6 %collective-permute-start.35 = (s16[25,16,128]{2,1,0:T(8,128)(2,1)S(1)}, s16[25,16,128]{2,1,0:T(8,128)(2,1)S(1)}, u32[]{:S(2)}, u32[]{:S(2)}) collective-permute-start(s16[25,16,128]{2,1,0:T(8,128)(2,1)S(1)} %get-tuple-element.128), channel_id=1, source_target_pairs={{0,12},{4,16},{8,20},{12,24},{16,28},{20,0},{24,4},{28,8},{1,13},{... | collective-permute-start | bytes 307208 | tf_op jit(solution)/shard_map/ppermute | solution.py:470
  137.1 13.2 %collective-permute-start.36 = (s16[25,16,128]{2,1,0:T(8,128)(2,1)S(1)}, s16[25,16,128]{2,1,0:T(8,128)(2,1)S(1)}, u32[]{:S(2)}, u32[]{:S(2)}) collective-permute-start(s16[25,16,128]{2,1,0:T(8,128)(2,1)S(1)} %get-tuple-element.129), channel_id=1, source_target_pairs={{0,16},{4,20},{8,24},{12,28},{16,0},{20,4},{24,8},{28,12},{1,17},{... | collective-permute-start | bytes 307208 | tf_op jit(solution)/shard_map/ppermute | solution.py:470
  143.4 21.6 %collective-permute-start.26 = (s16[33,16,128]{2,1,0:T(8,128)(2,1)S(1)}, s16[33,16,128]{2,1,0:T(8,128)(2,1)S(1)}, u32[]{:S(2)}, u32[]{:S(2)}) collective-permute-start(s16[33,16,128]{2,1,0:T(8,128)(2,1)S(1)} %get-tuple-element.117), channel_id=1, source_target_pairs={{0,4},{4,8},{8,12},{12,16},{16,20},{20,24},{24,28},{28,0},{1,5},{5... | collective-permute-start | bytes 405512 | tf_op jit(solution)/shard_map/ppermute | solution.py:470
  146.0 19.0 %collective-permute-start.27 = (s16[33,16,128]{2,1,0:T(8,128)(2,1)S(1)}, s16[33,16,128]{2,1,0:T(8,128)(2,1)S(1)}, u32[]{:S(2)}, u32[]{:S(2)}) collective-permute-start(s16[33,16,128]{2,1,0:T(8,128)(2,1)S(1)} %get-tuple-element.118), channel_id=1, source_target_pairs={{0,8},{4,12},{8,16},{12,20},{16,24},{20,28},{24,0},{28,4},{1,9},{5... | collective-permute-start | bytes 405512 | tf_op jit(solution)/shard_map/ppermute | solution.py:470
  147.1 11.2 %collective-permute-start.37 = (s16[25,16,128]{2,1,0:T(8,128)(2,1)S(1)}, s16[25,16,128]{2,1,0:T(8,128)(2,1)S(1)}, u32[]{:S(2)}, u32[]{:S(2)}) collective-permute-start(s16[25,16,128]{2,1,0:T(8,128)(2,1)S(1)} %get-tuple-element.130), channel_id=1, source_target_pairs={{0,20},{4,24},{8,28},{12,0},{16,4},{20,8},{24,12},{28,16},{1,21},{... | collective-permute-start | bytes 307208 | tf_op jit(solution)/shard_map/ppermute | solution.py:470
  147.7 13.9 %collective-permute-start.38 = (s16[25,16,128]{2,1,0:T(8,128)(2,1)S(1)}, s16[25,16,128]{2,1,0:T(8,128)(2,1)S(1)}, u32[]{:S(2)}, u32[]{:S(2)}) collective-permute-start(s16[25,16,128]{2,1,0:T(8,128)(2,1)S(1)} %get-tuple-element.131), channel_id=1, source_target_pairs={{0,24},{4,28},{8,0},{12,4},{16,8},{20,12},{24,16},{28,20},{1,25},{... | collective-permute-start | bytes 307208 | tf_op jit(solution)/shard_map/ppermute | solution.py:470
  150.2 12.4 %collective-permute-start.39 = (s16[25,16,128]{2,1,0:T(8,128)(2,1)S(1)}, s16[25,16,128]{2,1,0:T(8,128)(2,1)S(1)}, u32[]{:S(2)}, u32[]{:S(2)}) collective-permute-start(s16[25,16,128]{2,1,0:T(8,128)(2,1)S(1)} %get-tuple-element.132), channel_id=1, source_target_pairs={{0,28},{4,0},{8,4},{12,8},{16,12},{20,16},{24,20},{28,24},{1,29},{... | collective-permute-start | bytes 307208 | tf_op jit(solution)/shard_map/ppermute | solution.py:470
  158.3 10.1 %collective-permute-start.28 = (s16[33,16,128]{2,1,0:T(8,128)(2,1)S(1)}, s16[33,16,128]{2,1,0:T(8,128)(2,1)S(1)}, u32[]{:S(2)}, u32[]{:S(2)}) collective-permute-start(s16[33,16,128]{2,1,0:T(8,128)(2,1)S(1)} %get-tuple-element.119), channel_id=1, source_target_pairs={{0,12},{4,16},{8,20},{12,24},{16,28},{20,0},{24,4},{28,8},{1,13},{... | collective-permute-start | bytes 405512 | tf_op jit(solution)/shard_map/ppermute | solution.py:470
  161.6 14.5 %collective-permute-start.29 = (s16[33,16,128]{2,1,0:T(8,128)(2,1)S(1)}, s16[33,16,128]{2,1,0:T(8,128)(2,1)S(1)}, u32[]{:S(2)}, u32[]{:S(2)}) collective-permute-start(s16[33,16,128]{2,1,0:T(8,128)(2,1)S(1)} %get-tuple-element.120), channel_id=1, source_target_pairs={{0,16},{4,20},{8,24},{12,28},{16,0},{20,4},{24,8},{28,12},{1,17},{... | collective-permute-start | bytes 405512 | tf_op jit(solution)/shard_map/ppermute | solution.py:470
  162.7 13.4 %collective-permute-start.30 = (s16[33,16,128]{2,1,0:T(8,128)(2,1)S(1)}, s16[33,16,128]{2,1,0:T(8,128)(2,1)S(1)}, u32[]{:S(2)}, u32[]{:S(2)}) collective-permute-start(s16[33,16,128]{2,1,0:T(8,128)(2,1)S(1)} %get-tuple-element.121), channel_id=1, source_target_pairs={{0,20},{4,24},{8,28},{12,0},{16,4},{20,8},{24,12},{28,16},{1,21},{... | collective-permute-start | bytes 405512 | tf_op jit(solution)/shard_map/ppermute | solution.py:470
  165.0 16.1 %collective-permute-start.31 = (s16[33,16,128]{2,1,0:T(8,128)(2,1)S(1)}, s16[33,16,128]{2,1,0:T(8,128)(2,1)S(1)}, u32[]{:S(2)}, u32[]{:S(2)}) collective-permute-start(s16[33,16,128]{2,1,0:T(8,128)(2,1)S(1)} %get-tuple-element.122), channel_id=1, source_target_pairs={{0,24},{4,28},{8,0},{12,4},{16,8},{20,12},{24,16},{28,20},{1,25},{... | collective-permute-start | bytes 405512 | tf_op jit(solution)/shard_map/ppermute | solution.py:470
  165.0 17.7 %collective-permute-start.32 = (s16[33,16,128]{2,1,0:T(8,128)(2,1)S(1)}, s16[33,16,128]{2,1,0:T(8,128)(2,1)S(1)}, u32[]{:S(2)}, u32[]{:S(2)}) collective-permute-start(s16[33,16,128]{2,1,0:T(8,128)(2,1)S(1)} %get-tuple-element.123), channel_id=1, source_target_pairs={{0,28},{4,0},{8,4},{12,8},{16,12},{20,16},{24,20},{28,24},{1,29},{... | collective-permute-start | bytes 405512 | tf_op jit(solution)/shard_map/ppermute | solution.py:470
  (22 other events, 261.3 us)

commit v6 on v5

--- a/solution.py
+++ b/solution.py
@@ -13,6 +13,8 @@
 SUB = 16
 LANES = 128
 VMEM_LIMIT = 28 * 1024 * 1024
+VMEM_MORE = 40 * 1024 * 1024
+VMEM_ALL = 60 * 1024 * 1024
 F32 = jnp.float32
 BF16 = jnp.bfloat16
 
@@ -21,56 +23,63 @@
 VMEM = pl.BlockSpec(memory_space=pltpu.VMEM)
 
 
-def params():
-    return pltpu.CompilerParams(vmem_limit_bytes=VMEM_LIMIT)
+def params(limit=VMEM_LIMIT):
+    return pltpu.CompilerParams(vmem_limit_bytes=limit)
 
 
 def cost(flops, nbytes):
     return pl.CostEstimate(flops=int(flops), bytes_accessed=int(nbytes), transcendentals=0)
 
 
-def ask_body(cap, me, owners, slots, wanted, request, count):
-    n_dp = wanted.shape[0] // cap
+def ask_body(cap, owners, slots, me_out, wanted, request, count):
+    n_dp = wanted.shape[0]
+    me = lax.axis_index("dp")
+    me_out[0] = me
     for i in range(n_dp * cap):
-        wanted[i] = -1
         request[i] = -1
+        for asker in range(n_dp):
+            wanted[asker, i] = 0
     for d in range(n_dp):
         count[d] = 0
     for r in range(owners.size):
-        d = owners[r % 2, r // 2] - me[0]
+        d = owners[r % 2, r // 2] - me
         d = jnp.where(d < 0, d + n_dp, d)
         j = count[d]
         count[d] = j + 1
-        wanted[d * cap + j] = slots[r % 2, r // 2]
+        wanted[me, d * cap + j] = slots[r % 2, r // 2] + 1
         request[d * cap + j] = r
 
 
-def ask(me, owners, slots, n_dp, cap):
-    shape = jax.ShapeDtypeStruct((n_dp * cap,), jnp.int32)
+def ask(owners, slots, n_dp, cap):
     return pl.pallas_call(
         functools.partial(ask_body, cap),
-        out_shape=[shape, shape],
-        in_specs=[SMEM, SMEM, SMEM],
-        out_specs=[SMEM, SMEM],
+        out_shape=[
+            jax.ShapeDtypeStruct((1,), jnp.int32),
+            jax.ShapeDtypeStruct((n_dp, n_dp * cap), jnp.int32),
+            jax.ShapeDtypeStruct((n_dp * cap,), jnp.int32),
+        ],
+        in_specs=[SMEM, SMEM],
+        out_specs=[SMEM, SMEM, SMEM],
         scratch_shapes=[pltpu.SMEM((n_dp,), jnp.int32)],
         name="ask",
-    )(me, owners.T, slots.T)
+    )(owners.T, slots.T)
 
 
 def asked_of(asked, me, d, j):
     n_dp = asked.shape[0]
     asker = me[0] - d
     asker = jnp.where(asker < 0, asker + n_dp, asker)
-    return asked[asker, d * (asked.shape[1] // n_dp) + j]
-
-
-def pack_body(n_dp, n_chunks, me, asked, first, table, *rest):
+    return asked[asker, d * (asked.shape[1] // n_dp) + j] - 1
+
+
+def pack_body(n_dp, n_chunks, me, asked, table, *rest):
     outs, sem = rest[:-1], rest[-1]
     cap = outs[0].shape[0]
+    first = lax.axis_index("tensor") * (n_chunks * SUB)
 
     def each(act):
         for c in range(n_chunks):
-            row = pl.multiple_of(first[0] + c * SUB, SUB)
+            row = pl.multiple_of(first + c * SUB, SUB)
             for d in range(n_dp):
                 for j in range(cap):
                     slab = asked_of(asked, me, d, j)
@@ -89,19 +98,19 @@
     each(lambda copy: copy.wait())
 
 
-def pack(me, asked, first, table, n_chunks, cap):
+def pack(me, asked, table, n_chunks, cap):
     n_dp = asked.shape[0]
     enc = table.shape[2]
     return pl.pallas_call(
         functools.partial(pack_body, n_dp, n_chunks),
         out_shape=[jax.ShapeDtypeStruct((cap, SUB, enc), table.dtype)] * (n_chunks * n_dp),
-        in_specs=[SMEM, SMEM, SMEM, ANY],
+        in_specs=[SMEM, SMEM, ANY],
         out_specs=[VMEM] * (n_chunks * n_dp),
         scratch_shapes=[pltpu.SemaphoreType.DMA((n_chunks, n_dp * cap))],
-        compiler_params=params(),
+        compiler_params=params(VMEM_ALL),
         cost_estimate=cost(0, 4 * n_chunks * n_dp * cap * SUB * enc),
         name="pack_rows",
-    )(me, asked, first, table)
+    )(me, asked, table)
 
 
 def compact_body(n_dp, request, *refs):
@@ -184,78 +193,125 @@
     )(*pieces, wk, wv)
 
 
-def attend_body(places, n_kv, *refs):
-    kvs = refs[:n_kv]
-    q_ref, g_ref, att_ref, dq_ref = refs[n_kv : n_kv + 4]
-    grads = refs[n_kv + 4 :]
+def attend_body(places, n_kv, n_late, near, *refs):
+    kvs, late = refs[:n_kv], refs[n_kv : n_kv + n_late]
+    wk, wv, q_ref, g_ref, att_ref, dq_ref = refs[n_kv + n_late : n_kv + n_late + 6]
+    *grads, near_out, far_out, own_out, late_kv, own_all, core_all = refs[n_kv + n_late + 6 :]
+    step = pl.program_id(0)
     width = q_ref.shape[1]
+    enc = wk.shape[0]
     scale = 1.0 / math.sqrt(HD)
     heads = width // HD
     group = min(4, heads)
-
-    def keys_of(col):
-        parts = [ref[:, :, :, pl.ds(col, HD)].reshape(-1, HD) for ref in kvs]
-        return jnp.concatenate(parts, axis=0)
-
-    def put(col, grad):
-        for at, (ref, i) in enumerate(places):
-            block = grad[at * 2 * SUB : (at + 1) * 2 * SUB]
-            grads[ref][i, :, :, pl.ds(col, HD)] = block.reshape(2, SUB, HD)
-
     last = (((1,), (1,)), ((), ()))
     first = (((0,), (0,)), ((), ()))
 
     def dot(a, b, dims=(((1,), (0,)), ((), ()))):
         return lax.dot_general(a, b, dims, preferred_element_type=F32)
 
+    @pl.when(step == 0)
+    def _():
+        rows = jnp.concatenate([ref[...].reshape(-1, enc) for ref in late], axis=0)
+        shape = late_kv.shape[:3] + (width,)
+        late_kv[:, :, :, :width] = dot(rows, wk[...]).astype(BF16).reshape(shape)
+        late_kv[:, :, :, width:] = dot(rows, wv[...]).astype(BF16).reshape(shape)
+
+    mine = pl.ds(2 * step, 2)
+
+    def rows_of(col):
+        cols = pl.ds(col, HD)
+        parts = [ref[:, :, :, cols].reshape(-1, HD) for ref in kvs]
+        parts.append(late_kv[:, mine, :, cols].reshape(-1, HD))
+        return jnp.concatenate(parts, axis=0)
+
+    def put(col, grad):
+        cols = pl.ds(col, HD)
+        for at, (kind, i) in enumerate(places):
+            block = grad[at * 2 * SUB : (at + 1) * 2 * SUB].reshape(2, SUB, HD)
+            grads[kind][i, :, :, cols] = block
+            (own_all, core_all)[kind][i, mine, :, cols] = block
+
+    zero = jnp.zeros((SPAN, HD), BF16)
     for h0 in range(0, heads, group):
         hs = range(h0, h0 + group)
-        q = [q_ref[:, pl.ds(h * HD, HD)] for h in hs]
-        g = [g_ref[:, pl.ds(h * HD, HD)] for h in hs]
-        k = [keys_of(h * HD) for h in hs]
-        v = [keys_of(width + h * HD) for h in hs]
-        s = jnp.concatenate([dot(a, b, last) for a, b in zip(q, k)], axis=0) * scale
-        dw = jnp.concatenate([dot(a, b, last) for a, b in zip(g, v)], axis=0)
+        qg, kv = [], []
+        for h in hs:
+            cols = pl.ds(h * HD, HD)
+            top = jnp.concatenate([q_ref[:, cols], zero], axis=1)
+            low = jnp.concatenate([zero, g_ref[:, cols]], axis=1)
+            qg.append(jnp.concatenate([top, low], axis=0))
+            kv.append(jnp.concatenate([rows_of(h * HD), rows_of(width + h * HD)], axis=1))
+        both = [dot(a, b, last) for a, b in zip(qg, kv)]
+        s = jnp.concatenate([x[:SPAN] for x in both], axis=0) * scale
+        dw = jnp.concatenate([x[SPAN:] for x in both], axis=0)
         e = jnp.exp(s - jnp.max(s, axis=1, keepdims=True))
         p = e * (1.0 / jnp.sum(e, axis=1, keepdims=True))
         rs = jnp.sum(dw * p, axis=1, keepdims=True)
         w = p.astype(BF16)
         ds = (p * (dw - rs) * scale).astype(BF16)
-        ws = [w[i * SPAN : (i + 1) * SPAN] for i in range(group)]
-        dss = [ds[i * SPAN : (i + 1) * SPAN] for i in range(group)]
-        att = [dot(a, b).astype(BF16) for a, b in zip(ws, v)]
-        dq = [dot(a, b).astype(BF16) for a, b in zip(dss, k)]
-        dk = [dot(a, b, first).astype(BF16) for a, b in zip(dss, q)]
-        dv = [dot(a, b, first).astype(BF16) for a, b in zip(ws, g)]
+        span = [slice(i * SPAN, (i + 1) * SPAN) for i in range(group)]
+        dsw = [jnp.concatenate([ds[i], w[i]], axis=0) for i in span]
+        out = [dot(a, b).astype(BF16) for a, b in zip(dsw, kv)]
+        back = [dot(a, b, first).astype(BF16) for a, b in zip(dsw, qg)]
         for i, h in enumerate(hs):
-            att_ref[:, pl.ds(h * HD, HD)] = att[i]
-            dq_ref[:, pl.ds(h * HD, HD)] = dq[i]
-            put(h * HD, dk[i])
-            put(width + h * HD, dv[i])
-
-
-def attend(kvs, places, sizes, queries, cotangent):
+            dq_ref[:, pl.ds(h * HD, HD)] = out[i][:SPAN, :HD]
+            att_ref[:, pl.ds(h * HD, HD)] = out[i][SPAN:, HD:]
+            put(h * HD, back[i][:, :HD])
+            put(width + h * HD, back[i][:, HD:])
+
+    @pl.when(step == pl.num_programs(0) - 1)
+    def _():
+        count = own_out.shape[-1]
+        for ref, outs in ((core_all, (near_out, far_out)), (own_all, (own_out,))):
+            rows = ref[...].reshape(-1, 2 * width)
+            res = dot(rows[:, :width], wk[:count, :], last) + dot(rows[:, width:], wv[:count, :], last)
+            res = res.reshape(ref.shape[:3] + (count,))
+            if len(outs) == 1:
+                outs[0][...] = res
+            else:
+                outs[0][...] = res[:near]
+                outs[1][...] = res[near:]
+
+
+def attend(kvs, late, wk, wv, places, near, count, queries, cotangent):
     tokens, width = queries.shape
     spans = tokens // SPAN
     n = kvs[0].shape[1]
+    enc = wk.shape[0]
+    pieces = len(places) // 2
     rows = pl.BlockSpec((SPAN, width), lambda i: (i, 0))
 
     def kv_block(pieces):
         return pl.BlockSpec((pieces, 2, SUB, 2 * width), lambda i: (0, i, 0, 0))
 
+    def whole(shape):
+        return pl.BlockSpec(shape, lambda i: (0,) * len(shape))
+
     keys = len(places) * 2 * SUB
-    out = pl.pallas_call(
-        functools.partial(attend_body, places, len(kvs)),
+    parts = [(near, n, SUB, count), (pieces - near, n, SUB, count), (pieces, n, SUB, count)]
+    every = (pieces, n, SUB, 2 * width)
+    return pl.pallas_call(
+        functools.partial(attend_body, places, len(kvs), len(late), near),
         out_shape=[jax.ShapeDtypeStruct((tokens, width), BF16)] * 2
-        + [jax.ShapeDtypeStruct((size, n, SUB, 2 * width), BF16) for size in sizes],
+        + [jax.ShapeDtypeStruct(every, BF16)] * 2
+        + [jax.ShapeDtypeStruct(part, F32) for part in parts],
         grid=(spans,),
-        in_specs=[kv_block(kv.shape[0]) for kv in kvs] + [rows, rows],
-        out_specs=[rows, rows] + [kv_block(size) for size in sizes],
-        compiler_params=params(),
-        cost_estimate=cost(12 * tokens * width * keys, 8 * tokens * width + 8 * spans * keys * 2 * width),
+        in_specs=[kv_block(kv.shape[0]) for kv in kvs]
+        + [whole(x.shape) for x in late]
+        + [whole(wk.shape), whole(wv.shape), rows, rows],
+        out_specs=[rows, rows] + [kv_block(pieces)] * 2 + [whole(part) for part in parts],
+        scratch_shapes=[
+            pltpu.VMEM((len(late), n, SUB, 2 * width), BF16),
+            pltpu.VMEM(every, BF16),
+            pltpu.VMEM(every, BF16),
+        ],
+        compiler_params=params(VMEM_MORE),
+        cost_estimate=cost(
+            16 * tokens * width * keys + 4 * n * SUB * width * (len(late) * enc + 2 * pieces * count),
+            8 * tokens * width + 8 * spans * keys * 2 * width,
+        ),
         name="attend",
-    )(*kvs, queries, cotangent)
-    return out[0], out[1], out[2:]
+    )(*kvs, *late, wk, wv, queries, cotangent)
 
 
 def encode(x, axes):
@@ -295,26 +351,53 @@
         far_out[...] = full[near:]
 
 
-def own_grad_body(near, first, d_ref, wk, wv, near_got, far_got, near_out, *rest):
+def put_codes(far, codes):
+    pieces, n, sub, count = far.shape
+    near = codes[0].shape[0]
+    tiles = count // LANES
+    row = lax.broadcasted_iota(jnp.int32, (SUB, LANES), 0)
+    for i in range(pieces):
+        out, c = codes[i // near], i % near
+        code, power = encode(far[i], (1, 2))
+        for e in range(tiles):
+            out[c, e * n : (e + 1) * n] = code[:, :, e * LANES : (e + 1) * LANES]
+        note = jnp.zeros((SUB, LANES), F32)
+        for r in range(n):
+            note = jnp.where(row == r, power[r], note)
+        out[c, tiles * n] = note.astype(jnp.int32).astype(jnp.int16)
+
+
+def far_codes_body(mine, got, *codes):
+    put_codes(mine[...] + got[...], codes)
+
+
+def far_codes(own, got, near):
+    far, n, sub, count = got.shape
+    shape = (near, count // LANES * n + 1, sub, LANES)
+    return pl.pallas_call(
+        far_codes_body,
+        out_shape=[jax.ShapeDtypeStruct(shape, jnp.int16)] * (far // near),
+        grid=(1,),
+        in_specs=[
+            pl.BlockSpec((pl.Element(far), pl.Element(n), pl.Element(sub), pl.Element(count)), lambda i: (near, 0, 0, 0)),
+            pl.BlockSpec(got.shape, lambda i: (0, 0, 0, 0)),
+        ],
+        out_specs=[pl.BlockSpec(shape, lambda i: (0, 0, 0, 0))] * (far // near),
+        compiler_params=params(),
+        cost_estimate=cost(8 * got.size, 10 * got.size),
+        name="far_codes",
+    )(own, got)
+
+
+def own_grad_body(near, first, d_ref, wk, wv, far_got, near_out, *rest):
     codes, acc = rest[:-1], rest[-1]
     grad_step(first, d_ref, wk, wv, acc)
 
     @pl.when(pl.program_id(0) == pl.num_programs(0) - 1)
     def _():
         full = acc[...].reshape(d_ref.shape[:3] + acc.shape[1:])
-        near_out[...] = full[:near] + near_got[...]
-        n = d_ref.shape[1]
-        tiles = acc.shape[1] // LANES
-        row = lax.broadcasted_iota(jnp.int32, (SUB, LANES), 0)
-        for i in range(far_got.shape[0]):
-            out, c = codes[i // near], i % near
-            code, power = encode(full[near + i] + far_got[i], (1, 2))
-            for e in range(tiles):
-                out[c, e * n : (e + 1) * n] = code[:, :, e * LANES : (e + 1) * LANES]
-            note = jnp.zeros((SUB, LANES), F32)
-            for r in range(n):
-                note = jnp.where(row == r, power[r], note)
-            out[c, tiles * n] = note.astype(jnp.int32).astype(jnp.int16)
+        near_out[...] = full[:near]
+        put_codes(full[near:] + far_got[...], codes)
 
 
 def grads_of(d_kv, wk, wv, near, cols, got=None):
@@ -339,7 +422,7 @@
         grid=(4,),
         in_specs=[pl.BlockSpec((pieces, n, sub, step), lambda i: (0, 0, 0, i))]
         + weight_specs(wk.shape[0], step)
-        + ([] if got is None else [whole(near_shape), whole(far_shape)]),
+        + ([] if got is None else [whole(far_shape)]),
         out_specs=[whole(shape) for shape, _ in outs],
         scratch_shapes=[pltpu.VMEM((pieces * n * sub, count), F32)],
         compiler_params=params(),
@@ -349,19 +432,19 @@
         d_kv,
         wk,
         wv,
-        *([] if got is None else got),
+        *([] if got is None else [got]),
     )
     return out[0], out[1:]
 
 
-def send_body(n_dp, request, own, *rest):
+def send_body(n_dp, request, own, got, *rest):
     codes, outs, (stage, powers) = rest[: -n_dp - 2], rest[-n_dp - 2 : -2], rest[-2:]
-    n_chunks, n, sub, count = own.shape
+    n_chunks, n, sub, count = got.shape
     tiles = count // LANES
     cap = request.shape[0] // n_dp
     for c in range(n_chunks):
         for r in range(n):
-            total = own[c, r]
+            total = own[c, r] + got[c, r]
             for code in codes:
                 unit = jnp.exp2(code[c, tiles * n].astype(F32)[r : r + 1] - 15.0)
                 total = total + jnp.concatenate(
@@ -386,24 +469,26 @@
         outs[d][cap * n_chunks * tiles] = note.astype(jnp.int32).astype(jnp.int16)
 
 
-def send_codes(request, own, codes, n_dp):
-    n_chunks, n, sub, count = own.shape
+def send_codes(request, own, got, codes, n_dp):
+    n_chunks, n, sub, count = got.shape
+    block = pl.BlockSpec(got.shape, lambda i: (0, 0, 0, 0))
     tiles = count // LANES
     cap = request.shape[0] // n_dp
     shape = (cap * n_chunks * tiles + 1, SUB, LANES)
     return pl.pallas_call(
         functools.partial(send_body, n_dp),
         out_shape=[jax.ShapeDtypeStruct(shape, jnp.int16)] * n_dp,
-        in_specs=[SMEM, VMEM] + [VMEM] * len(codes),
+        grid=(1,),
+        in_specs=[SMEM, block, block] + [VMEM] * len(codes),
         out_specs=[VMEM] * n_dp,
         scratch_shapes=[
             pltpu.VMEM((n, n_chunks * tiles, SUB, LANES), jnp.int16),
             pltpu.VMEM((n, n_chunks, SUB, LANES), F32),
         ],
         compiler_params=params(),
-        cost_estimate=cost(10 * own.size, 6 * own.size + 2 * n_dp * math.prod(shape)),
+        cost_estimate=cost(10 * got.size, 6 * got.size + 2 * n_dp * math.prod(shape)),
         name="send_codes",
-    )(request, own, *codes)
+    )(request, own, got, *codes)
 
 
 def gather_body(n_dp, n_chunks, first, me, asked, *refs):
@@ -475,16 +560,14 @@
         got = {d: over_dp(xs[d], sign * d) for d in distances}
         return got
 
-    me = lax.axis_index("dp").astype(jnp.int32).reshape(1)
-    wanted, request = ask(me, owners, slots, n_dp, cap)
-    asked = lax.all_gather(wanted, "dp")
-    first = (lax.axis_index("tensor") * share).astype(jnp.int32).reshape(1)
+    me, wanted, request = ask(owners, slots, n_dp, cap)
+    asked = lax.psum(wanted, "dp")
 
     def place(c, kind, d):
         return (kind, c if d == 0 else n_chunks * d + c)
 
     kvs, places = [], []
-    packed = pack(me, asked, first, table, n_chunks, cap)
+    packed = pack(me, asked, table, n_chunks, cap)
     early = {}
     for c in range(n_chunks):
         sent = packed[c * n_dp : (c + 1) * n_dp]
@@ -507,27 +590,29 @@
         else:
             near = project(near, key_weight, value_weight)
             near, far = lax.optimization_barrier((near, far))
-            far = far + [over_core(x) for x in far]
-            kvs = kvs + [near, project(far, key_weight, value_weight)]
+            late = far + [over_core(x) for x in far]
+            kvs = kvs + [near]
         places += near_at + far_at
-
-    sizes = [n_chunks * n_x, n_chunks * n_x]
-    attended, d_query, (d_own, d_core) = attend(kvs, places, sizes, queries, cotangent)
 
     lead = 3 * LANES
     parts = ((0, lead), (lead, enc - lead))
-    d_table, got, before = None, [], None
-    for cols in parts:
-        near, (far,) = grads_of(d_core, key_weight, value_weight, n_chunks, cols)
-        if got:
-            got, near = lax.optimization_barrier((got, near))
-        got = got + [(over_core(near), over_core(far))]
-    for cols, sums in zip(parts, got):
-        own, codes = grads_of(d_own, key_weight, value_weight, n_chunks, cols, sums)
+    attended, d_query, d_own, d_core, near, far, own = attend(
+        kvs, late, key_weight, value_weight, places, n_chunks, lead, queries, cotangent
+    )
+    near_got, far_got = over_core(near), over_core(far)
+    near, (far,) = grads_of(d_core, key_weight, value_weight, n_chunks, parts[1])
+    far_got, near = lax.optimization_barrier((far_got, near))
+    sums = [(own, near_got, far_codes(own, far_got, n_chunks))]
+    near_got, far_got = over_core(near), over_core(far)
+    own, codes = grads_of(d_own, key_weight, value_weight, n_chunks, parts[1], far_got)
+    sums.append((own, near_got, codes))
+
+    d_table, before = None, None
+    for cols, (own, got, codes) in zip(parts, sums):
         if before is not None:
             codes, before = lax.optimization_barrier((codes, before))
         codes = before = [over_x(code, n_x - d) for d, code in enumerate(codes, 1)]
-        sent = send_codes(request, own, codes, n_dp)
+        sent = send_codes(request, own, got, codes, n_dp)
         came = to_all(sent, 1)
         arrived = [sent[0]] + [came[d] for d in range(1, n_dp)]
         d_table = gather_grads(me, asked, arrived, n_slabs, n_chunks, enc, cols, d_table)

time: 185 us -> 190 us (1.027)
  waiting for transfers between devices: 62.4 us -> 67.4 us
    pallas_call x2 -> x3, Pallas kernels: 14.3 us -> 24.1 us  [the longest x1 22.2 us: attend(): pl.pallas_call(functools.partial(attend_body, places, len(kvs), len(late)...]
    pallas_call x4 -> x2, Pallas kernels: 19.2 us -> 9.76 us  [grads_of(): pl.pallas_call(functools.partial(body, near, first), out_shape=[jax.Shape...]
    psum x0 -> x1, blocking collectives: none -> 8.59 us  [on_device(): asked = lax.psum(wanted, 'dp')]
    unnamed x1 -> x0, blocking collectives: 7.86 us -> none
    pallas_call x3 -> x2, Pallas kernels: 13.4 us -> 9.76 us  [project(): pl.pallas_call(functools.partial(project_body, n_in), out_shape=jax.Shape...]
    ppermute x8, waiting for transfers between devices: 2.63 us -> 5.89 us  [over_core(): return lax.ppermute(x, 'tensor', [(t, t ^ 1) for t in range(n_tp)])]
    ppermute x28, starting transfers between devices: 35.5 us -> 37.8 us  [over_dp(): return lax.ppermute(x, 'dp', [(i, (i + d) % n_dp) for i in range(n_dp)])]
    unnamed x15 -> x22, local copies, waits for them, and re-layouts: 4.17 us -> 3.13 us
  transfers between devices with their start and end apart: 40 -> 40, of which waited for: 17 -> 21; matrix products, arithmetic and copies ran while one was open for 0% -> 0% of each run, Pallas kernels for 16% -> 11%
where the time goes in v6:
time: 190 us; the launch traced here: 189 us
  waiting for transfers between devices  67.4 us (35%)
  Pallas kernels  60.2 us (32%)
  starting transfers between devices  48.9 us (26%)
  blocking collectives  8.59 us (5%)
  local copies, waits for them, and re-layouts  3.13 us (2%)
    ppermute x28, waiting for transfers between devices, over_dp(): return lax.ppermute(x, 'dp', [(i, (i + d) % n_dp) for i in range(n_dp)])  43.7 us
    ppermute x28, starting transfers between devices, over_dp(): return lax.ppermute(x, 'dp', [(i, (i + d) % n_dp) for i in range(n_dp)])  37.8 us
    pallas_call x1, Pallas kernels, attend(): pl.pallas_call(functools.partial(attend_body, places, len(kvs), len(late)...  22.2 us
    ppermute x4, waiting for transfers between devices, over_x(): lax.ppermute(x, 'tensor', [(t, (t + 2 * d) % n_tp) for t in range(n_tp)])  17.8 us
    pallas_call x2, Pallas kernels, grads_of(): pl.pallas_call(functools.partial(body, near, first), out_shape=[jax.Shape...  9.76 us
    pallas_call x2, Pallas kernels, project(): pl.pallas_call(functools.partial(project_body, n_in), out_shape=jax.Shape...  9.76 us
    ppermute x8, starting transfers between devices, over_core(): return lax.ppermute(x, 'tensor', [(t, t ^ 1) for t in range(n_tp)])  8.93 us
    psum x1, blocking collectives, on_device(): asked = lax.psum(wanted, 'dp')  8.59 us
  transfers between devices with their start and end apart: 40, of which 21 were waited for; matrix products, arithmetic and copies ran while one was open for 0% of the time, Pallas kernels for 11%

profile of v6, /device:TPU:13, one launch (start us, length us, event | category | flops | bytes accessed | tf_op | source)
XLA Modules:
  0.0 189.2 jit_solution(17583860793603460904)
XLA Ops:
  2.2 8.6 %psum.7.asked = s32[8,32]{1,0:T(8,128)} all-reduce(s32[8,32]{1,0:T(8,128)} %get-tuple-element.68), channel_id=1, replica_groups=mesh['dp'=8,'tensor'=4] {'dp'}, use_global_device_ids=true, to_apply=%region_0.0 | all-reduce | flops 256 | bytes 2048 | tf_op jit(solution)/shard_map/psum | solution.py:564
  10.8 4.8 %pack_rows.1 = (bf16[4,16,896]{2,1,0:T(8,128)(2,1)}, bf16[4,16,896]{2,1,0:T(8,128)(2,1)}, bf16[4,16,896]{2,1,0:T(8,128)(2,1)}, bf16[4,16,896]{2,1,0:T(8,128)(2,1...) custom-call(s32[1]{0:T(128)} %get-tuple-element.67.me, ...), custom_call_target="tpu_custom_call" | custom-call | bytes 3670016 | tf_op jit(solution)/shard_map/pack_rows/pallas_call | solution.py:104
  23.7 7.0 %collective-permute-done.8.refs_4_ = bf16[4,16,896]{2,1,0:T(8,128)(2,1)S(1)} collective-permute-done((bf16[4,16,896]{2,1,0:T(8,128)(2,1)}, bf16[4,16,896]{2,1,0:T(8,128)(2,1)S(1)}, u32[]{:S(2)}, u32[]{:S(2)}) %collective-permute-start.8) | collective-permute-done | bytes 114720 | tf_op jit(solution)/shard_map/ppermute | solution.py:555
  30.7 3.7 %collective-permute-done.9.refs_5_ = bf16[4,16,896]{2,1,0:T(8,128)(2,1)S(1)} collective-permute-done((bf16[4,16,896]{2,1,0:T(8,128)(2,1)}, bf16[4,16,896]{2,1,0:T(8,128)(2,1)S(1)}, u32[]{:S(2)}, u32[]{:S(2)}) %collective-permute-start.9) | collective-permute-done | bytes 114720 | tf_op jit(solution)/shard_map/ppermute | solution.py:555
  45.9 4.2 %collective-permute-start.15 = (bf16[16,16,896]{2,1,0:T(8,128)(2,1)S(1)}, bf16[16,16,896]{2,1,0:T(8,128)(2,1)S(1)}, u32[]{:S(2)}, u32[]{:S(2)}) collective-permute-start(bf16[16,16,896]{2,1,0:T(8,128)(2,1)S(1)} %compact_rows.2.refs_0_), channel_id=1, source_target_pairs={{0,1},{1,0},{2,3},{3,2},{4,5},{5,4},{6,7},{7,6},{8,9},{9,8},{10,11... | collective-permute-start | bytes 1376264 | tf_op jit(solution)/shard_map/ppermute | solution.py:549
  50.5 4.9 %collective-permute-done.4.refs_5_ = bf16[4,16,896]{2,1,0:T(8,128)(2,1)S(1)} collective-permute-done((bf16[4,16,896]{2,1,0:T(8,128)(2,1)}, bf16[4,16,896]{2,1,0:T(8,128)(2,1)S(1)}, u32[]{:S(2)}, u32[]{:S(2)}) %collective-permute-start.4) | collective-permute-done | bytes 114720 | tf_op jit(solution)/shard_map/ppermute | solution.py:555
  57.6 3.6 %collective-permute-start.1 = (bf16[4,16,896]{2,1,0:T(8,128)(2,1)}, bf16[4,16,896]{2,1,0:T(8,128)(2,1)S(1)}, u32[]{:S(2)}, u32[]{:S(2)}) collective-permute-start(bf16[4,16,896]{2,1,0:T(8,128)(2,1)} %get-tuple-element.71), channel_id=1, source_target_pairs={{0,24},{4,28},{8,0},{12,4},{16,8},{20,12},{24,16},{28,20},{1,25},{... | collective-permute-start | bytes 344072 | tf_op jit(solution)/shard_map/ppermute | solution.py:555
  61.3 6.2 %project.2.refs_0_ = bf16[4,16,16,2048]{3,2,1,0:T(8,128)(2,1)S(1)} custom-call(bf16[16,16,896]{2,1,0:T(8,128)(2,1)S(1)} %compact_rows.2.refs_0_, bf16[16,16,896]{2,1,0:T(8,128)(2,1)S(1)} %collective-permute-done.15.refs_1_, bf16[16,16,896]{2,1,0:T(8,128)(2,1)S(1)} %collective-permute-done.12.refs_2_, ...), custom_call_target="tpu_custom_call" | custom-call | flops 3758096384 | bytes 9699328 | tf_op jit(solution)/shard_map/project/pallas_call | solution.py:181
  73.3 3.6 %project.3.refs_1_ = bf16[2,16,16,2048]{3,2,1,0:T(8,128)(2,1)S(1)} custom-call(bf16[16,16,896]{2,1,0:T(8,128)(2,1)S(1)} %compact_rows.3.refs_0_, bf16[16,16,896]{2,1,0:T(8,128)(2,1)S(1)} %collective-permute-done.17.refs_1_, bf16[896,1024]{1,0:T(8,128)(2,1)S(1)} %copy-done.1, bf16[896,1024]{1,0:T(8,128)(2,1)S(1)} %copy-done.2), custom_call_target="tpu_custom_call" | custom-call | flops 1879048192 | bytes 6684672 | tf_op jit(solution)/shard_map/project/pallas_call | solution.py:181
  76.9 7.0 %collective-permute-done.18.refs_2_ = bf16[16,16,896]{2,1,0:T(8,128)(2,1)S(1)} collective-permute-done((bf16[16,16,896]{2,1,0:T(8,128)(2,1)S(1)}, bf16[16,16,896]{2,1,0:T(8,128)(2,1)S(1)}, u32[]{:S(2)}, u32[]{:S(2)}) %collective-permute-start.18) | collective-permute-done | bytes 458784 | tf_op jit(solution)/shard_map/ppermute | solution.py:552
  86.2 22.2 %attend.1 = (bf16[512,1024]{1,0:T(8,128)(2,1)}, bf16[512,1024]{1,0:T(8,128)(2,1)}, bf16[4,16,16,2048]{3,2,1,0:T(8,128)(2,1)}, bf16[4,16,16,2048]{3,2,1,0:T(8,128...) custom-call(bf16[4,16,16,2048]{3,2,1,0:T(8,128)(2,1)} %copy-done.10, ...), custom_call_target="tpu_custom_call" | custom-call | flops 7247757312 | bytes 37748736 | tf_op jit(solution)/shard_map/attend/pallas_call | solution.py:293
  110.6 4.7 %core_grads.1 = (f32[2,16,16,512]{3,2,1,0:T(8,128)S(1)}, f32[2,16,16,512]{3,2,1,0:T(8,128)S(1)}) custom-call(bf16[4,16,16,2048]{3,2,1,0:T(8,128)(2,1)S(1)} %copy-done.9, bf16[896,1024]{1,0:T(8,128)(2,1)S(1)} %copy-done.1, bf16[896,1024]{1,0:T(8,128)(2,1)S(1)} %copy-done.2), custom_call_target="tpu_custom_call" | custom-call | flops 2147483648 | bytes 6291456 | tf_op jit(solution)/shard_map/core_grads/pallas_call | solution.py:419
  116.0 3.3 %collective-permute-done.21.got = f32[2,16,16,384]{3,2,1,0:T(8,128)S(1)} collective-permute-done((f32[2,16,16,384]{3,2,1,0:T(8,128)S(1)}, f32[2,16,16,384]{3,2,1,0:T(8,128)S(1)}, u32[]{:S(2)}, u32[]{:S(2)}) %collective-permute-start.21) | collective-permute-done | bytes 786464 | tf_op jit(solution)/shard_map/ppermute | solution.py:549
  120.7 5.0 %own_grads.1 = (f32[2,16,16,512]{3,2,1,0:T(8,128)S(1)}, s16[2,65,16,128]{3,2,1,0:T(8,128)(2,1)S(1)}) custom-call(bf16[4,16,16,2048]{3,2,1,0:T(8,128)(2,1)S(1)} %copy-done, bf16[896,1024]{1,0:T(8,128)(2,1)S(1)} %copy-done.1, bf16[896,1024]{1,0:T(8,128)(2,1)S(1)} %copy-done.2, f32[2,16,16,512]{3,2,1,0:T(8,128)S(1)} %collective-permute-done.20.far_got), custom_call_target="tpu_custom_call" | custom-call | flops 2147483648 | bytes 6291456 | tf_op jit(solution)/shard_map/own_grads/pallas_call | solution.py:419
  125.8 5.0 %collective-permute-done.23.rest_0_ = s16[2,49,16,128]{3,2,1,0:T(8,128)(2,1)S(1)} collective-permute-done((s16[2,49,16,128]{3,2,1,0:T(8,128)(2,1)S(1)}, s16[2,49,16,128]{3,2,1,0:T(8,128)(2,1)S(1)}, u32[]{:S(2)}, u32[]{:S(2)}) %collective-permute-start.23) | collective-permute-done | bytes 401440 | tf_op jit(solution)/shard_map/ppermute | solution.py:552
  132.2 3.0 %collective-permute-start.33 = (s16[25,16,128]{2,1,0:T(8,128)(2,1)S(1)}, s16[25,16,128]{2,1,0:T(8,128)(2,1)S(1)}, u32[]{:S(2)}, u32[]{:S(2)}) collective-permute-start(s16[25,16,128]{2,1,0:T(8,128)(2,1)S(1)} %get-tuple-element.124), channel_id=1, source_target_pairs={{0,4},{4,8},{8,12},{12,16},{16,20},{20,24},{24,28},{28,0},{1,5},{5... | collective-permute-start | bytes 307208 | tf_op jit(solution)/shard_map/ppermute | solution.py:555
  137.7 5.7 %collective-permute-done.24.rest_0_ = s16[2,65,16,128]{3,2,1,0:T(8,128)(2,1)S(1)} collective-permute-done((s16[2,65,16,128]{3,2,1,0:T(8,128)(2,1)S(1)}, s16[2,65,16,128]{3,2,1,0:T(8,128)(2,1)S(1)}, u32[]{:S(2)}, u32[]{:S(2)}) %collective-permute-start.24) | collective-permute-done | bytes 532512 | tf_op jit(solution)/shard_map/ppermute | solution.py:552
  153.6 3.6 %collective-permute-done.37.refs_5_ = s16[25,16,128]{2,1,0:T(8,128)(2,1)S(1)} collective-permute-done((s16[25,16,128]{2,1,0:T(8,128)(2,1)S(1)}, s16[25,16,128]{2,1,0:T(8,128)(2,1)S(1)}, u32[]{:S(2)}, u32[]{:S(2)}) %collective-permute-start.37) | collective-permute-done | bytes 102432 | tf_op jit(solution)/shard_map/ppermute | solution.py:555
  159.5 2.8 %collective-permute-done.38.refs_6_ = s16[25,16,128]{2,1,0:T(8,128)(2,1)S(1)} collective-permute-done((s16[25,16,128]{2,1,0:T(8,128)(2,1)S(1)}, s16[25,16,128]{2,1,0:T(8,128)(2,1)S(1)}, u32[]{:S(2)}, u32[]{:S(2)}) %collective-permute-start.38) | collective-permute-done | bytes 102432 | tf_op jit(solution)/shard_map/ppermute | solution.py:555
  162.3 2.9 %collective-permute-start.28 = (s16[33,16,128]{2,1,0:T(8,128)(2,1)S(1)}, s16[33,16,128]{2,1,0:T(8,128)(2,1)S(1)}, u32[]{:S(2)}, u32[]{:S(2)}) collective-permute-start(s16[33,16,128]{2,1,0:T(8,128)(2,1)S(1)} %get-tuple-element.118), channel_id=1, source_target_pairs={{0,16},{4,20},{8,24},{12,28},{16,0},{20,4},{24,8},{28,12},{1,17},{... | collective-permute-start | bytes 405512 | tf_op jit(solution)/shard_map/ppermute | solution.py:555
  170.6 5.9 %collective-permute-done.28.refs_4_ = s16[33,16,128]{2,1,0:T(8,128)(2,1)S(1)} collective-permute-done((s16[33,16,128]{2,1,0:T(8,128)(2,1)S(1)}, s16[33,16,128]{2,1,0:T(8,128)(2,1)S(1)}, u32[]{:S(2)}, u32[]{:S(2)}) %collective-permute-start.28) | collective-permute-done | bytes 135200 | tf_op jit(solution)/shard_map/ppermute | solution.py:555
  176.5 3.0 %collective-permute-done.30.refs_6_ = s16[33,16,128]{2,1,0:T(8,128)(2,1)S(1)} collective-permute-done((s16[33,16,128]{2,1,0:T(8,128)(2,1)S(1)}, s16[33,16,128]{2,1,0:T(8,128)(2,1)S(1)}, u32[]{:S(2)}, u32[]{:S(2)}) %collective-permute-start.30) | collective-permute-done | bytes 135200 | tf_op jit(solution)/shard_map/ppermute | solution.py:555
  179.5 6.7 %collective-permute-done.31.refs_7_ = s16[33,16,128]{2,1,0:T(8,128)(2,1)S(1)} collective-permute-done((s16[33,16,128]{2,1,0:T(8,128)(2,1)S(1)}, s16[33,16,128]{2,1,0:T(8,128)(2,1)S(1)}, u32[]{:S(2)}, u32[]{:S(2)}) %collective-permute-start.31) | collective-permute-done | bytes 135200 | tf_op jit(solution)/shard_map/ppermute | solution.py:555
  186.2 2.8 %gather_grads.3 = f32[16,32,896]{2,1,0:T(8,128)} custom-call(s32[1]{0:T(128)} %get-tuple-element.67.me, s32[8,32]{1,0:T(8,128)S(1)} %copy-done.5, s16[33,16,128]{2,1,0:T(8,128)(2,1)S(1)} %get-tuple-element.114.refs_0_, s16[33,16,128]{2,1,0:T(8,128)(2,1)S(1)} %collective-permute-done.25.refs_1_, ...), custom_call_target="tpu_custom_call", output_to_operand_aliasing={{}: (10, {})} | custom-call | bytes 2097152 | tf_op jit(solution)/shard_map/gather_grads/pallas_call | solution.py:524
  (93 shorter events, 57.8 us)
Async XLA Ops:
  18.8 11.9 %collective-permute-start.8 = (bf16[4,16,896]{2,1,0:T(8,128)(2,1)}, bf16[4,16,896]{2,1,0:T(8,128)(2,1)S(1)}, u32[]{:S(2)}, u32[]{:S(2)}) collective-permute-start(bf16[4,16,896]{2,1,0:T(8,128)(2,1)} %get-tuple-element.80), channel_id=1, source_target_pairs={{0,16},{4,20},{8,24},{12,28},{16,0},{20,4},{24,8},{28,12},{1,17},{... | collective-permute-start | bytes 344072 | tf_op jit(solution)/shard_map/ppermute | solution.py:555
  20.2 14.2 %collective-permute-start.9 = (bf16[4,16,896]{2,1,0:T(8,128)(2,1)}, bf16[4,16,896]{2,1,0:T(8,128)(2,1)S(1)}, u32[]{:S(2)}, u32[]{:S(2)}) collective-permute-start(bf16[4,16,896]{2,1,0:T(8,128)(2,1)} %get-tuple-element.81), channel_id=1, source_target_pairs={{0,12},{4,16},{8,20},{12,24},{16,28},{20,0},{24,4},{28,8},{1,13},{... | collective-permute-start | bytes 344072 | tf_op jit(solution)/shard_map/ppermute | solution.py:555
  20.4 15.3 %collective-permute-start.10 = (bf16[4,16,896]{2,1,0:T(8,128)(2,1)}, bf16[4,16,896]{2,1,0:T(8,128)(2,1)S(1)}, u32[]{:S(2)}, u32[]{:S(2)}) collective-permute-start(bf16[4,16,896]{2,1,0:T(8,128)(2,1)} %get-tuple-element.82), channel_id=1, source_target_pairs={{0,8},{4,12},{8,16},{12,20},{16,24},{20,28},{24,0},{28,4},{1,9},{5... | collective-permute-start | bytes 344072 | tf_op jit(solution)/shard_map/ppermute | solution.py:555
  21.6 16.5 %collective-permute-start.11 = (bf16[4,16,896]{2,1,0:T(8,128)(2,1)}, bf16[4,16,896]{2,1,0:T(8,128)(2,1)S(1)}, u32[]{:S(2)}, u32[]{:S(2)}) collective-permute-start(bf16[4,16,896]{2,1,0:T(8,128)(2,1)} %get-tuple-element.83), channel_id=1, source_target_pairs={{0,4},{4,8},{8,12},{12,16},{16,20},{20,24},{24,28},{28,0},{1,5},{5... | collective-permute-start | bytes 344072 | tf_op jit(solution)/shard_map/ppermute | solution.py:555
  40.8 14.6 %collective-permute-start.12 = (bf16[16,16,896]{2,1,0:T(8,128)(2,1)S(1)}, bf16[16,16,896]{2,1,0:T(8,128)(2,1)S(1)}, u32[]{:S(2)}, u32[]{:S(2)}) collective-permute-start(bf16[16,16,896]{2,1,0:T(8,128)(2,1)S(1)} %compact_rows.2.refs_0_), channel_id=1, source_target_pairs={{0,2},{1,3},{2,0},{3,1},{4,6},{5,7},{6,4},{7,5},{8,10},{9,11},{10,... | collective-permute-start | bytes 1376264 | tf_op jit(solution)/shard_map/ppermute | solution.py:552
  45.9 15.2 %collective-permute-start.15 = (bf16[16,16,896]{2,1,0:T(8,128)(2,1)S(1)}, bf16[16,16,896]{2,1,0:T(8,128)(2,1)S(1)}, u32[]{:S(2)}, u32[]{:S(2)}) collective-permute-start(bf16[16,16,896]{2,1,0:T(8,128)(2,1)S(1)} %compact_rows.2.refs_0_), channel_id=1, source_target_pairs={{0,1},{1,0},{2,3},{3,2},{4,5},{5,4},{6,7},{7,6},{8,9},{9,8},{10,11... | collective-permute-start | bytes 1376264 | tf_op jit(solution)/shard_map/ppermute | solution.py:549
  56.7 10.7 %collective-permute-start = (bf16[4,16,896]{2,1,0:T(8,128)(2,1)}, bf16[4,16,896]{2,1,0:T(8,128)(2,1)S(1)}, u32[]{:S(2)}, u32[]{:S(2)}) collective-permute-start(bf16[4,16,896]{2,1,0:T(8,128)(2,1)} %get-tuple-element.70), channel_id=1, source_target_pairs={{0,28},{4,0},{8,4},{12,8},{16,12},{20,16},{24,20},{28,24},{1,29},{... | collective-permute-start | bytes 344072 | tf_op jit(solution)/shard_map/ppermute | solution.py:555
  71.8 12.1 %collective-permute-start.18 = (bf16[16,16,896]{2,1,0:T(8,128)(2,1)S(1)}, bf16[16,16,896]{2,1,0:T(8,128)(2,1)S(1)}, u32[]{:S(2)}, u32[]{:S(2)}) collective-permute-start(bf16[16,16,896]{2,1,0:T(8,128)(2,1)S(1)} %compact_rows.3.refs_0_), channel_id=1, source_target_pairs={{0,2},{1,3},{2,0},{3,1},{4,6},{5,7},{6,4},{7,5},{8,10},{9,11},{10,... | collective-permute-start | bytes 1376264 | tf_op jit(solution)/shard_map/ppermute | solution.py:552
  119.3 26.0 %collective-permute-start.22 = (f32[2,16,16,512]{3,2,1,0:T(8,128)S(1)}, f32[2,16,16,512]{3,2,1,0:T(8,128)S(1)}, u32[]{:S(2)}, u32[]{:S(2)}) collective-permute-start(f32[2,16,16,512]{3,2,1,0:T(8,128)S(1)} %get-tuple-element.109), channel_id=1, source_target_pairs={{0,1},{1,0},{2,3},{3,2},{4,5},{5,4},{6,7},{7,6},{8,9},{9,8},{10,11... | collective-permute-start | bytes 3145736 | tf_op jit(solution)/shard_map/ppermute | solution.py:549
  119.9 10.8 %collective-permute-start.23 = (s16[2,49,16,128]{3,2,1,0:T(8,128)(2,1)S(1)}, s16[2,49,16,128]{3,2,1,0:T(8,128)(2,1)S(1)}, u32[]{:S(2)}, u32[]{:S(2)}) collective-permute-start(s16[2,49,16,128]{3,2,1,0:T(8,128)(2,1)S(1)} %far_codes.1), channel_id=1, source_target_pairs={{0,2},{1,3},{2,0},{3,1},{4,6},{5,7},{6,4},{7,5},{8,10},{9,11},{10,... | collective-permute-start | bytes 1204232 | tf_op jit(solution)/shard_map/ppermute | solution.py:552
  120.3 10.7 %collective-permute-start.32 = (f32[2,16,16,384]{3,2,1,0:T(8,128)S(1)}, f32[2,16,16,384]{3,2,1,0:T(8,128)S(1)}, u32[]{:S(2)}, u32[]{:S(2)}) collective-permute-start(f32[2,16,16,384]{3,2,1,0:T(8,128)S(1)} %get-tuple-element.122), channel_id=1, source_target_pairs={{0,1},{1,0},{2,3},{3,2},{4,5},{5,4},{6,7},{7,6},{8,9},{9,8},{10,11... | collective-permute-start | bytes 2359304 | tf_op jit(solution)/shard_map/ppermute | solution.py:549
  130.8 12.6 %collective-permute-start.24 = (s16[2,65,16,128]{3,2,1,0:T(8,128)(2,1)S(1)}, s16[2,65,16,128]{3,2,1,0:T(8,128)(2,1)S(1)}, u32[]{:S(2)}, u32[]{:S(2)}) collective-permute-start(s16[2,65,16,128]{3,2,1,0:T(8,128)(2,1)S(1)} %get-tuple-element.113), channel_id=1, source_target_pairs={{0,2},{1,3},{2,0},{3,1},{4,6},{5,7},{6,4},{7,5},{8,10},{9,11},{10,... | collective-permute-start | bytes 1597448 | tf_op jit(solution)/shard_map/ppermute | solution.py:552
  132.2 16.9 %collective-permute-start.33 = (s16[25,16,128]{2,1,0:T(8,128)(2,1)S(1)}, s16[25,16,128]{2,1,0:T(8,128)(2,1)S(1)}, u32[]{:S(2)}, u32[]{:S(2)}) collective-permute-start(s16[25,16,128]{2,1,0:T(8,128)(2,1)S(1)} %get-tuple-element.124), channel_id=1, source_target_pairs={{0,4},{4,8},{8,12},{12,16},{16,20},{20,24},{24,28},{28,0},{1,5},{5... | collective-permute-start | bytes 307208 | tf_op jit(solution)/shard_map/ppermute | solution.py:555
  135.3 14.6 %collective-permute-start.34 = (s16[25,16,128]{2,1,0:T(8,128)(2,1)S(1)}, s16[25,16,128]{2,1,0:T(8,128)(2,1)S(1)}, u32[]{:S(2)}, u32[]{:S(2)}) collective-permute-start(s16[25,16,128]{2,1,0:T(8,128)(2,1)S(1)} %get-tuple-element.125), channel_id=1, source_target_pairs={{0,8},{4,12},{8,16},{12,20},{16,24},{20,28},{24,0},{28,4},{1,9},{5... | collective-permute-start | bytes 307208 | tf_op jit(solution)/shard_map/ppermute | solution.py:555
  135.5 14.3 %collective-permute-start.35 = (s16[25,16,128]{2,1,0:T(8,128)(2,1)S(1)}, s16[25,16,128]{2,1,0:T(8,128)(2,1)S(1)}, u32[]{:S(2)}, u32[]{:S(2)}) collective-permute-start(s16[25,16,128]{2,1,0:T(8,128)(2,1)S(1)} %get-tuple-element.126), channel_id=1, source_target_pairs={{0,12},{4,16},{8,20},{12,24},{16,28},{20,0},{24,4},{28,8},{1,13},{... | collective-permute-start | bytes 307208 | tf_op jit(solution)/shard_map/ppermute | solution.py:555
  146.5 21.0 %collective-permute-start.25 = (s16[33,16,128]{2,1,0:T(8,128)(2,1)S(1)}, s16[33,16,128]{2,1,0:T(8,128)(2,1)S(1)}, u32[]{:S(2)}, u32[]{:S(2)}) collective-permute-start(s16[33,16,128]{2,1,0:T(8,128)(2,1)S(1)} %get-tuple-element.115), channel_id=1, source_target_pairs={{0,4},{4,8},{8,12},{12,16},{16,20},{20,24},{24,28},{28,0},{1,5},{5... | collective-permute-start | bytes 405512 | tf_op jit(solution)/shard_map/ppermute | solution.py:555
  149.2 18.4 %collective-permute-start.26 = (s16[33,16,128]{2,1,0:T(8,128)(2,1)S(1)}, s16[33,16,128]{2,1,0:T(8,128)(2,1)S(1)}, u32[]{:S(2)}, u32[]{:S(2)}) collective-permute-start(s16[33,16,128]{2,1,0:T(8,128)(2,1)S(1)} %get-tuple-element.116), channel_id=1, source_target_pairs={{0,8},{4,12},{8,16},{12,20},{16,24},{20,28},{24,0},{28,4},{1,9},{5... | collective-permute-start | bytes 405512 | tf_op jit(solution)/shard_map/ppermute | solution.py:555
  149.9 12.4 %collective-permute-start.38 = (s16[25,16,128]{2,1,0:T(8,128)(2,1)S(1)}, s16[25,16,128]{2,1,0:T(8,128)(2,1)S(1)}, u32[]{:S(2)}, u32[]{:S(2)}) collective-permute-start(s16[25,16,128]{2,1,0:T(8,128)(2,1)S(1)} %get-tuple-element.129), channel_id=1, source_target_pairs={{0,24},{4,28},{8,0},{12,4},{16,8},{20,12},{24,16},{28,20},{1,25},{... | collective-permute-start | bytes 307208 | tf_op jit(solution)/shard_map/ppermute | solution.py:555
  152.3 13.6 %collective-permute-start.39 = (s16[25,16,128]{2,1,0:T(8,128)(2,1)S(1)}, s16[25,16,128]{2,1,0:T(8,128)(2,1)S(1)}, u32[]{:S(2)}, u32[]{:S(2)}) collective-permute-start(s16[25,16,128]{2,1,0:T(8,128)(2,1)S(1)} %get-tuple-element.130), channel_id=1, source_target_pairs={{0,28},{4,0},{8,4},{12,8},{16,12},{20,16},{24,20},{28,24},{1,29},{... | collective-permute-start | bytes 307208 | tf_op jit(solution)/shard_map/ppermute | solution.py:555
  157.2 13.4 %collective-permute-start.27 = (s16[33,16,128]{2,1,0:T(8,128)(2,1)S(1)}, s16[33,16,128]{2,1,0:T(8,128)(2,1)S(1)}, u32[]{:S(2)}, u32[]{:S(2)}) collective-permute-start(s16[33,16,128]{2,1,0:T(8,128)(2,1)S(1)} %get-tuple-element.117), channel_id=1, source_target_pairs={{0,12},{4,16},{8,20},{12,24},{16,28},{20,0},{24,4},{28,8},{1,13},{... | collective-permute-start | bytes 405512 | tf_op jit(solution)/shard_map/ppermute | solution.py:555
  162.3 14.2 %collective-permute-start.28 = (s16[33,16,128]{2,1,0:T(8,128)(2,1)S(1)}, s16[33,16,128]{2,1,0:T(8,128)(2,1)S(1)}, u32[]{:S(2)}, u32[]{:S(2)}) collective-permute-start(s16[33,16,128]{2,1,0:T(8,128)(2,1)S(1)} %get-tuple-element.118), channel_id=1, source_target_pairs={{0,16},{4,20},{8,24},{12,28},{16,0},{20,4},{24,8},{28,12},{1,17},{... | collective-permute-start | bytes 405512 | tf_op jit(solution)/shard_map/ppermute | solution.py:555
  165.8 10.7 %collective-permute-start.29 = (s16[33,16,128]{2,1,0:T(8,128)(2,1)S(1)}, s16[33,16,128]{2,1,0:T(8,128)(2,1)S(1)}, u32[]{:S(2)}, u32[]{:S(2)}) collective-permute-start(s16[33,16,128]{2,1,0:T(8,128)(2,1)S(1)} %get-tuple-element.119), channel_id=1, source_target_pairs={{0,20},{4,24},{8,28},{12,0},{16,4},{20,8},{24,12},{28,16},{1,21},{... | collective-permute-start | bytes 405512 | tf_op jit(solution)/shard_map/ppermute | solution.py:555
  167.5 12.0 %collective-permute-start.30 = (s16[33,16,128]{2,1,0:T(8,128)(2,1)S(1)}, s16[33,16,128]{2,1,0:T(8,128)(2,1)S(1)}, u32[]{:S(2)}, u32[]{:S(2)}) collective-permute-start(s16[33,16,128]{2,1,0:T(8,128)(2,1)S(1)} %get-tuple-element.120), channel_id=1, source_target_pairs={{0,24},{4,28},{8,0},{12,4},{16,8},{20,12},{24,16},{28,20},{1,25},{... | collective-permute-start | bytes 405512 | tf_op jit(solution)/shard_map/ppermute | solution.py:555
  167.5 18.6 %collective-permute-start.31 = (s16[33,16,128]{2,1,0:T(8,128)(2,1)S(1)}, s16[33,16,128]{2,1,0:T(8,128)(2,1)S(1)}, u32[]{:S(2)}, u32[]{:S(2)}) collective-permute-start(s16[33,16,128]{2,1,0:T(8,128)(2,1)S(1)} %get-tuple-element.121), channel_id=1, source_target_pairs={{0,28},{4,0},{8,4},{12,8},{16,12},{20,16},{24,20},{28,24},{1,29},{... | collective-permute-start | bytes 405512 | tf_op jit(solution)/shard_map/ppermute | solution.py:555
  (27 other events, 337.0 us)

commit v7 on v6

--- a/solution.py
+++ b/solution.py
@@ -72,43 +72,36 @@
     return asked[asker, d * (asked.shape[1] // n_dp) + j] - 1
 
 
-def pack_body(n_dp, n_chunks, me, asked, table, *rest):
+def pack_body(n_dp, chunk, share, me, asked, table, *rest):
     outs, sem = rest[:-1], rest[-1]
     cap = outs[0].shape[0]
-    first = lax.axis_index("tensor") * (n_chunks * SUB)
+    row = pl.multiple_of(lax.axis_index("tensor") * share + chunk * SUB, SUB)
 
     def each(act):
-        for c in range(n_chunks):
-            row = pl.multiple_of(first + c * SUB, SUB)
-            for d in range(n_dp):
-                for j in range(cap):
-                    slab = asked_of(asked, me, d, j)
-
-                    @pl.when(slab >= 0)
-                    def _():
-                        act(
-                            pltpu.make_async_copy(
-                                table.at[slab, pl.ds(row, SUB)],
-                                outs[c * n_dp + d].at[j],
-                                sem.at[c, d * cap + j],
-                            )
-                        )
+        for d in range(n_dp):
+            for j in range(cap):
+                slab = asked_of(asked, me, d, j)
+
+                @pl.when(slab >= 0)
+                def _():
+                    source = table.at[slab, pl.ds(row, SUB)]
+                    act(pltpu.make_async_copy(source, outs[d].at[j], sem.at[d * cap + j]))
 
     each(lambda copy: copy.start())
     each(lambda copy: copy.wait())
 
 
-def pack(me, asked, table, n_chunks, cap):
+def pack(me, asked, table, chunk, share, cap):
     n_dp = asked.shape[0]
     enc = table.shape[2]
     return pl.pallas_call(
-        functools.partial(pack_body, n_dp, n_chunks),
-        out_shape=[jax.ShapeDtypeStruct((cap, SUB, enc), table.dtype)] * (n_chunks * n_dp),
+        functools.partial(pack_body, n_dp, chunk, share),
+        out_shape=[jax.ShapeDtypeStruct((cap, SUB, enc), table.dtype)] * n_dp,
         in_specs=[SMEM, SMEM, ANY],
-        out_specs=[VMEM] * (n_chunks * n_dp),
-        scratch_shapes=[pltpu.SemaphoreType.DMA((n_chunks, n_dp * cap))],
+        out_specs=[VMEM] * n_dp,
+        scratch_shapes=[pltpu.SemaphoreType.DMA((n_dp * cap,))],
         compiler_params=params(VMEM_ALL),
-        cost_estimate=cost(0, 4 * n_chunks * n_dp * cap * SUB * enc),
+        cost_estimate=cost(0, 4 * n_dp * cap * SUB * enc),
         name="pack_rows",
     )(me, asked, table)
 
@@ -202,7 +195,7 @@
     enc = wk.shape[0]
     scale = 1.0 / math.sqrt(HD)
     heads = width // HD
-    group = min(4, heads)
+    group = min(8, heads)
     last = (((1,), (1,)), ((), ()))
     first = (((0,), (0,)), ((), ()))
 
@@ -321,34 +314,51 @@
     return code.astype(jnp.int32).astype(jnp.int16), power
 
 
-def grad_step(first, d_ref, wk, wv, acc):
+def grads_body(near, first, core_ref, own_ref, wk, wv, near_out, far_out, own_out, core_acc, own_acc):
     i = pl.program_id(0)
-    pieces, n, sub, step = d_ref.shape
-    rows = d_ref[...].reshape(pieces * n * sub, step)
 
     def act(w):
-        w = w[first : first + acc.shape[1], :]
-        part = lax.dot_general(rows, w, (((1,), (1,)), ((), ())), preferred_element_type=F32)
-
-        @pl.when(i == 0)
-        def _():
-            acc[...] = part
-
-        @pl.when(i > 0)
-        def _():
-            acc[...] += part
+        w = w[first : first + own_acc.shape[1], :]
+        for ref, acc in ((core_ref, core_acc), (own_ref, own_acc)):
+            rows = ref[...].reshape(acc.shape[0], -1)
+            part = lax.dot_general(rows, w, (((1,), (1,)), ((), ())), preferred_element_type=F32)
+
+            @pl.when(i == 0)
+            def _():
+                acc[...] = part
+
+            @pl.when(i > 0)
+            def _():
+                acc[...] += part
 
     with_weight(wk, wv, act)
 
-
-def core_grad_body(near, first, d_ref, wk, wv, near_out, far_out, acc):
-    grad_step(first, d_ref, wk, wv, acc)
-
-    @pl.when(pl.program_id(0) == pl.num_programs(0) - 1)
+    @pl.when(i == pl.num_programs(0) - 1)
     def _():
-        full = acc[...].reshape(d_ref.shape[:3] + acc.shape[1:])
-        near_out[...] = full[:near]
-        far_out[...] = full[near:]
+        core = core_acc[...].reshape(core_ref.shape[:3] + core_acc.shape[1:])
+        near_out[...] = core[:near]
+        far_out[...] = core[near:]
+        own_out[...] = own_acc[...].reshape(own_out.shape)
+
+
+def grads_of(d_core, d_own, wk, wv, near, cols):
+    pieces, n, sub, width = d_own.shape
+    first, count = cols
+    step = width // 4
+    shapes = [(near, n, sub, count), (pieces - near, n, sub, count), (pieces, n, sub, count)]
+    rows = pieces * n * sub
+    return pl.pallas_call(
+        functools.partial(grads_body, near, first),
+        out_shape=[jax.ShapeDtypeStruct(shape, F32) for shape in shapes],
+        grid=(4,),
+        in_specs=[pl.BlockSpec((pieces, n, sub, step), lambda i: (0, 0, 0, i))] * 2
+        + weight_specs(wk.shape[0], step),
+        out_specs=[pl.BlockSpec(shape, lambda i: (0, 0, 0, 0)) for shape in shapes],
+        scratch_shapes=[pltpu.VMEM((rows, count), F32)] * 2,
+        compiler_params=params(VMEM_ALL),
+        cost_estimate=cost(4 * rows * count * width, 2 * (count + 2 * rows) * width + 8 * rows * count),
+        name="grads",
+    )(d_core, d_own, wk, wv)
 
 
 def put_codes(far, codes):
@@ -387,54 +397,6 @@
         cost_estimate=cost(8 * got.size, 10 * got.size),
         name="far_codes",
     )(own, got)
-
-
-def own_grad_body(near, first, d_ref, wk, wv, far_got, near_out, *rest):
-    codes, acc = rest[:-1], rest[-1]
-    grad_step(first, d_ref, wk, wv, acc)
-
-    @pl.when(pl.program_id(0) == pl.num_programs(0) - 1)
-    def _():
-        full = acc[...].reshape(d_ref.shape[:3] + acc.shape[1:])
-        near_out[...] = full[:near]
-        put_codes(full[near:] + far_got[...], codes)
-
-
-def grads_of(d_kv, wk, wv, near, cols, got=None):
-    pieces, n, sub, width = d_kv.shape
-    far = pieces - near
-    first, count = cols
-    step = width // 4
-    tiles = count // LANES
-    near_shape, far_shape = (near, n, sub, count), (far, n, sub, count)
-
-    def whole(shape):
-        return pl.BlockSpec(shape, lambda i: (0,) * len(shape))
-
-    if got is None:
-        body, outs = core_grad_body, [(near_shape, F32), (far_shape, F32)]
-    else:
-        body = own_grad_body
-        outs = [(near_shape, F32)] + [((near, tiles * n + 1, sub, LANES), jnp.int16)] * (far // near)
-    out = pl.pallas_call(
-        functools.partial(body, near, first),
-        out_shape=[jax.ShapeDtypeStruct(*o) for o in outs],
-        grid=(4,),
-        in_specs=[pl.BlockSpec((pieces, n, sub, step), lambda i: (0, 0, 0, i))]
-        + weight_specs(wk.shape[0], step)
-        + ([] if got is None else [whole(far_shape)]),
-        out_specs=[whole(shape) for shape, _ in outs],
-        scratch_shapes=[pltpu.VMEM((pieces * n * sub, count), F32)],
-        compiler_params=params(),
-        cost_estimate=cost(2 * pieces * n * sub * count * width, 2 * (count + pieces * n * sub) * width),
-        name="core_grads" if got is None else "own_grads",
-    )(
-        d_kv,
-        wk,
-        wv,
-        *([] if got is None else [got]),
-    )
-    return out[0], out[1:]
 
 
 def send_body(n_dp, request, own, got, *rest):
@@ -567,14 +529,17 @@
         return (kind, c if d == 0 else n_chunks * d + c)
 
     kvs, places = [], []
-    packed = pack(me, asked, table, n_chunks, cap)
     early = {}
+    sent = pack(me, asked, table, 0, share, cap)
     for c in range(n_chunks):
-        sent = packed[c * n_dp : (c + 1) * n_dp]
         rest = [d for d in farthest_first if d not in early]
         arrived = [sent[0]] + [None] * (n_dp - 1)
         for d, x in {**early, **to_all(sent, -1, rest)}.items():
             arrived[d] = x
+        if c < n_chunks - 1:
+            sent = pack(me, asked, table, c + 1, share, cap)
+            early = to_all(sent, -1, farthest_first[:1])
+            early, arrived = lax.optimization_barrier((early, arrived))
         if kvs:
             arrived, kvs = lax.optimization_barrier((arrived, kvs))
         mine = compact(request, arrived, n_requests)
@@ -583,7 +548,7 @@
         near_at = [place(c, kind, 0) for kind in range(2)]
         far_at = [place(c, kind, d) for kind in range(2) for d in range(1, n_x)]
         if c < n_chunks - 1:
-            early = to_all(packed[(c + 1) * n_dp : (c + 2) * n_dp], -1, farthest_first[:3])
+            early = {**early, **to_all(sent, -1, farthest_first[1:4])}
             early, far = lax.optimization_barrier((early, far))
             far = far + [over_core(x) for x in far]
             kvs = kvs + [project(near + far, key_weight, value_weight)]
@@ -594,28 +559,33 @@
             kvs = kvs + [near]
         places += near_at + far_at
 
-    lead = 3 * LANES
-    parts = ((0, lead), (lead, enc - lead))
+    split = 3 * LANES
+    parts = ((0, split), (split, enc - split))
     attended, d_query, d_own, d_core, near, far, own = attend(
-        kvs, late, key_weight, value_weight, places, n_chunks, lead, queries, cotangent
+        kvs, late, key_weight, value_weight, places, n_chunks, split, queries, cotangent
     )
-    near_got, far_got = over_core(near), over_core(far)
-    near, (far,) = grads_of(d_core, key_weight, value_weight, n_chunks, parts[1])
-    far_got, near = lax.optimization_barrier((far_got, near))
-    sums = [(own, near_got, far_codes(own, far_got, n_chunks))]
-    near_got, far_got = over_core(near), over_core(far)
-    own, codes = grads_of(d_own, key_weight, value_weight, n_chunks, parts[1], far_got)
-    sums.append((own, near_got, codes))
-
-    d_table, before = None, None
-    for cols, (own, got, codes) in zip(parts, sums):
-        if before is not None:
-            codes, before = lax.optimization_barrier((codes, before))
-        codes = before = [over_x(code, n_x - d) for d, code in enumerate(codes, 1)]
-        sent = send_codes(request, own, got, codes, n_dp)
+    far_got = over_core(far)
+    near_got = over_core(near)
+    codes = far_codes(own, far_got, n_chunks)
+    near_b, far_b, own_b = grads_of(d_core, d_own, key_weight, value_weight, n_chunks, parts[1])
+
+    d_table = None
+    for part in range(2):
+        codes = [over_x(code, n_x - d) for d, code in enumerate(codes, 1)]
+        sent = send_codes(request, own, near_got, codes, n_dp)
+        if part == 0:
+            sent, near_b, far_b = lax.optimization_barrier((sent, near_b, far_b))
         came = to_all(sent, 1)
+        if part == 0:
+            far_got = over_core(far_b)
+            near_got = over_core(near_b)
+            own = own_b
+            lead = {d: came[d] for d in farthest_first[:2]}
+            far_got, lead = lax.optimization_barrier((far_got, lead))
+            came.update(lead)
+            codes = far_codes(own, far_got, n_chunks)
         arrived = [sent[0]] + [came[d] for d in range(1, n_dp)]
-        d_table = gather_grads(me, asked, arrived, n_slabs, n_chunks, enc, cols, d_table)
+        d_table = gather_grads(me, asked, arrived, n_slabs, n_chunks, enc, parts[part], d_table)
     return (attended, d_query, d_table)
 
 

time: 190 us -> 192 us (1.011)
  waiting for transfers between devices: 67.4 us -> 57.2 us
  starting transfers between devices: 48.9 us -> 57.4 us
  Pallas kernels: 60.2 us -> 62.7 us
    ppermute x28, waiting for transfers between devices: 43.7 us -> 36.6 us  [over_dp(): return lax.ppermute(x, 'dp', [(i, (i + d) % n_dp) for i in range(n_dp)])]
    ppermute x8, starting transfers between devices: 8.93 us -> 13.9 us  [over_core(): return lax.ppermute(x, 'tensor', [(t, t ^ 1) for t in range(n_tp)])]
    pallas_call x3, Pallas kernels: 14.6 us -> 19 us  [the longest x1 11.9 us: grads_of(): pl.pallas_call(functools.partial(grads_body, near, first), out_shape=[jax...]
    ppermute x28, starting transfers between devices: 37.8 us -> 40.5 us  [over_dp(): return lax.ppermute(x, 'dp', [(i, (i + d) % n_dp) for i in range(n_dp)])]
    pallas_call x1, Pallas kernels: 22.2 us -> 19.8 us  [attend(): pl.pallas_call(functools.partial(attend_body, places, len(kvs), len(late)...]
  transfers between devices with their start and end apart: 40 -> 40, of which waited for: 21 -> 17; matrix products, arithmetic and copies ran while one was open for 0% -> 0% of each run, Pallas kernels for 11% -> 16%
where the time goes in v7:
time: 192 us; the launch traced here: 191 us
  Pallas kernels  62.7 us (33%)
  starting transfers between devices  57.4 us (30%)
  waiting for transfers between devices  57.2 us (30%)
  blocking collectives  8.6 us (4%)
  local copies, waits for them, and re-layouts  3.53 us (2%)
    ppermute x28, starting transfers between devices, over_dp(): return lax.ppermute(x, 'dp', [(i, (i + d) % n_dp) for i in range(n_dp)])  40.5 us
    ppermute x28, waiting for transfers between devices, over_dp(): return lax.ppermute(x, 'dp', [(i, (i + d) % n_dp) for i in range(n_dp)])  36.6 us
    pallas_call x1, Pallas kernels, attend(): pl.pallas_call(functools.partial(attend_body, places, len(kvs), len(late)...  19.8 us
    ppermute x4, waiting for transfers between devices, over_x(): lax.ppermute(x, 'tensor', [(t, (t + 2 * d) % n_tp) for t in range(n_tp)])  16.1 us
    ppermute x8, starting transfers between devices, over_core(): return lax.ppermute(x, 'tensor', [(t, t ^ 1) for t in range(n_tp)])  13.9 us
    pallas_call x1, Pallas kernels, grads_of(): pl.pallas_call(functools.partial(grads_body, near, first), out_shape=[jax...  11.9 us
    pallas_call x2, Pallas kernels, project(): pl.pallas_call(functools.partial(project_body, n_in), out_shape=jax.Shape...  9.73 us
    psum x1, blocking collectives, on_device(): asked = lax.psum(wanted, 'dp')  8.6 us
  transfers between devices with their start and end apart: 40, of which 17 were waited for; matrix products, arithmetic and copies ran while one was open for 0% of the time, Pallas kernels for 16%

profile of v7, /device:TPU:13, one launch (start us, length us, event | category | flops | bytes accessed | tf_op | source)
XLA Modules:
  0.0 190.5 jit_solution(6358041272005760480)
XLA Ops:
  2.2 8.6 %psum.7.asked = s32[8,32]{1,0:T(8,128)} all-reduce(s32[8,32]{1,0:T(8,128)} %get-tuple-element.87), channel_id=1, replica_groups=mesh['dp'=8,'tensor'=4] {'dp'}, use_global_device_ids=true, to_apply=%region_0.0 | all-reduce | flops 256 | bytes 2048 | tf_op jit(solution)/shard_map/psum | solution.py:526
  10.8 3.5 %pack_rows.3 = (bf16[4,16,896]{2,1,0:T(8,128)(2,1)}, bf16[4,16,896]{2,1,0:T(8,128)(2,1)}, bf16[4,16,896]{2,1,0:T(8,128)(2,1)}, bf16[4,16,896]{2,1,0:T(8,128)(2,1...) custom-call(s32[1]{0:T(128)} %get-tuple-element.86.me, ...), custom_call_target="tpu_custom_call" | custom-call | bytes 1835008 | tf_op jit(solution)/shard_map/pack_rows/pallas_call | solution.py:97
  19.1 3.7 %pack_rows.2 = (bf16[4,16,896]{2,1,0:T(8,128)(2,1)}, bf16[4,16,896]{2,1,0:T(8,128)(2,1)}, bf16[4,16,896]{2,1,0:T(8,128)(2,1)}, bf16[4,16,896]{2,1,0:T(8,128)(2,1...) custom-call(s32[1]{0:T(128)} %get-tuple-element.86.me, ...), custom_call_target="tpu_custom_call" | custom-call | bytes 1835008 | tf_op jit(solution)/shard_map/pack_rows/pallas_call | solution.py:97
  26.1 5.8 %collective-permute-start.3 = (bf16[4,16,896]{2,1,0:T(8,128)(2,1)}, bf16[4,16,896]{2,1,0:T(8,128)(2,1)S(1)}, u32[]{:S(2)}, u32[]{:S(2)}) collective-permute-start(bf16[4,16,896]{2,1,0:T(8,128)(2,1)} %get-tuple-element.92), channel_id=1, source_target_pairs={{0,16},{4,20},{8,24},{12,28},{16,0},{20,4},{24,8},{28,12},{1,17},{... | collective-permute-start | bytes 344072 | tf_op jit(solution)/shard_map/ppermute | solution.py:517
  31.9 2.5 %collective-permute-done.8.refs_5_ = bf16[4,16,896]{2,1,0:T(8,128)(2,1)S(1)} collective-permute-done((bf16[4,16,896]{2,1,0:T(8,128)(2,1)}, bf16[4,16,896]{2,1,0:T(8,128)(2,1)S(1)}, u32[]{:S(2)}, u32[]{:S(2)}) %collective-permute-start.8) | collective-permute-done | bytes 114720 | tf_op jit(solution)/shard_map/ppermute | solution.py:517
  38.5 2.6 %collective-permute-done.3.refs_4_ = bf16[4,16,896]{2,1,0:T(8,128)(2,1)S(1)} collective-permute-done((bf16[4,16,896]{2,1,0:T(8,128)(2,1)}, bf16[4,16,896]{2,1,0:T(8,128)(2,1)S(1)}, u32[]{:S(2)}, u32[]{:S(2)}) %collective-permute-start.3) | collective-permute-done | bytes 114720 | tf_op jit(solution)/shard_map/ppermute | solution.py:517
  47.5 6.6 %collective-permute-start.15 = (bf16[16,16,896]{2,1,0:T(8,128)(2,1)S(1)}, bf16[16,16,896]{2,1,0:T(8,128)(2,1)S(1)}, u32[]{:S(2)}, u32[]{:S(2)}) collective-permute-start(bf16[16,16,896]{2,1,0:T(8,128)(2,1)S(1)} %compact_rows.2.refs_0_), channel_id=1, source_target_pairs={{0,1},{1,0},{2,3},{3,2},{4,5},{5,4},{6,7},{7,6},{8,9},{9,8},{10,11... | collective-permute-start | bytes 1376264 | tf_op jit(solution)/shard_map/ppermute | solution.py:511
  54.1 4.4 %collective-permute-start.16 = (bf16[16,16,896]{2,1,0:T(8,128)(2,1)S(1)}, bf16[16,16,896]{2,1,0:T(8,128)(2,1)S(1)}, u32[]{:S(2)}, u32[]{:S(2)}) collective-permute-start(bf16[16,16,896]{2,1,0:T(8,128)(2,1)S(1)} %collective-permute-done.12.refs_2_), channel_id=1, source_target_pairs={{0,1},{1,0},{2,3},{3,2},{4,5},{5,4},{6,7},{7,6},{8,9},{9,8},{10,11... | collective-permute-start | bytes 1376264 | tf_op jit(solution)/shard_map/ppermute | solution.py:511
  64.3 6.1 %project.2.refs_0_ = bf16[4,16,16,2048]{3,2,1,0:T(8,128)(2,1)S(1)} custom-call(bf16[16,16,896]{2,1,0:T(8,128)(2,1)S(1)} %compact_rows.2.refs_0_, bf16[16,16,896]{2,1,0:T(8,128)(2,1)S(1)} %collective-permute-done.15.refs_1_, bf16[16,16,896]{2,1,0:T(8,128)(2,1)S(1)} %collective-permute-done.12.refs_2_, ...), custom_call_target="tpu_custom_call" | custom-call | flops 3758096384 | bytes 9699328 | tf_op jit(solution)/shard_map/project/pallas_call | solution.py:174
  76.6 3.6 %project.3.refs_1_ = bf16[2,16,16,2048]{3,2,1,0:T(8,128)(2,1)S(1)} custom-call(bf16[16,16,896]{2,1,0:T(8,128)(2,1)S(1)} %compact_rows.3.refs_0_, bf16[16,16,896]{2,1,0:T(8,128)(2,1)S(1)} %collective-permute-done.17.refs_1_, bf16[896,1024]{1,0:T(8,128)(2,1)S(1)} %copy-done.5, bf16[896,1024]{1,0:T(8,128)(2,1)S(1)} %copy-done.7), custom_call_target="tpu_custom_call" | custom-call | flops 1879048192 | bytes 6684672 | tf_op jit(solution)/shard_map/project/pallas_call | solution.py:174
  80.2 7.1 %collective-permute-done.18.refs_2_ = bf16[16,16,896]{2,1,0:T(8,128)(2,1)S(1)} collective-permute-done((bf16[16,16,896]{2,1,0:T(8,128)(2,1)S(1)}, bf16[16,16,896]{2,1,0:T(8,128)(2,1)S(1)}, u32[]{:S(2)}, u32[]{:S(2)}) %collective-permute-start.18) | collective-permute-done | bytes 458784 | tf_op jit(solution)/shard_map/ppermute | solution.py:514
  89.6 19.8 %attend.1 = (bf16[512,1024]{1,0:T(8,128)(2,1)}, bf16[512,1024]{1,0:T(8,128)(2,1)}, bf16[4,16,16,2048]{3,2,1,0:T(8,128)(2,1)}, bf16[4,16,16,2048]{3,2,1,0:T(8,128...) custom-call(bf16[4,16,16,2048]{3,2,1,0:T(8,128)(2,1)} %copy-done.11, ...), custom_call_target="tpu_custom_call" | custom-call | flops 7247757312 | bytes 37748736 | tf_op jit(solution)/shard_map/attend/pallas_call | solution.py:286
  112.3 11.9 %grads.1 = (f32[2,16,16,512]{3,2,1,0:T(8,128)}, f32[2,16,16,512]{3,2,1,0:T(8,128)}, f32[4,16,16,512]{3,2,1,0:T(8,128)}) custom-call(bf16[4,16,16,2048]{3,2,1,0:T(8,128)(2,1)} %get-tuple-element.132.core_ref, bf16[4,16,16,2048]{3,2,1,0:T(8,128)(2,1)} %get-tuple-element.133.own_ref, bf16[896,1024]{1,0:T(8,128)(2,1)} %wk.1, bf16[896,1024]{1,0:T(8,128)(2,1)} %wv.1), custom_call_target="tpu_custom_call" | custom-call | flops 4294967296 | bytes 14680064 | tf_op jit(solution)/shard_map/grads/pallas_call | solution.py:350
  128.7 2.4 %collective-permute-done.25.refs_3_ = s16[25,16,128]{2,1,0:T(8,128)(2,1)S(1)} collective-permute-done((s16[25,16,128]{2,1,0:T(8,128)(2,1)S(1)}, s16[25,16,128]{2,1,0:T(8,128)(2,1)S(1)}, u32[]{:S(2)}, u32[]{:S(2)}) %collective-permute-start.25) | collective-permute-done | bytes 102432 | tf_op jit(solution)/shard_map/ppermute | solution.py:517
  131.0 4.8 %collective-permute-done.26.refs_4_ = s16[25,16,128]{2,1,0:T(8,128)(2,1)S(1)} collective-permute-done((s16[25,16,128]{2,1,0:T(8,128)(2,1)S(1)}, s16[25,16,128]{2,1,0:T(8,128)(2,1)S(1)}, u32[]{:S(2)}, u32[]{:S(2)}) %collective-permute-start.26) | collective-permute-done | bytes 102432 | tf_op jit(solution)/shard_map/ppermute | solution.py:517
  139.5 9.1 %collective-permute-done.27.rest_0_ = s16[2,65,16,128]{3,2,1,0:T(8,128)(2,1)S(1)} collective-permute-done((s16[2,65,16,128]{3,2,1,0:T(8,128)(2,1)S(1)}, s16[2,65,16,128]{3,2,1,0:T(8,128)(2,1)S(1)}, u32[]{:S(2)}, u32[]{:S(2)}) %collective-permute-start.27) | collective-permute-done | bytes 532512 | tf_op jit(solution)/shard_map/ppermute | solution.py:514
  154.4 3.3 %collective-permute-start.38 = (s16[25,16,128]{2,1,0:T(8,128)(2,1)S(1)}, s16[25,16,128]{2,1,0:T(8,128)(2,1)S(1)}, u32[]{:S(2)}, u32[]{:S(2)}) collective-permute-start(s16[25,16,128]{2,1,0:T(8,128)(2,1)S(1)} %get-tuple-element.167), channel_id=1, source_target_pairs={{0,24},{4,28},{8,0},{12,4},{16,8},{20,12},{24,16},{28,20},{1,25},{... | collective-permute-start | bytes 307208 | tf_op jit(solution)/shard_map/ppermute | solution.py:517
  160.2 3.6 %collective-permute-start.30 = (s16[33,16,128]{2,1,0:T(8,128)(2,1)S(1)}, s16[33,16,128]{2,1,0:T(8,128)(2,1)S(1)}, u32[]{:S(2)}, u32[]{:S(2)}) collective-permute-start(s16[33,16,128]{2,1,0:T(8,128)(2,1)S(1)} %get-tuple-element.156), channel_id=1, source_target_pairs={{0,12},{4,16},{8,20},{12,24},{16,28},{20,0},{24,4},{28,8},{1,13},{... | collective-permute-start | bytes 405512 | tf_op jit(solution)/shard_map/ppermute | solution.py:517
  163.8 2.8 %collective-permute-done.38.refs_6_ = s16[25,16,128]{2,1,0:T(8,128)(2,1)S(1)} collective-permute-done((s16[25,16,128]{2,1,0:T(8,128)(2,1)S(1)}, s16[25,16,128]{2,1,0:T(8,128)(2,1)S(1)}, u32[]{:S(2)}, u32[]{:S(2)}) %collective-permute-start.38) | collective-permute-done | bytes 102432 | tf_op jit(solution)/shard_map/ppermute | solution.py:517
  170.3 2.7 %gather_grads.2.refs_8_ = f32[16,32,896]{2,1,0:T(8,128)} custom-call(s32[1]{0:T(128)} %get-tuple-element.86.me, s32[8,32]{1,0:T(8,128)S(1)} %copy-done.3, s16[25,16,128]{2,1,0:T(8,128)(2,1)S(1)} %get-tuple-element.161.refs_0_, s16[25,16,128]{2,1,0:T(8,128)(2,1)S(1)} %collective-permute-done.35.refs_1_, ...), custom_call_target="tpu_custom_call" | custom-call | bytes 1572864 | tf_op jit(solution)/shard_map/gather_grads/pallas_call | solution.py:486
  173.0 6.0 %collective-permute-done.31.refs_4_ = s16[33,16,128]{2,1,0:T(8,128)(2,1)S(1)} collective-permute-done((s16[33,16,128]{2,1,0:T(8,128)(2,1)S(1)}, s16[33,16,128]{2,1,0:T(8,128)(2,1)S(1)}, u32[]{:S(2)}, u32[]{:S(2)}) %collective-permute-start.31) | collective-permute-done | bytes 135200 | tf_op jit(solution)/shard_map/ppermute | solution.py:517
  179.0 4.2 %collective-permute-done.33.refs_6_ = s16[33,16,128]{2,1,0:T(8,128)(2,1)S(1)} collective-permute-done((s16[33,16,128]{2,1,0:T(8,128)(2,1)S(1)}, s16[33,16,128]{2,1,0:T(8,128)(2,1)S(1)}, u32[]{:S(2)}, u32[]{:S(2)}) %collective-permute-start.33) | collective-permute-done | bytes 135200 | tf_op jit(solution)/shard_map/ppermute | solution.py:517
  183.1 4.4 %collective-permute-done.34.refs_7_ = s16[33,16,128]{2,1,0:T(8,128)(2,1)S(1)} collective-permute-done((s16[33,16,128]{2,1,0:T(8,128)(2,1)S(1)}, s16[33,16,128]{2,1,0:T(8,128)(2,1)S(1)}, u32[]{:S(2)}, u32[]{:S(2)}) %collective-permute-start.34) | collective-permute-done | bytes 135200 | tf_op jit(solution)/shard_map/ppermute | solution.py:517
  187.5 2.8 %gather_grads.3 = f32[16,32,896]{2,1,0:T(8,128)} custom-call(s32[1]{0:T(128)} %get-tuple-element.86.me, s32[8,32]{1,0:T(8,128)S(1)} %copy-done.3, s16[33,16,128]{2,1,0:T(8,128)(2,1)S(1)} %get-tuple-element.153.refs_0_, s16[33,16,128]{2,1,0:T(8,128)(2,1)S(1)} %collective-permute-done.28.refs_1_, ...), custom_call_target="tpu_custom_call", output_to_operand_aliasing={{}: (10, {})} | custom-call | bytes 2097152 | tf_op jit(solution)/shard_map/gather_grads/pallas_call | solution.py:486
  (100 shorter events, 57.3 us)
Async XLA Ops:
  17.5 14.3 %collective-permute-start.7 = (bf16[4,16,896]{2,1,0:T(8,128)(2,1)}, bf16[4,16,896]{2,1,0:T(8,128)(2,1)S(1)}, u32[]{:S(2)}, u32[]{:S(2)}) collective-permute-start(bf16[4,16,896]{2,1,0:T(8,128)(2,1)} %get-tuple-element.97), channel_id=1, source_target_pairs={{0,16},{4,20},{8,24},{12,28},{16,0},{20,4},{24,8},{28,12},{1,17},{... | collective-permute-start | bytes 344072 | tf_op jit(solution)/shard_map/ppermute | solution.py:517
  18.8 15.5 %collective-permute-start.8 = (bf16[4,16,896]{2,1,0:T(8,128)(2,1)}, bf16[4,16,896]{2,1,0:T(8,128)(2,1)S(1)}, u32[]{:S(2)}, u32[]{:S(2)}) collective-permute-start(bf16[4,16,896]{2,1,0:T(8,128)(2,1)} %get-tuple-element.98), channel_id=1, source_target_pairs={{0,12},{4,16},{8,20},{12,24},{16,28},{20,0},{24,4},{28,8},{1,13},{... | collective-permute-start | bytes 344072 | tf_op jit(solution)/shard_map/ppermute | solution.py:517
  22.8 13.9 %collective-permute-start.9 = (bf16[4,16,896]{2,1,0:T(8,128)(2,1)S(1)}, bf16[4,16,896]{2,1,0:T(8,128)(2,1)S(1)}, u32[]{:S(2)}, u32[]{:S(2)}) collective-permute-start(bf16[4,16,896]{2,1,0:T(8,128)(2,1)S(1)} %copy-done.13), channel_id=1, source_target_pairs={{0,8},{4,12},{8,16},{12,20},{16,24},{20,28},{24,0},{28,4},{1,9},{5... | collective-permute-start | bytes 344072 | tf_op jit(solution)/shard_map/ppermute | solution.py:517
  24.0 14.5 %collective-permute-start.10 = (bf16[4,16,896]{2,1,0:T(8,128)(2,1)S(1)}, bf16[4,16,896]{2,1,0:T(8,128)(2,1)S(1)}, u32[]{:S(2)}, u32[]{:S(2)}) collective-permute-start(bf16[4,16,896]{2,1,0:T(8,128)(2,1)S(1)} %copy-done.12), channel_id=1, source_target_pairs={{0,4},{4,8},{8,12},{12,16},{16,20},{20,24},{24,28},{28,0},{1,5},{5... | collective-permute-start | bytes 344072 | tf_op jit(solution)/shard_map/ppermute | solution.py:517
  26.1 15.0 %collective-permute-start.3 = (bf16[4,16,896]{2,1,0:T(8,128)(2,1)}, bf16[4,16,896]{2,1,0:T(8,128)(2,1)S(1)}, u32[]{:S(2)}, u32[]{:S(2)}) collective-permute-start(bf16[4,16,896]{2,1,0:T(8,128)(2,1)} %get-tuple-element.92), channel_id=1, source_target_pairs={{0,16},{4,20},{8,24},{12,28},{16,0},{20,4},{24,8},{28,12},{1,17},{... | collective-permute-start | bytes 344072 | tf_op jit(solution)/shard_map/ppermute | solution.py:517
  42.9 11.2 %collective-permute-start.12 = (bf16[16,16,896]{2,1,0:T(8,128)(2,1)S(1)}, bf16[16,16,896]{2,1,0:T(8,128)(2,1)S(1)}, u32[]{:S(2)}, u32[]{:S(2)}) collective-permute-start(bf16[16,16,896]{2,1,0:T(8,128)(2,1)S(1)} %compact_rows.2.refs_0_), channel_id=1, source_target_pairs={{0,2},{1,3},{2,0},{3,1},{4,6},{5,7},{6,4},{7,5},{8,10},{9,11},{10,... | collective-permute-start | bytes 1376264 | tf_op jit(solution)/shard_map/ppermute | solution.py:514
  47.5 15.3 %collective-permute-start.15 = (bf16[16,16,896]{2,1,0:T(8,128)(2,1)S(1)}, bf16[16,16,896]{2,1,0:T(8,128)(2,1)S(1)}, u32[]{:S(2)}, u32[]{:S(2)}) collective-permute-start(bf16[16,16,896]{2,1,0:T(8,128)(2,1)S(1)} %compact_rows.2.refs_0_), channel_id=1, source_target_pairs={{0,1},{1,0},{2,3},{3,2},{4,5},{5,4},{6,7},{7,6},{8,9},{9,8},{10,11... | collective-permute-start | bytes 1376264 | tf_op jit(solution)/shard_map/ppermute | solution.py:511
  58.6 13.8 %collective-permute-start = (bf16[4,16,896]{2,1,0:T(8,128)(2,1)}, bf16[4,16,896]{2,1,0:T(8,128)(2,1)S(1)}, u32[]{:S(2)}, u32[]{:S(2)}) collective-permute-start(bf16[4,16,896]{2,1,0:T(8,128)(2,1)} %get-tuple-element.89), channel_id=1, source_target_pairs={{0,28},{4,0},{8,4},{12,8},{16,12},{20,16},{24,20},{28,24},{1,29},{... | collective-permute-start | bytes 344072 | tf_op jit(solution)/shard_map/ppermute | solution.py:517
  58.6 13.8 %collective-permute-start.13 = (bf16[4,16,896]{2,1,0:T(8,128)(2,1)}, bf16[4,16,896]{2,1,0:T(8,128)(2,1)S(1)}, u32[]{:S(2)}, u32[]{:S(2)}) collective-permute-start(bf16[4,16,896]{2,1,0:T(8,128)(2,1)} %get-tuple-element.116), channel_id=1, source_target_pairs={{0,8},{4,12},{8,16},{12,20},{16,24},{20,28},{24,0},{28,4},{1,9},{5... | collective-permute-start | bytes 344072 | tf_op jit(solution)/shard_map/ppermute | solution.py:517
  60.8 11.7 %collective-permute-start.14 = (bf16[4,16,896]{2,1,0:T(8,128)(2,1)}, bf16[4,16,896]{2,1,0:T(8,128)(2,1)S(1)}, u32[]{:S(2)}, u32[]{:S(2)}) collective-permute-start(bf16[4,16,896]{2,1,0:T(8,128)(2,1)} %get-tuple-element.117), channel_id=1, source_target_pairs={{0,4},{4,8},{8,12},{12,16},{16,20},{20,24},{24,28},{28,0},{1,5},{5... | collective-permute-start | bytes 344072 | tf_op jit(solution)/shard_map/ppermute | solution.py:517
  75.1 12.1 %collective-permute-start.18 = (bf16[16,16,896]{2,1,0:T(8,128)(2,1)S(1)}, bf16[16,16,896]{2,1,0:T(8,128)(2,1)S(1)}, u32[]{:S(2)}, u32[]{:S(2)}) collective-permute-start(bf16[16,16,896]{2,1,0:T(8,128)(2,1)S(1)} %compact_rows.3.refs_0_), channel_id=1, source_target_pairs={{0,2},{1,3},{2,0},{3,1},{4,6},{5,7},{6,4},{7,5},{8,10},{9,11},{10,... | collective-permute-start | bytes 1376264 | tf_op jit(solution)/shard_map/ppermute | solution.py:514
  109.8 14.3 %collective-permute-start.20 = (f32[2,16,16,384]{3,2,1,0:T(8,128)S(1)}, f32[2,16,16,384]{3,2,1,0:T(8,128)S(1)}, u32[]{:S(2)}, u32[]{:S(2)}) collective-permute-start(f32[2,16,16,384]{3,2,1,0:T(8,128)S(1)} %get-tuple-element.136), channel_id=1, source_target_pairs={{0,1},{1,0},{2,3},{3,2},{4,5},{5,4},{6,7},{7,6},{8,9},{9,8},{10,11... | collective-permute-start | bytes 2359304 | tf_op jit(solution)/shard_map/ppermute | solution.py:511
  112.0 12.2 %collective-permute-start.22 = (s16[2,49,16,128]{3,2,1,0:T(8,128)(2,1)S(1)}, s16[2,49,16,128]{3,2,1,0:T(8,128)(2,1)S(1)}, u32[]{:S(2)}, u32[]{:S(2)}) collective-permute-start(s16[2,49,16,128]{3,2,1,0:T(8,128)(2,1)S(1)} %far_codes.2), channel_id=1, source_target_pairs={{0,2},{1,3},{2,0},{3,1},{4,6},{5,7},{6,4},{7,5},{8,10},{9,11},{10,... | collective-permute-start | bytes 1204232 | tf_op jit(solution)/shard_map/ppermute | solution.py:514
  126.0 13.4 %collective-permute-start.23 = (f32[2,16,16,512]{3,2,1,0:T(8,128)}, f32[2,16,16,512]{3,2,1,0:T(8,128)S(1)}, u32[]{:S(2)}, u32[]{:S(2)}) collective-permute-start(f32[2,16,16,512]{3,2,1,0:T(8,128)} %get-tuple-element.148), channel_id=1, source_target_pairs={{0,1},{1,0},{2,3},{3,2},{4,5},{5,4},{6,7},{7,6},{8,9},{9,8},{10,11... | collective-permute-start | bytes 3145736 | tf_op jit(solution)/shard_map/ppermute | solution.py:511
  136.2 12.4 %collective-permute-start.27 = (s16[2,65,16,128]{3,2,1,0:T(8,128)(2,1)S(1)}, s16[2,65,16,128]{3,2,1,0:T(8,128)(2,1)S(1)}, u32[]{:S(2)}, u32[]{:S(2)}) collective-permute-start(s16[2,65,16,128]{3,2,1,0:T(8,128)(2,1)S(1)} %far_codes.3), channel_id=1, source_target_pairs={{0,2},{1,3},{2,0},{3,1},{4,6},{5,7},{6,4},{7,5},{8,10},{9,11},{10,... | collective-permute-start | bytes 1597448 | tf_op jit(solution)/shard_map/ppermute | solution.py:514
  137.4 17.0 %collective-permute-start.35 = (s16[25,16,128]{2,1,0:T(8,128)(2,1)S(1)}, s16[25,16,128]{2,1,0:T(8,128)(2,1)S(1)}, u32[]{:S(2)}, u32[]{:S(2)}) collective-permute-start(s16[25,16,128]{2,1,0:T(8,128)(2,1)S(1)} %get-tuple-element.162), channel_id=1, source_target_pairs={{0,4},{4,8},{8,12},{12,16},{16,20},{20,24},{24,28},{28,0},{1,5},{5... | collective-permute-start | bytes 307208 | tf_op jit(solution)/shard_map/ppermute | solution.py:517
  138.0 19.7 %collective-permute-start.36 = (s16[25,16,128]{2,1,0:T(8,128)(2,1)S(1)}, s16[25,16,128]{2,1,0:T(8,128)(2,1)S(1)}, u32[]{:S(2)}, u32[]{:S(2)}) collective-permute-start(s16[25,16,128]{2,1,0:T(8,128)(2,1)S(1)} %get-tuple-element.163), channel_id=1, source_target_pairs={{0,8},{4,12},{8,16},{12,20},{16,24},{20,28},{24,0},{28,4},{1,9},{5... | collective-permute-start | bytes 307208 | tf_op jit(solution)/shard_map/ppermute | solution.py:517
  150.1 18.3 %collective-permute-start.28 = (s16[33,16,128]{2,1,0:T(8,128)(2,1)S(1)}, s16[33,16,128]{2,1,0:T(8,128)(2,1)S(1)}, u32[]{:S(2)}, u32[]{:S(2)}) collective-permute-start(s16[33,16,128]{2,1,0:T(8,128)(2,1)S(1)} %get-tuple-element.154), channel_id=1, source_target_pairs={{0,4},{4,8},{8,12},{12,16},{16,20},{20,24},{24,28},{28,0},{1,5},{5... | collective-permute-start | bytes 405512 | tf_op jit(solution)/shard_map/ppermute | solution.py:517
  151.4 17.5 %collective-permute-start.29 = (s16[33,16,128]{2,1,0:T(8,128)(2,1)S(1)}, s16[33,16,128]{2,1,0:T(8,128)(2,1)S(1)}, u32[]{:S(2)}, u32[]{:S(2)}) collective-permute-start(s16[33,16,128]{2,1,0:T(8,128)(2,1)S(1)} %get-tuple-element.155), channel_id=1, source_target_pairs={{0,8},{4,12},{8,16},{12,20},{16,24},{20,28},{24,0},{28,4},{1,9},{5... | collective-permute-start | bytes 405512 | tf_op jit(solution)/shard_map/ppermute | solution.py:517
  154.4 12.3 %collective-permute-start.38 = (s16[25,16,128]{2,1,0:T(8,128)(2,1)S(1)}, s16[25,16,128]{2,1,0:T(8,128)(2,1)S(1)}, u32[]{:S(2)}, u32[]{:S(2)}) collective-permute-start(s16[25,16,128]{2,1,0:T(8,128)(2,1)S(1)} %get-tuple-element.167), channel_id=1, source_target_pairs={{0,24},{4,28},{8,0},{12,4},{16,8},{20,12},{24,16},{28,20},{1,25},{... | collective-permute-start | bytes 307208 | tf_op jit(solution)/shard_map/ppermute | solution.py:517
  160.2 12.8 %collective-permute-start.30 = (s16[33,16,128]{2,1,0:T(8,128)(2,1)S(1)}, s16[33,16,128]{2,1,0:T(8,128)(2,1)S(1)}, u32[]{:S(2)}, u32[]{:S(2)}) collective-permute-start(s16[33,16,128]{2,1,0:T(8,128)(2,1)S(1)} %get-tuple-element.156), channel_id=1, source_target_pairs={{0,12},{4,16},{8,20},{12,24},{16,28},{20,0},{24,4},{28,8},{1,13},{... | collective-permute-start | bytes 405512 | tf_op jit(solution)/shard_map/ppermute | solution.py:517
  166.7 12.3 %collective-permute-start.31 = (s16[33,16,128]{2,1,0:T(8,128)(2,1)S(1)}, s16[33,16,128]{2,1,0:T(8,128)(2,1)S(1)}, u32[]{:S(2)}, u32[]{:S(2)}) collective-permute-start(s16[33,16,128]{2,1,0:T(8,128)(2,1)S(1)} %get-tuple-element.157), channel_id=1, source_target_pairs={{0,16},{4,20},{8,24},{12,28},{16,0},{20,4},{24,8},{28,12},{1,17},{... | collective-permute-start | bytes 405512 | tf_op jit(solution)/shard_map/ppermute | solution.py:517
  168.4 14.7 %collective-permute-start.33 = (s16[33,16,128]{2,1,0:T(8,128)(2,1)S(1)}, s16[33,16,128]{2,1,0:T(8,128)(2,1)S(1)}, u32[]{:S(2)}, u32[]{:S(2)}) collective-permute-start(s16[33,16,128]{2,1,0:T(8,128)(2,1)S(1)} %get-tuple-element.159), channel_id=1, source_target_pairs={{0,24},{4,28},{8,0},{12,4},{16,8},{20,12},{24,16},{28,20},{1,25},{... | collective-permute-start | bytes 405512 | tf_op jit(solution)/shard_map/ppermute | solution.py:517
  168.9 18.6 %collective-permute-start.34 = (s16[33,16,128]{2,1,0:T(8,128)(2,1)S(1)}, s16[33,16,128]{2,1,0:T(8,128)(2,1)S(1)}, u32[]{:S(2)}, u32[]{:S(2)}) collective-permute-start(s16[33,16,128]{2,1,0:T(8,128)(2,1)S(1)} %get-tuple-element.160), channel_id=1, source_target_pairs={{0,28},{4,0},{8,4},{12,8},{16,12},{20,16},{24,20},{28,24},{1,29},{... | collective-permute-start | bytes 405512 | tf_op jit(solution)/shard_map/ppermute | solution.py:517
  (30 other events, 361.8 us)

commit v8 on v7

--- a/solution.py
+++ b/solution.py
@@ -178,7 +178,7 @@
         in_specs=[pl.BlockSpec((n, sub, enc), lambda i: (0, 0, 0))] * n_in
         + weight_specs(enc, step),
         out_specs=pl.BlockSpec((n_in, n, sub, step), lambda i: (0, 0, 0, i)),
-        compiler_params=params(),
+        compiler_params=params(VMEM_ALL),
         cost_estimate=cost(
             2 * n_in * n * sub * enc * width, 2 * (n_in * n * sub * (enc + width) + enc * width)
         ),
@@ -529,7 +529,7 @@
         return (kind, c if d == 0 else n_chunks * d + c)
 
     kvs, places = [], []
-    early = {}
+    early, pieces = {}, []
     sent = pack(me, asked, table, 0, share, cap)
     for c in range(n_chunks):
         rest = [d for d in farthest_first if d not in early]
@@ -540,9 +540,10 @@
             sent = pack(me, asked, table, c + 1, share, cap)
             early = to_all(sent, -1, farthest_first[:1])
             early, arrived = lax.optimization_barrier((early, arrived))
-        if kvs:
-            arrived, kvs = lax.optimization_barrier((arrived, kvs))
         mine = compact(request, arrived, n_requests)
+        if pieces:
+            mine, pieces = lax.optimization_barrier((mine, pieces))
+            kvs = kvs + [project(pieces, key_weight, value_weight)]
         near = [mine, over_core(mine)]
         far = [over_x(mine, d) for d in range(1, n_x)]
         near_at = [place(c, kind, 0) for kind in range(2)]
@@ -551,12 +552,11 @@
             early = {**early, **to_all(sent, -1, farthest_first[1:4])}
             early, far = lax.optimization_barrier((early, far))
             far = far + [over_core(x) for x in far]
-            kvs = kvs + [project(near + far, key_weight, value_weight)]
+            pieces = near + far
         else:
-            near = project(near, key_weight, value_weight)
-            near, far = lax.optimization_barrier((near, far))
+            kvs = kvs + [project(near, key_weight, value_weight)]
+            kvs, far = lax.optimization_barrier((kvs, far))
             late = far + [over_core(x) for x in far]
-            kvs = kvs + [near]
         places += near_at + far_at
 
     split = 3 * LANES
@@ -569,23 +569,23 @@
     codes = far_codes(own, far_got, n_chunks)
     near_b, far_b, own_b = grads_of(d_core, d_own, key_weight, value_weight, n_chunks, parts[1])
 
-    d_table = None
-    for part in range(2):
-        codes = [over_x(code, n_x - d) for d, code in enumerate(codes, 1)]
-        sent = send_codes(request, own, near_got, codes, n_dp)
-        if part == 0:
-            sent, near_b, far_b = lax.optimization_barrier((sent, near_b, far_b))
-        came = to_all(sent, 1)
-        if part == 0:
-            far_got = over_core(far_b)
-            near_got = over_core(near_b)
-            own = own_b
-            lead = {d: came[d] for d in farthest_first[:2]}
-            far_got, lead = lax.optimization_barrier((far_got, lead))
-            came.update(lead)
-            codes = far_codes(own, far_got, n_chunks)
-        arrived = [sent[0]] + [came[d] for d in range(1, n_dp)]
-        d_table = gather_grads(me, asked, arrived, n_slabs, n_chunks, enc, parts[part], d_table)
+    codes = [over_x(code, n_x - d) for d, code in enumerate(codes, 1)]
+    sent = send_codes(request, own, near_got, codes, n_dp)
+    sent, near_b, far_b = lax.optimization_barrier((sent, near_b, far_b))
+    came = to_all(sent, 1)
+    far_got = over_core(far_b)
+    near_got = over_core(near_b)
+    codes = far_codes(own_b, far_got, n_chunks)
+    codes = [over_x(code, n_x - d) for d, code in enumerate(codes, 1)]
+    lead = {d: came[d] for d in farthest_first[:6]}
+    codes, lead = lax.optimization_barrier((codes, lead))
+    came.update(lead)
+    arrived = [sent[0]] + [came[d] for d in range(1, n_dp)]
+    d_table = gather_grads(me, asked, arrived, n_slabs, n_chunks, enc, parts[0], None)
+    sent = send_codes(request, own_b, near_got, codes, n_dp)
+    came = to_all(sent, 1)
+    arrived = [sent[0]] + [came[d] for d in range(1, n_dp)]
+    d_table = gather_grads(me, asked, arrived, n_slabs, n_chunks, enc, parts[1], d_table)
     return (attended, d_query, d_table)
 
 

time: 192 us -> 195 us (1.016)
  waiting for transfers between devices: 57.2 us -> 48.2 us
  Pallas kernels: 62.7 us -> 67.9 us
  local copies, waits for them, and re-layouts: 3.53 us -> 7.62 us
    ppermute x4, waiting for transfers between devices: 16.1 us -> 0.01 us  [over_x(): lax.ppermute(x, 'tensor', [(t, (t + 2 * d) % n_tp) for t in range(n_tp)])]
    ppermute x28, waiting for transfers between devices: 36.6 us -> 42.5 us  [over_dp(): return lax.ppermute(x, 'dp', [(i, (i + d) % n_dp) for i in range(n_dp)])]
    pallas_call x2, Pallas kernels: 9.73 us -> 15.1 us  [project(): pl.pallas_call(functools.partial(project_body, n_in), out_shape=jax.Shape...]
    unnamed x28 -> x36, local copies, waits for them, and re-layouts: 3.53 us -> 7.62 us
  transfers between devices with their start and end apart: 40 -> 40, of which waited for: 17 -> 15; matrix products, arithmetic and copies ran while one was open for 0% -> 0% of each run, Pallas kernels for 16% -> 19%
where the time goes in v8:
time: 195 us; the launch traced here: 192 us
  Pallas kernels  67.9 us (35%)
  starting transfers between devices  58.9 us (30%)
  waiting for transfers between devices  48.2 us (25%)
  blocking collectives  8.6 us (4%)
  local copies, waits for them, and re-layouts  7.62 us (4%)
    ppermute x28, waiting for transfers between devices, over_dp(): return lax.ppermute(x, 'dp', [(i, (i + d) % n_dp) for i in range(n_dp)])  42.5 us
    ppermute x28, starting transfers between devices, over_dp(): return lax.ppermute(x, 'dp', [(i, (i + d) % n_dp) for i in range(n_dp)])  42.3 us
    pallas_call x1, Pallas kernels, attend(): pl.pallas_call(functools.partial(attend_body, places, len(kvs), len(late)...  19.8 us
    pallas_call x2, Pallas kernels, project(): pl.pallas_call(functools.partial(project_body, n_in), out_shape=jax.Shape...  15.1 us
    ppermute x8, starting transfers between devices, over_core(): return lax.ppermute(x, 'tensor', [(t, t ^ 1) for t in range(n_tp)])  13.4 us
    pallas_call x1, Pallas kernels, grads_of(): pl.pallas_call(functools.partial(grads_body, near, first), out_shape=[jax...  11.9 us
    psum x1, blocking collectives, on_device(): asked = lax.psum(wanted, 'dp')  8.6 us
    unnamed x36, local copies, waits for them, and re-layouts  7.62 us
  transfers between devices with their start and end apart: 40, of which 15 were waited for; matrix products, arithmetic and copies ran while one was open for 0% of the time, Pallas kernels for 19%

profile of v8, /device:TPU:13, one launch (start us, length us, event | category | flops | bytes accessed | tf_op | source)
XLA Modules:
  0.0 192.3 jit_solution(2096601957881760837)
XLA Ops:
  2.2 8.6 %psum.7.asked = s32[8,32]{1,0:T(8,128)} all-reduce(s32[8,32]{1,0:T(8,128)} %get-tuple-element.89), channel_id=1, replica_groups=mesh['dp'=8,'tensor'=4] {'dp'}, use_global_device_ids=true, to_apply=%region_0.0 | all-reduce | flops 256 | bytes 2048 | tf_op jit(solution)/shard_map/psum | solution.py:526
  10.8 3.5 %pack_rows.3 = (bf16[4,16,896]{2,1,0:T(8,128)(2,1)}, bf16[4,16,896]{2,1,0:T(8,128)(2,1)}, bf16[4,16,896]{2,1,0:T(8,128)(2,1)}, bf16[4,16,896]{2,1,0:T(8,128)(2,1...) custom-call(s32[1]{0:T(128)} %get-tuple-element.88.me, ...), custom_call_target="tpu_custom_call" | custom-call | bytes 1835008 | tf_op jit(solution)/shard_map/pack_rows/pallas_call | solution.py:97
  19.2 3.6 %pack_rows.2 = (bf16[4,16,896]{2,1,0:T(8,128)(2,1)}, bf16[4,16,896]{2,1,0:T(8,128)(2,1)}, bf16[4,16,896]{2,1,0:T(8,128)(2,1)}, bf16[4,16,896]{2,1,0:T(8,128)(2,1...) custom-call(s32[1]{0:T(128)} %get-tuple-element.88.me, ...), custom_call_target="tpu_custom_call" | custom-call | bytes 1835008 | tf_op jit(solution)/shard_map/pack_rows/pallas_call | solution.py:97
  26.0 5.8 %collective-permute-start.3 = (bf16[4,16,896]{2,1,0:T(8,128)(2,1)}, bf16[4,16,896]{2,1,0:T(8,128)(2,1)S(1)}, u32[]{:S(2)}, u32[]{:S(2)}) collective-permute-start(bf16[4,16,896]{2,1,0:T(8,128)(2,1)} %get-tuple-element.94), channel_id=1, source_target_pairs={{0,16},{4,20},{8,24},{12,28},{16,0},{20,4},{24,8},{28,12},{1,17},{... | collective-permute-start | bytes 344072 | tf_op jit(solution)/shard_map/ppermute | solution.py:517
  31.8 2.6 %collective-permute-done.8.refs_5_ = bf16[4,16,896]{2,1,0:T(8,128)(2,1)S(1)} collective-permute-done((bf16[4,16,896]{2,1,0:T(8,128)(2,1)}, bf16[4,16,896]{2,1,0:T(8,128)(2,1)S(1)}, u32[]{:S(2)}, u32[]{:S(2)}) %collective-permute-start.8) | collective-permute-done | bytes 114720 | tf_op jit(solution)/shard_map/ppermute | solution.py:517
  34.4 2.3 %collective-permute-done.9.refs_6_ = bf16[4,16,896]{2,1,0:T(8,128)(2,1)S(1)} collective-permute-done((bf16[4,16,896]{2,1,0:T(8,128)(2,1)S(1)}, bf16[4,16,896]{2,1,0:T(8,128)(2,1)S(1)}, u32[]{:S(2)}, u32[]{:S(2)}) %collective-permute-start.9) | collective-permute-done | bytes 114720 | tf_op jit(solution)/shard_map/ppermute | solution.py:517
  38.5 2.6 %collective-permute-done.3.refs_4_ = bf16[4,16,896]{2,1,0:T(8,128)(2,1)S(1)} collective-permute-done((bf16[4,16,896]{2,1,0:T(8,128)(2,1)}, bf16[4,16,896]{2,1,0:T(8,128)(2,1)S(1)}, u32[]{:S(2)}, u32[]{:S(2)}) %collective-permute-start.3) | collective-permute-done | bytes 114720 | tf_op jit(solution)/shard_map/ppermute | solution.py:517
  47.5 6.5 %collective-permute-start.15 = (bf16[16,16,896]{2,1,0:T(8,128)(2,1)S(1)}, bf16[16,16,896]{2,1,0:T(8,128)(2,1)S(1)}, u32[]{:S(2)}, u32[]{:S(2)}) collective-permute-start(bf16[16,16,896]{2,1,0:T(8,128)(2,1)S(1)} %compact_rows.2.refs_0_), channel_id=1, source_target_pairs={{0,1},{1,0},{2,3},{3,2},{4,5},{5,4},{6,7},{7,6},{8,9},{9,8},{10,11... | collective-permute-start | bytes 1376264 | tf_op jit(solution)/shard_map/ppermute | solution.py:511
  54.1 4.5 %collective-permute-start.16 = (bf16[16,16,896]{2,1,0:T(8,128)(2,1)S(1)}, bf16[16,16,896]{2,1,0:T(8,128)(2,1)S(1)}, u32[]{:S(2)}, u32[]{:S(2)}) collective-permute-start(bf16[16,16,896]{2,1,0:T(8,128)(2,1)S(1)} %collective-permute-done.12.refs_2_), channel_id=1, source_target_pairs={{0,1},{1,0},{2,3},{3,2},{4,5},{5,4},{6,7},{7,6},{8,9},{9,8},{10,11... | collective-permute-start | bytes 1376264 | tf_op jit(solution)/shard_map/ppermute | solution.py:511
  64.4 2.8 %collective-permute-done.14.refs_7_ = bf16[4,16,896]{2,1,0:T(8,128)(2,1)S(1)} collective-permute-done((bf16[4,16,896]{2,1,0:T(8,128)(2,1)}, bf16[4,16,896]{2,1,0:T(8,128)(2,1)S(1)}, u32[]{:S(2)}, u32[]{:S(2)}) %collective-permute-start.14) | collective-permute-done | bytes 114720 | tf_op jit(solution)/shard_map/ppermute | solution.py:517
  71.1 8.8 %project.2.refs_0_ = bf16[4,16,16,2048]{3,2,1,0:T(8,128)(2,1)} custom-call(bf16[16,16,896]{2,1,0:T(8,128)(2,1)} %copy-done.1, bf16[16,16,896]{2,1,0:T(8,128)(2,1)} %copy-done.13, bf16[16,16,896]{2,1,0:T(8,128)(2,1)} %copy-done.12, bf16[16,16,896]{2,1,0:T(8,128)(2,1)} %copy-done.14, bf16[896,1024]{1,0:T(8,128)(2,1)} %wk.1, bf16[896,1024]{1,0:T(8,128)(2,1)} %wv.1), custom_call_target="tpu_custom_call" | custom-call | flops 3758096384 | bytes 9699328 | tf_op jit(solution)/shard_map/project/pallas_call | solution.py:174
  80.6 6.3 %project.3.refs_1_ = bf16[2,16,16,2048]{3,2,1,0:T(8,128)(2,1)} custom-call(bf16[16,16,896]{2,1,0:T(8,128)(2,1)} %copy-done.2, bf16[16,16,896]{2,1,0:T(8,128)(2,1)} %copy-done.15, bf16[896,1024]{1,0:T(8,128)(2,1)} %wk.1, bf16[896,1024]{1,0:T(8,128)(2,1)} %wv.1), custom_call_target="tpu_custom_call" | custom-call | flops 1879048192 | bytes 6684672 | tf_op jit(solution)/shard_map/project/pallas_call | solution.py:174
  94.7 19.8 %attend.1 = (bf16[512,1024]{1,0:T(8,128)(2,1)}, bf16[512,1024]{1,0:T(8,128)(2,1)}, bf16[4,16,16,2048]{3,2,1,0:T(8,128)(2,1)}, bf16[4,16,16,2048]{3,2,1,0:T(8,128...) custom-call(bf16[4,16,16,2048]{3,2,1,0:T(8,128)(2,1)} %project.2.refs_0_, ...), custom_call_target="tpu_custom_call" | custom-call | flops 7247757312 | bytes 37748736 | tf_op jit(solution)/shard_map/attend/pallas_call | solution.py:286
  118.1 11.9 %grads.1 = (f32[2,16,16,512]{3,2,1,0:T(8,128)}, f32[2,16,16,512]{3,2,1,0:T(8,128)}, f32[4,16,16,512]{3,2,1,0:T(8,128)}) custom-call(bf16[4,16,16,2048]{3,2,1,0:T(8,128)(2,1)} %get-tuple-element.130.core_ref, bf16[4,16,16,2048]{3,2,1,0:T(8,128)(2,1)} %get-tuple-element.131.own_ref, bf16[896,1024]{1,0:T(8,128)(2,1)} %wk.1, bf16[896,1024]{1,0:T(8,128)(2,1)} %wv.1), custom_call_target="tpu_custom_call" | custom-call | flops 4294967296 | bytes 14680064 | tf_op jit(solution)/shard_map/grads/pallas_call | solution.py:350
  132.2 2.4 %collective-permute-done.24.got = f32[2,16,16,512]{3,2,1,0:T(8,128)S(1)} collective-permute-done((f32[2,16,16,512]{3,2,1,0:T(8,128)}, f32[2,16,16,512]{3,2,1,0:T(8,128)S(1)}, u32[]{:S(2)}, u32[]{:S(2)}) %collective-permute-start.24) | collective-permute-done | bytes 1048608 | tf_op jit(solution)/shard_map/ppermute | solution.py:511
  143.2 2.5 %collective-permute-start.30 = (s16[25,16,128]{2,1,0:T(8,128)(2,1)S(1)}, s16[25,16,128]{2,1,0:T(8,128)(2,1)S(1)}, u32[]{:S(2)}, u32[]{:S(2)}) collective-permute-start(s16[25,16,128]{2,1,0:T(8,128)(2,1)S(1)} %get-tuple-element.152), channel_id=1, source_target_pairs={{0,20},{4,24},{8,28},{12,0},{16,4},{20,8},{24,12},{28,16},{1,21},{... | collective-permute-start | bytes 307208 | tf_op jit(solution)/shard_map/ppermute | solution.py:517
  145.7 3.8 %collective-permute-done.28.refs_3_ = s16[25,16,128]{2,1,0:T(8,128)(2,1)S(1)} collective-permute-done((s16[25,16,128]{2,1,0:T(8,128)(2,1)S(1)}, s16[25,16,128]{2,1,0:T(8,128)(2,1)S(1)}, u32[]{:S(2)}, u32[]{:S(2)}) %collective-permute-start.28) | collective-permute-done | bytes 102432 | tf_op jit(solution)/shard_map/ppermute | solution.py:517
  149.5 5.5 %collective-permute-done.29.refs_4_ = s16[25,16,128]{2,1,0:T(8,128)(2,1)S(1)} collective-permute-done((s16[25,16,128]{2,1,0:T(8,128)(2,1)S(1)}, s16[25,16,128]{2,1,0:T(8,128)(2,1)S(1)}, u32[]{:S(2)}, u32[]{:S(2)}) %collective-permute-start.29) | collective-permute-done | bytes 102432 | tf_op jit(solution)/shard_map/ppermute | solution.py:517
  154.9 5.3 %collective-permute-done.31.refs_6_ = s16[25,16,128]{2,1,0:T(8,128)(2,1)S(1)} collective-permute-done((s16[25,16,128]{2,1,0:T(8,128)(2,1)S(1)}, s16[25,16,128]{2,1,0:T(8,128)(2,1)S(1)}, u32[]{:S(2)}, u32[]{:S(2)}) %collective-permute-start.31) | collective-permute-done | bytes 102432 | tf_op jit(solution)/shard_map/ppermute | solution.py:517
  168.7 3.6 %collective-permute-start.38 = (s16[33,16,128]{2,1,0:T(8,128)(2,1)S(1)}, s16[33,16,128]{2,1,0:T(8,128)(2,1)S(1)}, u32[]{:S(2)}, u32[]{:S(2)}) collective-permute-start(s16[33,16,128]{2,1,0:T(8,128)(2,1)S(1)} %get-tuple-element.162), channel_id=1, source_target_pairs={{0,28},{4,0},{8,4},{12,8},{16,12},{20,16},{24,20},{28,24},{1,29},{... | collective-permute-start | bytes 405512 | tf_op jit(solution)/shard_map/ppermute | solution.py:517
  172.4 2.7 %gather_grads.2.refs_8_ = f32[16,32,896]{2,1,0:T(8,128)} custom-call(s32[1]{0:T(128)} %get-tuple-element.88.me, s32[8,32]{1,0:T(8,128)S(1)} %copy-done.5, s16[25,16,128]{2,1,0:T(8,128)(2,1)S(1)} %get-tuple-element.163.refs_0_, s16[25,16,128]{2,1,0:T(8,128)(2,1)S(1)} %collective-permute-done.26.refs_1_, ...), custom_call_target="tpu_custom_call" | custom-call | bytes 1572864 | tf_op jit(solution)/shard_map/gather_grads/pallas_call | solution.py:486
  175.1 6.1 %collective-permute-done.35.refs_4_ = s16[33,16,128]{2,1,0:T(8,128)(2,1)S(1)} collective-permute-done((s16[33,16,128]{2,1,0:T(8,128)(2,1)S(1)}, s16[33,16,128]{2,1,0:T(8,128)(2,1)S(1)}, u32[]{:S(2)}, u32[]{:S(2)}) %collective-permute-start.35) | collective-permute-done | bytes 135200 | tf_op jit(solution)/shard_map/ppermute | solution.py:517
  181.2 6.6 %collective-permute-done.37.refs_6_ = s16[33,16,128]{2,1,0:T(8,128)(2,1)S(1)} collective-permute-done((s16[33,16,128]{2,1,0:T(8,128)(2,1)S(1)}, s16[33,16,128]{2,1,0:T(8,128)(2,1)S(1)}, u32[]{:S(2)}, u32[]{:S(2)}) %collective-permute-start.37) | collective-permute-done | bytes 135200 | tf_op jit(solution)/shard_map/ppermute | solution.py:517
  189.2 2.8 %gather_grads.3 = f32[16,32,896]{2,1,0:T(8,128)} custom-call(s32[1]{0:T(128)} %get-tuple-element.88.me, s32[8,32]{1,0:T(8,128)S(1)} %copy-done.5, s16[33,16,128]{2,1,0:T(8,128)(2,1)S(1)} %get-tuple-element.155.refs_0_, s16[33,16,128]{2,1,0:T(8,128)(2,1)S(1)} %collective-permute-done.32.refs_1_, ...), custom_call_target="tpu_custom_call", output_to_operand_aliasing={{}: (10, {})} | custom-call | bytes 2097152 | tf_op jit(solution)/shard_map/gather_grads/pallas_call | solution.py:486
  (108 shorter events, 60.2 us)
Async XLA Ops:
  15.7 10.3 %collective-permute-start.6 = (bf16[4,16,896]{2,1,0:T(8,128)(2,1)}, bf16[4,16,896]{2,1,0:T(8,128)(2,1)S(1)}, u32[]{:S(2)}, u32[]{:S(2)}) collective-permute-start(bf16[4,16,896]{2,1,0:T(8,128)(2,1)} %get-tuple-element.98), channel_id=1, source_target_pairs={{0,20},{4,24},{8,28},{12,0},{16,4},{20,8},{24,12},{28,16},{1,21},{... | collective-permute-start | bytes 344072 | tf_op jit(solution)/shard_map/ppermute | solution.py:517
  17.6 14.2 %collective-permute-start.7 = (bf16[4,16,896]{2,1,0:T(8,128)(2,1)}, bf16[4,16,896]{2,1,0:T(8,128)(2,1)S(1)}, u32[]{:S(2)}, u32[]{:S(2)}) collective-permute-start(bf16[4,16,896]{2,1,0:T(8,128)(2,1)} %get-tuple-element.99), channel_id=1, source_target_pairs={{0,16},{4,20},{8,24},{12,28},{16,0},{20,4},{24,8},{28,12},{1,17},{... | collective-permute-start | bytes 344072 | tf_op jit(solution)/shard_map/ppermute | solution.py:517
  19.0 15.4 %collective-permute-start.8 = (bf16[4,16,896]{2,1,0:T(8,128)(2,1)}, bf16[4,16,896]{2,1,0:T(8,128)(2,1)S(1)}, u32[]{:S(2)}, u32[]{:S(2)}) collective-permute-start(bf16[4,16,896]{2,1,0:T(8,128)(2,1)} %get-tuple-element.100), channel_id=1, source_target_pairs={{0,12},{4,16},{8,20},{12,24},{16,28},{20,0},{24,4},{28,8},{1,13},{... | collective-permute-start | bytes 344072 | tf_op jit(solution)/shard_map/ppermute | solution.py:517
  22.8 13.9 %collective-permute-start.9 = (bf16[4,16,896]{2,1,0:T(8,128)(2,1)S(1)}, bf16[4,16,896]{2,1,0:T(8,128)(2,1)S(1)}, u32[]{:S(2)}, u32[]{:S(2)}) collective-permute-start(bf16[4,16,896]{2,1,0:T(8,128)(2,1)S(1)} %copy-done.17), channel_id=1, source_target_pairs={{0,8},{4,12},{8,16},{12,20},{16,24},{20,28},{24,0},{28,4},{1,9},{5... | collective-permute-start | bytes 344072 | tf_op jit(solution)/shard_map/ppermute | solution.py:517
  23.9 14.6 %collective-permute-start.10 = (bf16[4,16,896]{2,1,0:T(8,128)(2,1)S(1)}, bf16[4,16,896]{2,1,0:T(8,128)(2,1)S(1)}, u32[]{:S(2)}, u32[]{:S(2)}) collective-permute-start(bf16[4,16,896]{2,1,0:T(8,128)(2,1)S(1)} %copy-done.16), channel_id=1, source_target_pairs={{0,4},{4,8},{8,12},{12,16},{16,20},{20,24},{24,28},{28,0},{1,5},{5... | collective-permute-start | bytes 344072 | tf_op jit(solution)/shard_map/ppermute | solution.py:517
  26.0 15.1 %collective-permute-start.3 = (bf16[4,16,896]{2,1,0:T(8,128)(2,1)}, bf16[4,16,896]{2,1,0:T(8,128)(2,1)S(1)}, u32[]{:S(2)}, u32[]{:S(2)}) collective-permute-start(bf16[4,16,896]{2,1,0:T(8,128)(2,1)} %get-tuple-element.94), channel_id=1, source_target_pairs={{0,16},{4,20},{8,24},{12,28},{16,0},{20,4},{24,8},{28,12},{1,17},{... | collective-permute-start | bytes 344072 | tf_op jit(solution)/shard_map/ppermute | solution.py:517
  42.9 11.1 %collective-permute-start.12 = (bf16[16,16,896]{2,1,0:T(8,128)(2,1)S(1)}, bf16[16,16,896]{2,1,0:T(8,128)(2,1)S(1)}, u32[]{:S(2)}, u32[]{:S(2)}) collective-permute-start(bf16[16,16,896]{2,1,0:T(8,128)(2,1)S(1)} %compact_rows.2.refs_0_), channel_id=1, source_target_pairs={{0,2},{1,3},{2,0},{3,1},{4,6},{5,7},{6,4},{7,5},{8,10},{9,11},{10,... | collective-permute-start | bytes 1376264 | tf_op jit(solution)/shard_map/ppermute | solution.py:514
  44.2 9.8 %collective-permute-start.1 = (bf16[4,16,896]{2,1,0:T(8,128)(2,1)}, bf16[4,16,896]{2,1,0:T(8,128)(2,1)S(1)}, u32[]{:S(2)}, u32[]{:S(2)}) collective-permute-start(bf16[4,16,896]{2,1,0:T(8,128)(2,1)} %get-tuple-element.92), channel_id=1, source_target_pairs={{0,24},{4,28},{8,0},{12,4},{16,8},{20,12},{24,16},{28,20},{1,25},{... | collective-permute-start | bytes 344072 | tf_op jit(solution)/shard_map/ppermute | solution.py:517
  44.2 9.8 %collective-permute-start.2 = (bf16[4,16,896]{2,1,0:T(8,128)(2,1)}, bf16[4,16,896]{2,1,0:T(8,128)(2,1)S(1)}, u32[]{:S(2)}, u32[]{:S(2)}) collective-permute-start(bf16[4,16,896]{2,1,0:T(8,128)(2,1)} %get-tuple-element.93), channel_id=1, source_target_pairs={{0,20},{4,24},{8,28},{12,0},{16,4},{20,8},{24,12},{28,16},{1,21},{... | collective-permute-start | bytes 344072 | tf_op jit(solution)/shard_map/ppermute | solution.py:517
  47.5 22.6 %collective-permute-start.15 = (bf16[16,16,896]{2,1,0:T(8,128)(2,1)S(1)}, bf16[16,16,896]{2,1,0:T(8,128)(2,1)S(1)}, u32[]{:S(2)}, u32[]{:S(2)}) collective-permute-start(bf16[16,16,896]{2,1,0:T(8,128)(2,1)S(1)} %compact_rows.2.refs_0_), channel_id=1, source_target_pairs={{0,1},{1,0},{2,3},{3,2},{4,5},{5,4},{6,7},{7,6},{8,9},{9,8},{10,11... | collective-permute-start | bytes 1376264 | tf_op jit(solution)/shard_map/ppermute | solution.py:511
  54.1 16.0 %collective-permute-start.16 = (bf16[16,16,896]{2,1,0:T(8,128)(2,1)S(1)}, bf16[16,16,896]{2,1,0:T(8,128)(2,1)S(1)}, u32[]{:S(2)}, u32[]{:S(2)}) collective-permute-start(bf16[16,16,896]{2,1,0:T(8,128)(2,1)S(1)} %collective-permute-done.12.refs_2_), channel_id=1, source_target_pairs={{0,1},{1,0},{2,3},{3,2},{4,5},{5,4},{6,7},{7,6},{8,9},{9,8},{10,11... | collective-permute-start | bytes 1376264 | tf_op jit(solution)/shard_map/ppermute | solution.py:511
  70.7 16.2 %collective-permute-start.18 = (bf16[16,16,896]{2,1,0:T(8,128)(2,1)S(1)}, bf16[16,16,896]{2,1,0:T(8,128)(2,1)S(1)}, u32[]{:S(2)}, u32[]{:S(2)}) collective-permute-start(bf16[16,16,896]{2,1,0:T(8,128)(2,1)S(1)} %compact_rows.3.refs_0_), channel_id=1, source_target_pairs={{0,2},{1,3},{2,0},{3,1},{4,6},{5,7},{6,4},{7,5},{8,10},{9,11},{10,... | collective-permute-start | bytes 1376264 | tf_op jit(solution)/shard_map/ppermute | solution.py:514
  114.8 15.2 %collective-permute-start.20 = (f32[2,16,16,384]{3,2,1,0:T(8,128)S(1)}, f32[2,16,16,384]{3,2,1,0:T(8,128)S(1)}, u32[]{:S(2)}, u32[]{:S(2)}) collective-permute-start(f32[2,16,16,384]{3,2,1,0:T(8,128)S(1)} %get-tuple-element.134), channel_id=1, source_target_pairs={{0,1},{1,0},{2,3},{3,2},{4,5},{5,4},{6,7},{7,6},{8,9},{9,8},{10,11... | collective-permute-start | bytes 2359304 | tf_op jit(solution)/shard_map/ppermute | solution.py:511
  117.0 13.0 %collective-permute-start.22 = (s16[2,49,16,128]{3,2,1,0:T(8,128)(2,1)S(1)}, s16[2,49,16,128]{3,2,1,0:T(8,128)(2,1)S(1)}, u32[]{:S(2)}, u32[]{:S(2)}) collective-permute-start(s16[2,49,16,128]{3,2,1,0:T(8,128)(2,1)S(1)} %far_codes.2), channel_id=1, source_target_pairs={{0,2},{1,3},{2,0},{3,1},{4,6},{5,7},{6,4},{7,5},{8,10},{9,11},{10,... | collective-permute-start | bytes 1204232 | tf_op jit(solution)/shard_map/ppermute | solution.py:514
  132.1 28.1 %collective-permute-start.23 = (f32[2,16,16,512]{3,2,1,0:T(8,128)}, f32[2,16,16,512]{3,2,1,0:T(8,128)S(1)}, u32[]{:S(2)}, u32[]{:S(2)}) collective-permute-start(f32[2,16,16,512]{3,2,1,0:T(8,128)} %get-tuple-element.146), channel_id=1, source_target_pairs={{0,1},{1,0},{2,3},{3,2},{4,5},{5,4},{6,7},{7,6},{8,9},{9,8},{10,11... | collective-permute-start | bytes 3145736 | tf_op jit(solution)/shard_map/ppermute | solution.py:511
  135.0 25.3 %collective-permute-start.25 = (s16[2,65,16,128]{3,2,1,0:T(8,128)(2,1)S(1)}, s16[2,65,16,128]{3,2,1,0:T(8,128)(2,1)S(1)}, u32[]{:S(2)}, u32[]{:S(2)}) collective-permute-start(s16[2,65,16,128]{3,2,1,0:T(8,128)(2,1)S(1)} %far_codes.3), channel_id=1, source_target_pairs={{0,2},{1,3},{2,0},{3,1},{4,6},{5,7},{6,4},{7,5},{8,10},{9,11},{10,... | collective-permute-start | bytes 1597448 | tf_op jit(solution)/shard_map/ppermute | solution.py:514
  141.5 13.4 %collective-permute-start.29 = (s16[25,16,128]{2,1,0:T(8,128)(2,1)S(1)}, s16[25,16,128]{2,1,0:T(8,128)(2,1)S(1)}, u32[]{:S(2)}, u32[]{:S(2)}) collective-permute-start(s16[25,16,128]{2,1,0:T(8,128)(2,1)S(1)} %get-tuple-element.151), channel_id=1, source_target_pairs={{0,16},{4,20},{8,24},{12,28},{16,0},{20,4},{24,8},{28,12},{1,17},{... | collective-permute-start | bytes 307208 | tf_op jit(solution)/shard_map/ppermute | solution.py:517
  143.2 11.8 %collective-permute-start.30 = (s16[25,16,128]{2,1,0:T(8,128)(2,1)S(1)}, s16[25,16,128]{2,1,0:T(8,128)(2,1)S(1)}, u32[]{:S(2)}, u32[]{:S(2)}) collective-permute-start(s16[25,16,128]{2,1,0:T(8,128)(2,1)S(1)} %get-tuple-element.152), channel_id=1, source_target_pairs={{0,20},{4,24},{8,28},{12,0},{16,4},{20,8},{24,12},{28,16},{1,21},{... | collective-permute-start | bytes 307208 | tf_op jit(solution)/shard_map/ppermute | solution.py:517
  149.5 10.8 %collective-permute-start.31 = (s16[25,16,128]{2,1,0:T(8,128)(2,1)S(1)}, s16[25,16,128]{2,1,0:T(8,128)(2,1)S(1)}, u32[]{:S(2)}, u32[]{:S(2)}) collective-permute-start(s16[25,16,128]{2,1,0:T(8,128)(2,1)S(1)} %get-tuple-element.153), channel_id=1, source_target_pairs={{0,24},{4,28},{8,0},{12,4},{16,8},{20,12},{24,16},{28,20},{1,25},{... | collective-permute-start | bytes 307208 | tf_op jit(solution)/shard_map/ppermute | solution.py:517
  163.0 12.1 %collective-permute-start.34 = (s16[33,16,128]{2,1,0:T(8,128)(2,1)S(1)}, s16[33,16,128]{2,1,0:T(8,128)(2,1)S(1)}, u32[]{:S(2)}, u32[]{:S(2)}) collective-permute-start(s16[33,16,128]{2,1,0:T(8,128)(2,1)S(1)} %get-tuple-element.158), channel_id=1, source_target_pairs={{0,12},{4,16},{8,20},{12,24},{16,28},{20,0},{24,4},{28,8},{1,13},{... | collective-permute-start | bytes 405512 | tf_op jit(solution)/shard_map/ppermute | solution.py:517
  165.1 16.1 %collective-permute-start.35 = (s16[33,16,128]{2,1,0:T(8,128)(2,1)S(1)}, s16[33,16,128]{2,1,0:T(8,128)(2,1)S(1)}, u32[]{:S(2)}, u32[]{:S(2)}) collective-permute-start(s16[33,16,128]{2,1,0:T(8,128)(2,1)S(1)} %get-tuple-element.159), channel_id=1, source_target_pairs={{0,16},{4,20},{8,24},{12,28},{16,0},{20,4},{24,8},{28,12},{1,17},{... | collective-permute-start | bytes 405512 | tf_op jit(solution)/shard_map/ppermute | solution.py:517
  166.4 14.8 %collective-permute-start.36 = (s16[33,16,128]{2,1,0:T(8,128)(2,1)S(1)}, s16[33,16,128]{2,1,0:T(8,128)(2,1)S(1)}, u32[]{:S(2)}, u32[]{:S(2)}) collective-permute-start(s16[33,16,128]{2,1,0:T(8,128)(2,1)S(1)} %get-tuple-element.160), channel_id=1, source_target_pairs={{0,20},{4,24},{8,28},{12,0},{16,4},{20,8},{24,12},{28,16},{1,21},{... | collective-permute-start | bytes 405512 | tf_op jit(solution)/shard_map/ppermute | solution.py:517
  168.7 19.1 %collective-permute-start.37 = (s16[33,16,128]{2,1,0:T(8,128)(2,1)S(1)}, s16[33,16,128]{2,1,0:T(8,128)(2,1)S(1)}, u32[]{:S(2)}, u32[]{:S(2)}) collective-permute-start(s16[33,16,128]{2,1,0:T(8,128)(2,1)S(1)} %get-tuple-element.161), channel_id=1, source_target_pairs={{0,24},{4,28},{8,0},{12,4},{16,8},{20,12},{24,16},{28,20},{1,25},{... | collective-permute-start | bytes 405512 | tf_op jit(solution)/shard_map/ppermute | solution.py:517
  168.7 20.5 %collective-permute-start.38 = (s16[33,16,128]{2,1,0:T(8,128)(2,1)S(1)}, s16[33,16,128]{2,1,0:T(8,128)(2,1)S(1)}, u32[]{:S(2)}, u32[]{:S(2)}) collective-permute-start(s16[33,16,128]{2,1,0:T(8,128)(2,1)S(1)} %get-tuple-element.162), channel_id=1, source_target_pairs={{0,28},{4,0},{8,4},{12,8},{16,12},{20,16},{24,20},{28,24},{1,29},{... | collective-permute-start | bytes 405512 | tf_op jit(solution)/shard_map/ppermute | solution.py:517
  (34 other events, 287.8 us)

commit v9 on v8

--- a/solution.py
+++ b/solution.py
@@ -10,8 +10,8 @@
 
 HD = 128
 SPAN = 64
-SUB = 16
 LANES = 128
+WINDOW = 3
 VMEM_LIMIT = 28 * 1024 * 1024
 VMEM_MORE = 40 * 1024 * 1024
 VMEM_ALL = 60 * 1024 * 1024
@@ -72,10 +72,10 @@
     return asked[asker, d * (asked.shape[1] // n_dp) + j] - 1
 
 
-def pack_body(n_dp, chunk, share, me, asked, table, *rest):
+def pack_body(n_dp, me, asked, table, *rest):
     outs, sem = rest[:-1], rest[-1]
-    cap = outs[0].shape[0]
-    row = pl.multiple_of(lax.axis_index("tensor") * share + chunk * SUB, SUB)
+    cap, share, _ = outs[0].shape
+    row = pl.multiple_of(lax.axis_index("tensor") * share, share)
 
     def each(act):
         for d in range(n_dp):
@@ -84,30 +84,30 @@
 
                 @pl.when(slab >= 0)
                 def _():
-                    source = table.at[slab, pl.ds(row, SUB)]
+                    source = table.at[slab, pl.ds(row, share)]
                     act(pltpu.make_async_copy(source, outs[d].at[j], sem.at[d * cap + j]))
 
     each(lambda copy: copy.start())
     each(lambda copy: copy.wait())
 
 
-def pack(me, asked, table, chunk, share, cap):
+def pack(me, asked, table, share, cap):
     n_dp = asked.shape[0]
     enc = table.shape[2]
     return pl.pallas_call(
-        functools.partial(pack_body, n_dp, chunk, share),
-        out_shape=[jax.ShapeDtypeStruct((cap, SUB, enc), table.dtype)] * n_dp,
+        functools.partial(pack_body, n_dp),
+        out_shape=[jax.ShapeDtypeStruct((cap, share, enc), table.dtype)] * n_dp,
         in_specs=[SMEM, SMEM, ANY],
         out_specs=[VMEM] * n_dp,
         scratch_shapes=[pltpu.SemaphoreType.DMA((n_dp * cap,))],
         compiler_params=params(VMEM_ALL),
-        cost_estimate=cost(0, 4 * n_dp * cap * SUB * enc),
+        cost_estimate=cost(0, 4 * n_dp * cap * share * enc),
         name="pack_rows",
     )(me, asked, table)
 
 
-def compact_body(n_dp, request, *refs):
-    arrived, out, sem = refs[:n_dp], refs[n_dp], refs[n_dp + 1]
+def compact_body(n_dp, n_out, request, *refs):
+    arrived, outs, sem = refs[: n_dp * n_out], refs[n_dp * n_out : -1], refs[-1]
     cap = arrived[0].shape[0]
 
     def each(act):
@@ -117,24 +117,27 @@
 
                 @pl.when(r >= 0)
                 def _():
-                    act(pltpu.make_async_copy(arrived[d].at[j], out.at[r], sem.at[d * cap + j]))
+                    for i in range(n_out):
+                        source = arrived[i * n_dp + d].at[j]
+                        act(pltpu.make_async_copy(source, outs[i].at[r], sem.at[i, d * cap + j]))
 
     each(lambda copy: copy.start())
     each(lambda copy: copy.wait())
 
 
-def compact(request, arrived, n):
-    shape = (n,) + arrived[0].shape[1:]
-    return pl.pallas_call(
-        functools.partial(compact_body, len(arrived)),
-        out_shape=jax.ShapeDtypeStruct(shape, arrived[0].dtype),
-        in_specs=[SMEM] + [ANY] * len(arrived),
-        out_specs=VMEM,
-        scratch_shapes=[pltpu.SemaphoreType.DMA((request.shape[0],))],
+def compact(request, lists, n):
+    n_dp, n_out = len(lists[0]), len(lists)
+    shape = (n,) + lists[0][0].shape[1:]
+    return pl.pallas_call(
+        functools.partial(compact_body, n_dp, n_out),
+        out_shape=[jax.ShapeDtypeStruct(shape, lists[0][0].dtype)] * n_out,
+        in_specs=[SMEM] + [ANY] * (n_dp * n_out),
+        out_specs=[VMEM] * n_out,
+        scratch_shapes=[pltpu.SemaphoreType.DMA((n_out, request.shape[0]))],
         compiler_params=params(),
-        cost_estimate=cost(0, 4 * math.prod(shape)),
+        cost_estimate=cost(0, 4 * n_out * math.prod(shape)),
         name="compact_rows",
-    )(request, *arrived)
+    )(request, *[block for blocks in lists for block in blocks])
 
 
 def weight_specs(rows, step):
@@ -178,7 +181,7 @@
         in_specs=[pl.BlockSpec((n, sub, enc), lambda i: (0, 0, 0))] * n_in
         + weight_specs(enc, step),
         out_specs=pl.BlockSpec((n_in, n, sub, step), lambda i: (0, 0, 0, i)),
-        compiler_params=params(VMEM_ALL),
+        compiler_params=params(),
         cost_estimate=cost(
             2 * n_in * n * sub * enc * width, 2 * (n_in * n * sub * (enc + width) + enc * width)
         ),
@@ -193,6 +196,7 @@
     step = pl.program_id(0)
     width = q_ref.shape[1]
     enc = wk.shape[0]
+    sub = late_kv.shape[2]
     scale = 1.0 / math.sqrt(HD)
     heads = width // HD
     group = min(8, heads)
@@ -220,7 +224,7 @@
     def put(col, grad):
         cols = pl.ds(col, HD)
         for at, (kind, i) in enumerate(places):
-            block = grad[at * 2 * SUB : (at + 1) * 2 * SUB].reshape(2, SUB, HD)
+            block = grad[at * 2 * sub : (at + 1) * 2 * sub].reshape(2, sub, HD)
             grads[kind][i, :, :, cols] = block
             (own_all, core_all)[kind][i, mine, :, cols] = block
 
@@ -269,20 +273,20 @@
 def attend(kvs, late, wk, wv, places, near, count, queries, cotangent):
     tokens, width = queries.shape
     spans = tokens // SPAN
-    n = kvs[0].shape[1]
+    n, sub = kvs[0].shape[1:3]
     enc = wk.shape[0]
     pieces = len(places) // 2
     rows = pl.BlockSpec((SPAN, width), lambda i: (i, 0))
 
     def kv_block(pieces):
-        return pl.BlockSpec((pieces, 2, SUB, 2 * width), lambda i: (0, i, 0, 0))
+        return pl.BlockSpec((pieces, 2, sub, 2 * width), lambda i: (0, i, 0, 0))
 
     def whole(shape):
         return pl.BlockSpec(shape, lambda i: (0,) * len(shape))
 
-    keys = len(places) * 2 * SUB
-    parts = [(near, n, SUB, count), (pieces - near, n, SUB, count), (pieces, n, SUB, count)]
-    every = (pieces, n, SUB, 2 * width)
+    keys = len(places) * 2 * sub
+    parts = [(near, n, sub, count), (pieces - near, n, sub, count), (pieces, n, sub, count)]
+    every = (pieces, n, sub, 2 * width)
     return pl.pallas_call(
         functools.partial(attend_body, places, len(kvs), len(late), near),
         out_shape=[jax.ShapeDtypeStruct((tokens, width), BF16)] * 2
@@ -294,13 +298,13 @@
         + [whole(wk.shape), whole(wv.shape), rows, rows],
         out_specs=[rows, rows] + [kv_block(pieces)] * 2 + [whole(part) for part in parts],
         scratch_shapes=[
-            pltpu.VMEM((len(late), n, SUB, 2 * width), BF16),
+            pltpu.VMEM((len(late), n, sub, 2 * width), BF16),
             pltpu.VMEM(every, BF16),
             pltpu.VMEM(every, BF16),
         ],
         compiler_params=params(VMEM_MORE),
         cost_estimate=cost(
-            16 * tokens * width * keys + 4 * n * SUB * width * (len(late) * enc + 2 * pieces * count),
+            16 * tokens * width * keys + 4 * n * sub * width * (len(late) * enc + 2 * pieces * count),
             8 * tokens * width + 8 * spans * keys * 2 * width,
         ),
         name="attend",
@@ -365,13 +369,13 @@
     pieces, n, sub, count = far.shape
     near = codes[0].shape[0]
     tiles = count // LANES
-    row = lax.broadcasted_iota(jnp.int32, (SUB, LANES), 0)
+    row = lax.broadcasted_iota(jnp.int32, (sub, LANES), 0)
     for i in range(pieces):
         out, c = codes[i // near], i % near
         code, power = encode(far[i], (1, 2))
         for e in range(tiles):
             out[c, e * n : (e + 1) * n] = code[:, :, e * LANES : (e + 1) * LANES]
-        note = jnp.zeros((SUB, LANES), F32)
+        note = jnp.zeros((sub, LANES), F32)
         for r in range(n):
             note = jnp.where(row == r, power[r], note)
         out[c, tiles * n] = note.astype(jnp.int32).astype(jnp.int16)
@@ -415,10 +419,10 @@
             coded, power = encode(total, (0, 1))
             for e in range(tiles):
                 stage[r, c * tiles + e] = coded[:, e * LANES : (e + 1) * LANES]
-            powers[r, c] = jnp.broadcast_to(power, (SUB, LANES))
-    row = lax.broadcasted_iota(jnp.int32, (SUB, LANES), 0)
+            powers[r, c] = jnp.broadcast_to(power, (sub, LANES))
+    row = lax.broadcasted_iota(jnp.int32, (sub, LANES), 0)
     for d in range(n_dp):
-        note = jnp.zeros((SUB, LANES), F32)
+        note = jnp.zeros((sub, LANES), F32)
         for j in range(cap):
             r = request[d * cap + j]
 
@@ -436,7 +440,7 @@
     block = pl.BlockSpec(got.shape, lambda i: (0, 0, 0, 0))
     tiles = count // LANES
     cap = request.shape[0] // n_dp
-    shape = (cap * n_chunks * tiles + 1, SUB, LANES)
+    shape = (cap * n_chunks * tiles + 1, sub, LANES)
     return pl.pallas_call(
         functools.partial(send_body, n_dp),
         out_shape=[jax.ShapeDtypeStruct(shape, jnp.int16)] * n_dp,
@@ -444,8 +448,8 @@
         in_specs=[SMEM, block, block] + [VMEM] * len(codes),
         out_specs=[VMEM] * n_dp,
         scratch_shapes=[
-            pltpu.VMEM((n, n_chunks * tiles, SUB, LANES), jnp.int16),
-            pltpu.VMEM((n, n_chunks, SUB, LANES), F32),
+            pltpu.VMEM((n, n_chunks * tiles, sub, LANES), jnp.int16),
+            pltpu.VMEM((n, n_chunks, sub, LANES), F32),
         ],
         compiler_params=params(),
         cost_estimate=cost(10 * got.size, 6 * got.size + 2 * n_dp * math.prod(shape)),
@@ -456,7 +460,7 @@
 def gather_body(n_dp, n_chunks, first, me, asked, *refs):
     arrived = refs[:n_dp]
     out, total, sem = refs[-3:]
-    count = total.shape[2]
+    sub, count = total.shape[1] // n_chunks, total.shape[2]
     tiles = count // LANES
     cap = asked.shape[1] // n_dp
     total[...] = jnp.zeros_like(total)
@@ -472,19 +476,18 @@
                     unit = jnp.exp2(note[at : at + 1] - 15.0)
                     for e in range(tiles):
                         value = arrived[d][at * tiles + e].astype(F32) * unit
-                        total[slab, pl.ds(c * SUB, SUB), pl.ds(e * LANES, LANES)] += value
+                        total[slab, pl.ds(c * sub, sub), pl.ds(e * LANES, LANES)] += value
 
     copy = pltpu.make_async_copy(total, out.at[:, :, pl.ds(first, count)], sem)
     copy.start()
     copy.wait()
 
 
-def gather_grads(me, asked, arrived, n_slabs, n_chunks, enc, cols, before):
+def gather_grads(me, asked, arrived, n_slabs, rows, enc, cols, before):
     first, count = cols
     n_dp = asked.shape[0]
-    rows = n_chunks * SUB
-    return pl.pallas_call(
-        functools.partial(gather_body, n_dp, n_chunks, first),
+    return pl.pallas_call(
+        functools.partial(gather_body, n_dp, 1, first),
         out_shape=jax.ShapeDtypeStruct((n_slabs, rows, enc), F32),
         in_specs=[SMEM, SMEM] + [VMEM] * n_dp + [ANY] * (before is not None),
         out_specs=ANY,
@@ -505,7 +508,6 @@
     n_slabs, n_tokens, enc = table.shape
     cap = max(2, (4 * spans + n_dp - 1) // n_dp)
     share = n_tokens // n_tp
-    n_chunks = share // SUB
 
     def over_core(x):
         return lax.ppermute(x, "tensor", [(t, t ^ 1) for t in range(n_tp)])
@@ -525,49 +527,41 @@
     me, wanted, request = ask(owners, slots, n_dp, cap)
     asked = lax.psum(wanted, "dp")
 
-    def place(c, kind, d):
-        return (kind, c if d == 0 else n_chunks * d + c)
-
-    kvs, places = [], []
-    early, pieces = {}, []
-    sent = pack(me, asked, table, 0, share, cap)
-    for c in range(n_chunks):
-        rest = [d for d in farthest_first if d not in early]
-        arrived = [sent[0]] + [None] * (n_dp - 1)
-        for d, x in {**early, **to_all(sent, -1, rest)}.items():
-            arrived[d] = x
-        if c < n_chunks - 1:
-            sent = pack(me, asked, table, c + 1, share, cap)
-            early = to_all(sent, -1, farthest_first[:1])
-            early, arrived = lax.optimization_barrier((early, arrived))
-        mine = compact(request, arrived, n_requests)
-        if pieces:
-            mine, pieces = lax.optimization_barrier((mine, pieces))
-            kvs = kvs + [project(pieces, key_weight, value_weight)]
-        near = [mine, over_core(mine)]
-        far = [over_x(mine, d) for d in range(1, n_x)]
-        near_at = [place(c, kind, 0) for kind in range(2)]
-        far_at = [place(c, kind, d) for kind in range(2) for d in range(1, n_x)]
-        if c < n_chunks - 1:
-            early = {**early, **to_all(sent, -1, farthest_first[1:4])}
-            early, far = lax.optimization_barrier((early, far))
-            far = far + [over_core(x) for x in far]
-            pieces = near + far
-        else:
-            kvs = kvs + [project(near, key_weight, value_weight)]
-            kvs, far = lax.optimization_barrier((kvs, far))
-            late = far + [over_core(x) for x in far]
-        places += near_at + far_at
+    sent = pack(me, asked, table, share, cap)
+    mine = {0: sent[0]}
+    far = {0: [over_x(sent[0], k) for k in range(1, n_x)]}
+    for i, d in enumerate(farthest_first):
+        block = sent[d]
+        if i >= WINDOW:
+            held = farthest_first[i - WINDOW]
+            block, mine[held] = lax.optimization_barrier((block, mine[held]))
+            far[held] = [over_x(mine[held], k) for k in range(1, n_x)]
+            if i > WINDOW:
+                passed = farthest_first[i - WINDOW - 1]
+                block, far[passed] = lax.optimization_barrier((block, far[passed]))
+            else:
+                block, far[0] = lax.optimization_barrier((block, far[0]))
+        mine[d] = over_dp(block, -d)
+    for d in farthest_first[-WINDOW:]:
+        far[d] = [over_x(mine[d], k) for k in range(1, n_x)]
+    lists = [[mine[d] for d in range(n_dp)]]
+    lists += [[far[d][k] for d in range(n_dp)] for k in range(n_x - 1)]
+    mine, *far = compact(request, lists, n_requests)
+
+    early = [mine, *far]
+    late = [over_core(x) for x in early]
+    kvs = [project(early, key_weight, value_weight)]
+    places = [(kind, k) for kind in range(2) for k in range(n_x)]
 
     split = 3 * LANES
     parts = ((0, split), (split, enc - split))
     attended, d_query, d_own, d_core, near, far, own = attend(
-        kvs, late, key_weight, value_weight, places, n_chunks, split, queries, cotangent
+        kvs, late, key_weight, value_weight, places, 1, split, queries, cotangent
     )
     far_got = over_core(far)
     near_got = over_core(near)
-    codes = far_codes(own, far_got, n_chunks)
-    near_b, far_b, own_b = grads_of(d_core, d_own, key_weight, value_weight, n_chunks, parts[1])
+    codes = far_codes(own, far_got, 1)
+    near_b, far_b, own_b = grads_of(d_core, d_own, key_weight, value_weight, 1, parts[1])
 
     codes = [over_x(code, n_x - d) for d, code in enumerate(codes, 1)]
     sent = send_codes(request, own, near_got, codes, n_dp)
@@ -575,17 +569,17 @@
     came = to_all(sent, 1)
     far_got = over_core(far_b)
     near_got = over_core(near_b)
-    codes = far_codes(own_b, far_got, n_chunks)
+    codes = far_codes(own_b, far_got, 1)
     codes = [over_x(code, n_x - d) for d, code in enumerate(codes, 1)]
     lead = {d: came[d] for d in farthest_first[:6]}
     codes, lead = lax.optimization_barrier((codes, lead))
     came.update(lead)
     arrived = [sent[0]] + [came[d] for d in range(1, n_dp)]
-    d_table = gather_grads(me, asked, arrived, n_slabs, n_chunks, enc, parts[0], None)
+    d_table = gather_grads(me, asked, arrived, n_slabs, share, enc, parts[0], None)
     sent = send_codes(request, own_b, near_got, codes, n_dp)
     came = to_all(sent, 1)
     arrived = [sent[0]] + [came[d] for d in range(1, n_dp)]
-    d_table = gather_grads(me, asked, arrived, n_slabs, n_chunks, enc, parts[1], d_table)
+    d_table = gather_grads(me, asked, arrived, n_slabs, share, enc, parts[1], d_table)
     return (attended, d_query, d_table)
 
 

time: 195 us -> 195 us (level)
  waiting for transfers between devices: 48.2 us -> 65 us
  Pallas kernels: 67.9 us -> 58.7 us
  starting transfers between devices: 58.9 us -> 54.4 us
  local copies, waits for them, and re-layouts: 7.62 us -> 4.63 us
    ppermute x4 -> x10, waiting for transfers between devices: 0.01 us -> 15.1 us  [over_x(): lax.ppermute(x, 'tensor', [(t, (t + 2 * d) % n_tp) for t in range(n_tp)])]
    ppermute x8 -> x6, starting transfers between devices: 13.4 us -> 3.99 us  [over_core(): return lax.ppermute(x, 'tensor', [(t, t ^ 1) for t in range(n_tp)])]
    pallas_call x2 -> x1, Pallas kernels: 15.1 us -> 6.15 us  [project(): pl.pallas_call(functools.partial(project_body, n_in), out_shape=jax.Shape...]
    ppermute x4 -> x10, starting transfers between devices: 3.21 us -> 8.88 us  [over_x(): lax.ppermute(x, 'tensor', [(t, (t + 2 * d) % n_tp) for t in range(n_tp)])]
    ppermute x28 -> x21, waiting for transfers between devices: 42.5 us -> 45.7 us  [over_dp(): return lax.ppermute(x, 'dp', [(i, (i + d) % n_dp) for i in range(n_dp)])]
    unnamed x36 -> x22, local copies, waits for them, and re-layouts: 7.62 us -> 4.63 us
    pallas_call x6 -> x4, Pallas kernels: 16.3 us -> 14 us  [the longest x2 5.62 us: gather_grads(): pl.pallas_call(functools.partial(gather_body, n_dp, 1, first), out_shape=...]
    pallas_call x1, Pallas kernels: 19.8 us -> 22 us  [attend(): pl.pallas_call(functools.partial(attend_body, places, len(kvs), len(late)...]
  transfers between devices with their start and end apart: 40 -> 37, of which waited for: 15 -> 16; matrix products, arithmetic and copies ran while one was open for 0% -> 0% of each run, Pallas kernels for 19% -> 11%
where the time goes in v9:
time: 195 us; the launch traced here: 192 us
  waiting for transfers between devices  65 us (33%)
  Pallas kernels  58.7 us (30%)
  starting transfers between devices  54.4 us (28%)
  blocking collectives  8.59 us (4%)
  local copies, waits for them, and re-layouts  4.63 us (2%)
    ppermute x21, waiting for transfers between devices, over_dp(): return lax.ppermute(x, 'dp', [(i, (i + d) % n_dp) for i in range(n_dp)])  45.7 us
    ppermute x21, starting transfers between devices, over_dp(): return lax.ppermute(x, 'dp', [(i, (i + d) % n_dp) for i in range(n_dp)])  41.6 us
    pallas_call x1, Pallas kernels, attend(): pl.pallas_call(functools.partial(attend_body, places, len(kvs), len(late)...  22 us
    ppermute x10, waiting for transfers between devices, over_x(): lax.ppermute(x, 'tensor', [(t, (t + 2 * d) % n_tp) for t in range(n_tp)])  15.1 us
    pallas_call x1, Pallas kernels, grads_of(): pl.pallas_call(functools.partial(grads_body, near, first), out_shape=[jax...  11.8 us
    ppermute x10, starting transfers between devices, over_x(): lax.ppermute(x, 'tensor', [(t, (t + 2 * d) % n_tp) for t in range(n_tp)])  8.88 us
    psum x1, blocking collectives, on_device(): asked = lax.psum(wanted, 'dp')  8.59 us
    pallas_call x1, Pallas kernels, project(): pl.pallas_call(functools.partial(project_body, n_in), out_shape=jax.Shape...  6.15 us
  transfers between devices with their start and end apart: 37, of which 16 were waited for; matrix products, arithmetic and copies ran while one was open for 0% of the time, Pallas kernels for 11%

profile of v9, /device:TPU:13, one launch (start us, length us, event | category | flops | bytes accessed | tf_op | source)
XLA Modules:
  0.0 192.4 jit_solution(5778825811702645269)
XLA Ops:
  2.2 8.6 %psum.7.asked = s32[8,32]{1,0:T(8,128)} all-reduce(s32[8,32]{1,0:T(8,128)} %get-tuple-element.77), channel_id=1, replica_groups=mesh['dp'=8,'tensor'=4] {'dp'}, use_global_device_ids=true, to_apply=%region_0.0 | all-reduce | flops 256 | bytes 2048 | tf_op jit(solution)/shard_map/psum | solution.py:528
  10.8 4.2 %pack_rows.1 = (bf16[4,32,896]{2,1,0:T(8,128)(2,1)}, bf16[4,32,896]{2,1,0:T(8,128)(2,1)}, bf16[4,32,896]{2,1,0:T(8,128)(2,1)}, bf16[4,32,896]{2,1,0:T(8,128)(2,1...) custom-call(s32[1]{0:T(128)} %get-tuple-element.76.me, ...), custom_call_target="tpu_custom_call" | custom-call | bytes 3670016 | tf_op jit(solution)/shard_map/pack_rows/pallas_call | solution.py:97
  23.2 13.1 %collective-permute-done.4.refs_4_ = bf16[4,32,896]{2,1,0:T(8,128)(2,1)S(1)} collective-permute-done((bf16[4,32,896]{2,1,0:T(8,128)(2,1)}, bf16[4,32,896]{2,1,0:T(8,128)(2,1)S(1)}, u32[]{:S(2)}, u32[]{:S(2)}) %collective-permute-start.4) | collective-permute-done | bytes 229408 | tf_op jit(solution)/shard_map/ppermute | solution.py:519
  37.5 4.4 %collective-permute-start.6 = (bf16[4,32,896]{2,1,0:T(8,128)(2,1)}, bf16[4,32,896]{2,1,0:T(8,128)(2,1)S(1)}, u32[]{:S(2)}, u32[]{:S(2)}) collective-permute-start(bf16[4,32,896]{2,1,0:T(8,128)(2,1)} %get-tuple-element.90), channel_id=1, source_target_pairs={{0,24},{4,28},{8,0},{12,4},{16,8},{20,12},{24,16},{28,20},{1,25},{... | collective-permute-start | bytes 688136 | tf_op jit(solution)/shard_map/ppermute | solution.py:519
  42.9 4.3 %collective-permute-start.3 = (bf16[4,32,896]{2,1,0:T(8,128)(2,1)}, bf16[4,32,896]{2,1,0:T(8,128)(2,1)S(1)}, u32[]{:S(2)}, u32[]{:S(2)}) collective-permute-start(bf16[4,32,896]{2,1,0:T(8,128)(2,1)} %get-tuple-element.85), channel_id=1, source_target_pairs={{0,28},{4,0},{8,4},{12,8},{16,12},{20,16},{24,20},{28,24},{1,29},{... | collective-permute-start | bytes 688136 | tf_op jit(solution)/shard_map/ppermute | solution.py:519
  47.7 7.6 %collective-permute-start.10 = (bf16[4,32,896]{2,1,0:T(8,128)(2,1)}, bf16[4,32,896]{2,1,0:T(8,128)(2,1)S(1)}, u32[]{:S(2)}, u32[]{:S(2)}) collective-permute-start(bf16[4,32,896]{2,1,0:T(8,128)(2,1)} %get-tuple-element.97), channel_id=1, source_target_pairs={{0,4},{4,8},{8,12},{12,16},{16,20},{20,24},{24,28},{28,0},{1,5},{5... | collective-permute-start | bytes 688136 | tf_op jit(solution)/shard_map/ppermute | solution.py:519
  57.4 2.8 %collective-permute-done.10.refs_7_ = bf16[4,32,896]{2,1,0:T(8,128)(2,1)S(1)} collective-permute-done((bf16[4,32,896]{2,1,0:T(8,128)(2,1)}, bf16[4,32,896]{2,1,0:T(8,128)(2,1)S(1)}, u32[]{:S(2)}, u32[]{:S(2)}) %collective-permute-start.10) | collective-permute-done | bytes 229408 | tf_op jit(solution)/shard_map/ppermute | solution.py:519
  60.8 4.8 %collective-permute-done.11.refs_9_ = bf16[4,32,896]{2,1,0:T(8,128)(2,1)S(1)} collective-permute-done((bf16[4,32,896]{2,1,0:T(8,128)(2,1)S(1)}, bf16[4,32,896]{2,1,0:T(8,128)(2,1)S(1)}, u32[]{:S(2)}, u32[]{:S(2)}) %collective-permute-start.11) | collective-permute-done | bytes 229408 | tf_op jit(solution)/shard_map/ppermute | solution.py:516
  65.6 4.9 %collective-permute-done.13.refs_14_ = bf16[4,32,896]{2,1,0:T(8,128)(2,1)S(1)} collective-permute-done((bf16[4,32,896]{2,1,0:T(8,128)(2,1)S(1)}, bf16[4,32,896]{2,1,0:T(8,128)(2,1)S(1)}, u32[]{:S(2)}, u32[]{:S(2)}) %collective-permute-start.13) | collective-permute-done | bytes 229408 | tf_op jit(solution)/shard_map/ppermute | solution.py:516
  70.5 4.9 %collective-permute-done.14.refs_15_ = bf16[4,32,896]{2,1,0:T(8,128)(2,1)S(1)} collective-permute-done((bf16[4,32,896]{2,1,0:T(8,128)(2,1)S(1)}, bf16[4,32,896]{2,1,0:T(8,128)(2,1)S(1)}, u32[]{:S(2)}, u32[]{:S(2)}) %collective-permute-start.14) | collective-permute-done | bytes 229408 | tf_op jit(solution)/shard_map/ppermute | solution.py:516
  76.4 4.2 %compact_rows.1 = (bf16[16,32,896]{2,1,0:T(8,128)(2,1)S(1)}, bf16[16,32,896]{2,1,0:T(8,128)(2,1)S(1)}) custom-call(s32[32]{0:T(128)S(1)} %copy-done.3, bf16[4,32,896]{2,1,0:T(8,128)(2,1)S(1)} %copy-done.1, bf16[4,32,896]{2,1,0:T(8,128)(2,1)S(1)} %collective-permute-done.3.refs_1_, bf16[4,32,896]{2,1,0:T(8,128)(2,1)S(1)} %collective-permute-done.6.refs_2_, ...), custom_call_target="tpu_custom_call" | custom-call | bytes 3670016 | tf_op jit(solution)/shard_map/compact_rows/pallas_call | solution.py:131
  84.9 6.2 %project.1.refs_0_ = bf16[2,16,32,2048]{3,2,1,0:T(8,128)(2,1)S(1)} custom-call(bf16[16,32,896]{2,1,0:T(8,128)(2,1)S(1)} %get-tuple-element.102.refs_0_, bf16[16,32,896]{2,1,0:T(8,128)(2,1)S(1)} %get-tuple-element.103.refs_1_, bf16[896,1024]{1,0:T(8,128)(2,1)S(1)} %copy-done.4, bf16[896,1024]{1,0:T(8,128)(2,1)S(1)} %copy-done.6), custom_call_target="tpu_custom_call" | custom-call | flops 3758096384 | bytes 9699328 | tf_op jit(solution)/shard_map/project/pallas_call | solution.py:177
  93.1 22.0 %attend.1 = (bf16[512,1024]{1,0:T(8,128)(2,1)}, bf16[512,1024]{1,0:T(8,128)(2,1)}, bf16[2,16,32,2048]{3,2,1,0:T(8,128)(2,1)}, bf16[2,16,32,2048]{3,2,1,0:T(8,128...) custom-call(bf16[2,16,32,2048]{3,2,1,0:T(8,128)(2,1)} %copy-done.10, ...), custom_call_target="tpu_custom_call" | custom-call | flops 9126805504 | bytes 37748736 | tf_op jit(solution)/shard_map/attend/pallas_call | solution.py:290
  118.5 11.8 %grads.1 = (f32[1,16,32,512]{3,2,1,0:T(8,128)}, f32[1,16,32,512]{3,2,1,0:T(8,128)}, f32[2,16,32,512]{3,2,1,0:T(8,128)}) custom-call(bf16[2,16,32,2048]{3,2,1,0:T(8,128)(2,1)} %get-tuple-element.106.core_ref, bf16[2,16,32,2048]{3,2,1,0:T(8,128)(2,1)} %get-tuple-element.107.own_ref, bf16[896,1024]{1,0:T(8,128)(2,1)} %wk.1, bf16[896,1024]{1,0:T(8,128)(2,1)} %wv.1), custom_call_target="tpu_custom_call" | custom-call | flops 4294967296 | bytes 14680064 | tf_op jit(solution)/shard_map/grads/pallas_call | solution.py:354
  136.4 4.8 %collective-permute-start.25 = (s16[13,32,128]{2,1,0:T(8,128)(2,1)S(1)}, s16[13,32,128]{2,1,0:T(8,128)(2,1)S(1)}, u32[]{:S(2)}, u32[]{:S(2)}) collective-permute-start(s16[13,32,128]{2,1,0:T(8,128)(2,1)S(1)} %get-tuple-element.126), channel_id=1, source_target_pairs={{0,12},{4,16},{8,20},{12,24},{16,28},{20,0},{24,4},{28,8},{1,13},{... | collective-permute-start | bytes 319496 | tf_op jit(solution)/shard_map/ppermute | solution.py:519
  141.2 2.7 %collective-permute-start.26 = (s16[13,32,128]{2,1,0:T(8,128)(2,1)S(1)}, s16[13,32,128]{2,1,0:T(8,128)(2,1)S(1)}, u32[]{:S(2)}, u32[]{:S(2)}) collective-permute-start(s16[13,32,128]{2,1,0:T(8,128)(2,1)S(1)} %get-tuple-element.127), channel_id=1, source_target_pairs={{0,16},{4,20},{8,24},{12,28},{16,0},{20,4},{24,8},{28,12},{1,17},{... | collective-permute-start | bytes 319496 | tf_op jit(solution)/shard_map/ppermute | solution.py:519
  147.0 6.2 %collective-permute-done.26.refs_4_ = s16[13,32,128]{2,1,0:T(8,128)(2,1)S(1)} collective-permute-done((s16[13,32,128]{2,1,0:T(8,128)(2,1)S(1)}, s16[13,32,128]{2,1,0:T(8,128)(2,1)S(1)}, u32[]{:S(2)}, u32[]{:S(2)}) %collective-permute-start.26) | collective-permute-done | bytes 106528 | tf_op jit(solution)/shard_map/ppermute | solution.py:519
  153.2 7.3 %collective-permute-done.28.refs_6_ = s16[13,32,128]{2,1,0:T(8,128)(2,1)S(1)} collective-permute-done((s16[13,32,128]{2,1,0:T(8,128)(2,1)S(1)}, s16[13,32,128]{2,1,0:T(8,128)(2,1)S(1)}, u32[]{:S(2)}, u32[]{:S(2)}) %collective-permute-start.28) | collective-permute-done | bytes 106528 | tf_op jit(solution)/shard_map/ppermute | solution.py:519
  167.0 3.4 %collective-permute-start.33 = (s16[17,32,128]{2,1,0:T(8,128)(2,1)S(1)}, s16[17,32,128]{2,1,0:T(8,128)(2,1)S(1)}, u32[]{:S(2)}, u32[]{:S(2)}) collective-permute-start(s16[17,32,128]{2,1,0:T(8,128)(2,1)S(1)} %get-tuple-element.136), channel_id=1, source_target_pairs={{0,20},{4,24},{8,28},{12,0},{16,4},{20,8},{24,12},{28,16},{1,21},{... | collective-permute-start | bytes 417800 | tf_op jit(solution)/shard_map/ppermute | solution.py:519
  172.8 2.7 %gather_grads.2.refs_8_ = f32[16,32,896]{2,1,0:T(8,128)} custom-call(s32[1]{0:T(128)} %get-tuple-element.76.me, s32[8,32]{1,0:T(8,128)S(1)} %copy-done.2, s16[13,32,128]{2,1,0:T(8,128)(2,1)S(1)} %get-tuple-element.139.refs_0_, s16[13,32,128]{2,1,0:T(8,128)(2,1)S(1)} %collective-permute-done.23.refs_1_, ...), custom_call_target="tpu_custom_call" | custom-call | bytes 1572864 | tf_op jit(solution)/shard_map/gather_grads/pallas_call | solution.py:489
  175.5 4.8 %collective-permute-done.31.refs_3_ = s16[17,32,128]{2,1,0:T(8,128)(2,1)S(1)} collective-permute-done((s16[17,32,128]{2,1,0:T(8,128)(2,1)S(1)}, s16[17,32,128]{2,1,0:T(8,128)(2,1)S(1)}, u32[]{:S(2)}, u32[]{:S(2)}) %collective-permute-start.31) | collective-permute-done | bytes 139296 | tf_op jit(solution)/shard_map/ppermute | solution.py:519
  180.3 4.3 %collective-permute-done.32.refs_4_ = s16[17,32,128]{2,1,0:T(8,128)(2,1)S(1)} collective-permute-done((s16[17,32,128]{2,1,0:T(8,128)(2,1)S(1)}, s16[17,32,128]{2,1,0:T(8,128)(2,1)S(1)}, u32[]{:S(2)}, u32[]{:S(2)}) %collective-permute-start.32) | collective-permute-done | bytes 139296 | tf_op jit(solution)/shard_map/ppermute | solution.py:519
  184.6 3.5 %collective-permute-done.34.refs_6_ = s16[17,32,128]{2,1,0:T(8,128)(2,1)S(1)} collective-permute-done((s16[17,32,128]{2,1,0:T(8,128)(2,1)S(1)}, s16[17,32,128]{2,1,0:T(8,128)(2,1)S(1)}, u32[]{:S(2)}, u32[]{:S(2)}) %collective-permute-start.34) | collective-permute-done | bytes 139296 | tf_op jit(solution)/shard_map/ppermute | solution.py:519
  189.3 2.9 %gather_grads.3 = f32[16,32,896]{2,1,0:T(8,128)} custom-call(s32[1]{0:T(128)} %get-tuple-element.76.me, s32[8,32]{1,0:T(8,128)S(1)} %copy-done.2, s16[17,32,128]{2,1,0:T(8,128)(2,1)S(1)} %get-tuple-element.131.refs_0_, s16[17,32,128]{2,1,0:T(8,128)(2,1)S(1)} %collective-permute-done.29.refs_1_, ...), custom_call_target="tpu_custom_call", output_to_operand_aliasing={{}: (10, {})} | custom-call | bytes 2097152 | tf_op jit(solution)/shard_map/gather_grads/pallas_call | solution.py:489
  (85 shorter events, 45.1 us)
Async XLA Ops:
  16.0 20.3 %collective-permute-start.4 = (bf16[4,32,896]{2,1,0:T(8,128)(2,1)}, bf16[4,32,896]{2,1,0:T(8,128)(2,1)S(1)}, u32[]{:S(2)}, u32[]{:S(2)}) collective-permute-start(bf16[4,32,896]{2,1,0:T(8,128)(2,1)} %get-tuple-element.88), channel_id=1, source_target_pairs={{0,16},{4,20},{8,24},{12,28},{16,0},{20,4},{24,8},{28,12},{1,17},{... | collective-permute-start | bytes 688136 | tf_op jit(solution)/shard_map/ppermute | solution.py:519
  16.1 21.5 %collective-permute-start.5 = (bf16[4,32,896]{2,1,0:T(8,128)(2,1)}, bf16[4,32,896]{2,1,0:T(8,128)(2,1)S(1)}, u32[]{:S(2)}, u32[]{:S(2)}) collective-permute-start(bf16[4,32,896]{2,1,0:T(8,128)(2,1)} %get-tuple-element.78.refs_0_), channel_id=1, source_target_pairs={{0,2},{1,3},{2,0},{3,1},{4,6},{5,7},{6,4},{7,5},{8,10},{9,11},{10,... | collective-permute-start | bytes 688136 | tf_op jit(solution)/shard_map/ppermute | solution.py:516
  17.3 24.7 %collective-permute-start = (bf16[4,32,896]{2,1,0:T(8,128)(2,1)}, bf16[4,32,896]{2,1,0:T(8,128)(2,1)S(1)}, u32[]{:S(2)}, u32[]{:S(2)}) collective-permute-start(bf16[4,32,896]{2,1,0:T(8,128)(2,1)} %get-tuple-element.80), channel_id=1, source_target_pairs={{0,12},{4,16},{8,20},{12,24},{16,28},{20,0},{24,4},{28,8},{1,13},{... | collective-permute-start | bytes 688136 | tf_op jit(solution)/shard_map/ppermute | solution.py:519
  22.0 20.9 %collective-permute-start.2 = (bf16[4,32,896]{2,1,0:T(8,128)(2,1)S(1)}, bf16[4,32,896]{2,1,0:T(8,128)(2,1)S(1)}, u32[]{:S(2)}, u32[]{:S(2)}) collective-permute-start(bf16[4,32,896]{2,1,0:T(8,128)(2,1)S(1)} %collective-permute-done.1.refs_3_), channel_id=1, source_target_pairs={{0,2},{1,3},{2,0},{3,1},{4,6},{5,7},{6,4},{7,5},{8,10},{9,11},{10,... | collective-permute-start | bytes 688136 | tf_op jit(solution)/shard_map/ppermute | solution.py:516
  36.4 10.8 %collective-permute-start.7 = (bf16[4,32,896]{2,1,0:T(8,128)(2,1)S(1)}, bf16[4,32,896]{2,1,0:T(8,128)(2,1)S(1)}, u32[]{:S(2)}, u32[]{:S(2)}) collective-permute-start(bf16[4,32,896]{2,1,0:T(8,128)(2,1)S(1)} %collective-permute-done.4.refs_4_), channel_id=1, source_target_pairs={{0,2},{1,3},{2,0},{3,1},{4,6},{5,7},{6,4},{7,5},{8,10},{9,11},{10,... | collective-permute-start | bytes 688136 | tf_op jit(solution)/shard_map/ppermute | solution.py:516
  37.5 9.6 %collective-permute-start.6 = (bf16[4,32,896]{2,1,0:T(8,128)(2,1)}, bf16[4,32,896]{2,1,0:T(8,128)(2,1)S(1)}, u32[]{:S(2)}, u32[]{:S(2)}) collective-permute-start(bf16[4,32,896]{2,1,0:T(8,128)(2,1)} %get-tuple-element.90), channel_id=1, source_target_pairs={{0,24},{4,28},{8,0},{12,4},{16,8},{20,12},{24,16},{28,20},{1,25},{... | collective-permute-start | bytes 688136 | tf_op jit(solution)/shard_map/ppermute | solution.py:519
  42.9 13.1 %collective-permute-start.3 = (bf16[4,32,896]{2,1,0:T(8,128)(2,1)}, bf16[4,32,896]{2,1,0:T(8,128)(2,1)S(1)}, u32[]{:S(2)}, u32[]{:S(2)}) collective-permute-start(bf16[4,32,896]{2,1,0:T(8,128)(2,1)} %get-tuple-element.85), channel_id=1, source_target_pairs={{0,28},{4,0},{8,4},{12,8},{16,12},{20,16},{24,20},{28,24},{1,29},{... | collective-permute-start | bytes 688136 | tf_op jit(solution)/shard_map/ppermute | solution.py:519
  47.7 12.5 %collective-permute-start.10 = (bf16[4,32,896]{2,1,0:T(8,128)(2,1)}, bf16[4,32,896]{2,1,0:T(8,128)(2,1)S(1)}, u32[]{:S(2)}, u32[]{:S(2)}) collective-permute-start(bf16[4,32,896]{2,1,0:T(8,128)(2,1)} %get-tuple-element.97), channel_id=1, source_target_pairs={{0,4},{4,8},{8,12},{12,16},{16,20},{20,24},{24,28},{28,0},{1,5},{5... | collective-permute-start | bytes 688136 | tf_op jit(solution)/shard_map/ppermute | solution.py:519
  56.0 9.6 %collective-permute-start.11 = (bf16[4,32,896]{2,1,0:T(8,128)(2,1)S(1)}, bf16[4,32,896]{2,1,0:T(8,128)(2,1)S(1)}, u32[]{:S(2)}, u32[]{:S(2)}) collective-permute-start(bf16[4,32,896]{2,1,0:T(8,128)(2,1)S(1)} %collective-permute-done.3.refs_1_), channel_id=1, source_target_pairs={{0,2},{1,3},{2,0},{3,1},{4,6},{5,7},{6,4},{7,5},{8,10},{9,11},{10,... | collective-permute-start | bytes 688136 | tf_op jit(solution)/shard_map/ppermute | solution.py:516
  56.7 13.8 %collective-permute-start.13 = (bf16[4,32,896]{2,1,0:T(8,128)(2,1)S(1)}, bf16[4,32,896]{2,1,0:T(8,128)(2,1)S(1)}, u32[]{:S(2)}, u32[]{:S(2)}) collective-permute-start(bf16[4,32,896]{2,1,0:T(8,128)(2,1)S(1)} %collective-permute-done.8.refs_6_), channel_id=1, source_target_pairs={{0,2},{1,3},{2,0},{3,1},{4,6},{5,7},{6,4},{7,5},{8,10},{9,11},{10,... | collective-permute-start | bytes 688136 | tf_op jit(solution)/shard_map/ppermute | solution.py:516
  60.2 15.2 %collective-permute-start.14 = (bf16[4,32,896]{2,1,0:T(8,128)(2,1)S(1)}, bf16[4,32,896]{2,1,0:T(8,128)(2,1)S(1)}, u32[]{:S(2)}, u32[]{:S(2)}) collective-permute-start(bf16[4,32,896]{2,1,0:T(8,128)(2,1)S(1)} %collective-permute-done.10.refs_7_), channel_id=1, source_target_pairs={{0,2},{1,3},{2,0},{3,1},{4,6},{5,7},{6,4},{7,5},{8,10},{9,11},{10,... | collective-permute-start | bytes 688136 | tf_op jit(solution)/shard_map/ppermute | solution.py:516
  80.5 12.6 %collective-permute-start.15 = (bf16[16,32,896]{2,1,0:T(8,128)(2,1)S(1)}, bf16[16,32,896]{2,1,0:T(8,128)(2,1)S(1)}, u32[]{:S(2)}, u32[]{:S(2)}) collective-permute-start(bf16[16,32,896]{2,1,0:T(8,128)(2,1)S(1)} %get-tuple-element.102.refs_0_), channel_id=1, source_target_pairs={{0,1},{1,0},{2,3},{3,2},{4,5},{5,4},{6,7},{7,6},{8,9},{9,8},{10,11... | collective-permute-start | bytes 2752520 | tf_op jit(solution)/shard_map/ppermute | solution.py:513
  83.1 9.9 %collective-permute-start.16 = (bf16[16,32,896]{2,1,0:T(8,128)(2,1)S(1)}, bf16[16,32,896]{2,1,0:T(8,128)(2,1)S(1)}, u32[]{:S(2)}, u32[]{:S(2)}) collective-permute-start(bf16[16,32,896]{2,1,0:T(8,128)(2,1)S(1)} %get-tuple-element.103.refs_1_), channel_id=1, source_target_pairs={{0,1},{1,0},{2,3},{3,2},{4,5},{5,4},{6,7},{7,6},{8,9},{9,8},{10,11... | collective-permute-start | bytes 2752520 | tf_op jit(solution)/shard_map/ppermute | solution.py:513
  115.5 14.8 %collective-permute-start.17 = (f32[1,16,32,384]{3,2,1,0:T(8,128)S(1)}, f32[1,16,32,384]{3,2,1,0:T(8,128)S(1)}, u32[]{:S(2)}, u32[]{:S(2)}) collective-permute-start(f32[1,16,32,384]{3,2,1,0:T(8,128)S(1)} %get-tuple-element.110), channel_id=1, source_target_pairs={{0,1},{1,0},{2,3},{3,2},{4,5},{5,4},{6,7},{7,6},{8,9},{9,8},{10,11... | collective-permute-start | bytes 2359304 | tf_op jit(solution)/shard_map/ppermute | solution.py:513
  117.6 12.7 %collective-permute-start.19 = (s16[1,49,32,128]{3,2,1,0:T(8,128)(2,1)S(1)}, s16[1,49,32,128]{3,2,1,0:T(8,128)(2,1)S(1)}, u32[]{:S(2)}, u32[]{:S(2)}) collective-permute-start(s16[1,49,32,128]{3,2,1,0:T(8,128)(2,1)S(1)} %far_codes.2), channel_id=1, source_target_pairs={{0,2},{1,3},{2,0},{3,1},{4,6},{5,7},{6,4},{7,5},{8,10},{9,11},{10,... | collective-permute-start | bytes 1204232 | tf_op jit(solution)/shard_map/ppermute | solution.py:516
  132.4 28.1 %collective-permute-start.20 = (f32[1,16,32,512]{3,2,1,0:T(8,128)}, f32[1,16,32,512]{3,2,1,0:T(8,128)S(1)}, u32[]{:S(2)}, u32[]{:S(2)}) collective-permute-start(f32[1,16,32,512]{3,2,1,0:T(8,128)} %get-tuple-element.122), channel_id=1, source_target_pairs={{0,1},{1,0},{2,3},{3,2},{4,5},{5,4},{6,7},{7,6},{8,9},{9,8},{10,11... | collective-permute-start | bytes 3145736 | tf_op jit(solution)/shard_map/ppermute | solution.py:513
  135.3 25.3 %collective-permute-start.22 = (s16[1,65,32,128]{3,2,1,0:T(8,128)(2,1)S(1)}, s16[1,65,32,128]{3,2,1,0:T(8,128)(2,1)S(1)}, u32[]{:S(2)}, u32[]{:S(2)}) collective-permute-start(s16[1,65,32,128]{3,2,1,0:T(8,128)(2,1)S(1)} %far_codes.3), channel_id=1, source_target_pairs={{0,2},{1,3},{2,0},{3,1},{4,6},{5,7},{6,4},{7,5},{8,10},{9,11},{10,... | collective-permute-start | bytes 1597448 | tf_op jit(solution)/shard_map/ppermute | solution.py:516
  141.2 12.1 %collective-permute-start.26 = (s16[13,32,128]{2,1,0:T(8,128)(2,1)S(1)}, s16[13,32,128]{2,1,0:T(8,128)(2,1)S(1)}, u32[]{:S(2)}, u32[]{:S(2)}) collective-permute-start(s16[13,32,128]{2,1,0:T(8,128)(2,1)S(1)} %get-tuple-element.127), channel_id=1, source_target_pairs={{0,16},{4,20},{8,24},{12,28},{16,0},{20,4},{24,8},{28,12},{1,17},{... | collective-permute-start | bytes 319496 | tf_op jit(solution)/shard_map/ppermute | solution.py:519
  145.6 14.9 %collective-permute-start.28 = (s16[13,32,128]{2,1,0:T(8,128)(2,1)S(1)}, s16[13,32,128]{2,1,0:T(8,128)(2,1)S(1)}, u32[]{:S(2)}, u32[]{:S(2)}) collective-permute-start(s16[13,32,128]{2,1,0:T(8,128)(2,1)S(1)} %get-tuple-element.129), channel_id=1, source_target_pairs={{0,24},{4,28},{8,0},{12,4},{16,8},{20,12},{24,16},{28,20},{1,25},{... | collective-permute-start | bytes 319496 | tf_op jit(solution)/shard_map/ppermute | solution.py:519
  163.3 17.0 %collective-permute-start.31 = (s16[17,32,128]{2,1,0:T(8,128)(2,1)S(1)}, s16[17,32,128]{2,1,0:T(8,128)(2,1)S(1)}, u32[]{:S(2)}, u32[]{:S(2)}) collective-permute-start(s16[17,32,128]{2,1,0:T(8,128)(2,1)S(1)} %get-tuple-element.134), channel_id=1, source_target_pairs={{0,12},{4,16},{8,20},{12,24},{16,28},{20,0},{24,4},{28,8},{1,13},{... | collective-permute-start | bytes 417800 | tf_op jit(solution)/shard_map/ppermute | solution.py:519
  165.5 19.2 %collective-permute-start.32 = (s16[17,32,128]{2,1,0:T(8,128)(2,1)S(1)}, s16[17,32,128]{2,1,0:T(8,128)(2,1)S(1)}, u32[]{:S(2)}, u32[]{:S(2)}) collective-permute-start(s16[17,32,128]{2,1,0:T(8,128)(2,1)S(1)} %get-tuple-element.135), channel_id=1, source_target_pairs={{0,16},{4,20},{8,24},{12,28},{16,0},{20,4},{24,8},{28,12},{1,17},{... | collective-permute-start | bytes 417800 | tf_op jit(solution)/shard_map/ppermute | solution.py:519
  167.0 17.6 %collective-permute-start.33 = (s16[17,32,128]{2,1,0:T(8,128)(2,1)S(1)}, s16[17,32,128]{2,1,0:T(8,128)(2,1)S(1)}, u32[]{:S(2)}, u32[]{:S(2)}) collective-permute-start(s16[17,32,128]{2,1,0:T(8,128)(2,1)S(1)} %get-tuple-element.136), channel_id=1, source_target_pairs={{0,20},{4,24},{8,28},{12,0},{16,4},{20,8},{24,12},{28,16},{1,21},{... | collective-permute-start | bytes 417800 | tf_op jit(solution)/shard_map/ppermute | solution.py:519
  170.4 17.7 %collective-permute-start.34 = (s16[17,32,128]{2,1,0:T(8,128)(2,1)S(1)}, s16[17,32,128]{2,1,0:T(8,128)(2,1)S(1)}, u32[]{:S(2)}, u32[]{:S(2)}) collective-permute-start(s16[17,32,128]{2,1,0:T(8,128)(2,1)S(1)} %get-tuple-element.137), channel_id=1, source_target_pairs={{0,24},{4,28},{8,0},{12,4},{16,8},{20,12},{24,16},{28,20},{1,25},{... | collective-permute-start | bytes 417800 | tf_op jit(solution)/shard_map/ppermute | solution.py:519
  170.4 18.9 %collective-permute-start.35 = (s16[17,32,128]{2,1,0:T(8,128)(2,1)S(1)}, s16[17,32,128]{2,1,0:T(8,128)(2,1)S(1)}, u32[]{:S(2)}, u32[]{:S(2)}) collective-permute-start(s16[17,32,128]{2,1,0:T(8,128)(2,1)S(1)} %get-tuple-element.138), channel_id=1, source_target_pairs={{0,28},{4,0},{8,4},{12,8},{16,12},{20,16},{24,20},{28,24},{1,29},{... | collective-permute-start | bytes 417800 | tf_op jit(solution)/shard_map/ppermute | solution.py:519
  (24 other events, 314.1 us)

commit v10 on v9

--- a/solution.py
+++ b/solution.py
@@ -11,7 +11,7 @@
 HD = 128
 SPAN = 64
 LANES = 128
-WINDOW = 3
+WINDOW = 4
 VMEM_LIMIT = 28 * 1024 * 1024
 VMEM_MORE = 40 * 1024 * 1024
 VMEM_ALL = 60 * 1024 * 1024
@@ -318,108 +318,128 @@
     return code.astype(jnp.int32).astype(jnp.int16), power
 
 
-def grads_body(near, first, core_ref, own_ref, wk, wv, near_out, far_out, own_out, core_acc, own_acc):
+def grads_body(first, core_ref, own_ref, wk, wv, near_out, far_out, own_out, part, sem):
     i = pl.program_id(0)
-
-    def act(w):
-        w = w[first : first + own_acc.shape[1], :]
-        for ref, acc in ((core_ref, core_acc), (own_ref, own_acc)):
-            rows = ref[...].reshape(acc.shape[0], -1)
-            part = lax.dot_general(rows, w, (((1,), (1,)), ((), ())), preferred_element_type=F32)
-
-            @pl.when(i == 0)
-            def _():
-                acc[...] = part
-
-            @pl.when(i > 0)
-            def _():
-                acc[...] += part
-
-    with_weight(wk, wv, act)
+    n_x = own_out.shape[0]
+    width, count = wk.shape[1], part.shape[-1]
+    last = (((1,), (1,)), ((), ()))
+
+    def act(ref):
+        rows = ref[...].reshape(-1, 2 * width)
+        res = lax.dot_general(
+            rows[:, :width], wk[first : first + count, :], last, preferred_element_type=F32
+        )
+        res += lax.dot_general(
+            rows[:, width:], wv[first : first + count, :], last, preferred_element_type=F32
+        )
+        part[i] = res.reshape(part.shape[1:])
+
+    @pl.when(i < n_x)
+    def _():
+        act(core_ref)
+
+    @pl.when(i >= n_x)
+    def _():
+        act(own_ref)
+
+    outs = [near_out.at[0]] + [far_out.at[k] for k in range(n_x - 1)]
+    outs += [own_out.at[k] for k in range(n_x)]
+    copies = [pltpu.make_async_copy(part.at[k], out, sem.at[k]) for k, out in enumerate(outs)]
+    for k, copy in enumerate(copies):
+
+        @pl.when(i == k)
+        def _():
+            copy.start()
 
     @pl.when(i == pl.num_programs(0) - 1)
     def _():
-        core = core_acc[...].reshape(core_ref.shape[:3] + core_acc.shape[1:])
-        near_out[...] = core[:near]
-        far_out[...] = core[near:]
-        own_out[...] = own_acc[...].reshape(own_out.shape)
-
-
-def grads_of(d_core, d_own, wk, wv, near, cols):
-    pieces, n, sub, width = d_own.shape
+        for copy in copies:
+            copy.wait()
+
+
+def grads_of(d_core, d_own, wk, wv, cols):
+    n_x, n, sub, width = d_own.shape
     first, count = cols
-    step = width // 4
-    shapes = [(near, n, sub, count), (pieces - near, n, sub, count), (pieces, n, sub, count)]
-    rows = pieces * n * sub
-    return pl.pallas_call(
-        functools.partial(grads_body, near, first),
+    shapes = [(1, n, sub, count), (n_x - 1, n, sub, count), (n_x, n, sub, count)]
+    rows = n_x * n * sub
+    return pl.pallas_call(
+        functools.partial(grads_body, first),
         out_shape=[jax.ShapeDtypeStruct(shape, F32) for shape in shapes],
-        grid=(4,),
-        in_specs=[pl.BlockSpec((pieces, n, sub, step), lambda i: (0, 0, 0, i))] * 2
-        + weight_specs(wk.shape[0], step),
-        out_specs=[pl.BlockSpec(shape, lambda i: (0, 0, 0, 0)) for shape in shapes],
-        scratch_shapes=[pltpu.VMEM((rows, count), F32)] * 2,
-        compiler_params=params(VMEM_ALL),
+        grid=(2 * n_x,),
+        in_specs=[
+            pl.BlockSpec((1, n, sub, width), lambda i: (jnp.minimum(i, n_x - 1), 0, 0, 0)),
+            pl.BlockSpec((1, n, sub, width), lambda i: (jnp.maximum(i - n_x, 0), 0, 0, 0)),
+            pl.BlockSpec(wk.shape, lambda i: (0, 0)),
+            pl.BlockSpec(wv.shape, lambda i: (0, 0)),
+        ],
+        out_specs=[ANY] * 3,
+        scratch_shapes=[
+            pltpu.VMEM((2 * n_x, n, sub, count), F32),
+            pltpu.SemaphoreType.DMA((2 * n_x,)),
+        ],
+        compiler_params=params(),
         cost_estimate=cost(4 * rows * count * width, 2 * (count + 2 * rows) * width + 8 * rows * count),
         name="grads",
     )(d_core, d_own, wk, wv)
 
 
-def put_codes(far, codes):
-    pieces, n, sub, count = far.shape
-    near = codes[0].shape[0]
-    tiles = count // LANES
+def far_codes_body(cuts, mine, got, *codes):
+    far, n, sub, count = got.shape
     row = lax.broadcasted_iota(jnp.int32, (sub, LANES), 0)
-    for i in range(pieces):
-        out, c = codes[i // near], i % near
-        code, power = encode(far[i], (1, 2))
-        for e in range(tiles):
-            out[c, e * n : (e + 1) * n] = code[:, :, e * LANES : (e + 1) * LANES]
+    for k in range(far):
+        code, power = encode(mine[k] + got[k], (1, 2))
+        e = 0
+        for cut, out in zip(cuts, codes[k * len(cuts) :]):
+            for at in range(cut):
+                out[at * n : (at + 1) * n] = code[:, :, e * LANES : (e + 1) * LANES]
+                e += 1
         note = jnp.zeros((sub, LANES), F32)
         for r in range(n):
             note = jnp.where(row == r, power[r], note)
-        out[c, tiles * n] = note.astype(jnp.int32).astype(jnp.int16)
-
-
-def far_codes_body(mine, got, *codes):
-    put_codes(mine[...] + got[...], codes)
-
-
-def far_codes(own, got, near):
+        codes[k * len(cuts)][cuts[0] * n] = note.astype(jnp.int32).astype(jnp.int16)
+
+
+def far_codes(own, got, cuts):
     far, n, sub, count = got.shape
-    shape = (near, count // LANES * n + 1, sub, LANES)
-    return pl.pallas_call(
-        far_codes_body,
-        out_shape=[jax.ShapeDtypeStruct(shape, jnp.int16)] * (far // near),
+    shapes = [(cut * n + (q == 0), sub, LANES) for q, cut in enumerate(cuts)] * far
+
+    def whole(shape):
+        return pl.BlockSpec(shape, lambda i: (0,) * len(shape))
+
+    mine = pl.BlockSpec(tuple(pl.Element(size) for size in got.shape), lambda i: (1, 0, 0, 0))
+    out = pl.pallas_call(
+        functools.partial(far_codes_body, cuts),
+        out_shape=[jax.ShapeDtypeStruct(shape, jnp.int16) for shape in shapes],
         grid=(1,),
-        in_specs=[
-            pl.BlockSpec((pl.Element(far), pl.Element(n), pl.Element(sub), pl.Element(count)), lambda i: (near, 0, 0, 0)),
-            pl.BlockSpec(got.shape, lambda i: (0, 0, 0, 0)),
-        ],
-        out_specs=[pl.BlockSpec(shape, lambda i: (0, 0, 0, 0))] * (far // near),
+        in_specs=[mine, whole(got.shape)],
+        out_specs=[whole(shape) for shape in shapes],
         compiler_params=params(),
         cost_estimate=cost(8 * got.size, 10 * got.size),
         name="far_codes",
     )(own, got)
-
-
-def send_body(n_dp, request, own, got, *rest):
+    return [out[k * len(cuts) : (k + 1) * len(cuts)] for k in range(far)]
+
+
+def send_body(n_dp, cuts, request, own, got, *rest):
     codes, outs, (stage, powers) = rest[: -n_dp - 2], rest[-n_dp - 2 : -2], rest[-2:]
-    n_chunks, n, sub, count = got.shape
+    _, n, sub, count = got.shape
     tiles = count // LANES
     cap = request.shape[0] // n_dp
-    for c in range(n_chunks):
-        for r in range(n):
-            total = own[c, r] + got[c, r]
-            for code in codes:
-                unit = jnp.exp2(code[c, tiles * n].astype(F32)[r : r + 1] - 15.0)
-                total = total + jnp.concatenate(
-                    [code[c, e * n + r].astype(F32) * unit for e in range(tiles)], axis=1
-                )
-            coded, power = encode(total, (0, 1))
-            for e in range(tiles):
-                stage[r, c * tiles + e] = coded[:, e * LANES : (e + 1) * LANES]
-            powers[r, c] = jnp.broadcast_to(power, (sub, LANES))
+    notes = [code[cuts[0] * n].astype(F32) for code in codes[:: len(cuts)]]
+    for r in range(n):
+        total = own[0, r] + got[0, r]
+        for k, note in enumerate(notes):
+            unit = jnp.exp2(note[r : r + 1] - 15.0)
+            blocks = [
+                code[at * n + r].astype(F32) * unit
+                for cut, code in zip(cuts, codes[k * len(cuts) :])
+                for at in range(cut)
+            ]
+            total = total + jnp.concatenate(blocks, axis=1)
+        coded, power = encode(total, (0, 1))
+        for e in range(tiles):
+            stage[r, e] = coded[:, e * LANES : (e + 1) * LANES]
+        powers[r] = jnp.broadcast_to(power, (sub, LANES))
     row = lax.broadcasted_iota(jnp.int32, (sub, LANES), 0)
     for d in range(n_dp):
         note = jnp.zeros((sub, LANES), F32)
@@ -428,28 +448,28 @@
 
             @pl.when(r >= 0)
             def _():
-                outs[d][pl.ds(j * n_chunks * tiles, n_chunks * tiles)] = stage[r]
-
-            for c in range(n_chunks):
-                note = jnp.where(row == j * n_chunks + c, powers[jnp.maximum(r, 0), c], note)
-        outs[d][cap * n_chunks * tiles] = note.astype(jnp.int32).astype(jnp.int16)
-
-
-def send_codes(request, own, got, codes, n_dp):
-    n_chunks, n, sub, count = got.shape
+                outs[d][pl.ds(j * tiles, tiles)] = stage[r]
+
+            note = jnp.where(row == j, powers[jnp.maximum(r, 0)], note)
+        outs[d][cap * tiles] = note.astype(jnp.int32).astype(jnp.int16)
+
+
+def send_codes(request, own, got, codes, cuts, n_dp):
+    _, n, sub, count = got.shape
     block = pl.BlockSpec(got.shape, lambda i: (0, 0, 0, 0))
     tiles = count // LANES
     cap = request.shape[0] // n_dp
-    shape = (cap * n_chunks * tiles + 1, sub, LANES)
-    return pl.pallas_call(
-        functools.partial(send_body, n_dp),
+    shape = (cap * tiles + 1, sub, LANES)
+    codes = [x for piece in codes for x in piece]
+    return pl.pallas_call(
+        functools.partial(send_body, n_dp, cuts),
         out_shape=[jax.ShapeDtypeStruct(shape, jnp.int16)] * n_dp,
         grid=(1,),
         in_specs=[SMEM, block, block] + [VMEM] * len(codes),
         out_specs=[VMEM] * n_dp,
         scratch_shapes=[
-            pltpu.VMEM((n, n_chunks * tiles, sub, LANES), jnp.int16),
-            pltpu.VMEM((n, n_chunks, sub, LANES), F32),
+            pltpu.VMEM((n, tiles, sub, LANES), jnp.int16),
+            pltpu.VMEM((n, sub, LANES), F32),
         ],
         compiler_params=params(),
         cost_estimate=cost(10 * got.size, 6 * got.size + 2 * n_dp * math.prod(shape)),
@@ -457,11 +477,10 @@
     )(request, own, got, *codes)
 
 
-def gather_body(n_dp, n_chunks, first, me, asked, *refs):
+def gather_body(n_dp, first, me, asked, *refs):
     arrived = refs[:n_dp]
     out, total, sem = refs[-3:]
-    sub, count = total.shape[1] // n_chunks, total.shape[2]
-    tiles = count // LANES
+    tiles = total.shape[2] // LANES
     cap = asked.shape[1] // n_dp
     total[...] = jnp.zeros_like(total)
     for d in range(n_dp):
@@ -470,15 +489,13 @@
 
             @pl.when(slab >= 0)
             def _():
-                note = arrived[d][cap * n_chunks * tiles].astype(F32)
-                for c in range(n_chunks):
-                    at = j * n_chunks + c
-                    unit = jnp.exp2(note[at : at + 1] - 15.0)
-                    for e in range(tiles):
-                        value = arrived[d][at * tiles + e].astype(F32) * unit
-                        total[slab, pl.ds(c * sub, sub), pl.ds(e * LANES, LANES)] += value
-
-    copy = pltpu.make_async_copy(total, out.at[:, :, pl.ds(first, count)], sem)
+                note = arrived[d][cap * tiles].astype(F32)
+                unit = jnp.exp2(note[j : j + 1] - 15.0)
+                for e in range(tiles):
+                    value = arrived[d][j * tiles + e].astype(F32) * unit
+                    total[slab, :, pl.ds(e * LANES, LANES)] += value
+
+    copy = pltpu.make_async_copy(total, out.at[:, :, pl.ds(first, total.shape[2])], sem)
     copy.start()
     copy.wait()
 
@@ -487,7 +504,7 @@
     first, count = cols
     n_dp = asked.shape[0]
     return pl.pallas_call(
-        functools.partial(gather_body, n_dp, 1, first),
+        functools.partial(gather_body, n_dp, first),
         out_shape=jax.ShapeDtypeStruct((n_slabs, rows, enc), F32),
         in_specs=[SMEM, SMEM] + [VMEM] * n_dp + [ANY] * (before is not None),
         out_specs=ANY,
@@ -518,6 +535,7 @@
     def over_dp(x, d):
         return lax.ppermute(x, "dp", [(i, (i + d) % n_dp) for i in range(n_dp)])
 
+    nearest_first = sorted(range(1, n_dp), key=lambda d: min(d, n_dp - d))
     farthest_first = sorted(range(1, n_dp), key=lambda d: -min(d, n_dp - d))
 
     def to_all(xs, sign, distances=farthest_first):
@@ -529,21 +547,13 @@
 
     sent = pack(me, asked, table, share, cap)
     mine = {0: sent[0]}
-    far = {0: [over_x(sent[0], k) for k in range(1, n_x)]}
-    for i, d in enumerate(farthest_first):
+    for i, d in enumerate(nearest_first):
         block = sent[d]
         if i >= WINDOW:
-            held = farthest_first[i - WINDOW]
+            held = nearest_first[i - WINDOW]
             block, mine[held] = lax.optimization_barrier((block, mine[held]))
-            far[held] = [over_x(mine[held], k) for k in range(1, n_x)]
-            if i > WINDOW:
-                passed = farthest_first[i - WINDOW - 1]
-                block, far[passed] = lax.optimization_barrier((block, far[passed]))
-            else:
-                block, far[0] = lax.optimization_barrier((block, far[0]))
         mine[d] = over_dp(block, -d)
-    for d in farthest_first[-WINDOW:]:
-        far[d] = [over_x(mine[d], k) for k in range(1, n_x)]
+    far = [[over_x(mine[d], k) for k in range(1, n_x)] for d in range(n_dp)]
     lists = [[mine[d] for d in range(n_dp)]]
     lists += [[far[d][k] for d in range(n_dp)] for k in range(n_x - 1)]
     mine, *far = compact(request, lists, n_requests)
@@ -560,23 +570,25 @@
     )
     far_got = over_core(far)
     near_got = over_core(near)
-    codes = far_codes(own, far_got, 1)
-    near_b, far_b, own_b = grads_of(d_core, d_own, key_weight, value_weight, 1, parts[1])
-
-    codes = [over_x(code, n_x - d) for d, code in enumerate(codes, 1)]
-    sent = send_codes(request, own, near_got, codes, n_dp)
-    sent, near_b, far_b = lax.optimization_barrier((sent, near_b, far_b))
+    cuts = (2, 1)
+    codes = far_codes(own, far_got, cuts)
+    near_b, far_b, own_b = grads_of(d_core, d_own, key_weight, value_weight, parts[1])
+
+    codes = [[over_x(x, n_x - k) for x in piece] for k, piece in enumerate(codes, 1)]
+    lead, near_b, far_b = lax.optimization_barrier(([piece[0] for piece in codes], near_b, far_b))
+    codes = [[x, *piece[1:]] for x, piece in zip(lead, codes)]
+    far_got_b = over_core(far_b)
+    near_got_b = over_core(near_b)
+    sent = send_codes(request, own, near_got, codes, cuts, n_dp)
     came = to_all(sent, 1)
-    far_got = over_core(far_b)
-    near_got = over_core(near_b)
-    codes = far_codes(own_b, far_got, 1)
-    codes = [over_x(code, n_x - d) for d, code in enumerate(codes, 1)]
-    lead = {d: came[d] for d in farthest_first[:6]}
-    codes, lead = lax.optimization_barrier((codes, lead))
-    came.update(lead)
     arrived = [sent[0]] + [came[d] for d in range(1, n_dp)]
     d_table = gather_grads(me, asked, arrived, n_slabs, share, enc, parts[0], None)
-    sent = send_codes(request, own_b, near_got, codes, n_dp)
+
+    cuts = (parts[1][1] // LANES,)
+    codes = far_codes(own_b, far_got_b, cuts)
+    codes, before = lax.optimization_barrier((codes, sent[0]))
+    codes = [[over_x(x, n_x - k) for x in piece] for k, piece in enumerate(codes, 1)]
+    sent = send_codes(request, own_b, near_got_b, codes, cuts, n_dp)
     came = to_all(sent, 1)
     arrived = [sent[0]] + [came[d] for d in range(1, n_dp)]
     d_table = gather_grads(me, asked, arrived, n_slabs, share, enc, parts[1], d_table)

time: 195 us -> 189 us (0.969); the launches traced: 192 us -> 189 us
  waiting for transfers between devices: 65 us -> 55.7 us
  starting transfers between devices: 54.4 us -> 62.1 us
  Pallas kernels: 58.7 us -> 52.4 us
  local copies, waits for them, and re-layouts: 4.63 us -> 8.82 us
    ppermute x21, waiting for transfers between devices: 45.7 us -> 36.2 us  [over_dp(): return lax.ppermute(x, 'dp', [(i, (i + d) % n_dp) for i in range(n_dp)])]
    ppermute x6, starting transfers between devices: 3.99 us -> 11.4 us  [over_core(): return lax.ppermute(x, 'tensor', [(t, t ^ 1) for t in range(n_tp)])]
    pallas_call x7, Pallas kernels: 20.7 us -> 14.3 us  [the longest x2 5.73 us: gather_grads(): pl.pallas_call(functools.partial(gather_body, n_dp, first), out_shape=jax...]
    unnamed x22, local copies, waits for them, and re-layouts: 4.63 us -> 8.82 us
    ppermute x10 -> x11, starting transfers between devices: 8.88 us -> 9.58 us  [over_x(): lax.ppermute(x, 'tensor', [(t, (t + 2 * d) % n_tp) for t in range(n_tp)])]
    ppermute x10 -> x11, waiting for transfers between devices: 15.1 us -> 14.9 us  [over_x(): lax.ppermute(x, 'tensor', [(t, (t + 2 * d) % n_tp) for t in range(n_tp)])]
  transfers between devices with their start and end apart: 37 -> 38, of which waited for: 16 -> 17; matrix products, arithmetic and copies ran while one was open for 0% -> 0% of each run, Pallas kernels for 11% -> 9%
where the time goes in v10:
time: 189 us
  starting transfers between devices  62.1 us (33%)
  waiting for transfers between devices  55.7 us (29%)
  Pallas kernels  52.4 us (28%)
  local copies, waits for them, and re-layouts  8.82 us (5%)
  blocking collectives  8.6 us (5%)
    ppermute x21, starting transfers between devices, over_dp(): return lax.ppermute(x, 'dp', [(i, (i + d) % n_dp) for i in range(n_dp)])  41.1 us
    ppermute x21, waiting for transfers between devices, over_dp(): return lax.ppermute(x, 'dp', [(i, (i + d) % n_dp) for i in range(n_dp)])  36.2 us
    pallas_call x1, Pallas kernels, attend(): pl.pallas_call(functools.partial(attend_body, places, len(kvs), len(late)...  22 us
    ppermute x11, waiting for transfers between devices, over_x(): lax.ppermute(x, 'tensor', [(t, (t + 2 * d) % n_tp) for t in range(n_tp)])  14.9 us
    ppermute x6, starting transfers between devices, over_core(): return lax.ppermute(x, 'tensor', [(t, t ^ 1) for t in range(n_tp)])  11.4 us
    ppermute x11, starting transfers between devices, over_x(): lax.ppermute(x, 'tensor', [(t, (t + 2 * d) % n_tp) for t in range(n_tp)])  9.58 us
    unnamed x22, local copies, waits for them, and re-layouts  8.82 us
    psum x1, blocking collectives, on_device(): asked = lax.psum(wanted, 'dp')  8.6 us
  transfers between devices with their start and end apart: 38, of which 17 were waited for; matrix products, arithmetic and copies ran while one was open for 0% of the time, Pallas kernels for 9%

profile of v10, /device:TPU:13, one launch (start us, length us, event | category | flops | bytes accessed | tf_op | source)
XLA Modules:
  0.0 188.6 jit_solution(6880511004560019673)
XLA Ops:
  2.2 8.6 %psum.7.asked = s32[8,32]{1,0:T(8,128)} all-reduce(s32[8,32]{1,0:T(8,128)} %get-tuple-element.56), channel_id=1, replica_groups=mesh['dp'=8,'tensor'=4] {'dp'}, use_global_device_ids=true, to_apply=%region_0.0 | all-reduce | flops 256 | bytes 2048 | tf_op jit(solution)/shard_map/psum | solution.py:546
  10.8 4.3 %pack_rows.1 = (bf16[4,32,896]{2,1,0:T(8,128)(2,1)}, bf16[4,32,896]{2,1,0:T(8,128)(2,1)}, bf16[4,32,896]{2,1,0:T(8,128)(2,1)}, bf16[4,32,896]{2,1,0:T(8,128)(2,1...) custom-call(s32[1]{0:T(128)} %get-tuple-element.55.me, ...), custom_call_target="tpu_custom_call" | custom-call | bytes 3670016 | tf_op jit(solution)/shard_map/pack_rows/pallas_call | solution.py:97
  30.9 5.7 %collective-permute-start.5 = (bf16[4,32,896]{2,1,0:T(8,128)(2,1)}, bf16[4,32,896]{2,1,0:T(8,128)(2,1)S(1)}, u32[]{:S(2)}, u32[]{:S(2)}) collective-permute-start(bf16[4,32,896]{2,1,0:T(8,128)(2,1)} %get-tuple-element.68), channel_id=1, source_target_pairs={{0,12},{4,16},{8,20},{12,24},{16,28},{20,0},{24,4},{28,8},{1,13},{... | collective-permute-start | bytes 688136 | tf_op jit(solution)/shard_map/ppermute | solution.py:536
  38.1 8.3 %collective-permute-done.3.refs_4_ = bf16[4,32,896]{2,1,0:T(8,128)(2,1)S(1)} collective-permute-done((bf16[4,32,896]{2,1,0:T(8,128)(2,1)}, bf16[4,32,896]{2,1,0:T(8,128)(2,1)S(1)}, u32[]{:S(2)}, u32[]{:S(2)}) %collective-permute-start.3) | collective-permute-done | bytes 229408 | tf_op jit(solution)/shard_map/ppermute | solution.py:536
  47.8 3.4 %collective-permute-done.5.refs_5_ = bf16[4,32,896]{2,1,0:T(8,128)(2,1)S(1)} collective-permute-done((bf16[4,32,896]{2,1,0:T(8,128)(2,1)}, bf16[4,32,896]{2,1,0:T(8,128)(2,1)S(1)}, u32[]{:S(2)}, u32[]{:S(2)}) %collective-permute-start.5) | collective-permute-done | bytes 229408 | tf_op jit(solution)/shard_map/ppermute | solution.py:536
  52.5 4.6 %collective-permute-done.11.refs_12_ = bf16[4,32,896]{2,1,0:T(8,128)(2,1)S(1)} collective-permute-done((bf16[4,32,896]{2,1,0:T(8,128)(2,1)S(1)}, bf16[4,32,896]{2,1,0:T(8,128)(2,1)S(1)}, u32[]{:S(2)}, u32[]{:S(2)}) %collective-permute-start.11) | collective-permute-done | bytes 229408 | tf_op jit(solution)/shard_map/ppermute | solution.py:533
  57.0 4.9 %collective-permute-done.12.refs_13_ = bf16[4,32,896]{2,1,0:T(8,128)(2,1)S(1)} collective-permute-done((bf16[4,32,896]{2,1,0:T(8,128)(2,1)S(1)}, bf16[4,32,896]{2,1,0:T(8,128)(2,1)S(1)}, u32[]{:S(2)}, u32[]{:S(2)}) %collective-permute-start.12) | collective-permute-done | bytes 229408 | tf_op jit(solution)/shard_map/ppermute | solution.py:533
  62.9 4.2 %compact_rows.1 = (bf16[16,32,896]{2,1,0:T(8,128)(2,1)S(1)}, bf16[16,32,896]{2,1,0:T(8,128)(2,1)S(1)}) custom-call(s32[32]{0:T(128)S(1)} %copy-done.2, bf16[4,32,896]{2,1,0:T(8,128)(2,1)S(1)} %copy-done, bf16[4,32,896]{2,1,0:T(8,128)(2,1)S(1)} %collective-permute-done.refs_1_, bf16[4,32,896]{2,1,0:T(8,128)(2,1)S(1)} %collective-permute-done.1.refs_2_, ...), custom_call_target="tpu_custom_call" | custom-call | bytes 3670016 | tf_op jit(solution)/shard_map/compact_rows/pallas_call | solution.py:131
  67.1 9.7 %collective-permute-start.15 = (bf16[16,32,896]{2,1,0:T(8,128)(2,1)S(1)}, bf16[16,32,896]{2,1,0:T(8,128)(2,1)S(1)}, u32[]{:S(2)}, u32[]{:S(2)}) collective-permute-start(bf16[16,32,896]{2,1,0:T(8,128)(2,1)S(1)} %get-tuple-element.71.refs_0_), channel_id=1, source_target_pairs={{0,1},{1,0},{2,3},{3,2},{4,5},{5,4},{6,7},{7,6},{8,9},{9,8},{10,11... | collective-permute-start | bytes 2752520 | tf_op jit(solution)/shard_map/ppermute | solution.py:530
  78.4 6.1 %project.1.refs_0_ = bf16[2,16,32,2048]{3,2,1,0:T(8,128)(2,1)S(1)} custom-call(bf16[16,32,896]{2,1,0:T(8,128)(2,1)S(1)} %get-tuple-element.71.refs_0_, bf16[16,32,896]{2,1,0:T(8,128)(2,1)S(1)} %get-tuple-element.72.refs_1_, bf16[896,1024]{1,0:T(8,128)(2,1)S(1)} %copy-done.3, bf16[896,1024]{1,0:T(8,128)(2,1)S(1)} %copy-done.4), custom_call_target="tpu_custom_call" | custom-call | flops 3758096384 | bytes 9699328 | tf_op jit(solution)/shard_map/project/pallas_call | solution.py:177
  86.5 22.0 %attend.1 = (bf16[512,1024]{1,0:T(8,128)(2,1)}, bf16[512,1024]{1,0:T(8,128)(2,1)}, bf16[2,16,32,2048]{3,2,1,0:T(8,128)(2,1)}, bf16[2,16,32,2048]{3,2,1,0:T(8,128...) custom-call(bf16[2,16,32,2048]{3,2,1,0:T(8,128)(2,1)} %copy-done.10, ...), custom_call_target="tpu_custom_call" | custom-call | flops 9126805504 | bytes 37748736 | tf_op jit(solution)/shard_map/attend/pallas_call | solution.py:290
  116.7 5.6 %grads.1 = (f32[1,16,32,512]{3,2,1,0:T(8,128)S(1)}, f32[1,16,32,512]{3,2,1,0:T(8,128)S(1)}, f32[2,16,32,512]{3,2,1,0:T(8,128)S(1)}) custom-call(bf16[2,16,32,2048]{3,2,1,0:T(8,128)(2,1)S(1)} %copy-done.9, bf16[2,16,32,2048]{3,2,1,0:T(8,128)(2,1)S(1)} %copy-done.8, bf16[896,1024]{1,0:T(8,128)(2,1)S(1)} %copy-done.3, bf16[896,1024]{1,0:T(8,128)(2,1)S(1)} %copy-done.5), custom_call_target="tpu_custom_call" | custom-call | flops 4294967296 | bytes 14680064 | tf_op jit(solution)/shard_map/grads/pallas_call | solution.py:365
  130.5 5.2 %collective-permute-start.31 = (s16[13,32,128]{2,1,0:T(8,128)(2,1)S(1)}, s16[13,32,128]{2,1,0:T(8,128)(2,1)S(1)}, u32[]{:S(2)}, u32[]{:S(2)}) collective-permute-start(s16[13,32,128]{2,1,0:T(8,128)(2,1)S(1)} %get-tuple-element.98), channel_id=1, source_target_pairs={{0,4},{4,8},{8,12},{12,16},{16,20},{20,24},{24,28},{28,0},{1,5},{5... | collective-permute-start | bytes 319496 | tf_op jit(solution)/shard_map/ppermute | solution.py:536
  136.6 3.2 %collective-permute-start.34 = (s16[13,32,128]{2,1,0:T(8,128)(2,1)S(1)}, s16[13,32,128]{2,1,0:T(8,128)(2,1)S(1)}, u32[]{:S(2)}, u32[]{:S(2)}) collective-permute-start(s16[13,32,128]{2,1,0:T(8,128)(2,1)S(1)} %get-tuple-element.101), channel_id=1, source_target_pairs={{0,16},{4,20},{8,24},{12,28},{16,0},{20,4},{24,8},{28,12},{1,17},{... | collective-permute-start | bytes 319496 | tf_op jit(solution)/shard_map/ppermute | solution.py:536
  139.8 3.2 %collective-permute-done.23.rest_0_ = s16[65,32,128]{2,1,0:T(8,128)(2,1)S(1)} collective-permute-done((s16[65,32,128]{2,1,0:T(8,128)(2,1)S(1)}, s16[65,32,128]{2,1,0:T(8,128)(2,1)S(1)}, u32[]{:S(2)}, u32[]{:S(2)}) %collective-permute-start.23) | collective-permute-done | bytes 532512 | tf_op jit(solution)/shard_map/ppermute | solution.py:533
  144.3 5.4 %collective-permute-start.24 = (s16[17,32,128]{2,1,0:T(8,128)(2,1)S(1)}, s16[17,32,128]{2,1,0:T(8,128)(2,1)S(1)}, u32[]{:S(2)}, u32[]{:S(2)}) collective-permute-start(s16[17,32,128]{2,1,0:T(8,128)(2,1)S(1)} %get-tuple-element.91), channel_id=1, source_target_pairs={{0,4},{4,8},{8,12},{12,16},{16,20},{20,24},{24,28},{28,0},{1,5},{5... | collective-permute-start | bytes 417800 | tf_op jit(solution)/shard_map/ppermute | solution.py:536
  151.6 3.2 %collective-permute-start.37 = (s16[13,32,128]{2,1,0:T(8,128)(2,1)S(1)}, s16[13,32,128]{2,1,0:T(8,128)(2,1)S(1)}, u32[]{:S(2)}, u32[]{:S(2)}) collective-permute-start(s16[13,32,128]{2,1,0:T(8,128)(2,1)S(1)} %get-tuple-element.104), channel_id=1, source_target_pairs={{0,28},{4,0},{8,4},{12,8},{16,12},{20,16},{24,20},{28,24},{1,29},{... | collective-permute-start | bytes 319496 | tf_op jit(solution)/shard_map/ppermute | solution.py:536
  154.8 3.5 %collective-permute-done.35.refs_5_ = s16[13,32,128]{2,1,0:T(8,128)(2,1)S(1)} collective-permute-done((s16[13,32,128]{2,1,0:T(8,128)(2,1)S(1)}, s16[13,32,128]{2,1,0:T(8,128)(2,1)S(1)}, u32[]{:S(2)}, u32[]{:S(2)}) %collective-permute-start.35) | collective-permute-done | bytes 106528 | tf_op jit(solution)/shard_map/ppermute | solution.py:536
  158.4 3.1 %collective-permute-start.26 = (s16[17,32,128]{2,1,0:T(8,128)(2,1)S(1)}, s16[17,32,128]{2,1,0:T(8,128)(2,1)S(1)}, u32[]{:S(2)}, u32[]{:S(2)}) collective-permute-start(s16[17,32,128]{2,1,0:T(8,128)(2,1)S(1)} %get-tuple-element.93), channel_id=1, source_target_pairs={{0,12},{4,16},{8,20},{12,24},{16,28},{20,0},{24,4},{28,8},{1,13},{... | collective-permute-start | bytes 417800 | tf_op jit(solution)/shard_map/ppermute | solution.py:536
  161.9 3.5 %collective-permute-start.27 = (s16[17,32,128]{2,1,0:T(8,128)(2,1)S(1)}, s16[17,32,128]{2,1,0:T(8,128)(2,1)S(1)}, u32[]{:S(2)}, u32[]{:S(2)}) collective-permute-start(s16[17,32,128]{2,1,0:T(8,128)(2,1)S(1)} %get-tuple-element.94), channel_id=1, source_target_pairs={{0,16},{4,20},{8,24},{12,28},{16,0},{20,4},{24,8},{28,12},{1,17},{... | collective-permute-start | bytes 417800 | tf_op jit(solution)/shard_map/ppermute | solution.py:536
  171.0 5.3 %collective-permute-done.26.refs_3_ = s16[17,32,128]{2,1,0:T(8,128)(2,1)S(1)} collective-permute-done((s16[17,32,128]{2,1,0:T(8,128)(2,1)S(1)}, s16[17,32,128]{2,1,0:T(8,128)(2,1)S(1)}, u32[]{:S(2)}, u32[]{:S(2)}) %collective-permute-start.26) | collective-permute-done | bytes 139296 | tf_op jit(solution)/shard_map/ppermute | solution.py:536
  176.2 3.0 %collective-permute-done.27.refs_4_ = s16[17,32,128]{2,1,0:T(8,128)(2,1)S(1)} collective-permute-done((s16[17,32,128]{2,1,0:T(8,128)(2,1)S(1)}, s16[17,32,128]{2,1,0:T(8,128)(2,1)S(1)}, u32[]{:S(2)}, u32[]{:S(2)}) %collective-permute-start.27) | collective-permute-done | bytes 139296 | tf_op jit(solution)/shard_map/ppermute | solution.py:536
  180.9 4.5 %collective-permute-done.30.refs_7_ = s16[17,32,128]{2,1,0:T(8,128)(2,1)S(1)} collective-permute-done((s16[17,32,128]{2,1,0:T(8,128)(2,1)S(1)}, s16[17,32,128]{2,1,0:T(8,128)(2,1)S(1)}, u32[]{:S(2)}, u32[]{:S(2)}) %collective-permute-start.30) | collective-permute-done | bytes 139296 | tf_op jit(solution)/shard_map/ppermute | solution.py:536
  185.5 2.9 %gather_grads.3 = f32[16,32,896]{2,1,0:T(8,128)} custom-call(s32[1]{0:T(128)} %get-tuple-element.55.me, s32[8,32]{1,0:T(8,128)S(1)} %copy-done.1, s16[17,32,128]{2,1,0:T(8,128)(2,1)S(1)} %get-tuple-element.90.refs_0_, s16[17,32,128]{2,1,0:T(8,128)(2,1)S(1)} %collective-permute-done.24.refs_1_, ...), custom_call_target="tpu_custom_call", output_to_operand_aliasing={{}: (10, {})} | custom-call | bytes 2097152 | tf_op jit(solution)/shard_map/gather_grads/pallas_call | solution.py:506
  (87 shorter events, 54.2 us)
Async XLA Ops:
  19.0 11.9 %collective-permute-start.7 = (bf16[4,32,896]{2,1,0:T(8,128)(2,1)}, bf16[4,32,896]{2,1,0:T(8,128)(2,1)S(1)}, u32[]{:S(2)}, u32[]{:S(2)}) collective-permute-start(bf16[4,32,896]{2,1,0:T(8,128)(2,1)} %get-tuple-element.57.refs_0_), channel_id=1, source_target_pairs={{0,2},{1,3},{2,0},{3,1},{4,6},{5,7},{6,4},{7,5},{8,10},{9,11},{10,... | collective-permute-start | bytes 688136 | tf_op jit(solution)/shard_map/ppermute | solution.py:533
  21.2 15.4 %collective-permute-start.2 = (bf16[4,32,896]{2,1,0:T(8,128)(2,1)}, bf16[4,32,896]{2,1,0:T(8,128)(2,1)S(1)}, u32[]{:S(2)}, u32[]{:S(2)}) collective-permute-start(bf16[4,32,896]{2,1,0:T(8,128)(2,1)} %get-tuple-element.64), channel_id=1, source_target_pairs={{0,20},{4,24},{8,28},{12,0},{16,4},{20,8},{24,12},{28,16},{1,21},{... | collective-permute-start | bytes 688136 | tf_op jit(solution)/shard_map/ppermute | solution.py:536
  21.3 15.5 %collective-permute-start.8 = (bf16[4,32,896]{2,1,0:T(8,128)(2,1)S(1)}, bf16[4,32,896]{2,1,0:T(8,128)(2,1)S(1)}, u32[]{:S(2)}, u32[]{:S(2)}) collective-permute-start(bf16[4,32,896]{2,1,0:T(8,128)(2,1)S(1)} %collective-permute-done.refs_1_), channel_id=1, source_target_pairs={{0,2},{1,3},{2,0},{3,1},{4,6},{5,7},{6,4},{7,5},{8,10},{9,11},{10,... | collective-permute-start | bytes 688136 | tf_op jit(solution)/shard_map/ppermute | solution.py:533
  25.3 21.1 %collective-permute-start.3 = (bf16[4,32,896]{2,1,0:T(8,128)(2,1)}, bf16[4,32,896]{2,1,0:T(8,128)(2,1)S(1)}, u32[]{:S(2)}, u32[]{:S(2)}) collective-permute-start(bf16[4,32,896]{2,1,0:T(8,128)(2,1)} %get-tuple-element.65), channel_id=1, source_target_pairs={{0,16},{4,20},{8,24},{12,28},{16,0},{20,4},{24,8},{28,12},{1,17},{... | collective-permute-start | bytes 688136 | tf_op jit(solution)/shard_map/ppermute | solution.py:536
  29.8 17.8 %collective-permute-start.9 = (bf16[4,32,896]{2,1,0:T(8,128)(2,1)S(1)}, bf16[4,32,896]{2,1,0:T(8,128)(2,1)S(1)}, u32[]{:S(2)}, u32[]{:S(2)}) collective-permute-start(bf16[4,32,896]{2,1,0:T(8,128)(2,1)S(1)} %collective-permute-done.1.refs_2_), channel_id=1, source_target_pairs={{0,2},{1,3},{2,0},{3,1},{4,6},{5,7},{6,4},{7,5},{8,10},{9,11},{10,... | collective-permute-start | bytes 688136 | tf_op jit(solution)/shard_map/ppermute | solution.py:533
  30.9 20.4 %collective-permute-start.5 = (bf16[4,32,896]{2,1,0:T(8,128)(2,1)}, bf16[4,32,896]{2,1,0:T(8,128)(2,1)S(1)}, u32[]{:S(2)}, u32[]{:S(2)}) collective-permute-start(bf16[4,32,896]{2,1,0:T(8,128)(2,1)} %get-tuple-element.68), channel_id=1, source_target_pairs={{0,12},{4,16},{8,20},{12,24},{16,28},{20,0},{24,4},{28,8},{1,13},{... | collective-permute-start | bytes 688136 | tf_op jit(solution)/shard_map/ppermute | solution.py:536
  36.6 15.8 %collective-permute-start.14 = (bf16[4,32,896]{2,1,0:T(8,128)(2,1)S(1)}, bf16[4,32,896]{2,1,0:T(8,128)(2,1)S(1)}, u32[]{:S(2)}, u32[]{:S(2)}) collective-permute-start(bf16[4,32,896]{2,1,0:T(8,128)(2,1)S(1)} %collective-permute-done.4.refs_7_), channel_id=1, source_target_pairs={{0,2},{1,3},{2,0},{3,1},{4,6},{5,7},{6,4},{7,5},{8,10},{9,11},{10,... | collective-permute-start | bytes 688136 | tf_op jit(solution)/shard_map/ppermute | solution.py:533
  36.9 15.6 %collective-permute-start.13 = (bf16[4,32,896]{2,1,0:T(8,128)(2,1)S(1)}, bf16[4,32,896]{2,1,0:T(8,128)(2,1)S(1)}, u32[]{:S(2)}, u32[]{:S(2)}) collective-permute-start(bf16[4,32,896]{2,1,0:T(8,128)(2,1)S(1)} %collective-permute-done.6.refs_6_), channel_id=1, source_target_pairs={{0,2},{1,3},{2,0},{3,1},{4,6},{5,7},{6,4},{7,5},{8,10},{9,11},{10,... | collective-permute-start | bytes 688136 | tf_op jit(solution)/shard_map/ppermute | solution.py:533
  67.1 19.4 %collective-permute-start.15 = (bf16[16,32,896]{2,1,0:T(8,128)(2,1)S(1)}, bf16[16,32,896]{2,1,0:T(8,128)(2,1)S(1)}, u32[]{:S(2)}, u32[]{:S(2)}) collective-permute-start(bf16[16,32,896]{2,1,0:T(8,128)(2,1)S(1)} %get-tuple-element.71.refs_0_), channel_id=1, source_target_pairs={{0,1},{1,0},{2,3},{3,2},{4,5},{5,4},{6,7},{7,6},{8,9},{9,8},{10,11... | collective-permute-start | bytes 2752520 | tf_op jit(solution)/shard_map/ppermute | solution.py:530
  111.1 11.2 %collective-permute-start.18 = (s16[33,32,128]{2,1,0:T(8,128)(2,1)S(1)}, s16[33,32,128]{2,1,0:T(8,128)(2,1)S(1)}, u32[]{:S(2)}, u32[]{:S(2)}) collective-permute-start(s16[33,32,128]{2,1,0:T(8,128)(2,1)S(1)} %get-tuple-element.80), channel_id=1, source_target_pairs={{0,2},{1,3},{2,0},{3,1},{4,6},{5,7},{6,4},{7,5},{8,10},{9,11},{10,... | collective-permute-start | bytes 811016 | tf_op jit(solution)/shard_map/ppermute | solution.py:533
  123.1 13.5 %collective-permute-start.19 = (f32[1,16,32,512]{3,2,1,0:T(8,128)S(1)}, f32[1,16,32,512]{3,2,1,0:T(8,128)S(1)}, u32[]{:S(2)}, u32[]{:S(2)}) collective-permute-start(f32[1,16,32,512]{3,2,1,0:T(8,128)S(1)} %get-tuple-element.83), channel_id=1, source_target_pairs={{0,1},{1,0},{2,3},{3,2},{4,5},{5,4},{6,7},{7,6},{8,9},{9,8},{10,11... | collective-permute-start | bytes 3145736 | tf_op jit(solution)/shard_map/ppermute | solution.py:530
  130.2 12.8 %collective-permute-start.23 = (s16[65,32,128]{2,1,0:T(8,128)(2,1)S(1)}, s16[65,32,128]{2,1,0:T(8,128)(2,1)S(1)}, u32[]{:S(2)}, u32[]{:S(2)}) collective-permute-start(s16[65,32,128]{2,1,0:T(8,128)(2,1)S(1)} %far_codes.3), channel_id=1, source_target_pairs={{0,2},{1,3},{2,0},{3,1},{4,6},{5,7},{6,4},{7,5},{8,10},{9,11},{10,... | collective-permute-start | bytes 1597448 | tf_op jit(solution)/shard_map/ppermute | solution.py:533
  130.5 19.1 %collective-permute-start.31 = (s16[13,32,128]{2,1,0:T(8,128)(2,1)S(1)}, s16[13,32,128]{2,1,0:T(8,128)(2,1)S(1)}, u32[]{:S(2)}, u32[]{:S(2)}) collective-permute-start(s16[13,32,128]{2,1,0:T(8,128)(2,1)S(1)} %get-tuple-element.98), channel_id=1, source_target_pairs={{0,4},{4,8},{8,12},{12,16},{16,20},{20,24},{24,28},{28,0},{1,5},{5... | collective-permute-start | bytes 319496 | tf_op jit(solution)/shard_map/ppermute | solution.py:536
  135.8 13.9 %collective-permute-start.32 = (s16[13,32,128]{2,1,0:T(8,128)(2,1)S(1)}, s16[13,32,128]{2,1,0:T(8,128)(2,1)S(1)}, u32[]{:S(2)}, u32[]{:S(2)}) collective-permute-start(s16[13,32,128]{2,1,0:T(8,128)(2,1)S(1)} %get-tuple-element.99), channel_id=1, source_target_pairs={{0,8},{4,12},{8,16},{12,20},{16,24},{20,28},{24,0},{28,4},{1,9},{5... | collective-permute-start | bytes 319496 | tf_op jit(solution)/shard_map/ppermute | solution.py:536
  135.8 15.8 %collective-permute-start.33 = (s16[13,32,128]{2,1,0:T(8,128)(2,1)S(1)}, s16[13,32,128]{2,1,0:T(8,128)(2,1)S(1)}, u32[]{:S(2)}, u32[]{:S(2)}) collective-permute-start(s16[13,32,128]{2,1,0:T(8,128)(2,1)S(1)} %get-tuple-element.100), channel_id=1, source_target_pairs={{0,12},{4,16},{8,20},{12,24},{16,28},{20,0},{24,4},{28,8},{1,13},{... | collective-permute-start | bytes 319496 | tf_op jit(solution)/shard_map/ppermute | solution.py:536
  136.6 15.1 %collective-permute-start.34 = (s16[13,32,128]{2,1,0:T(8,128)(2,1)S(1)}, s16[13,32,128]{2,1,0:T(8,128)(2,1)S(1)}, u32[]{:S(2)}, u32[]{:S(2)}) collective-permute-start(s16[13,32,128]{2,1,0:T(8,128)(2,1)S(1)} %get-tuple-element.101), channel_id=1, source_target_pairs={{0,16},{4,20},{8,24},{12,28},{16,0},{20,4},{24,8},{28,12},{1,17},{... | collective-permute-start | bytes 319496 | tf_op jit(solution)/shard_map/ppermute | solution.py:536
  144.3 23.6 %collective-permute-start.24 = (s16[17,32,128]{2,1,0:T(8,128)(2,1)S(1)}, s16[17,32,128]{2,1,0:T(8,128)(2,1)S(1)}, u32[]{:S(2)}, u32[]{:S(2)}) collective-permute-start(s16[17,32,128]{2,1,0:T(8,128)(2,1)S(1)} %get-tuple-element.91), channel_id=1, source_target_pairs={{0,4},{4,8},{8,12},{12,16},{16,20},{20,24},{24,28},{28,0},{1,5},{5... | collective-permute-start | bytes 417800 | tf_op jit(solution)/shard_map/ppermute | solution.py:536
  149.6 18.2 %collective-permute-start.25 = (s16[17,32,128]{2,1,0:T(8,128)(2,1)S(1)}, s16[17,32,128]{2,1,0:T(8,128)(2,1)S(1)}, u32[]{:S(2)}, u32[]{:S(2)}) collective-permute-start(s16[17,32,128]{2,1,0:T(8,128)(2,1)S(1)} %get-tuple-element.92), channel_id=1, source_target_pairs={{0,8},{4,12},{8,16},{12,20},{16,24},{20,28},{24,0},{28,4},{1,9},{5... | collective-permute-start | bytes 417800 | tf_op jit(solution)/shard_map/ppermute | solution.py:536
  151.6 13.8 %collective-permute-start.37 = (s16[13,32,128]{2,1,0:T(8,128)(2,1)S(1)}, s16[13,32,128]{2,1,0:T(8,128)(2,1)S(1)}, u32[]{:S(2)}, u32[]{:S(2)}) collective-permute-start(s16[13,32,128]{2,1,0:T(8,128)(2,1)S(1)} %get-tuple-element.104), channel_id=1, source_target_pairs={{0,28},{4,0},{8,4},{12,8},{16,12},{20,16},{24,20},{28,24},{1,29},{... | collective-permute-start | bytes 319496 | tf_op jit(solution)/shard_map/ppermute | solution.py:536
  158.4 17.9 %collective-permute-start.26 = (s16[17,32,128]{2,1,0:T(8,128)(2,1)S(1)}, s16[17,32,128]{2,1,0:T(8,128)(2,1)S(1)}, u32[]{:S(2)}, u32[]{:S(2)}) collective-permute-start(s16[17,32,128]{2,1,0:T(8,128)(2,1)S(1)} %get-tuple-element.93), channel_id=1, source_target_pairs={{0,12},{4,16},{8,20},{12,24},{16,28},{20,0},{24,4},{28,8},{1,13},{... | collective-permute-start | bytes 417800 | tf_op jit(solution)/shard_map/ppermute | solution.py:536
  161.9 17.3 %collective-permute-start.27 = (s16[17,32,128]{2,1,0:T(8,128)(2,1)S(1)}, s16[17,32,128]{2,1,0:T(8,128)(2,1)S(1)}, u32[]{:S(2)}, u32[]{:S(2)}) collective-permute-start(s16[17,32,128]{2,1,0:T(8,128)(2,1)S(1)} %get-tuple-element.94), channel_id=1, source_target_pairs={{0,16},{4,20},{8,24},{12,28},{16,0},{20,4},{24,8},{28,12},{1,17},{... | collective-permute-start | bytes 417800 | tf_op jit(solution)/shard_map/ppermute | solution.py:536
  165.5 13.8 %collective-permute-start.28 = (s16[17,32,128]{2,1,0:T(8,128)(2,1)S(1)}, s16[17,32,128]{2,1,0:T(8,128)(2,1)S(1)}, u32[]{:S(2)}, u32[]{:S(2)}) collective-permute-start(s16[17,32,128]{2,1,0:T(8,128)(2,1)S(1)} %get-tuple-element.95), channel_id=1, source_target_pairs={{0,20},{4,24},{8,28},{12,0},{16,4},{20,8},{24,12},{28,16},{1,21},{... | collective-permute-start | bytes 417800 | tf_op jit(solution)/shard_map/ppermute | solution.py:536
  167.8 13.1 %collective-permute-start.29 = (s16[17,32,128]{2,1,0:T(8,128)(2,1)S(1)}, s16[17,32,128]{2,1,0:T(8,128)(2,1)S(1)}, u32[]{:S(2)}, u32[]{:S(2)}) collective-permute-start(s16[17,32,128]{2,1,0:T(8,128)(2,1)S(1)} %get-tuple-element.96), channel_id=1, source_target_pairs={{0,24},{4,28},{8,0},{12,4},{16,8},{20,12},{24,16},{28,20},{1,25},{... | collective-permute-start | bytes 417800 | tf_op jit(solution)/shard_map/ppermute | solution.py:536
  167.8 17.7 %collective-permute-start.30 = (s16[17,32,128]{2,1,0:T(8,128)(2,1)S(1)}, s16[17,32,128]{2,1,0:T(8,128)(2,1)S(1)}, u32[]{:S(2)}, u32[]{:S(2)}) collective-permute-start(s16[17,32,128]{2,1,0:T(8,128)(2,1)S(1)} %get-tuple-element.97), channel_id=1, source_target_pairs={{0,28},{4,0},{8,4},{12,8},{16,12},{20,16},{24,20},{28,24},{1,29},{... | collective-permute-start | bytes 417800 | tf_op jit(solution)/shard_map/ppermute | solution.py:536
  (25 other events, 302.2 us)

commit v11 on v10

--- a/solution.py
+++ b/solution.py
@@ -11,9 +11,10 @@
 HD = 128
 SPAN = 64
 LANES = 128
+TILE = 16
 WINDOW = 4
 VMEM_LIMIT = 28 * 1024 * 1024
-VMEM_MORE = 40 * 1024 * 1024
+VMEM_MORE = 46 * 1024 * 1024
 VMEM_ALL = 60 * 1024 * 1024
 F32 = jnp.float32
 BF16 = jnp.bfloat16
@@ -140,63 +141,15 @@
     )(request, *[block for blocks in lists for block in blocks])
 
 
-def weight_specs(rows, step):
-    return [
-        pl.BlockSpec((rows, step), lambda i: (0, jnp.minimum(i, 1))),
-        pl.BlockSpec((rows, step), lambda i: (0, jnp.maximum(i - 2, 0))),
-    ]
-
-
-def with_weight(wk, wv, act):
-    @pl.when(pl.program_id(0) < 2)
-    def _():
-        act(wk)
-
-    @pl.when(pl.program_id(0) >= 2)
-    def _():
-        act(wv)
-
-
-def project_body(n_in, *refs):
-    wk, wv, out = refs[n_in : n_in + 3]
-    n, sub, enc = refs[0].shape
-    rows = jnp.concatenate([ref[...].reshape(n * sub, enc) for ref in refs[:n_in]], axis=0)
-
-    def act(w):
-        res = jnp.dot(rows, w[...], preferred_element_type=F32)
-        out[...] = res.astype(BF16).reshape(out.shape)
-
-    with_weight(wk, wv, act)
-
-
-def project(pieces, wk, wv):
-    n_in = len(pieces)
-    n, sub, enc = pieces[0].shape
-    width = 2 * wk.shape[1]
-    step = width // 4
-    return pl.pallas_call(
-        functools.partial(project_body, n_in),
-        out_shape=jax.ShapeDtypeStruct((n_in, n, sub, width), BF16),
-        grid=(4,),
-        in_specs=[pl.BlockSpec((n, sub, enc), lambda i: (0, 0, 0))] * n_in
-        + weight_specs(enc, step),
-        out_specs=pl.BlockSpec((n_in, n, sub, step), lambda i: (0, 0, 0, i)),
-        compiler_params=params(),
-        cost_estimate=cost(
-            2 * n_in * n * sub * enc * width, 2 * (n_in * n * sub * (enc + width) + enc * width)
-        ),
-        name="project",
-    )(*pieces, wk, wv)
-
-
-def attend_body(places, n_kv, n_late, near, *refs):
-    kvs, late = refs[:n_kv], refs[n_kv : n_kv + n_late]
-    wk, wv, q_ref, g_ref, att_ref, dq_ref = refs[n_kv + n_late : n_kv + n_late + 6]
-    *grads, near_out, far_out, own_out, late_kv, own_all, core_all = refs[n_kv + n_late + 6 :]
+def attend_body(places, near, *refs):
+    n_in = len(places)
+    pieces = refs[:n_in]
+    wk, wv, q_ref, g_ref, att_ref, dq_ref = refs[n_in : n_in + 6]
+    *grads, near_out, far_out, own_out, key_value, own_all, core_all = refs[n_in + 6 :]
     step = pl.program_id(0)
     width = q_ref.shape[1]
     enc = wk.shape[0]
-    sub = late_kv.shape[2]
+    sub = key_value.shape[2]
     scale = 1.0 / math.sqrt(HD)
     heads = width // HD
     group = min(8, heads)
@@ -208,18 +161,16 @@
 
     @pl.when(step == 0)
     def _():
-        rows = jnp.concatenate([ref[...].reshape(-1, enc) for ref in late], axis=0)
-        shape = late_kv.shape[:3] + (width,)
-        late_kv[:, :, :, :width] = dot(rows, wk[...]).astype(BF16).reshape(shape)
-        late_kv[:, :, :, width:] = dot(rows, wv[...]).astype(BF16).reshape(shape)
+        for i, ref in enumerate(pieces):
+            rows = ref[...].reshape(-1, enc)
+            shape = ref.shape[:2] + (width,)
+            key_value[i, :, :, :width] = dot(rows, wk[...]).astype(BF16).reshape(shape)
+            key_value[i, :, :, width:] = dot(rows, wv[...]).astype(BF16).reshape(shape)
 
     mine = pl.ds(2 * step, 2)
 
     def rows_of(col):
-        cols = pl.ds(col, HD)
-        parts = [ref[:, :, :, cols].reshape(-1, HD) for ref in kvs]
-        parts.append(late_kv[:, mine, :, cols].reshape(-1, HD))
-        return jnp.concatenate(parts, axis=0)
+        return key_value[:, mine, :, pl.ds(col, HD)].reshape(-1, HD)
 
     def put(col, grad):
         cols = pl.ds(col, HD)
@@ -270,45 +221,42 @@
                 outs[1][...] = res[near:]
 
 
-def attend(kvs, late, wk, wv, places, near, count, queries, cotangent):
+def attend(pieces, wk, wv, places, near, count, queries, cotangent):
     tokens, width = queries.shape
-    spans = tokens // SPAN
-    n, sub = kvs[0].shape[1:3]
-    enc = wk.shape[0]
-    pieces = len(places) // 2
+    n, sub, enc = pieces[0].shape
+    total = len(places)
+    half = total // 2
     rows = pl.BlockSpec((SPAN, width), lambda i: (i, 0))
-
-    def kv_block(pieces):
-        return pl.BlockSpec((pieces, 2, sub, 2 * width), lambda i: (0, i, 0, 0))
+    grads = pl.BlockSpec((half, 2, sub, 2 * width), lambda i: (0, i, 0, 0))
+
+    def once(shape):
+        return pl.BlockSpec(shape, lambda i: (0,) * len(shape), pipeline_mode=pl.Buffered(1))
 
     def whole(shape):
         return pl.BlockSpec(shape, lambda i: (0,) * len(shape))
 
-    keys = len(places) * 2 * sub
-    parts = [(near, n, sub, count), (pieces - near, n, sub, count), (pieces, n, sub, count)]
-    every = (pieces, n, sub, 2 * width)
-    return pl.pallas_call(
-        functools.partial(attend_body, places, len(kvs), len(late), near),
+    parts = [(near, n, sub, count), (half - near, n, sub, count), (half, n, sub, count)]
+    every = (half, n, sub, 2 * width)
+    return pl.pallas_call(
+        functools.partial(attend_body, places, near),
         out_shape=[jax.ShapeDtypeStruct((tokens, width), BF16)] * 2
         + [jax.ShapeDtypeStruct(every, BF16)] * 2
         + [jax.ShapeDtypeStruct(part, F32) for part in parts],
-        grid=(spans,),
-        in_specs=[kv_block(kv.shape[0]) for kv in kvs]
-        + [whole(x.shape) for x in late]
-        + [whole(wk.shape), whole(wv.shape), rows, rows],
-        out_specs=[rows, rows] + [kv_block(pieces)] * 2 + [whole(part) for part in parts],
+        grid=(tokens // SPAN,),
+        in_specs=[once(x.shape) for x in pieces] + [once(wk.shape), once(wv.shape), rows, rows],
+        out_specs=[rows, rows, grads, grads] + [whole(part) for part in parts],
         scratch_shapes=[
-            pltpu.VMEM((len(late), n, sub, 2 * width), BF16),
+            pltpu.VMEM((total, n, sub, 2 * width), BF16),
             pltpu.VMEM(every, BF16),
             pltpu.VMEM(every, BF16),
         ],
         compiler_params=params(VMEM_MORE),
         cost_estimate=cost(
-            16 * tokens * width * keys + 4 * n * sub * width * (len(late) * enc + 2 * pieces * count),
-            8 * tokens * width + 8 * spans * keys * 2 * width,
+            16 * tokens * width * total * 2 * sub + 4 * n * sub * width * total * (enc + count),
+            8 * tokens * width + 8 * total * n * sub * width,
         ),
         name="attend",
-    )(*kvs, *late, wk, wv, queries, cotangent)
+    )(*pieces, wk, wv, queries, cotangent)
 
 
 def encode(x, axes):
@@ -377,7 +325,7 @@
             pltpu.VMEM((2 * n_x, n, sub, count), F32),
             pltpu.SemaphoreType.DMA((2 * n_x,)),
         ],
-        compiler_params=params(),
+        compiler_params=params(VMEM_ALL),
         cost_estimate=cost(4 * rows * count * width, 2 * (count + 2 * rows) * width + 8 * rows * count),
         name="grads",
     )(d_core, d_own, wk, wv)
@@ -438,28 +386,31 @@
             total = total + jnp.concatenate(blocks, axis=1)
         coded, power = encode(total, (0, 1))
         for e in range(tiles):
-            stage[r, e] = coded[:, e * LANES : (e + 1) * LANES]
-        powers[r] = jnp.broadcast_to(power, (sub, LANES))
-    row = lax.broadcasted_iota(jnp.int32, (sub, LANES), 0)
+            for h in range(sub // TILE):
+                block = coded[h * TILE : (h + 1) * TILE, e * LANES : (e + 1) * LANES]
+                stage[r, e * (sub // TILE) + h] = block
+        powers[r] = jnp.broadcast_to(power, (TILE, LANES))
+    row = lax.broadcasted_iota(jnp.int32, (TILE, LANES), 0)
+    size = stage.shape[1]
     for d in range(n_dp):
-        note = jnp.zeros((sub, LANES), F32)
+        note = jnp.zeros((TILE, LANES), F32)
         for j in range(cap):
             r = request[d * cap + j]
 
             @pl.when(r >= 0)
             def _():
-                outs[d][pl.ds(j * tiles, tiles)] = stage[r]
+                outs[d][pl.ds(j * size, size)] = stage[r]
 
             note = jnp.where(row == j, powers[jnp.maximum(r, 0)], note)
-        outs[d][cap * tiles] = note.astype(jnp.int32).astype(jnp.int16)
+        outs[d][cap * size] = note.astype(jnp.int32).astype(jnp.int16)
 
 
 def send_codes(request, own, got, codes, cuts, n_dp):
     _, n, sub, count = got.shape
     block = pl.BlockSpec(got.shape, lambda i: (0, 0, 0, 0))
-    tiles = count // LANES
+    size = count // LANES * (sub // TILE)
     cap = request.shape[0] // n_dp
-    shape = (cap * tiles + 1, sub, LANES)
+    shape = (cap * size + 1, TILE, LANES)
     codes = [x for piece in codes for x in piece]
     return pl.pallas_call(
         functools.partial(send_body, n_dp, cuts),
@@ -468,8 +419,8 @@
         in_specs=[SMEM, block, block] + [VMEM] * len(codes),
         out_specs=[VMEM] * n_dp,
         scratch_shapes=[
-            pltpu.VMEM((n, tiles, sub, LANES), jnp.int16),
-            pltpu.VMEM((n, sub, LANES), F32),
+            pltpu.VMEM((n, size, TILE, LANES), jnp.int16),
+            pltpu.VMEM((n, TILE, LANES), F32),
         ],
         compiler_params=params(),
         cost_estimate=cost(10 * got.size, 6 * got.size + 2 * n_dp * math.prod(shape)),
@@ -480,7 +431,8 @@
 def gather_body(n_dp, first, me, asked, *refs):
     arrived = refs[:n_dp]
     out, total, sem = refs[-3:]
-    tiles = total.shape[2] // LANES
+    tiles, halves = total.shape[2] // LANES, total.shape[1] // TILE
+    size = tiles * halves
     cap = asked.shape[1] // n_dp
     total[...] = jnp.zeros_like(total)
     for d in range(n_dp):
@@ -489,11 +441,12 @@
 
             @pl.when(slab >= 0)
             def _():
-                note = arrived[d][cap * tiles].astype(F32)
+                note = arrived[d][cap * size].astype(F32)
                 unit = jnp.exp2(note[j : j + 1] - 15.0)
                 for e in range(tiles):
-                    value = arrived[d][j * tiles + e].astype(F32) * unit
-                    total[slab, :, pl.ds(e * LANES, LANES)] += value
+                    for h in range(halves):
+                        value = arrived[d][j * size + e * halves + h].astype(F32) * unit
+                        total[slab, pl.ds(h * TILE, TILE), pl.ds(e * LANES, LANES)] += value
 
     copy = pltpu.make_async_copy(total, out.at[:, :, pl.ds(first, total.shape[2])], sem)
     copy.start()
@@ -558,15 +511,14 @@
     lists += [[far[d][k] for d in range(n_dp)] for k in range(n_x - 1)]
     mine, *far = compact(request, lists, n_requests)
 
-    early = [mine, *far]
-    late = [over_core(x) for x in early]
-    kvs = [project(early, key_weight, value_weight)]
+    pieces = [mine, *far]
+    pieces += [over_core(x) for x in pieces]
     places = [(kind, k) for kind in range(2) for k in range(n_x)]
 
     split = 3 * LANES
     parts = ((0, split), (split, enc - split))
     attended, d_query, d_own, d_core, near, far, own = attend(
-        kvs, late, key_weight, value_weight, places, 1, split, queries, cotangent
+        pieces, key_weight, value_weight, places, 1, split, queries, cotangent
     )
     far_got = over_core(far)
     near_got = over_core(near)

time: 189 us -> 189 us (level)
  local copies, waits for them, and re-layouts: 8.82 us -> 2.37 us
  Pallas kernels: 52.4 us -> 56.6 us
  starting transfers between devices: 62.1 us -> 64.8 us
    unnamed x22 -> x16, local copies, waits for them, and re-layouts: 8.82 us -> 2.37 us
    pallas_call x1, Pallas kernels: 5.55 us -> 10.3 us  [grads_of(): pl.pallas_call(functools.partial(grads_body, first), out_shape=[jax.Shape...]
    ppermute x6, waiting for transfers between devices: 4.53 us -> 8.99 us  [over_core(): return lax.ppermute(x, 'tensor', [(t, t ^ 1) for t in range(n_tp)])]
    ppermute x21, waiting for transfers between devices: 36.2 us -> 33.2 us  [over_dp(): return lax.ppermute(x, 'dp', [(i, (i + d) % n_dp) for i in range(n_dp)])]
    ppermute x21, starting transfers between devices: 41.1 us -> 43 us  [over_dp(): return lax.ppermute(x, 'dp', [(i, (i + d) % n_dp) for i in range(n_dp)])]
    pallas_call x2 -> x1, Pallas kernels: 28.1 us -> 27.5 us  [attend(): pl.pallas_call(functools.partial(attend_body, places, near), out_shape=[j...]
  transfers between devices with their start and end apart: 38 -> 38, of which waited for: 17 -> 18; matrix products, arithmetic and copies ran while one was open for 0% -> 0% of each run, Pallas kernels for 9% -> 9%
where the time goes in v11:
time: 189 us
  starting transfers between devices  64.8 us (34%)
  Pallas kernels  56.6 us (30%)
  waiting for transfers between devices  55.3 us (29%)
  blocking collectives  8.6 us (5%)
  local copies, waits for them, and re-layouts  2.37 us (1%)
    ppermute x21, starting transfers between devices, over_dp(): return lax.ppermute(x, 'dp', [(i, (i + d) % n_dp) for i in range(n_dp)])  43 us
    ppermute x21, waiting for transfers between devices, over_dp(): return lax.ppermute(x, 'dp', [(i, (i + d) % n_dp) for i in range(n_dp)])  33.2 us
    pallas_call x1, Pallas kernels, attend(): pl.pallas_call(functools.partial(attend_body, places, near), out_shape=[j...  27.5 us
    ppermute x11, waiting for transfers between devices, over_x(): lax.ppermute(x, 'tensor', [(t, (t + 2 * d) % n_tp) for t in range(n_tp)])  13.1 us
    ppermute x6, starting transfers between devices, over_core(): return lax.ppermute(x, 'tensor', [(t, t ^ 1) for t in range(n_tp)])  11.8 us
    pallas_call x1, Pallas kernels, grads_of(): pl.pallas_call(functools.partial(grads_body, first), out_shape=[jax.Shape...  10.3 us
    ppermute x11, starting transfers between devices, over_x(): lax.ppermute(x, 'tensor', [(t, (t + 2 * d) % n_tp) for t in range(n_tp)])  9.97 us
    ppermute x6, waiting for transfers between devices, over_core(): return lax.ppermute(x, 'tensor', [(t, t ^ 1) for t in range(n_tp)])  8.99 us
  transfers between devices with their start and end apart: 38, of which 18 were waited for; matrix products, arithmetic and copies ran while one was open for 0% of the time, Pallas kernels for 9%

profile of v11, /device:TPU:13, one launch (start us, length us, event | category | flops | bytes accessed | tf_op | source)
XLA Modules:
  0.0 188.7 jit_solution(5155806177812971563)
XLA Ops:
  2.2 8.6 %psum.7.asked = s32[8,32]{1,0:T(8,128)} all-reduce(s32[8,32]{1,0:T(8,128)} %get-tuple-element.56), channel_id=1, replica_groups=mesh['dp'=8,'tensor'=4] {'dp'}, use_global_device_ids=true, to_apply=%region_0.0 | all-reduce | flops 256 | bytes 2048 | tf_op jit(solution)/shard_map/psum | solution.py:499
  10.8 4.1 %pack_rows.1 = (bf16[4,32,896]{2,1,0:T(8,128)(2,1)}, bf16[4,32,896]{2,1,0:T(8,128)(2,1)}, bf16[4,32,896]{2,1,0:T(8,128)(2,1)}, bf16[4,32,896]{2,1,0:T(8,128)(2,1...) custom-call(s32[1]{0:T(128)} %get-tuple-element.55.me, ...), custom_call_target="tpu_custom_call" | custom-call | bytes 3670016 | tf_op jit(solution)/shard_map/pack_rows/pallas_call | solution.py:98
  22.3 3.0 %collective-permute-done.4.refs_7_ = bf16[4,32,896]{2,1,0:T(8,128)(2,1)S(1)} collective-permute-done((bf16[4,32,896]{2,1,0:T(8,128)(2,1)}, bf16[4,32,896]{2,1,0:T(8,128)(2,1)S(1)}, u32[]{:S(2)}, u32[]{:S(2)}) %collective-permute-start.4) | collective-permute-done | bytes 229408 | tf_op jit(solution)/shard_map/ppermute | solution.py:489
  30.8 5.7 %collective-permute-start.5 = (bf16[4,32,896]{2,1,0:T(8,128)(2,1)}, bf16[4,32,896]{2,1,0:T(8,128)(2,1)S(1)}, u32[]{:S(2)}, u32[]{:S(2)}) collective-permute-start(bf16[4,32,896]{2,1,0:T(8,128)(2,1)} %get-tuple-element.68), channel_id=1, source_target_pairs={{0,12},{4,16},{8,20},{12,24},{16,28},{20,0},{24,4},{28,8},{1,13},{... | collective-permute-start | bytes 688136 | tf_op jit(solution)/shard_map/ppermute | solution.py:489
  37.9 8.0 %collective-permute-done.3.refs_4_ = bf16[4,32,896]{2,1,0:T(8,128)(2,1)S(1)} collective-permute-done((bf16[4,32,896]{2,1,0:T(8,128)(2,1)}, bf16[4,32,896]{2,1,0:T(8,128)(2,1)S(1)}, u32[]{:S(2)}, u32[]{:S(2)}) %collective-permute-start.3) | collective-permute-done | bytes 229408 | tf_op jit(solution)/shard_map/ppermute | solution.py:489
  47.4 3.4 %collective-permute-done.5.refs_5_ = bf16[4,32,896]{2,1,0:T(8,128)(2,1)S(1)} collective-permute-done((bf16[4,32,896]{2,1,0:T(8,128)(2,1)}, bf16[4,32,896]{2,1,0:T(8,128)(2,1)S(1)}, u32[]{:S(2)}, u32[]{:S(2)}) %collective-permute-start.5) | collective-permute-done | bytes 229408 | tf_op jit(solution)/shard_map/ppermute | solution.py:489
  52.2 4.0 %collective-permute-done.11.refs_12_ = bf16[4,32,896]{2,1,0:T(8,128)(2,1)S(1)} collective-permute-done((bf16[4,32,896]{2,1,0:T(8,128)(2,1)S(1)}, bf16[4,32,896]{2,1,0:T(8,128)(2,1)S(1)}, u32[]{:S(2)}, u32[]{:S(2)}) %collective-permute-start.11) | collective-permute-done | bytes 229408 | tf_op jit(solution)/shard_map/ppermute | solution.py:486
  56.2 4.9 %collective-permute-done.12.refs_13_ = bf16[4,32,896]{2,1,0:T(8,128)(2,1)S(1)} collective-permute-done((bf16[4,32,896]{2,1,0:T(8,128)(2,1)S(1)}, bf16[4,32,896]{2,1,0:T(8,128)(2,1)S(1)}, u32[]{:S(2)}, u32[]{:S(2)}) %collective-permute-start.12) | collective-permute-done | bytes 229408 | tf_op jit(solution)/shard_map/ppermute | solution.py:486
  62.1 4.2 %compact_rows.1 = (bf16[16,32,896]{2,1,0:T(8,128)(2,1)S(1)}, bf16[16,32,896]{2,1,0:T(8,128)(2,1)S(1)}) custom-call(s32[32]{0:T(128)S(1)} %copy-done.5, bf16[4,32,896]{2,1,0:T(8,128)(2,1)S(1)} %copy-done.3, bf16[4,32,896]{2,1,0:T(8,128)(2,1)S(1)} %collective-permute-done.refs_1_, bf16[4,32,896]{2,1,0:T(8,128)(2,1)S(1)} %collective-permute-done.1.refs_2_, ...), custom_call_target="tpu_custom_call" | custom-call | bytes 3670016 | tf_op jit(solution)/shard_map/compact_rows/pallas_call | solution.py:132
  66.3 10.1 %collective-permute-start.15 = (bf16[16,32,896]{2,1,0:T(8,128)(2,1)S(1)}, bf16[16,32,896]{2,1,0:T(8,128)(2,1)S(1)}, u32[]{:S(2)}, u32[]{:S(2)}) collective-permute-start(bf16[16,32,896]{2,1,0:T(8,128)(2,1)S(1)} %get-tuple-element.71.refs_0_), channel_id=1, source_target_pairs={{0,1},{1,0},{2,3},{3,2},{4,5},{5,4},{6,7},{7,6},{8,9},{9,8},{10,11... | collective-permute-start | bytes 2752520 | tf_op jit(solution)/shard_map/ppermute | solution.py:483
  79.8 27.5 %attend.1 = (bf16[512,1024]{1,0:T(8,128)(2,1)}, bf16[512,1024]{1,0:T(8,128)(2,1)}, bf16[2,16,32,2048]{3,2,1,0:T(8,128)(2,1)}, bf16[2,16,32,2048]{3,2,1,0:T(8,128...) custom-call(bf16[16,32,896]{2,1,0:T(8,128)(2,1)S(1)} %get-tuple-element.71.refs_0, ...), custom_call_target="tpu_custom_call" | custom-call | flops 12884901888 | bytes 20971520 | tf_op jit(solution)/shard_map/attend/pallas_call | solution.py:240
  112.7 10.3 %grads.1 = (f32[1,16,32,512]{3,2,1,0:T(8,128)}, f32[1,16,32,512]{3,2,1,0:T(8,128)}, f32[2,16,32,512]{3,2,1,0:T(8,128)}) custom-call(bf16[2,16,32,2048]{3,2,1,0:T(8,128)(2,1)} %get-tuple-element.75.core_ref, bf16[2,16,32,2048]{3,2,1,0:T(8,128)(2,1)} %get-tuple-element.76.own_ref, bf16[896,1024]{1,0:T(8,128)(2,1)} %wk.1, bf16[896,1024]{1,0:T(8,128)(2,1)} %wv.1), custom_call_target="tpu_custom_call" | custom-call | flops 4294967296 | bytes 14680064 | tf_op jit(solution)/shard_map/grads/pallas_call | solution.py:313
  124.4 3.7 %collective-permute-done.21.got = f32[1,16,32,384]{3,2,1,0:T(8,128)S(1)} collective-permute-done((f32[1,16,32,384]{3,2,1,0:T(8,128)S(1)}, f32[1,16,32,384]{3,2,1,0:T(8,128)S(1)}, u32[]{:S(2)}, u32[]{:S(2)}) %collective-permute-start.21) | collective-permute-done | bytes 786464 | tf_op jit(solution)/shard_map/ppermute | solution.py:483
  131.3 5.4 %collective-permute-start.31 = (s16[25,16,128]{2,1,0:T(8,128)(2,1)S(1)}, s16[25,16,128]{2,1,0:T(8,128)(2,1)S(1)}, u32[]{:S(2)}, u32[]{:S(2)}) collective-permute-start(s16[25,16,128]{2,1,0:T(8,128)(2,1)S(1)} %get-tuple-element.98), channel_id=1, source_target_pairs={{0,4},{4,8},{8,12},{12,16},{16,20},{20,24},{24,28},{28,0},{1,5},{5... | collective-permute-start | bytes 307208 | tf_op jit(solution)/shard_map/ppermute | solution.py:489
  137.7 3.2 %collective-permute-start.34 = (s16[25,16,128]{2,1,0:T(8,128)(2,1)S(1)}, s16[25,16,128]{2,1,0:T(8,128)(2,1)S(1)}, u32[]{:S(2)}, u32[]{:S(2)}) collective-permute-start(s16[25,16,128]{2,1,0:T(8,128)(2,1)S(1)} %get-tuple-element.101), channel_id=1, source_target_pairs={{0,16},{4,20},{8,24},{12,28},{16,0},{20,4},{24,8},{28,12},{1,17},{... | collective-permute-start | bytes 307208 | tf_op jit(solution)/shard_map/ppermute | solution.py:489
  140.9 3.0 %collective-permute-done.23.rest_0_ = s16[65,32,128]{2,1,0:T(8,128)(2,1)S(1)} collective-permute-done((s16[65,32,128]{2,1,0:T(8,128)(2,1)S(1)}, s16[65,32,128]{2,1,0:T(8,128)(2,1)S(1)}, u32[]{:S(2)}, u32[]{:S(2)}) %collective-permute-start.23) | collective-permute-done | bytes 532512 | tf_op jit(solution)/shard_map/ppermute | solution.py:486
  145.2 5.3 %collective-permute-start.24 = (s16[33,16,128]{2,1,0:T(8,128)(2,1)S(1)}, s16[33,16,128]{2,1,0:T(8,128)(2,1)S(1)}, u32[]{:S(2)}, u32[]{:S(2)}) collective-permute-start(s16[33,16,128]{2,1,0:T(8,128)(2,1)S(1)} %get-tuple-element.91), channel_id=1, source_target_pairs={{0,4},{4,8},{8,12},{12,16},{16,20},{20,24},{24,28},{28,0},{1,5},{5... | collective-permute-start | bytes 405512 | tf_op jit(solution)/shard_map/ppermute | solution.py:489
  152.7 3.2 %collective-permute-start.37 = (s16[25,16,128]{2,1,0:T(8,128)(2,1)S(1)}, s16[25,16,128]{2,1,0:T(8,128)(2,1)S(1)}, u32[]{:S(2)}, u32[]{:S(2)}) collective-permute-start(s16[25,16,128]{2,1,0:T(8,128)(2,1)S(1)} %get-tuple-element.104), channel_id=1, source_target_pairs={{0,28},{4,0},{8,4},{12,8},{16,12},{20,16},{24,20},{28,24},{1,29},{... | collective-permute-start | bytes 307208 | tf_op jit(solution)/shard_map/ppermute | solution.py:489
  158.0 4.4 %collective-permute-start.26 = (s16[33,16,128]{2,1,0:T(8,128)(2,1)S(1)}, s16[33,16,128]{2,1,0:T(8,128)(2,1)S(1)}, u32[]{:S(2)}, u32[]{:S(2)}) collective-permute-start(s16[33,16,128]{2,1,0:T(8,128)(2,1)S(1)} %get-tuple-element.93), channel_id=1, source_target_pairs={{0,12},{4,16},{8,20},{12,24},{16,28},{20,0},{24,4},{28,8},{1,13},{... | collective-permute-start | bytes 405512 | tf_op jit(solution)/shard_map/ppermute | solution.py:489
  162.4 3.8 %collective-permute-start.27 = (s16[33,16,128]{2,1,0:T(8,128)(2,1)S(1)}, s16[33,16,128]{2,1,0:T(8,128)(2,1)S(1)}, u32[]{:S(2)}, u32[]{:S(2)}) collective-permute-start(s16[33,16,128]{2,1,0:T(8,128)(2,1)S(1)} %get-tuple-element.94), channel_id=1, source_target_pairs={{0,16},{4,20},{8,24},{12,28},{16,0},{20,4},{24,8},{28,12},{1,17},{... | collective-permute-start | bytes 405512 | tf_op jit(solution)/shard_map/ppermute | solution.py:489
  171.7 5.7 %collective-permute-done.26.refs_3_ = s16[33,16,128]{2,1,0:T(8,128)(2,1)S(1)} collective-permute-done((s16[33,16,128]{2,1,0:T(8,128)(2,1)S(1)}, s16[33,16,128]{2,1,0:T(8,128)(2,1)S(1)}, u32[]{:S(2)}, u32[]{:S(2)}) %collective-permute-start.26) | collective-permute-done | bytes 135200 | tf_op jit(solution)/shard_map/ppermute | solution.py:489
  177.4 2.9 %collective-permute-done.27.refs_4_ = s16[33,16,128]{2,1,0:T(8,128)(2,1)S(1)} collective-permute-done((s16[33,16,128]{2,1,0:T(8,128)(2,1)S(1)}, s16[33,16,128]{2,1,0:T(8,128)(2,1)S(1)}, u32[]{:S(2)}, u32[]{:S(2)}) %collective-permute-start.27) | collective-permute-done | bytes 135200 | tf_op jit(solution)/shard_map/ppermute | solution.py:489
  180.7 4.9 %collective-permute-done.30.refs_7_ = s16[33,16,128]{2,1,0:T(8,128)(2,1)S(1)} collective-permute-done((s16[33,16,128]{2,1,0:T(8,128)(2,1)S(1)}, s16[33,16,128]{2,1,0:T(8,128)(2,1)S(1)}, u32[]{:S(2)}, u32[]{:S(2)}) %collective-permute-start.30) | collective-permute-done | bytes 135200 | tf_op jit(solution)/shard_map/ppermute | solution.py:489
  185.6 2.9 %gather_grads.3 = f32[16,32,896]{2,1,0:T(8,128)} custom-call(s32[1]{0:T(128)} %get-tuple-element.55.me, s32[8,32]{1,0:T(8,128)S(1)} %copy-done.4, s16[33,16,128]{2,1,0:T(8,128)(2,1)S(1)} %get-tuple-element.90.refs_0_, s16[33,16,128]{2,1,0:T(8,128)(2,1)S(1)} %collective-permute-done.24.refs_1_, ...), custom_call_target="tpu_custom_call", output_to_operand_aliasing={{}: (10, {})} | custom-call | bytes 2097152 | tf_op jit(solution)/shard_map/gather_grads/pallas_call | solution.py:459
  (80 shorter events, 45.5 us)
Async XLA Ops:
  18.8 12.0 %collective-permute-start.7 = (bf16[4,32,896]{2,1,0:T(8,128)(2,1)}, bf16[4,32,896]{2,1,0:T(8,128)(2,1)S(1)}, u32[]{:S(2)}, u32[]{:S(2)}) collective-permute-start(bf16[4,32,896]{2,1,0:T(8,128)(2,1)} %get-tuple-element.57.refs_0_), channel_id=1, source_target_pairs={{0,2},{1,3},{2,0},{3,1},{4,6},{5,7},{6,4},{7,5},{8,10},{9,11},{10,... | collective-permute-start | bytes 688136 | tf_op jit(solution)/shard_map/ppermute | solution.py:486
  21.0 15.4 %collective-permute-start.2 = (bf16[4,32,896]{2,1,0:T(8,128)(2,1)}, bf16[4,32,896]{2,1,0:T(8,128)(2,1)S(1)}, u32[]{:S(2)}, u32[]{:S(2)}) collective-permute-start(bf16[4,32,896]{2,1,0:T(8,128)(2,1)} %get-tuple-element.64), channel_id=1, source_target_pairs={{0,20},{4,24},{8,28},{12,0},{16,4},{20,8},{24,12},{28,16},{1,21},{... | collective-permute-start | bytes 688136 | tf_op jit(solution)/shard_map/ppermute | solution.py:489
  21.0 15.6 %collective-permute-start.8 = (bf16[4,32,896]{2,1,0:T(8,128)(2,1)S(1)}, bf16[4,32,896]{2,1,0:T(8,128)(2,1)S(1)}, u32[]{:S(2)}, u32[]{:S(2)}) collective-permute-start(bf16[4,32,896]{2,1,0:T(8,128)(2,1)S(1)} %collective-permute-done.refs_1_), channel_id=1, source_target_pairs={{0,2},{1,3},{2,0},{3,1},{4,6},{5,7},{6,4},{7,5},{8,10},{9,11},{10,... | collective-permute-start | bytes 688136 | tf_op jit(solution)/shard_map/ppermute | solution.py:486
  25.3 20.6 %collective-permute-start.3 = (bf16[4,32,896]{2,1,0:T(8,128)(2,1)}, bf16[4,32,896]{2,1,0:T(8,128)(2,1)S(1)}, u32[]{:S(2)}, u32[]{:S(2)}) collective-permute-start(bf16[4,32,896]{2,1,0:T(8,128)(2,1)} %get-tuple-element.65), channel_id=1, source_target_pairs={{0,16},{4,20},{8,24},{12,28},{16,0},{20,4},{24,8},{28,12},{1,17},{... | collective-permute-start | bytes 688136 | tf_op jit(solution)/shard_map/ppermute | solution.py:489
  29.2 18.0 %collective-permute-start.9 = (bf16[4,32,896]{2,1,0:T(8,128)(2,1)S(1)}, bf16[4,32,896]{2,1,0:T(8,128)(2,1)S(1)}, u32[]{:S(2)}, u32[]{:S(2)}) collective-permute-start(bf16[4,32,896]{2,1,0:T(8,128)(2,1)S(1)} %collective-permute-done.1.refs_2_), channel_id=1, source_target_pairs={{0,2},{1,3},{2,0},{3,1},{4,6},{5,7},{6,4},{7,5},{8,10},{9,11},{10,... | collective-permute-start | bytes 688136 | tf_op jit(solution)/shard_map/ppermute | solution.py:486
  30.8 20.1 %collective-permute-start.5 = (bf16[4,32,896]{2,1,0:T(8,128)(2,1)}, bf16[4,32,896]{2,1,0:T(8,128)(2,1)S(1)}, u32[]{:S(2)}, u32[]{:S(2)}) collective-permute-start(bf16[4,32,896]{2,1,0:T(8,128)(2,1)} %get-tuple-element.68), channel_id=1, source_target_pairs={{0,12},{4,16},{8,20},{12,24},{16,28},{20,0},{24,4},{28,8},{1,13},{... | collective-permute-start | bytes 688136 | tf_op jit(solution)/shard_map/ppermute | solution.py:489
  36.4 15.7 %collective-permute-start.14 = (bf16[4,32,896]{2,1,0:T(8,128)(2,1)S(1)}, bf16[4,32,896]{2,1,0:T(8,128)(2,1)S(1)}, u32[]{:S(2)}, u32[]{:S(2)}) collective-permute-start(bf16[4,32,896]{2,1,0:T(8,128)(2,1)S(1)} %collective-permute-done.4.refs_7_), channel_id=1, source_target_pairs={{0,2},{1,3},{2,0},{3,1},{4,6},{5,7},{6,4},{7,5},{8,10},{9,11},{10,... | collective-permute-start | bytes 688136 | tf_op jit(solution)/shard_map/ppermute | solution.py:486
  36.7 15.5 %collective-permute-start.13 = (bf16[4,32,896]{2,1,0:T(8,128)(2,1)S(1)}, bf16[4,32,896]{2,1,0:T(8,128)(2,1)S(1)}, u32[]{:S(2)}, u32[]{:S(2)}) collective-permute-start(bf16[4,32,896]{2,1,0:T(8,128)(2,1)S(1)} %collective-permute-done.6.refs_6_), channel_id=1, source_target_pairs={{0,2},{1,3},{2,0},{3,1},{4,6},{5,7},{6,4},{7,5},{8,10},{9,11},{10,... | collective-permute-start | bytes 688136 | tf_op jit(solution)/shard_map/ppermute | solution.py:486
  66.3 12.2 %collective-permute-start.15 = (bf16[16,32,896]{2,1,0:T(8,128)(2,1)S(1)}, bf16[16,32,896]{2,1,0:T(8,128)(2,1)S(1)}, u32[]{:S(2)}, u32[]{:S(2)}) collective-permute-start(bf16[16,32,896]{2,1,0:T(8,128)(2,1)S(1)} %get-tuple-element.71.refs_0_), channel_id=1, source_target_pairs={{0,1},{1,0},{2,3},{3,2},{4,5},{5,4},{6,7},{7,6},{8,9},{9,8},{10,11... | collective-permute-start | bytes 2752520 | tf_op jit(solution)/shard_map/ppermute | solution.py:483
  111.3 11.7 %collective-permute-start.18 = (s16[33,32,128]{2,1,0:T(8,128)(2,1)S(1)}, s16[33,32,128]{2,1,0:T(8,128)(2,1)S(1)}, u32[]{:S(2)}, u32[]{:S(2)}) collective-permute-start(s16[33,32,128]{2,1,0:T(8,128)(2,1)S(1)} %get-tuple-element.80), channel_id=1, source_target_pairs={{0,2},{1,3},{2,0},{3,1},{4,6},{5,7},{6,4},{7,5},{8,10},{9,11},{10,... | collective-permute-start | bytes 811016 | tf_op jit(solution)/shard_map/ppermute | solution.py:486
  123.8 13.9 %collective-permute-start.19 = (f32[1,16,32,512]{3,2,1,0:T(8,128)}, f32[1,16,32,512]{3,2,1,0:T(8,128)S(1)}, u32[]{:S(2)}, u32[]{:S(2)}) collective-permute-start(f32[1,16,32,512]{3,2,1,0:T(8,128)} %get-tuple-element.83), channel_id=1, source_target_pairs={{0,1},{1,0},{2,3},{3,2},{4,5},{5,4},{6,7},{7,6},{8,9},{9,8},{10,11... | collective-permute-start | bytes 3145736 | tf_op jit(solution)/shard_map/ppermute | solution.py:483
  131.1 12.8 %collective-permute-start.23 = (s16[65,32,128]{2,1,0:T(8,128)(2,1)S(1)}, s16[65,32,128]{2,1,0:T(8,128)(2,1)S(1)}, u32[]{:S(2)}, u32[]{:S(2)}) collective-permute-start(s16[65,32,128]{2,1,0:T(8,128)(2,1)S(1)} %far_codes.3), channel_id=1, source_target_pairs={{0,2},{1,3},{2,0},{3,1},{4,6},{5,7},{6,4},{7,5},{8,10},{9,11},{10,... | collective-permute-start | bytes 1597448 | tf_op jit(solution)/shard_map/ppermute | solution.py:486
  131.3 19.2 %collective-permute-start.31 = (s16[25,16,128]{2,1,0:T(8,128)(2,1)S(1)}, s16[25,16,128]{2,1,0:T(8,128)(2,1)S(1)}, u32[]{:S(2)}, u32[]{:S(2)}) collective-permute-start(s16[25,16,128]{2,1,0:T(8,128)(2,1)S(1)} %get-tuple-element.98), channel_id=1, source_target_pairs={{0,4},{4,8},{8,12},{12,16},{16,20},{20,24},{24,28},{28,0},{1,5},{5... | collective-permute-start | bytes 307208 | tf_op jit(solution)/shard_map/ppermute | solution.py:489
  136.7 13.8 %collective-permute-start.32 = (s16[25,16,128]{2,1,0:T(8,128)(2,1)S(1)}, s16[25,16,128]{2,1,0:T(8,128)(2,1)S(1)}, u32[]{:S(2)}, u32[]{:S(2)}) collective-permute-start(s16[25,16,128]{2,1,0:T(8,128)(2,1)S(1)} %get-tuple-element.99), channel_id=1, source_target_pairs={{0,8},{4,12},{8,16},{12,20},{16,24},{20,28},{24,0},{28,4},{1,9},{5... | collective-permute-start | bytes 307208 | tf_op jit(solution)/shard_map/ppermute | solution.py:489
  136.7 16.0 %collective-permute-start.33 = (s16[25,16,128]{2,1,0:T(8,128)(2,1)S(1)}, s16[25,16,128]{2,1,0:T(8,128)(2,1)S(1)}, u32[]{:S(2)}, u32[]{:S(2)}) collective-permute-start(s16[25,16,128]{2,1,0:T(8,128)(2,1)S(1)} %get-tuple-element.100), channel_id=1, source_target_pairs={{0,12},{4,16},{8,20},{12,24},{16,28},{20,0},{24,4},{28,8},{1,13},{... | collective-permute-start | bytes 307208 | tf_op jit(solution)/shard_map/ppermute | solution.py:489
  137.7 15.0 %collective-permute-start.34 = (s16[25,16,128]{2,1,0:T(8,128)(2,1)S(1)}, s16[25,16,128]{2,1,0:T(8,128)(2,1)S(1)}, u32[]{:S(2)}, u32[]{:S(2)}) collective-permute-start(s16[25,16,128]{2,1,0:T(8,128)(2,1)S(1)} %get-tuple-element.101), channel_id=1, source_target_pairs={{0,16},{4,20},{8,24},{12,28},{16,0},{20,4},{24,8},{28,12},{1,17},{... | collective-permute-start | bytes 307208 | tf_op jit(solution)/shard_map/ppermute | solution.py:489
  145.2 23.4 %collective-permute-start.24 = (s16[33,16,128]{2,1,0:T(8,128)(2,1)S(1)}, s16[33,16,128]{2,1,0:T(8,128)(2,1)S(1)}, u32[]{:S(2)}, u32[]{:S(2)}) collective-permute-start(s16[33,16,128]{2,1,0:T(8,128)(2,1)S(1)} %get-tuple-element.91), channel_id=1, source_target_pairs={{0,4},{4,8},{8,12},{12,16},{16,20},{20,24},{24,28},{28,0},{1,5},{5... | collective-permute-start | bytes 405512 | tf_op jit(solution)/shard_map/ppermute | solution.py:489
  150.5 18.1 %collective-permute-start.25 = (s16[33,16,128]{2,1,0:T(8,128)(2,1)S(1)}, s16[33,16,128]{2,1,0:T(8,128)(2,1)S(1)}, u32[]{:S(2)}, u32[]{:S(2)}) collective-permute-start(s16[33,16,128]{2,1,0:T(8,128)(2,1)S(1)} %get-tuple-element.92), channel_id=1, source_target_pairs={{0,8},{4,12},{8,16},{12,20},{16,24},{20,28},{24,0},{28,4},{1,9},{5... | collective-permute-start | bytes 405512 | tf_op jit(solution)/shard_map/ppermute | solution.py:489
  152.7 13.5 %collective-permute-start.37 = (s16[25,16,128]{2,1,0:T(8,128)(2,1)S(1)}, s16[25,16,128]{2,1,0:T(8,128)(2,1)S(1)}, u32[]{:S(2)}, u32[]{:S(2)}) collective-permute-start(s16[25,16,128]{2,1,0:T(8,128)(2,1)S(1)} %get-tuple-element.104), channel_id=1, source_target_pairs={{0,28},{4,0},{8,4},{12,8},{16,12},{20,16},{24,20},{28,24},{1,29},{... | collective-permute-start | bytes 307208 | tf_op jit(solution)/shard_map/ppermute | solution.py:489
  158.0 19.5 %collective-permute-start.26 = (s16[33,16,128]{2,1,0:T(8,128)(2,1)S(1)}, s16[33,16,128]{2,1,0:T(8,128)(2,1)S(1)}, u32[]{:S(2)}, u32[]{:S(2)}) collective-permute-start(s16[33,16,128]{2,1,0:T(8,128)(2,1)S(1)} %get-tuple-element.93), channel_id=1, source_target_pairs={{0,12},{4,16},{8,20},{12,24},{16,28},{20,0},{24,4},{28,8},{1,13},{... | collective-permute-start | bytes 405512 | tf_op jit(solution)/shard_map/ppermute | solution.py:489
  162.4 18.0 %collective-permute-start.27 = (s16[33,16,128]{2,1,0:T(8,128)(2,1)S(1)}, s16[33,16,128]{2,1,0:T(8,128)(2,1)S(1)}, u32[]{:S(2)}, u32[]{:S(2)}) collective-permute-start(s16[33,16,128]{2,1,0:T(8,128)(2,1)S(1)} %get-tuple-element.94), channel_id=1, source_target_pairs={{0,16},{4,20},{8,24},{12,28},{16,0},{20,4},{24,8},{28,12},{1,17},{... | collective-permute-start | bytes 405512 | tf_op jit(solution)/shard_map/ppermute | solution.py:489
  166.2 14.1 %collective-permute-start.28 = (s16[33,16,128]{2,1,0:T(8,128)(2,1)S(1)}, s16[33,16,128]{2,1,0:T(8,128)(2,1)S(1)}, u32[]{:S(2)}, u32[]{:S(2)}) collective-permute-start(s16[33,16,128]{2,1,0:T(8,128)(2,1)S(1)} %get-tuple-element.95), channel_id=1, source_target_pairs={{0,20},{4,24},{8,28},{12,0},{16,4},{20,8},{24,12},{28,16},{1,21},{... | collective-permute-start | bytes 405512 | tf_op jit(solution)/shard_map/ppermute | solution.py:489
  168.6 12.1 %collective-permute-start.29 = (s16[33,16,128]{2,1,0:T(8,128)(2,1)S(1)}, s16[33,16,128]{2,1,0:T(8,128)(2,1)S(1)}, u32[]{:S(2)}, u32[]{:S(2)}) collective-permute-start(s16[33,16,128]{2,1,0:T(8,128)(2,1)S(1)} %get-tuple-element.96), channel_id=1, source_target_pairs={{0,24},{4,28},{8,0},{12,4},{16,8},{20,12},{24,16},{28,20},{1,25},{... | collective-permute-start | bytes 405512 | tf_op jit(solution)/shard_map/ppermute | solution.py:489
  168.6 17.0 %collective-permute-start.30 = (s16[33,16,128]{2,1,0:T(8,128)(2,1)S(1)}, s16[33,16,128]{2,1,0:T(8,128)(2,1)S(1)}, u32[]{:S(2)}, u32[]{:S(2)}) collective-permute-start(s16[33,16,128]{2,1,0:T(8,128)(2,1)S(1)} %get-tuple-element.97), channel_id=1, source_target_pairs={{0,28},{4,0},{8,4},{12,8},{16,12},{20,16},{24,20},{28,24},{1,29},{... | collective-permute-start | bytes 405512 | tf_op jit(solution)/shard_map/ppermute | solution.py:489
  (22 other events, 241.6 us)

commit v12 on v11

--- a/solution.py
+++ b/solution.py
@@ -14,8 +14,9 @@
 TILE = 16
 WINDOW = 4
 VMEM_LIMIT = 28 * 1024 * 1024
-VMEM_MORE = 46 * 1024 * 1024
+VMEM_MORE = 50 * 1024 * 1024
 VMEM_ALL = 60 * 1024 * 1024
+VMEM_GRADS = 56 * 1024 * 1024
 F32 = jnp.float32
 BF16 = jnp.bfloat16
 
@@ -145,7 +146,7 @@
     n_in = len(places)
     pieces = refs[:n_in]
     wk, wv, q_ref, g_ref, att_ref, dq_ref = refs[n_in : n_in + 6]
-    *grads, near_out, far_out, own_out, key_value, own_all, core_all = refs[n_in + 6 :]
+    *grads, near_out, far_out, own_out, rest_out, key_value, own_all, core_all = refs[n_in + 6 :]
     step = pl.program_id(0)
     width = q_ref.shape[1]
     enc = wk.shape[0]
@@ -210,15 +211,16 @@
     @pl.when(step == pl.num_programs(0) - 1)
     def _():
         count = own_out.shape[-1]
-        for ref, outs in ((core_all, (near_out, far_out)), (own_all, (own_out,))):
+
+        def part(ref, cols, out):
             rows = ref[...].reshape(-1, 2 * width)
-            res = dot(rows[:, :width], wk[:count, :], last) + dot(rows[:, width:], wv[:count, :], last)
-            res = res.reshape(ref.shape[:3] + (count,))
-            if len(outs) == 1:
-                outs[0][...] = res
-            else:
-                outs[0][...] = res[:near]
-                outs[1][...] = res[near:]
+            res = dot(rows[:, :width], wk[cols, :], last) + dot(rows[:, width:], wv[cols, :], last)
+            out[...] = res.reshape(out.shape)
+
+        part(core_all.at[near:], slice(0, count), far_out)
+        part(core_all.at[:near], slice(0, count), near_out)
+        part(own_all, slice(0, count), own_out)
+        part(core_all.at[near:], slice(count, enc), rest_out)
 
 
 def attend(pieces, wk, wv, places, near, count, queries, cotangent):
@@ -236,6 +238,7 @@
         return pl.BlockSpec(shape, lambda i: (0,) * len(shape))
 
     parts = [(near, n, sub, count), (half - near, n, sub, count), (half, n, sub, count)]
+    parts.append((half - near, n, sub, enc - count))
     every = (half, n, sub, 2 * width)
     return pl.pallas_call(
         functools.partial(attend_body, places, near),
@@ -266,7 +269,7 @@
     return code.astype(jnp.int32).astype(jnp.int16), power
 
 
-def grads_body(first, core_ref, own_ref, wk, wv, near_out, far_out, own_out, part, sem):
+def grads_body(first, core_ref, own_ref, wk, wv, near_out, own_out, part, sem):
     i = pl.program_id(0)
     n_x = own_out.shape[0]
     width, count = wk.shape[1], part.shape[-1]
@@ -282,16 +285,15 @@
         )
         part[i] = res.reshape(part.shape[1:])
 
+    @pl.when(i == n_x)
+    def _():
+        act(core_ref)
+
     @pl.when(i < n_x)
     def _():
-        act(core_ref)
-
-    @pl.when(i >= n_x)
-    def _():
         act(own_ref)
 
-    outs = [near_out.at[0]] + [far_out.at[k] for k in range(n_x - 1)]
-    outs += [own_out.at[k] for k in range(n_x)]
+    outs = [own_out.at[k] for k in range(n_x)] + [near_out.at[0]]
     copies = [pltpu.make_async_copy(part.at[k], out, sem.at[k]) for k, out in enumerate(outs)]
     for k, copy in enumerate(copies):
 
@@ -308,24 +310,26 @@
 def grads_of(d_core, d_own, wk, wv, cols):
     n_x, n, sub, width = d_own.shape
     first, count = cols
-    shapes = [(1, n, sub, count), (n_x - 1, n, sub, count), (n_x, n, sub, count)]
     rows = n_x * n * sub
     return pl.pallas_call(
         functools.partial(grads_body, first),
-        out_shape=[jax.ShapeDtypeStruct(shape, F32) for shape in shapes],
-        grid=(2 * n_x,),
+        out_shape=[
+            jax.ShapeDtypeStruct((1, n, sub, count), F32),
+            jax.ShapeDtypeStruct((n_x, n, sub, count), F32),
+        ],
+        grid=(n_x + 1,),
         in_specs=[
+            pl.BlockSpec((1, n, sub, width), lambda i: (0, 0, 0, 0)),
             pl.BlockSpec((1, n, sub, width), lambda i: (jnp.minimum(i, n_x - 1), 0, 0, 0)),
-            pl.BlockSpec((1, n, sub, width), lambda i: (jnp.maximum(i - n_x, 0), 0, 0, 0)),
             pl.BlockSpec(wk.shape, lambda i: (0, 0)),
             pl.BlockSpec(wv.shape, lambda i: (0, 0)),
         ],
-        out_specs=[ANY] * 3,
+        out_specs=[ANY] * 2,
         scratch_shapes=[
-            pltpu.VMEM((2 * n_x, n, sub, count), F32),
-            pltpu.SemaphoreType.DMA((2 * n_x,)),
+            pltpu.VMEM((n_x + 1, n, sub, count), F32),
+            pltpu.SemaphoreType.DMA((n_x + 1,)),
         ],
-        compiler_params=params(VMEM_ALL),
+        compiler_params=params(VMEM_GRADS),
         cost_estimate=cost(4 * rows * count * width, 2 * (count + 2 * rows) * width + 8 * rows * count),
         name="grads",
     )(d_core, d_own, wk, wv)
@@ -517,28 +521,29 @@
 
     split = 3 * LANES
     parts = ((0, split), (split, enc - split))
-    attended, d_query, d_own, d_core, near, far, own = attend(
+    attended, d_query, d_own, d_core, near, far, own, far_b = attend(
         pieces, key_weight, value_weight, places, 1, split, queries, cotangent
     )
     far_got = over_core(far)
     near_got = over_core(near)
-    cuts = (2, 1)
+    far_got_b = over_core(far_b)
+    cuts = (parts[0][1] // LANES,)
     codes = far_codes(own, far_got, cuts)
-    near_b, far_b, own_b = grads_of(d_core, d_own, key_weight, value_weight, parts[1])
+    near_got, d_own = lax.optimization_barrier((near_got, d_own))
+    near_b, own_b = grads_of(d_core, d_own, key_weight, value_weight, parts[1])
 
     codes = [[over_x(x, n_x - k) for x in piece] for k, piece in enumerate(codes, 1)]
-    lead, near_b, far_b = lax.optimization_barrier(([piece[0] for piece in codes], near_b, far_b))
-    codes = [[x, *piece[1:]] for x, piece in zip(lead, codes)]
-    far_got_b = over_core(far_b)
+    codes, near_b = lax.optimization_barrier((codes, near_b))
     near_got_b = over_core(near_b)
     sent = send_codes(request, own, near_got, codes, cuts, n_dp)
+    sent, near_got_b = lax.optimization_barrier((sent, near_got_b))
     came = to_all(sent, 1)
     arrived = [sent[0]] + [came[d] for d in range(1, n_dp)]
     d_table = gather_grads(me, asked, arrived, n_slabs, share, enc, parts[0], None)
 
     cuts = (parts[1][1] // LANES,)
+    far_got_b, _ = lax.optimization_barrier((far_got_b, codes))
     codes = far_codes(own_b, far_got_b, cuts)
-    codes, before = lax.optimization_barrier((codes, sent[0]))
     codes = [[over_x(x, n_x - k) for x in piece] for k, piece in enumerate(codes, 1)]
     sent = send_codes(request, own_b, near_got_b, codes, cuts, n_dp)
     came = to_all(sent, 1)

time: 189 us -> 190 us (level)
  local copies, waits for them, and re-layouts: 2.37 us -> 4.9 us
    unnamed x16 -> x18, local copies, waits for them, and re-layouts: 2.37 us -> 4.9 us
    pallas_call x1, Pallas kernels: 27.5 us -> 29.7 us  [attend(): pl.pallas_call(functools.partial(attend_body, places, near), out_shape=[j...]
    ppermute x21, waiting for transfers between devices: 33.2 us -> 35.3 us  [over_dp(): return lax.ppermute(x, 'dp', [(i, (i + d) % n_dp) for i in range(n_dp)])]
    pallas_call x1, Pallas kernels: 10.3 us -> 8.27 us  [grads_of(): pl.pallas_call(functools.partial(grads_body, first), out_shape=[jax.Shape...]
    ppermute x6, waiting for transfers between devices: 8.99 us -> 6.99 us  [over_core(): return lax.ppermute(x, 'tensor', [(t, t ^ 1) for t in range(n_tp)])]
    ppermute x11 -> x10, waiting for transfers between devices: 13.1 us -> 11.3 us  [over_x(): lax.ppermute(x, 'tensor', [(t, (t + 2 * d) % n_tp) for t in range(n_tp)])]
    ppermute x11 -> x10, starting transfers between devices: 9.97 us -> 11 us  [over_x(): lax.ppermute(x, 'tensor', [(t, (t + 2 * d) % n_tp) for t in range(n_tp)])]
  transfers between devices with their start and end apart: 38 -> 37, of which waited for: 18 -> 17; matrix products, arithmetic and copies ran while one was open for 0% -> 0% of each run, Pallas kernels for 9% -> 7%
where the time goes in v12:
time: 190 us; the launch traced here: 189 us
  starting transfers between devices  64.7 us (34%)
  Pallas kernels  56.5 us (30%)
  waiting for transfers between devices  53.6 us (28%)
  blocking collectives  8.59 us (5%)
  local copies, waits for them, and re-layouts  4.9 us (3%)
    ppermute x21, starting transfers between devices, over_dp(): return lax.ppermute(x, 'dp', [(i, (i + d) % n_dp) for i in range(n_dp)])  41.3 us
    ppermute x21, waiting for transfers between devices, over_dp(): return lax.ppermute(x, 'dp', [(i, (i + d) % n_dp) for i in range(n_dp)])  35.3 us
    pallas_call x1, Pallas kernels, attend(): pl.pallas_call(functools.partial(attend_body, places, near), out_shape=[j...  29.7 us
    ppermute x6, starting transfers between devices, over_core(): return lax.ppermute(x, 'tensor', [(t, t ^ 1) for t in range(n_tp)])  12.4 us
    ppermute x10, waiting for transfers between devices, over_x(): lax.ppermute(x, 'tensor', [(t, (t + 2 * d) % n_tp) for t in range(n_tp)])  11.3 us
    ppermute x10, starting transfers between devices, over_x(): lax.ppermute(x, 'tensor', [(t, (t + 2 * d) % n_tp) for t in range(n_tp)])  11 us
    psum x1, blocking collectives, on_device(): asked = lax.psum(wanted, 'dp')  8.59 us
    pallas_call x1, Pallas kernels, grads_of(): pl.pallas_call(functools.partial(grads_body, first), out_shape=[jax.Shape...  8.27 us
  transfers between devices with their start and end apart: 37, of which 17 were waited for; matrix products, arithmetic and copies ran while one was open for 0% of the time, Pallas kernels for 7%

profile of v12, /device:TPU:13, one launch (start us, length us, event | category | flops | bytes accessed | tf_op | source)
XLA Modules:
  0.0 189.2 jit_solution(15344051678478393176)
XLA Ops:
  2.2 8.6 %psum.7.asked = s32[8,32]{1,0:T(8,128)} all-reduce(s32[8,32]{1,0:T(8,128)} %get-tuple-element.64), channel_id=1, replica_groups=mesh['dp'=8,'tensor'=4] {'dp'}, use_global_device_ids=true, to_apply=%region_0.0 | all-reduce | flops 256 | bytes 2048 | tf_op jit(solution)/shard_map/psum | solution.py:503
  10.8 4.1 %pack_rows.1 = (bf16[4,32,896]{2,1,0:T(8,128)(2,1)}, bf16[4,32,896]{2,1,0:T(8,128)(2,1)}, bf16[4,32,896]{2,1,0:T(8,128)(2,1)}, bf16[4,32,896]{2,1,0:T(8,128)(2,1...) custom-call(s32[1]{0:T(128)} %get-tuple-element.63.me, ...), custom_call_target="tpu_custom_call" | custom-call | bytes 3670016 | tf_op jit(solution)/shard_map/pack_rows/pallas_call | solution.py:99
  22.2 3.0 %collective-permute-done.4.refs_7_ = bf16[4,32,896]{2,1,0:T(8,128)(2,1)S(1)} collective-permute-done((bf16[4,32,896]{2,1,0:T(8,128)(2,1)}, bf16[4,32,896]{2,1,0:T(8,128)(2,1)S(1)}, u32[]{:S(2)}, u32[]{:S(2)}) %collective-permute-start.4) | collective-permute-done | bytes 229408 | tf_op jit(solution)/shard_map/ppermute | solution.py:493
  30.5 5.9 %collective-permute-start.5 = (bf16[4,32,896]{2,1,0:T(8,128)(2,1)}, bf16[4,32,896]{2,1,0:T(8,128)(2,1)S(1)}, u32[]{:S(2)}, u32[]{:S(2)}) collective-permute-start(bf16[4,32,896]{2,1,0:T(8,128)(2,1)} %get-tuple-element.76), channel_id=1, source_target_pairs={{0,12},{4,16},{8,20},{12,24},{16,28},{20,0},{24,4},{28,8},{1,13},{... | collective-permute-start | bytes 688136 | tf_op jit(solution)/shard_map/ppermute | solution.py:493
  37.9 7.8 %collective-permute-done.3.refs_4_ = bf16[4,32,896]{2,1,0:T(8,128)(2,1)S(1)} collective-permute-done((bf16[4,32,896]{2,1,0:T(8,128)(2,1)}, bf16[4,32,896]{2,1,0:T(8,128)(2,1)S(1)}, u32[]{:S(2)}, u32[]{:S(2)}) %collective-permute-start.3) | collective-permute-done | bytes 229408 | tf_op jit(solution)/shard_map/ppermute | solution.py:493
  47.2 3.4 %collective-permute-done.5.refs_5_ = bf16[4,32,896]{2,1,0:T(8,128)(2,1)S(1)} collective-permute-done((bf16[4,32,896]{2,1,0:T(8,128)(2,1)}, bf16[4,32,896]{2,1,0:T(8,128)(2,1)S(1)}, u32[]{:S(2)}, u32[]{:S(2)}) %collective-permute-start.5) | collective-permute-done | bytes 229408 | tf_op jit(solution)/shard_map/ppermute | solution.py:493
  52.0 3.9 %collective-permute-done.11.refs_12_ = bf16[4,32,896]{2,1,0:T(8,128)(2,1)S(1)} collective-permute-done((bf16[4,32,896]{2,1,0:T(8,128)(2,1)S(1)}, bf16[4,32,896]{2,1,0:T(8,128)(2,1)S(1)}, u32[]{:S(2)}, u32[]{:S(2)}) %collective-permute-start.11) | collective-permute-done | bytes 229408 | tf_op jit(solution)/shard_map/ppermute | solution.py:490
  55.9 4.9 %collective-permute-done.12.refs_13_ = bf16[4,32,896]{2,1,0:T(8,128)(2,1)S(1)} collective-permute-done((bf16[4,32,896]{2,1,0:T(8,128)(2,1)S(1)}, bf16[4,32,896]{2,1,0:T(8,128)(2,1)S(1)}, u32[]{:S(2)}, u32[]{:S(2)}) %collective-permute-start.12) | collective-permute-done | bytes 229408 | tf_op jit(solution)/shard_map/ppermute | solution.py:490
  61.8 4.2 %compact_rows.1 = (bf16[16,32,896]{2,1,0:T(8,128)(2,1)S(1)}, bf16[16,32,896]{2,1,0:T(8,128)(2,1)S(1)}) custom-call(s32[32]{0:T(128)S(1)} %copy-done.6, bf16[4,32,896]{2,1,0:T(8,128)(2,1)S(1)} %copy-done.4, bf16[4,32,896]{2,1,0:T(8,128)(2,1)S(1)} %collective-permute-done.refs_1_, bf16[4,32,896]{2,1,0:T(8,128)(2,1)S(1)} %collective-permute-done.1.refs_2_, ...), custom_call_target="tpu_custom_call" | custom-call | bytes 3670016 | tf_op jit(solution)/shard_map/compact_rows/pallas_call | solution.py:133
  66.0 10.2 %collective-permute-start.15 = (bf16[16,32,896]{2,1,0:T(8,128)(2,1)S(1)}, bf16[16,32,896]{2,1,0:T(8,128)(2,1)S(1)}, u32[]{:S(2)}, u32[]{:S(2)}) collective-permute-start(bf16[16,32,896]{2,1,0:T(8,128)(2,1)S(1)} %get-tuple-element.79.refs_0_), channel_id=1, source_target_pairs={{0,1},{1,0},{2,3},{3,2},{4,5},{5,4},{6,7},{7,6},{8,9},{9,8},{10,11... | collective-permute-start | bytes 2752520 | tf_op jit(solution)/shard_map/ppermute | solution.py:487
  80.5 29.7 %attend.1 = (bf16[512,1024]{1,0:T(8,128)(2,1)}, bf16[512,1024]{1,0:T(8,128)(2,1)}, bf16[2,16,32,2048]{3,2,1,0:T(8,128)(2,1)}, bf16[2,16,32,2048]{3,2,1,0:T(8,128...) custom-call(bf16[16,32,896]{2,1,0:T(8,128)(2,1)S(1)} %get-tuple-elem, ...), custom_call_target="tpu_custom_call" | custom-call | flops 12884901888 | bytes 20971520 | tf_op jit(solution)/shard_map/attend/pallas_call | solution.py:243
  117.9 8.3 %grads.1 = (f32[1,16,32,512]{3,2,1,0:T(8,128)}, f32[2,16,32,512]{3,2,1,0:T(8,128)}) custom-call(bf16[2,16,32,2048]{3,2,1,0:T(8,128)(2,1)} %get-tuple-element.83.core_ref, bf16[2,16,32,2048]{3,2,1,0:T(8,128)(2,1)} %get-tuple-element.86.own_ref, bf16[896,1024]{1,0:T(8,128)(2,1)} %wk.1, bf16[896,1024]{1,0:T(8,128)(2,1)} %wv.1), custom_call_target="tpu_custom_call" | custom-call | flops 4294967296 | bytes 14680064 | tf_op jit(solution)/shard_map/grads/pallas_call | solution.py:314
  132.9 5.5 %collective-permute-start.30 = (s16[25,16,128]{2,1,0:T(8,128)(2,1)S(1)}, s16[25,16,128]{2,1,0:T(8,128)(2,1)S(1)}, u32[]{:S(2)}, u32[]{:S(2)}) collective-permute-start(s16[25,16,128]{2,1,0:T(8,128)(2,1)S(1)} %get-tuple-element.114), channel_id=1, source_target_pairs={{0,4},{4,8},{8,12},{12,16},{16,20},{20,24},{24,28},{28,0},{1,5},{5... | collective-permute-start | bytes 307208 | tf_op jit(solution)/shard_map/ppermute | solution.py:493
  139.2 3.3 %collective-permute-start.33 = (s16[25,16,128]{2,1,0:T(8,128)(2,1)S(1)}, s16[25,16,128]{2,1,0:T(8,128)(2,1)S(1)}, u32[]{:S(2)}, u32[]{:S(2)}) collective-permute-start(s16[25,16,128]{2,1,0:T(8,128)(2,1)S(1)} %get-tuple-element.117), channel_id=1, source_target_pairs={{0,16},{4,20},{8,24},{12,28},{16,0},{20,4},{24,8},{28,12},{1,17},{... | collective-permute-start | bytes 307208 | tf_op jit(solution)/shard_map/ppermute | solution.py:493
  145.3 5.6 %collective-permute-start.23 = (s16[33,16,128]{2,1,0:T(8,128)(2,1)S(1)}, s16[33,16,128]{2,1,0:T(8,128)(2,1)S(1)}, u32[]{:S(2)}, u32[]{:S(2)}) collective-permute-start(s16[33,16,128]{2,1,0:T(8,128)(2,1)S(1)} %get-tuple-element.106), channel_id=1, source_target_pairs={{0,4},{4,8},{8,12},{12,16},{16,20},{20,24},{24,28},{28,0},{1,5},{5... | collective-permute-start | bytes 405512 | tf_op jit(solution)/shard_map/ppermute | solution.py:493
  153.2 3.1 %collective-permute-start.36 = (s16[25,16,128]{2,1,0:T(8,128)(2,1)S(1)}, s16[25,16,128]{2,1,0:T(8,128)(2,1)S(1)}, u32[]{:S(2)}, u32[]{:S(2)}) collective-permute-start(s16[25,16,128]{2,1,0:T(8,128)(2,1)S(1)} %get-tuple-element.120), channel_id=1, source_target_pairs={{0,28},{4,0},{8,4},{12,8},{16,12},{20,16},{24,20},{28,24},{1,29},{... | collective-permute-start | bytes 307208 | tf_op jit(solution)/shard_map/ppermute | solution.py:493
  156.3 4.4 %collective-permute-done.34.refs_5_ = s16[25,16,128]{2,1,0:T(8,128)(2,1)S(1)} collective-permute-done((s16[25,16,128]{2,1,0:T(8,128)(2,1)S(1)}, s16[25,16,128]{2,1,0:T(8,128)(2,1)S(1)}, u32[]{:S(2)}, u32[]{:S(2)}) %collective-permute-start.34) | collective-permute-done | bytes 102432 | tf_op jit(solution)/shard_map/ppermute | solution.py:493
  160.8 2.9 %collective-permute-start.25 = (s16[33,16,128]{2,1,0:T(8,128)(2,1)S(1)}, s16[33,16,128]{2,1,0:T(8,128)(2,1)S(1)}, u32[]{:S(2)}, u32[]{:S(2)}) collective-permute-start(s16[33,16,128]{2,1,0:T(8,128)(2,1)S(1)} %get-tuple-element.108), channel_id=1, source_target_pairs={{0,12},{4,16},{8,20},{12,24},{16,28},{20,0},{24,4},{28,8},{1,13},{... | collective-permute-start | bytes 405512 | tf_op jit(solution)/shard_map/ppermute | solution.py:493
  163.6 3.3 %collective-permute-start.26 = (s16[33,16,128]{2,1,0:T(8,128)(2,1)S(1)}, s16[33,16,128]{2,1,0:T(8,128)(2,1)S(1)}, u32[]{:S(2)}, u32[]{:S(2)}) collective-permute-start(s16[33,16,128]{2,1,0:T(8,128)(2,1)S(1)} %get-tuple-element.109), channel_id=1, source_target_pairs={{0,16},{4,20},{8,24},{12,28},{16,0},{20,4},{24,8},{28,12},{1,17},{... | collective-permute-start | bytes 405512 | tf_op jit(solution)/shard_map/ppermute | solution.py:493
  169.7 2.7 %gather_grads.2.refs_8_ = f32[16,32,896]{2,1,0:T(8,128)} custom-call(s32[1]{0:T(128)} %get-tuple-element.63.me, s32[8,32]{1,0:T(8,128)S(1)} %copy-done.5, s16[25,16,128]{2,1,0:T(8,128)(2,1)S(1)} %get-tuple-element.113.refs_0_, s16[25,16,128]{2,1,0:T(8,128)(2,1)S(1)} %collective-permute-done.30.refs_1_, ...), custom_call_target="tpu_custom_call" | custom-call | bytes 1572864 | tf_op jit(solution)/shard_map/gather_grads/pallas_call | solution.py:463
  172.4 7.0 %collective-permute-done.26.refs_4_ = s16[33,16,128]{2,1,0:T(8,128)(2,1)S(1)} collective-permute-done((s16[33,16,128]{2,1,0:T(8,128)(2,1)S(1)}, s16[33,16,128]{2,1,0:T(8,128)(2,1)S(1)}, u32[]{:S(2)}, u32[]{:S(2)}) %collective-permute-start.26) | collective-permute-done | bytes 135200 | tf_op jit(solution)/shard_map/ppermute | solution.py:493
  179.4 3.3 %collective-permute-done.28.refs_6_ = s16[33,16,128]{2,1,0:T(8,128)(2,1)S(1)} collective-permute-done((s16[33,16,128]{2,1,0:T(8,128)(2,1)S(1)}, s16[33,16,128]{2,1,0:T(8,128)(2,1)S(1)}, u32[]{:S(2)}, u32[]{:S(2)}) %collective-permute-start.28) | collective-permute-done | bytes 135200 | tf_op jit(solution)/shard_map/ppermute | solution.py:493
  182.7 3.5 %collective-permute-done.29.refs_7_ = s16[33,16,128]{2,1,0:T(8,128)(2,1)S(1)} collective-permute-done((s16[33,16,128]{2,1,0:T(8,128)(2,1)S(1)}, s16[33,16,128]{2,1,0:T(8,128)(2,1)S(1)}, u32[]{:S(2)}, u32[]{:S(2)}) %collective-permute-start.29) | collective-permute-done | bytes 135200 | tf_op jit(solution)/shard_map/ppermute | solution.py:493
  186.2 2.9 %gather_grads.3 = f32[16,32,896]{2,1,0:T(8,128)} custom-call(s32[1]{0:T(128)} %get-tuple-element.63.me, s32[8,32]{1,0:T(8,128)S(1)} %copy-done.5, s16[33,16,128]{2,1,0:T(8,128)(2,1)S(1)} %get-tuple-element.105.refs_0_, s16[33,16,128]{2,1,0:T(8,128)(2,1)S(1)} %collective-permute-done.23.refs_1_, ...), custom_call_target="tpu_custom_call", output_to_operand_aliasing={{}: (10, {})} | custom-call | bytes 2097152 | tf_op jit(solution)/shard_map/gather_grads/pallas_call | solution.py:463
  (80 shorter events, 46.7 us)
Async XLA Ops:
  18.3 10.7 %collective-permute-start.6 = (bf16[4,32,896]{2,1,0:T(8,128)(2,1)}, bf16[4,32,896]{2,1,0:T(8,128)(2,1)S(1)}, u32[]{:S(2)}, u32[]{:S(2)}) collective-permute-start(bf16[4,32,896]{2,1,0:T(8,128)(2,1)} %get-tuple-element.77), channel_id=1, source_target_pairs={{0,8},{4,12},{8,16},{12,20},{16,24},{20,28},{24,0},{28,4},{1,9},{5... | collective-permute-start | bytes 688136 | tf_op jit(solution)/shard_map/ppermute | solution.py:493
  18.7 11.7 %collective-permute-start.7 = (bf16[4,32,896]{2,1,0:T(8,128)(2,1)}, bf16[4,32,896]{2,1,0:T(8,128)(2,1)S(1)}, u32[]{:S(2)}, u32[]{:S(2)}) collective-permute-start(bf16[4,32,896]{2,1,0:T(8,128)(2,1)} %get-tuple-element.65.refs_0_), channel_id=1, source_target_pairs={{0,2},{1,3},{2,0},{3,1},{4,6},{5,7},{6,4},{7,5},{8,10},{9,11},{10,... | collective-permute-start | bytes 688136 | tf_op jit(solution)/shard_map/ppermute | solution.py:490
  21.0 15.4 %collective-permute-start.2 = (bf16[4,32,896]{2,1,0:T(8,128)(2,1)}, bf16[4,32,896]{2,1,0:T(8,128)(2,1)S(1)}, u32[]{:S(2)}, u32[]{:S(2)}) collective-permute-start(bf16[4,32,896]{2,1,0:T(8,128)(2,1)} %get-tuple-element.72), channel_id=1, source_target_pairs={{0,20},{4,24},{8,28},{12,0},{16,4},{20,8},{24,12},{28,16},{1,21},{... | collective-permute-start | bytes 688136 | tf_op jit(solution)/shard_map/ppermute | solution.py:493
  21.0 15.8 %collective-permute-start.8 = (bf16[4,32,896]{2,1,0:T(8,128)(2,1)S(1)}, bf16[4,32,896]{2,1,0:T(8,128)(2,1)S(1)}, u32[]{:S(2)}, u32[]{:S(2)}) collective-permute-start(bf16[4,32,896]{2,1,0:T(8,128)(2,1)S(1)} %collective-permute-done.refs_1_), channel_id=1, source_target_pairs={{0,2},{1,3},{2,0},{3,1},{4,6},{5,7},{6,4},{7,5},{8,10},{9,11},{10,... | collective-permute-start | bytes 688136 | tf_op jit(solution)/shard_map/ppermute | solution.py:490
  25.2 20.5 %collective-permute-start.3 = (bf16[4,32,896]{2,1,0:T(8,128)(2,1)}, bf16[4,32,896]{2,1,0:T(8,128)(2,1)S(1)}, u32[]{:S(2)}, u32[]{:S(2)}) collective-permute-start(bf16[4,32,896]{2,1,0:T(8,128)(2,1)} %get-tuple-element.73), channel_id=1, source_target_pairs={{0,16},{4,20},{8,24},{12,28},{16,0},{20,4},{24,8},{28,12},{1,17},{... | collective-permute-start | bytes 688136 | tf_op jit(solution)/shard_map/ppermute | solution.py:493
  29.0 18.1 %collective-permute-start.9 = (bf16[4,32,896]{2,1,0:T(8,128)(2,1)S(1)}, bf16[4,32,896]{2,1,0:T(8,128)(2,1)S(1)}, u32[]{:S(2)}, u32[]{:S(2)}) collective-permute-start(bf16[4,32,896]{2,1,0:T(8,128)(2,1)S(1)} %collective-permute-done.1.refs_2_), channel_id=1, source_target_pairs={{0,2},{1,3},{2,0},{3,1},{4,6},{5,7},{6,4},{7,5},{8,10},{9,11},{10,... | collective-permute-start | bytes 688136 | tf_op jit(solution)/shard_map/ppermute | solution.py:490
  30.5 20.2 %collective-permute-start.5 = (bf16[4,32,896]{2,1,0:T(8,128)(2,1)}, bf16[4,32,896]{2,1,0:T(8,128)(2,1)S(1)}, u32[]{:S(2)}, u32[]{:S(2)}) collective-permute-start(bf16[4,32,896]{2,1,0:T(8,128)(2,1)} %get-tuple-element.76), channel_id=1, source_target_pairs={{0,12},{4,16},{8,20},{12,24},{16,28},{20,0},{24,4},{28,8},{1,13},{... | collective-permute-start | bytes 688136 | tf_op jit(solution)/shard_map/ppermute | solution.py:493
  36.4 15.6 %collective-permute-start.14 = (bf16[4,32,896]{2,1,0:T(8,128)(2,1)S(1)}, bf16[4,32,896]{2,1,0:T(8,128)(2,1)S(1)}, u32[]{:S(2)}, u32[]{:S(2)}) collective-permute-start(bf16[4,32,896]{2,1,0:T(8,128)(2,1)S(1)} %collective-permute-done.4.refs_7_), channel_id=1, source_target_pairs={{0,2},{1,3},{2,0},{3,1},{4,6},{5,7},{6,4},{7,5},{8,10},{9,11},{10,... | collective-permute-start | bytes 688136 | tf_op jit(solution)/shard_map/ppermute | solution.py:490
  36.8 15.2 %collective-permute-start.13 = (bf16[4,32,896]{2,1,0:T(8,128)(2,1)S(1)}, bf16[4,32,896]{2,1,0:T(8,128)(2,1)S(1)}, u32[]{:S(2)}, u32[]{:S(2)}) collective-permute-start(bf16[4,32,896]{2,1,0:T(8,128)(2,1)S(1)} %collective-permute-done.6.refs_6_), channel_id=1, source_target_pairs={{0,2},{1,3},{2,0},{3,1},{4,6},{5,7},{6,4},{7,5},{8,10},{9,11},{10,... | collective-permute-start | bytes 688136 | tf_op jit(solution)/shard_map/ppermute | solution.py:490
  66.0 12.3 %collective-permute-start.15 = (bf16[16,32,896]{2,1,0:T(8,128)(2,1)S(1)}, bf16[16,32,896]{2,1,0:T(8,128)(2,1)S(1)}, u32[]{:S(2)}, u32[]{:S(2)}) collective-permute-start(bf16[16,32,896]{2,1,0:T(8,128)(2,1)S(1)} %get-tuple-element.79.refs_0_), channel_id=1, source_target_pairs={{0,1},{1,0},{2,3},{3,2},{4,5},{5,4},{6,7},{7,6},{8,9},{9,8},{10,11... | collective-permute-start | bytes 2752520 | tf_op jit(solution)/shard_map/ppermute | solution.py:487
  110.8 17.5 %collective-permute-start.21 = (f32[1,16,32,512]{3,2,1,0:T(8,128)}, f32[1,16,32,512]{3,2,1,0:T(8,128)S(1)}, u32[]{:S(2)}, u32[]{:S(2)}) collective-permute-start(f32[1,16,32,512]{3,2,1,0:T(8,128)} %get-tuple-element.103), channel_id=1, source_target_pairs={{0,1},{1,0},{2,3},{3,2},{4,5},{5,4},{6,7},{7,6},{8,9},{9,8},{10,11... | collective-permute-start | bytes 3145736 | tf_op jit(solution)/shard_map/ppermute | solution.py:487
  130.2 13.8 %collective-permute-start.22 = (s16[65,32,128]{2,1,0:T(8,128)(2,1)S(1)}, s16[65,32,128]{2,1,0:T(8,128)(2,1)S(1)}, u32[]{:S(2)}, u32[]{:S(2)}) collective-permute-start(s16[65,32,128]{2,1,0:T(8,128)(2,1)S(1)} %far_codes.3), channel_id=1, source_target_pairs={{0,2},{1,3},{2,0},{3,1},{4,6},{5,7},{6,4},{7,5},{8,10},{9,11},{10,... | collective-permute-start | bytes 1597448 | tf_op jit(solution)/shard_map/ppermute | solution.py:490
  132.9 18.0 %collective-permute-start.30 = (s16[25,16,128]{2,1,0:T(8,128)(2,1)S(1)}, s16[25,16,128]{2,1,0:T(8,128)(2,1)S(1)}, u32[]{:S(2)}, u32[]{:S(2)}) collective-permute-start(s16[25,16,128]{2,1,0:T(8,128)(2,1)S(1)} %get-tuple-element.114), channel_id=1, source_target_pairs={{0,4},{4,8},{8,12},{12,16},{16,20},{20,24},{24,28},{28,0},{1,5},{5... | collective-permute-start | bytes 307208 | tf_op jit(solution)/shard_map/ppermute | solution.py:493
  138.3 12.6 %collective-permute-start.31 = (s16[25,16,128]{2,1,0:T(8,128)(2,1)S(1)}, s16[25,16,128]{2,1,0:T(8,128)(2,1)S(1)}, u32[]{:S(2)}, u32[]{:S(2)}) collective-permute-start(s16[25,16,128]{2,1,0:T(8,128)(2,1)S(1)} %get-tuple-element.115), channel_id=1, source_target_pairs={{0,8},{4,12},{8,16},{12,20},{16,24},{20,28},{24,0},{28,4},{1,9},{5... | collective-permute-start | bytes 307208 | tf_op jit(solution)/shard_map/ppermute | solution.py:493
  138.3 14.8 %collective-permute-start.32 = (s16[25,16,128]{2,1,0:T(8,128)(2,1)S(1)}, s16[25,16,128]{2,1,0:T(8,128)(2,1)S(1)}, u32[]{:S(2)}, u32[]{:S(2)}) collective-permute-start(s16[25,16,128]{2,1,0:T(8,128)(2,1)S(1)} %get-tuple-element.116), channel_id=1, source_target_pairs={{0,12},{4,16},{8,20},{12,24},{16,28},{20,0},{24,4},{28,8},{1,13},{... | collective-permute-start | bytes 307208 | tf_op jit(solution)/shard_map/ppermute | solution.py:493
  139.2 14.0 %collective-permute-start.33 = (s16[25,16,128]{2,1,0:T(8,128)(2,1)S(1)}, s16[25,16,128]{2,1,0:T(8,128)(2,1)S(1)}, u32[]{:S(2)}, u32[]{:S(2)}) collective-permute-start(s16[25,16,128]{2,1,0:T(8,128)(2,1)S(1)} %get-tuple-element.117), channel_id=1, source_target_pairs={{0,16},{4,20},{8,24},{12,28},{16,0},{20,4},{24,8},{28,12},{1,17},{... | collective-permute-start | bytes 307208 | tf_op jit(solution)/shard_map/ppermute | solution.py:493
  145.3 24.0 %collective-permute-start.23 = (s16[33,16,128]{2,1,0:T(8,128)(2,1)S(1)}, s16[33,16,128]{2,1,0:T(8,128)(2,1)S(1)}, u32[]{:S(2)}, u32[]{:S(2)}) collective-permute-start(s16[33,16,128]{2,1,0:T(8,128)(2,1)S(1)} %get-tuple-element.106), channel_id=1, source_target_pairs={{0,4},{4,8},{8,12},{12,16},{16,20},{20,24},{24,28},{28,0},{1,5},{5... | collective-permute-start | bytes 405512 | tf_op jit(solution)/shard_map/ppermute | solution.py:493
  150.9 18.4 %collective-permute-start.24 = (s16[33,16,128]{2,1,0:T(8,128)(2,1)S(1)}, s16[33,16,128]{2,1,0:T(8,128)(2,1)S(1)}, u32[]{:S(2)}, u32[]{:S(2)}) collective-permute-start(s16[33,16,128]{2,1,0:T(8,128)(2,1)S(1)} %get-tuple-element.107), channel_id=1, source_target_pairs={{0,8},{4,12},{8,16},{12,20},{16,24},{20,28},{24,0},{28,4},{1,9},{5... | collective-permute-start | bytes 405512 | tf_op jit(solution)/shard_map/ppermute | solution.py:493
  153.2 13.8 %collective-permute-start.36 = (s16[25,16,128]{2,1,0:T(8,128)(2,1)S(1)}, s16[25,16,128]{2,1,0:T(8,128)(2,1)S(1)}, u32[]{:S(2)}, u32[]{:S(2)}) collective-permute-start(s16[25,16,128]{2,1,0:T(8,128)(2,1)S(1)} %get-tuple-element.120), channel_id=1, source_target_pairs={{0,28},{4,0},{8,4},{12,8},{16,12},{20,16},{24,20},{28,24},{1,29},{... | collective-permute-start | bytes 307208 | tf_op jit(solution)/shard_map/ppermute | solution.py:493
  160.8 11.7 %collective-permute-start.25 = (s16[33,16,128]{2,1,0:T(8,128)(2,1)S(1)}, s16[33,16,128]{2,1,0:T(8,128)(2,1)S(1)}, u32[]{:S(2)}, u32[]{:S(2)}) collective-permute-start(s16[33,16,128]{2,1,0:T(8,128)(2,1)S(1)} %get-tuple-element.108), channel_id=1, source_target_pairs={{0,12},{4,16},{8,20},{12,24},{16,28},{20,0},{24,4},{28,8},{1,13},{... | collective-permute-start | bytes 405512 | tf_op jit(solution)/shard_map/ppermute | solution.py:493
  163.6 15.8 %collective-permute-start.26 = (s16[33,16,128]{2,1,0:T(8,128)(2,1)S(1)}, s16[33,16,128]{2,1,0:T(8,128)(2,1)S(1)}, u32[]{:S(2)}, u32[]{:S(2)}) collective-permute-start(s16[33,16,128]{2,1,0:T(8,128)(2,1)S(1)} %get-tuple-element.109), channel_id=1, source_target_pairs={{0,16},{4,20},{8,24},{12,28},{16,0},{20,4},{24,8},{28,12},{1,17},{... | collective-permute-start | bytes 405512 | tf_op jit(solution)/shard_map/ppermute | solution.py:493
  166.9 12.5 %collective-permute-start.27 = (s16[33,16,128]{2,1,0:T(8,128)(2,1)S(1)}, s16[33,16,128]{2,1,0:T(8,128)(2,1)S(1)}, u32[]{:S(2)}, u32[]{:S(2)}) collective-permute-start(s16[33,16,128]{2,1,0:T(8,128)(2,1)S(1)} %get-tuple-element.110), channel_id=1, source_target_pairs={{0,20},{4,24},{8,28},{12,0},{16,4},{20,8},{24,12},{28,16},{1,21},{... | collective-permute-start | bytes 405512 | tf_op jit(solution)/shard_map/ppermute | solution.py:493
  169.3 13.3 %collective-permute-start.28 = (s16[33,16,128]{2,1,0:T(8,128)(2,1)S(1)}, s16[33,16,128]{2,1,0:T(8,128)(2,1)S(1)}, u32[]{:S(2)}, u32[]{:S(2)}) collective-permute-start(s16[33,16,128]{2,1,0:T(8,128)(2,1)S(1)} %get-tuple-element.111), channel_id=1, source_target_pairs={{0,24},{4,28},{8,0},{12,4},{16,8},{20,12},{24,16},{28,20},{1,25},{... | collective-permute-start | bytes 405512 | tf_op jit(solution)/shard_map/ppermute | solution.py:493
  169.3 16.9 %collective-permute-start.29 = (s16[33,16,128]{2,1,0:T(8,128)(2,1)S(1)}, s16[33,16,128]{2,1,0:T(8,128)(2,1)S(1)}, u32[]{:S(2)}, u32[]{:S(2)}) collective-permute-start(s16[33,16,128]{2,1,0:T(8,128)(2,1)S(1)} %get-tuple-element.112), channel_id=1, source_target_pairs={{0,28},{4,0},{8,4},{12,8},{16,12},{20,16},{24,20},{28,24},{1,29},{... | collective-permute-start | bytes 405512 | tf_op jit(solution)/shard_map/ppermute | solution.py:493
  (22 other events, 201.6 us)

commit v13 on v12

--- a/solution.py
+++ b/solution.py
@@ -12,11 +12,9 @@
 SPAN = 64
 LANES = 128
 TILE = 16
-WINDOW = 4
 VMEM_LIMIT = 28 * 1024 * 1024
-VMEM_MORE = 50 * 1024 * 1024
+VMEM_MORE = 44 * 1024 * 1024
 VMEM_ALL = 60 * 1024 * 1024
-VMEM_GRADS = 56 * 1024 * 1024
 F32 = jnp.float32
 BF16 = jnp.bfloat16
 
@@ -74,10 +72,10 @@
     return asked[asker, d * (asked.shape[1] // n_dp) + j] - 1
 
 
-def pack_body(n_dp, me, asked, table, *rest):
+def pack_body(n_dp, chunk, share, me, asked, table, *rest):
     outs, sem = rest[:-1], rest[-1]
-    cap, share, _ = outs[0].shape
-    row = pl.multiple_of(lax.axis_index("tensor") * share, share)
+    cap = outs[0].shape[0]
+    row = pl.multiple_of(lax.axis_index("tensor") * share + chunk * TILE, TILE)
 
     def each(act):
         for d in range(n_dp):
@@ -86,30 +84,30 @@
 
                 @pl.when(slab >= 0)
                 def _():
-                    source = table.at[slab, pl.ds(row, share)]
+                    source = table.at[slab, pl.ds(row, TILE)]
                     act(pltpu.make_async_copy(source, outs[d].at[j], sem.at[d * cap + j]))
 
     each(lambda copy: copy.start())
     each(lambda copy: copy.wait())
 
 
-def pack(me, asked, table, share, cap):
+def pack(me, asked, table, chunk, share, cap):
     n_dp = asked.shape[0]
     enc = table.shape[2]
     return pl.pallas_call(
-        functools.partial(pack_body, n_dp),
-        out_shape=[jax.ShapeDtypeStruct((cap, share, enc), table.dtype)] * n_dp,
+        functools.partial(pack_body, n_dp, chunk, share),
+        out_shape=[jax.ShapeDtypeStruct((cap, TILE, enc), table.dtype)] * n_dp,
         in_specs=[SMEM, SMEM, ANY],
         out_specs=[VMEM] * n_dp,
         scratch_shapes=[pltpu.SemaphoreType.DMA((n_dp * cap,))],
         compiler_params=params(VMEM_ALL),
-        cost_estimate=cost(0, 4 * n_dp * cap * share * enc),
+        cost_estimate=cost(0, 4 * n_dp * cap * TILE * enc),
         name="pack_rows",
     )(me, asked, table)
 
 
-def compact_body(n_dp, n_out, request, *refs):
-    arrived, outs, sem = refs[: n_dp * n_out], refs[n_dp * n_out : -1], refs[-1]
+def compact_body(n_dp, request, *refs):
+    arrived, out, sem = refs[:n_dp], refs[n_dp], refs[n_dp + 1]
     cap = arrived[0].shape[0]
 
     def each(act):
@@ -119,38 +117,82 @@
 
                 @pl.when(r >= 0)
                 def _():
-                    for i in range(n_out):
-                        source = arrived[i * n_dp + d].at[j]
-                        act(pltpu.make_async_copy(source, outs[i].at[r], sem.at[i, d * cap + j]))
+                    act(pltpu.make_async_copy(arrived[d].at[j], out.at[r], sem.at[d * cap + j]))
 
     each(lambda copy: copy.start())
     each(lambda copy: copy.wait())
 
 
-def compact(request, lists, n):
-    n_dp, n_out = len(lists[0]), len(lists)
-    shape = (n,) + lists[0][0].shape[1:]
-    return pl.pallas_call(
-        functools.partial(compact_body, n_dp, n_out),
-        out_shape=[jax.ShapeDtypeStruct(shape, lists[0][0].dtype)] * n_out,
-        in_specs=[SMEM] + [ANY] * (n_dp * n_out),
-        out_specs=[VMEM] * n_out,
-        scratch_shapes=[pltpu.SemaphoreType.DMA((n_out, request.shape[0]))],
+def compact(request, arrived, n):
+    shape = (n,) + arrived[0].shape[1:]
+    return pl.pallas_call(
+        functools.partial(compact_body, len(arrived)),
+        out_shape=jax.ShapeDtypeStruct(shape, arrived[0].dtype),
+        in_specs=[SMEM] + [ANY] * len(arrived),
+        out_specs=VMEM,
+        scratch_shapes=[pltpu.SemaphoreType.DMA((request.shape[0],))],
         compiler_params=params(),
-        cost_estimate=cost(0, 4 * n_out * math.prod(shape)),
+        cost_estimate=cost(0, 4 * math.prod(shape)),
         name="compact_rows",
-    )(request, *[block for blocks in lists for block in blocks])
-
-
-def attend_body(places, near, *refs):
-    n_in = len(places)
-    pieces = refs[:n_in]
-    wk, wv, q_ref, g_ref, att_ref, dq_ref = refs[n_in : n_in + 6]
-    *grads, near_out, far_out, own_out, rest_out, key_value, own_all, core_all = refs[n_in + 6 :]
+    )(request, *arrived)
+
+
+def weight_specs(rows, step):
+    return [
+        pl.BlockSpec((rows, step), lambda i: (0, jnp.minimum(i, 1))),
+        pl.BlockSpec((rows, step), lambda i: (0, jnp.maximum(i - 2, 0))),
+    ]
+
+
+def with_weight(wk, wv, act):
+    @pl.when(pl.program_id(0) < 2)
+    def _():
+        act(wk)
+
+    @pl.when(pl.program_id(0) >= 2)
+    def _():
+        act(wv)
+
+
+def project_body(n_in, *refs):
+    wk, wv, out = refs[n_in : n_in + 3]
+    n, sub, enc = refs[0].shape
+    rows = jnp.concatenate([ref[...].reshape(n * sub, enc) for ref in refs[:n_in]], axis=0)
+
+    def act(w):
+        res = jnp.dot(rows, w[...], preferred_element_type=F32)
+        out[...] = res.astype(BF16).reshape(out.shape)
+
+    with_weight(wk, wv, act)
+
+
+def project(pieces, wk, wv):
+    n_in = len(pieces)
+    n, sub, enc = pieces[0].shape
+    width = 2 * wk.shape[1]
+    step = width // 4
+    return pl.pallas_call(
+        functools.partial(project_body, n_in),
+        out_shape=jax.ShapeDtypeStruct((n_in, n, sub, width), BF16),
+        grid=(4,),
+        in_specs=[pl.BlockSpec((n, sub, enc), lambda i: (0, 0, 0))] * n_in
+        + weight_specs(enc, step),
+        out_specs=pl.BlockSpec((n_in, n, sub, step), lambda i: (0, 0, 0, i)),
+        compiler_params=params(),
+        cost_estimate=cost(
+            2 * n_in * n * sub * enc * width, 2 * (n_in * n * sub * (enc + width) + enc * width)
+        ),
+        name="project",
+    )(*pieces, wk, wv)
+
+
+def attend_body(places, n_kv, n_late, near, *refs):
+    kvs, late = refs[:n_kv], refs[n_kv : n_kv + n_late]
+    wk, wv, q_ref, g_ref, att_ref, dq_ref = refs[n_kv + n_late : n_kv + n_late + 6]
+    *grads, near_out, far_out, own_out, rest_out, late_kv, own_all, core_all = refs[n_kv + n_late + 6 :]
     step = pl.program_id(0)
     width = q_ref.shape[1]
     enc = wk.shape[0]
-    sub = key_value.shape[2]
     scale = 1.0 / math.sqrt(HD)
     heads = width // HD
     group = min(8, heads)
@@ -162,23 +204,27 @@
 
     @pl.when(step == 0)
     def _():
-        for i, ref in enumerate(pieces):
+        for i, ref in enumerate(late):
             rows = ref[...].reshape(-1, enc)
             shape = ref.shape[:2] + (width,)
-            key_value[i, :, :, :width] = dot(rows, wk[...]).astype(BF16).reshape(shape)
-            key_value[i, :, :, width:] = dot(rows, wv[...]).astype(BF16).reshape(shape)
+            late_kv[i, :, :, :width] = dot(rows, wk[...]).astype(BF16).reshape(shape)
+            late_kv[i, :, :, width:] = dot(rows, wv[...]).astype(BF16).reshape(shape)
 
     mine = pl.ds(2 * step, 2)
 
     def rows_of(col):
-        return key_value[:, mine, :, pl.ds(col, HD)].reshape(-1, HD)
+        cols = pl.ds(col, HD)
+        parts = [ref[:, :, :, cols].reshape(-1, HD) for ref in kvs]
+        parts.append(late_kv[:, mine, :, cols].reshape(-1, HD))
+        return jnp.concatenate(parts, axis=0)
 
     def put(col, grad):
         cols = pl.ds(col, HD)
-        for at, (kind, i) in enumerate(places):
-            block = grad[at * 2 * sub : (at + 1) * 2 * sub].reshape(2, sub, HD)
-            grads[kind][i, :, :, cols] = block
-            (own_all, core_all)[kind][i, mine, :, cols] = block
+        for at, (kind, k, c) in enumerate(places):
+            block = grad[at * 2 * TILE : (at + 1) * 2 * TILE].reshape(2, TILE, HD)
+            tokens = pl.ds(c * TILE, TILE)
+            grads[kind][k, :, tokens, cols] = block
+            (own_all, core_all)[kind][k, mine, tokens, cols] = block
 
     zero = jnp.zeros((SPAN, HD), BF16)
     for h0 in range(0, heads, group):
@@ -223,13 +269,17 @@
         part(core_all.at[near:], slice(count, enc), rest_out)
 
 
-def attend(pieces, wk, wv, places, near, count, queries, cotangent):
+def attend(kvs, late, wk, wv, places, near, share, count, queries, cotangent):
     tokens, width = queries.shape
-    n, sub, enc = pieces[0].shape
-    total = len(places)
-    half = total // 2
+    n, enc = late[0].shape[0], wk.shape[0]
+    sub = share
+    half = len(places) // (2 * (share // TILE))
+    total = 2 * half
     rows = pl.BlockSpec((SPAN, width), lambda i: (i, 0))
     grads = pl.BlockSpec((half, 2, sub, 2 * width), lambda i: (0, i, 0, 0))
+
+    def kv_block(kv):
+        return pl.BlockSpec((kv.shape[0], 2, TILE, 2 * width), lambda i: (0, i, 0, 0))
 
     def once(shape):
         return pl.BlockSpec(shape, lambda i: (0,) * len(shape), pipeline_mode=pl.Buffered(1))
@@ -241,25 +291,27 @@
     parts.append((half - near, n, sub, enc - count))
     every = (half, n, sub, 2 * width)
     return pl.pallas_call(
-        functools.partial(attend_body, places, near),
+        functools.partial(attend_body, places, len(kvs), len(late), near),
         out_shape=[jax.ShapeDtypeStruct((tokens, width), BF16)] * 2
         + [jax.ShapeDtypeStruct(every, BF16)] * 2
         + [jax.ShapeDtypeStruct(part, F32) for part in parts],
         grid=(tokens // SPAN,),
-        in_specs=[once(x.shape) for x in pieces] + [once(wk.shape), once(wv.shape), rows, rows],
+        in_specs=[kv_block(kv) for kv in kvs]
+        + [once(x.shape) for x in late]
+        + [once(wk.shape), once(wv.shape), rows, rows],
         out_specs=[rows, rows, grads, grads] + [whole(part) for part in parts],
         scratch_shapes=[
-            pltpu.VMEM((total, n, sub, 2 * width), BF16),
+            pltpu.VMEM((len(late), n, TILE, 2 * width), BF16),
             pltpu.VMEM(every, BF16),
             pltpu.VMEM(every, BF16),
         ],
         compiler_params=params(VMEM_MORE),
         cost_estimate=cost(
-            16 * tokens * width * total * 2 * sub + 4 * n * sub * width * total * (enc + count),
+            16 * tokens * width * total * 2 * sub + 4 * n * width * (len(late) * TILE * enc + total * sub * count),
             8 * tokens * width + 8 * total * n * sub * width,
         ),
         name="attend",
-    )(*pieces, wk, wv, queries, cotangent)
+    )(*kvs, *late, wk, wv, queries, cotangent)
 
 
 def encode(x, axes):
@@ -329,7 +381,7 @@
             pltpu.VMEM((n_x + 1, n, sub, count), F32),
             pltpu.SemaphoreType.DMA((n_x + 1,)),
         ],
-        compiler_params=params(VMEM_GRADS),
+        compiler_params=params(),
         cost_estimate=cost(4 * rows * count * width, 2 * (count + 2 * rows) * width + 8 * rows * count),
         name="grads",
     )(d_core, d_own, wk, wv)
@@ -482,6 +534,7 @@
     n_slabs, n_tokens, enc = table.shape
     cap = max(2, (4 * spans + n_dp - 1) // n_dp)
     share = n_tokens // n_tp
+    n_chunks = share // TILE
 
     def over_core(x):
         return lax.ppermute(x, "tensor", [(t, t ^ 1) for t in range(n_tp)])
@@ -492,7 +545,6 @@
     def over_dp(x, d):
         return lax.ppermute(x, "dp", [(i, (i + d) % n_dp) for i in range(n_dp)])
 
-    nearest_first = sorted(range(1, n_dp), key=lambda d: min(d, n_dp - d))
     farthest_first = sorted(range(1, n_dp), key=lambda d: -min(d, n_dp - d))
 
     def to_all(xs, sign, distances=farthest_first):
@@ -502,34 +554,46 @@
     me, wanted, request = ask(owners, slots, n_dp, cap)
     asked = lax.psum(wanted, "dp")
 
-    sent = pack(me, asked, table, share, cap)
-    mine = {0: sent[0]}
-    for i, d in enumerate(nearest_first):
-        block = sent[d]
-        if i >= WINDOW:
-            held = nearest_first[i - WINDOW]
-            block, mine[held] = lax.optimization_barrier((block, mine[held]))
-        mine[d] = over_dp(block, -d)
-    far = [[over_x(mine[d], k) for k in range(1, n_x)] for d in range(n_dp)]
-    lists = [[mine[d] for d in range(n_dp)]]
-    lists += [[far[d][k] for d in range(n_dp)] for k in range(n_x - 1)]
-    mine, *far = compact(request, lists, n_requests)
-
-    pieces = [mine, *far]
-    pieces += [over_core(x) for x in pieces]
-    places = [(kind, k) for kind in range(2) for k in range(n_x)]
+    kvs, places = [], []
+    early = {}
+    sent = pack(me, asked, table, 0, share, cap)
+    for c in range(n_chunks):
+        rest = [d for d in farthest_first if d not in early]
+        arrived = [sent[0]] + [None] * (n_dp - 1)
+        for d, x in {**early, **to_all(sent, -1, rest)}.items():
+            arrived[d] = x
+        if c < n_chunks - 1:
+            sent = pack(me, asked, table, c + 1, share, cap)
+            early = to_all(sent, -1, farthest_first[:1])
+            early, arrived = lax.optimization_barrier((early, arrived))
+        if kvs:
+            arrived, kvs = lax.optimization_barrier((arrived, kvs))
+        mine = compact(request, arrived, n_requests)
+        near = [mine, over_core(mine)]
+        far = [over_x(mine, k) for k in range(1, n_x)]
+        if c < n_chunks - 1:
+            early = {**early, **to_all(sent, -1, farthest_first[1:4])}
+            early, far = lax.optimization_barrier((early, far))
+            far = far + [over_core(x) for x in far]
+            kvs = kvs + [project(near + far, key_weight, value_weight)]
+        else:
+            near = project(near, key_weight, value_weight)
+            near, far = lax.optimization_barrier((near, far))
+            late = far + [over_core(x) for x in far]
+            kvs = kvs + [near]
+        places += [(kind, 0, c) for kind in range(2)]
+        places += [(kind, k, c) for kind in range(2) for k in range(1, n_x)]
 
     split = 3 * LANES
     parts = ((0, split), (split, enc - split))
     attended, d_query, d_own, d_core, near, far, own, far_b = attend(
-        pieces, key_weight, value_weight, places, 1, split, queries, cotangent
+        kvs, late, key_weight, value_weight, places, 1, share, split, queries, cotangent
     )
     far_got = over_core(far)
     near_got = over_core(near)
     far_got_b = over_core(far_b)
     cuts = (parts[0][1] // LANES,)
     codes = far_codes(own, far_got, cuts)
-    near_got, d_own = lax.optimization_barrier((near_got, d_own))
     near_b, own_b = grads_of(d_core, d_own, key_weight, value_weight, parts[1])
 
     codes = [[over_x(x, n_x - k) for x in piece] for k, piece in enumerate(codes, 1)]

time: 190 us -> 183 us (0.963)
  waiting for transfers between devices: 53.6 us -> 46.1 us
  starting transfers between devices: 64.7 us -> 59.1 us
  local copies, waits for them, and re-layouts: 4.9 us -> 9.18 us
    ppermute x10 -> x4, starting transfers between devices: 11 us -> 2.52 us  [over_x(): lax.ppermute(x, 'tensor', [(t, (t + 2 * d) % n_tp) for t in range(n_tp)])]
    ppermute x21 -> x28, waiting for transfers between devices: 35.3 us -> 27.4 us  [over_dp(): return lax.ppermute(x, 'dp', [(i, (i + d) % n_dp) for i in range(n_dp)])]
    pallas_call x3 -> x7, Pallas kernels: 38 us -> 43.7 us  [the longest x1 22.1 us: attend(): pl.pallas_call(functools.partial(attend_body, places, len(kvs), len(late)...]
    unnamed x18 -> x30, local copies, waits for them, and re-layouts: 4.9 us -> 9.18 us
    pallas_call x1, Pallas kernels: 8.27 us -> 4.14 us  [grads_of(): pl.pallas_call(functools.partial(grads_body, first), out_shape=[jax.Shape...]
    ppermute x6 -> x8, starting transfers between devices: 12.4 us -> 14.3 us  [over_core(): return lax.ppermute(x, 'tensor', [(t, t ^ 1) for t in range(n_tp)])]
    ppermute x21 -> x28, starting transfers between devices: 41.3 us -> 42.3 us  [over_dp(): return lax.ppermute(x, 'dp', [(i, (i + d) % n_dp) for i in range(n_dp)])]
    ppermute x10 -> x4, waiting for transfers between devices: 11.3 us -> 11.7 us  [over_x(): lax.ppermute(x, 'tensor', [(t, (t + 2 * d) % n_tp) for t in range(n_tp)])]
  transfers between devices with their start and end apart: 37 -> 40, of which waited for: 17 -> 17; matrix products, arithmetic and copies ran while one was open for 0% -> 0% of each run, Pallas kernels for 7% -> 13%
where the time goes in v13:
time: 183 us; the launch traced here: 182 us
  starting transfers between devices  59.1 us (32%)
  Pallas kernels  58.3 us (32%)
  waiting for transfers between devices  46.1 us (25%)
  local copies, waits for them, and re-layouts  9.18 us (5%)
  blocking collectives  8.59 us (5%)
    ppermute x28, starting transfers between devices, over_dp(): return lax.ppermute(x, 'dp', [(i, (i + d) % n_dp) for i in range(n_dp)])  42.3 us
    ppermute x28, waiting for transfers between devices, over_dp(): return lax.ppermute(x, 'dp', [(i, (i + d) % n_dp) for i in range(n_dp)])  27.4 us
    pallas_call x1, Pallas kernels, attend(): pl.pallas_call(functools.partial(attend_body, places, len(kvs), len(late)...  22.1 us
    ppermute x8, starting transfers between devices, over_core(): return lax.ppermute(x, 'tensor', [(t, t ^ 1) for t in range(n_tp)])  14.3 us
    ppermute x4, waiting for transfers between devices, over_x(): lax.ppermute(x, 'tensor', [(t, (t + 2 * d) % n_tp) for t in range(n_tp)])  11.7 us
    pallas_call x2, Pallas kernels, project(): pl.pallas_call(functools.partial(project_body, n_in), out_shape=jax.Shape...  9.74 us
    unnamed x30, local copies, waits for them, and re-layouts  9.18 us
    psum x1, blocking collectives, on_device(): asked = lax.psum(wanted, 'dp')  8.59 us
  transfers between devices with their start and end apart: 40, of which 17 were waited for; matrix products, arithmetic and copies ran while one was open for 0% of the time, Pallas kernels for 13%

profile of v13, /device:TPU:13, one launch (start us, length us, event | category | flops | bytes accessed | tf_op | source)
XLA Modules:
  0.0 182.4 jit_solution(9199957977600739425)
XLA Ops:
  2.2 8.6 %psum.7.asked = s32[8,32]{1,0:T(8,128)} all-reduce(s32[8,32]{1,0:T(8,128)} %get-tuple-element.86), channel_id=1, replica_groups=mesh['dp'=8,'tensor'=4] {'dp'}, use_global_device_ids=true, to_apply=%region_0.0 | all-reduce | flops 256 | bytes 2048 | tf_op jit(solution)/shard_map/psum | solution.py:555
  10.8 4.0 %pack_rows.3 = (bf16[4,16,896]{2,1,0:T(8,128)(2,1)}, bf16[4,16,896]{2,1,0:T(8,128)(2,1)}, bf16[4,16,896]{2,1,0:T(8,128)(2,1)}, bf16[4,16,896]{2,1,0:T(8,128)(2,1...) custom-call(s32[1]{0:T(128)} %get-tuple-element.85.me, ...), custom_call_target="tpu_custom_call" | custom-call | bytes 1835008 | tf_op jit(solution)/shard_map/pack_rows/pallas_call | solution.py:97
  19.0 4.1 %pack_rows.2 = (bf16[4,16,896]{2,1,0:T(8,128)(2,1)}, bf16[4,16,896]{2,1,0:T(8,128)(2,1)}, bf16[4,16,896]{2,1,0:T(8,128)(2,1)}, bf16[4,16,896]{2,1,0:T(8,128)(2,1...) custom-call(s32[1]{0:T(128)} %get-tuple-element.85.me, ...), custom_call_target="tpu_custom_call" | custom-call | bytes 1835008 | tf_op jit(solution)/shard_map/pack_rows/pallas_call | solution.py:97
  26.5 5.8 %collective-permute-start.3 = (bf16[4,16,896]{2,1,0:T(8,128)(2,1)}, bf16[4,16,896]{2,1,0:T(8,128)(2,1)S(1)}, u32[]{:S(2)}, u32[]{:S(2)}) collective-permute-start(bf16[4,16,896]{2,1,0:T(8,128)(2,1)} %get-tuple-element.91), channel_id=1, source_target_pairs={{0,16},{4,20},{8,24},{12,28},{16,0},{20,4},{24,8},{28,12},{1,17},{... | collective-permute-start | bytes 344072 | tf_op jit(solution)/shard_map/ppermute | solution.py:546
  34.2 2.4 %collective-permute-done.9.refs_6_ = bf16[4,16,896]{2,1,0:T(8,128)(2,1)S(1)} collective-permute-done((bf16[4,16,896]{2,1,0:T(8,128)(2,1)S(1)}, bf16[4,16,896]{2,1,0:T(8,128)(2,1)S(1)}, u32[]{:S(2)}, u32[]{:S(2)}) %collective-permute-start.9) | collective-permute-done | bytes 114720 | tf_op jit(solution)/shard_map/ppermute | solution.py:546
  38.2 2.6 %collective-permute-done.3.refs_4_ = bf16[4,16,896]{2,1,0:T(8,128)(2,1)S(1)} collective-permute-done((bf16[4,16,896]{2,1,0:T(8,128)(2,1)}, bf16[4,16,896]{2,1,0:T(8,128)(2,1)S(1)}, u32[]{:S(2)}, u32[]{:S(2)}) %collective-permute-start.3) | collective-permute-done | bytes 114720 | tf_op jit(solution)/shard_map/ppermute | solution.py:546
  47.7 6.8 %collective-permute-start.15 = (bf16[16,16,896]{2,1,0:T(8,128)(2,1)S(1)}, bf16[16,16,896]{2,1,0:T(8,128)(2,1)S(1)}, u32[]{:S(2)}, u32[]{:S(2)}) collective-permute-start(bf16[16,16,896]{2,1,0:T(8,128)(2,1)S(1)} %compact_rows.2.refs_0_), channel_id=1, source_target_pairs={{0,1},{1,0},{2,3},{3,2},{4,5},{5,4},{6,7},{7,6},{8,9},{9,8},{10,11... | collective-permute-start | bytes 1376264 | tf_op jit(solution)/shard_map/ppermute | solution.py:540
  54.5 4.3 %collective-permute-start.16 = (bf16[16,16,896]{2,1,0:T(8,128)(2,1)S(1)}, bf16[16,16,896]{2,1,0:T(8,128)(2,1)S(1)}, u32[]{:S(2)}, u32[]{:S(2)}) collective-permute-start(bf16[16,16,896]{2,1,0:T(8,128)(2,1)S(1)} %collective-permute-done.12.refs_2_), channel_id=1, source_target_pairs={{0,1},{1,0},{2,3},{3,2},{4,5},{5,4},{6,7},{7,6},{8,9},{9,8},{10,11... | collective-permute-start | bytes 1376264 | tf_op jit(solution)/shard_map/ppermute | solution.py:540
  64.5 6.1 %project.2.refs_0_ = bf16[4,16,16,2048]{3,2,1,0:T(8,128)(2,1)S(1)} custom-call(bf16[16,16,896]{2,1,0:T(8,128)(2,1)S(1)} %compact_rows.2.refs_0_, bf16[16,16,896]{2,1,0:T(8,128)(2,1)S(1)} %collective-permute-done.15.refs_1_, bf16[16,16,896]{2,1,0:T(8,128)(2,1)S(1)} %collective-permute-done.12.refs_2_, ...), custom_call_target="tpu_custom_call" | custom-call | flops 3758096384 | bytes 9699328 | tf_op jit(solution)/shard_map/project/pallas_call | solution.py:174
  76.7 3.6 %project.3.refs_1_ = bf16[2,16,16,2048]{3,2,1,0:T(8,128)(2,1)S(1)} custom-call(bf16[16,16,896]{2,1,0:T(8,128)(2,1)S(1)} %compact_rows.3.refs_0_, bf16[16,16,896]{2,1,0:T(8,128)(2,1)S(1)} %collective-permute-done.17.refs_1_, bf16[896,1024]{1,0:T(8,128)(2,1)S(1)} %copy-done.4, bf16[896,1024]{1,0:T(8,128)(2,1)S(1)} %copy-done.5), custom_call_target="tpu_custom_call" | custom-call | flops 1879048192 | bytes 6684672 | tf_op jit(solution)/shard_map/project/pallas_call | solution.py:174
  81.6 5.8 %collective-permute-done.18.refs_2_ = bf16[16,16,896]{2,1,0:T(8,128)(2,1)S(1)} collective-permute-done((bf16[16,16,896]{2,1,0:T(8,128)(2,1)S(1)}, bf16[16,16,896]{2,1,0:T(8,128)(2,1)S(1)}, u32[]{:S(2)}, u32[]{:S(2)}) %collective-permute-start.18) | collective-permute-done | bytes 458784 | tf_op jit(solution)/shard_map/ppermute | solution.py:543
  89.7 22.1 %attend.1 = (bf16[512,1024]{1,0:T(8,128)(2,1)}, bf16[512,1024]{1,0:T(8,128)(2,1)}, bf16[2,16,32,2048]{3,2,1,0:T(8,128)(2,1)}, bf16[2,16,32,2048]{3,2,1,0:T(8,128...) custom-call(bf16[4,16,16,2048]{3,2,1,0:T(8,128)(2,1)} %copy-done.12,, ...), custom_call_target="tpu_custom_call" | custom-call | flops 7247757312 | bytes 20971520 | tf_op jit(solution)/shard_map/attend/pallas_call | solution.py:293
  119.1 4.1 %grads.1 = (f32[1,16,32,512]{3,2,1,0:T(8,128)S(1)}, f32[2,16,32,512]{3,2,1,0:T(8,128)S(1)}) custom-call(bf16[2,16,32,2048]{3,2,1,0:T(8,128)(2,1)S(1)} %copy-done.11, bf16[2,16,32,2048]{3,2,1,0:T(8,128)(2,1)S(1)} %copy-done.10, bf16[896,1024]{1,0:T(8,128)(2,1)S(1)} %copy-done.4, bf16[896,1024]{1,0:T(8,128)(2,1)S(1)} %copy-done.6), custom_call_target="tpu_custom_call" | custom-call | flops 4294967296 | bytes 14680064 | tf_op jit(solution)/shard_map/grads/pallas_call | solution.py:366
  126.8 2.7 %collective-permute-done.20.got = f32[1,16,32,384]{3,2,1,0:T(8,128)S(1)} collective-permute-done((f32[1,16,32,384]{3,2,1,0:T(8,128)S(1)}, f32[1,16,32,384]{3,2,1,0:T(8,128)S(1)}, u32[]{:S(2)}, u32[]{:S(2)}) %collective-permute-start.20) | collective-permute-done | bytes 786464 | tf_op jit(solution)/shard_map/ppermute | solution.py:540
  135.4 4.2 %collective-permute-done.25.rest_0_ = s16[65,32,128]{2,1,0:T(8,128)(2,1)S(1)} collective-permute-done((s16[65,32,128]{2,1,0:T(8,128)(2,1)S(1)}, s16[65,32,128]{2,1,0:T(8,128)(2,1)S(1)}, u32[]{:S(2)}, u32[]{:S(2)}) %collective-permute-start.25) | collective-permute-done | bytes 532512 | tf_op jit(solution)/shard_map/ppermute | solution.py:543
  143.7 2.3 %collective-permute-start.38 = (s16[25,16,128]{2,1,0:T(8,128)(2,1)S(1)}, s16[25,16,128]{2,1,0:T(8,128)(2,1)S(1)}, u32[]{:S(2)}, u32[]{:S(2)}) collective-permute-start(s16[25,16,128]{2,1,0:T(8,128)(2,1)S(1)} %get-tuple-element.165), channel_id=1, source_target_pairs={{0,24},{4,28},{8,0},{12,4},{16,8},{20,12},{24,16},{28,20},{1,25},{... | collective-permute-start | bytes 307208 | tf_op jit(solution)/shard_map/ppermute | solution.py:546
  146.0 6.6 %collective-permute-start.39 = (s16[25,16,128]{2,1,0:T(8,128)(2,1)S(1)}, s16[25,16,128]{2,1,0:T(8,128)(2,1)S(1)}, u32[]{:S(2)}, u32[]{:S(2)}) collective-permute-start(s16[25,16,128]{2,1,0:T(8,128)(2,1)S(1)} %get-tuple-element.166), channel_id=1, source_target_pairs={{0,28},{4,0},{8,4},{12,8},{16,12},{20,16},{24,20},{28,24},{1,29},{... | collective-permute-start | bytes 307208 | tf_op jit(solution)/shard_map/ppermute | solution.py:546
  154.8 3.0 %collective-permute-done.38.refs_6_ = s16[25,16,128]{2,1,0:T(8,128)(2,1)S(1)} collective-permute-done((s16[25,16,128]{2,1,0:T(8,128)(2,1)S(1)}, s16[25,16,128]{2,1,0:T(8,128)(2,1)S(1)}, u32[]{:S(2)}, u32[]{:S(2)}) %collective-permute-start.38) | collective-permute-done | bytes 102432 | tf_op jit(solution)/shard_map/ppermute | solution.py:546
  160.2 2.4 %collective-permute-start.32 = (s16[33,16,128]{2,1,0:T(8,128)(2,1)S(1)}, s16[33,16,128]{2,1,0:T(8,128)(2,1)S(1)}, u32[]{:S(2)}, u32[]{:S(2)}) collective-permute-start(s16[33,16,128]{2,1,0:T(8,128)(2,1)S(1)} %get-tuple-element.158), channel_id=1, source_target_pairs={{0,28},{4,0},{8,4},{12,8},{16,12},{20,16},{24,20},{28,24},{1,29},{... | collective-permute-start | bytes 405512 | tf_op jit(solution)/shard_map/ppermute | solution.py:546
  162.6 2.9 %gather_grads.2.refs_8_ = f32[16,32,896]{2,1,0:T(8,128)} custom-call(s32[1]{0:T(128)} %get-tuple-element.85.me, s32[8,32]{1,0:T(8,128)S(1)} %copy-done.2, s16[25,16,128]{2,1,0:T(8,128)(2,1)S(1)} %get-tuple-element.159.refs_0_, s16[25,16,128]{2,1,0:T(8,128)(2,1)S(1)} %collective-permute-done.33.refs_1_, ...), custom_call_target="tpu_custom_call" | custom-call | bytes 1572864 | tf_op jit(solution)/shard_map/gather_grads/pallas_call | solution.py:515
  165.4 4.6 %collective-permute-done.28.refs_3_ = s16[33,16,128]{2,1,0:T(8,128)(2,1)S(1)} collective-permute-done((s16[33,16,128]{2,1,0:T(8,128)(2,1)S(1)}, s16[33,16,128]{2,1,0:T(8,128)(2,1)S(1)}, u32[]{:S(2)}, u32[]{:S(2)}) %collective-permute-start.28) | collective-permute-done | bytes 135200 | tf_op jit(solution)/shard_map/ppermute | solution.py:546
  170.0 2.9 %collective-permute-done.29.refs_4_ = s16[33,16,128]{2,1,0:T(8,128)(2,1)S(1)} collective-permute-done((s16[33,16,128]{2,1,0:T(8,128)(2,1)S(1)}, s16[33,16,128]{2,1,0:T(8,128)(2,1)S(1)}, u32[]{:S(2)}, u32[]{:S(2)}) %collective-permute-start.29) | collective-permute-done | bytes 135200 | tf_op jit(solution)/shard_map/ppermute | solution.py:546
  172.9 4.5 %collective-permute-done.31.refs_6_ = s16[33,16,128]{2,1,0:T(8,128)(2,1)S(1)} collective-permute-done((s16[33,16,128]{2,1,0:T(8,128)(2,1)S(1)}, s16[33,16,128]{2,1,0:T(8,128)(2,1)S(1)}, u32[]{:S(2)}, u32[]{:S(2)}) %collective-permute-start.31) | collective-permute-done | bytes 135200 | tf_op jit(solution)/shard_map/ppermute | solution.py:546
  179.2 3.0 %gather_grads.3 = f32[16,32,896]{2,1,0:T(8,128)} custom-call(s32[1]{0:T(128)} %get-tuple-element.85.me, s32[8,32]{1,0:T(8,128)S(1)} %copy-done.2, s16[33,16,128]{2,1,0:T(8,128)(2,1)S(1)} %get-tuple-element.151.refs_0_, s16[33,16,128]{2,1,0:T(8,128)(2,1)S(1)} %collective-permute-done.26.refs_1_, ...), custom_call_target="tpu_custom_call", output_to_operand_aliasing={{}: (10, {})} | custom-call | bytes 2097152 | tf_op jit(solution)/shard_map/gather_grads/pallas_call | solution.py:515
  (102 shorter events, 61.9 us)
Async XLA Ops:
  17.7 14.5 %collective-permute-start.7 = (bf16[4,16,896]{2,1,0:T(8,128)(2,1)}, bf16[4,16,896]{2,1,0:T(8,128)(2,1)S(1)}, u32[]{:S(2)}, u32[]{:S(2)}) collective-permute-start(bf16[4,16,896]{2,1,0:T(8,128)(2,1)} %get-tuple-element.96), channel_id=1, source_target_pairs={{0,16},{4,20},{8,24},{12,28},{16,0},{20,4},{24,8},{28,12},{1,17},{... | collective-permute-start | bytes 344072 | tf_op jit(solution)/shard_map/ppermute | solution.py:546
  19.0 15.1 %collective-permute-start.8 = (bf16[4,16,896]{2,1,0:T(8,128)(2,1)}, bf16[4,16,896]{2,1,0:T(8,128)(2,1)S(1)}, u32[]{:S(2)}, u32[]{:S(2)}) collective-permute-start(bf16[4,16,896]{2,1,0:T(8,128)(2,1)} %get-tuple-element.97), channel_id=1, source_target_pairs={{0,12},{4,16},{8,20},{12,24},{16,28},{20,0},{24,4},{28,8},{1,13},{... | collective-permute-start | bytes 344072 | tf_op jit(solution)/shard_map/ppermute | solution.py:546
  23.2 13.4 %collective-permute-start.9 = (bf16[4,16,896]{2,1,0:T(8,128)(2,1)S(1)}, bf16[4,16,896]{2,1,0:T(8,128)(2,1)S(1)}, u32[]{:S(2)}, u32[]{:S(2)}) collective-permute-start(bf16[4,16,896]{2,1,0:T(8,128)(2,1)S(1)} %copy-done.14), channel_id=1, source_target_pairs={{0,8},{4,12},{8,16},{12,20},{16,24},{20,28},{24,0},{28,4},{1,9},{5... | collective-permute-start | bytes 344072 | tf_op jit(solution)/shard_map/ppermute | solution.py:546
  24.7 13.5 %collective-permute-start.10 = (bf16[4,16,896]{2,1,0:T(8,128)(2,1)S(1)}, bf16[4,16,896]{2,1,0:T(8,128)(2,1)S(1)}, u32[]{:S(2)}, u32[]{:S(2)}) collective-permute-start(bf16[4,16,896]{2,1,0:T(8,128)(2,1)S(1)} %copy-done.13), channel_id=1, source_target_pairs={{0,4},{4,8},{8,12},{12,16},{16,20},{20,24},{24,28},{28,0},{1,5},{5... | collective-permute-start | bytes 344072 | tf_op jit(solution)/shard_map/ppermute | solution.py:546
  26.5 14.3 %collective-permute-start.3 = (bf16[4,16,896]{2,1,0:T(8,128)(2,1)}, bf16[4,16,896]{2,1,0:T(8,128)(2,1)S(1)}, u32[]{:S(2)}, u32[]{:S(2)}) collective-permute-start(bf16[4,16,896]{2,1,0:T(8,128)(2,1)} %get-tuple-element.91), channel_id=1, source_target_pairs={{0,16},{4,20},{8,24},{12,28},{16,0},{20,4},{24,8},{28,12},{1,17},{... | collective-permute-start | bytes 344072 | tf_op jit(solution)/shard_map/ppermute | solution.py:546
  42.6 11.9 %collective-permute-start.12 = (bf16[16,16,896]{2,1,0:T(8,128)(2,1)S(1)}, bf16[16,16,896]{2,1,0:T(8,128)(2,1)S(1)}, u32[]{:S(2)}, u32[]{:S(2)}) collective-permute-start(bf16[16,16,896]{2,1,0:T(8,128)(2,1)S(1)} %compact_rows.2.refs_0_), channel_id=1, source_target_pairs={{0,2},{1,3},{2,0},{3,1},{4,6},{5,7},{6,4},{7,5},{8,10},{9,11},{10,... | collective-permute-start | bytes 1376264 | tf_op jit(solution)/shard_map/ppermute | solution.py:543
  47.7 15.2 %collective-permute-start.15 = (bf16[16,16,896]{2,1,0:T(8,128)(2,1)S(1)}, bf16[16,16,896]{2,1,0:T(8,128)(2,1)S(1)}, u32[]{:S(2)}, u32[]{:S(2)}) collective-permute-start(bf16[16,16,896]{2,1,0:T(8,128)(2,1)S(1)} %compact_rows.2.refs_0_), channel_id=1, source_target_pairs={{0,1},{1,0},{2,3},{3,2},{4,5},{5,4},{6,7},{7,6},{8,9},{9,8},{10,11... | collective-permute-start | bytes 1376264 | tf_op jit(solution)/shard_map/ppermute | solution.py:540
  58.8 13.8 %collective-permute-start = (bf16[4,16,896]{2,1,0:T(8,128)(2,1)}, bf16[4,16,896]{2,1,0:T(8,128)(2,1)S(1)}, u32[]{:S(2)}, u32[]{:S(2)}) collective-permute-start(bf16[4,16,896]{2,1,0:T(8,128)(2,1)} %get-tuple-element.88), channel_id=1, source_target_pairs={{0,28},{4,0},{8,4},{12,8},{16,12},{20,16},{24,20},{28,24},{1,29},{... | collective-permute-start | bytes 344072 | tf_op jit(solution)/shard_map/ppermute | solution.py:546
  58.8 13.8 %collective-permute-start.13 = (bf16[4,16,896]{2,1,0:T(8,128)(2,1)}, bf16[4,16,896]{2,1,0:T(8,128)(2,1)S(1)}, u32[]{:S(2)}, u32[]{:S(2)}) collective-permute-start(bf16[4,16,896]{2,1,0:T(8,128)(2,1)} %get-tuple-element.115), channel_id=1, source_target_pairs={{0,8},{4,12},{8,16},{12,20},{16,24},{20,28},{24,0},{28,4},{1,9},{5... | collective-permute-start | bytes 344072 | tf_op jit(solution)/shard_map/ppermute | solution.py:546
  61.0 11.6 %collective-permute-start.14 = (bf16[4,16,896]{2,1,0:T(8,128)(2,1)}, bf16[4,16,896]{2,1,0:T(8,128)(2,1)S(1)}, u32[]{:S(2)}, u32[]{:S(2)}) collective-permute-start(bf16[4,16,896]{2,1,0:T(8,128)(2,1)} %get-tuple-element.116), channel_id=1, source_target_pairs={{0,4},{4,8},{8,12},{12,16},{16,20},{20,24},{24,28},{28,0},{1,5},{5... | collective-permute-start | bytes 344072 | tf_op jit(solution)/shard_map/ppermute | solution.py:546
  75.3 12.1 %collective-permute-start.18 = (bf16[16,16,896]{2,1,0:T(8,128)(2,1)S(1)}, bf16[16,16,896]{2,1,0:T(8,128)(2,1)S(1)}, u32[]{:S(2)}, u32[]{:S(2)}) collective-permute-start(bf16[16,16,896]{2,1,0:T(8,128)(2,1)S(1)} %compact_rows.3.refs_0_), channel_id=1, source_target_pairs={{0,2},{1,3},{2,0},{3,1},{4,6},{5,7},{6,4},{7,5},{8,10},{9,11},{10,... | collective-permute-start | bytes 1376264 | tf_op jit(solution)/shard_map/ppermute | solution.py:543
  112.2 13.9 %collective-permute-start.24 = (f32[1,16,32,512]{3,2,1,0:T(8,128)S(1)}, f32[1,16,32,512]{3,2,1,0:T(8,128)S(1)}, u32[]{:S(2)}, u32[]{:S(2)}) collective-permute-start(f32[1,16,32,512]{3,2,1,0:T(8,128)S(1)} %get-tuple-element.149), channel_id=1, source_target_pairs={{0,1},{1,0},{2,3},{3,2},{4,5},{5,4},{6,7},{7,6},{8,9},{9,8},{10,11... | collective-permute-start | bytes 3145736 | tf_op jit(solution)/shard_map/ppermute | solution.py:540
  126.5 13.2 %collective-permute-start.25 = (s16[65,32,128]{2,1,0:T(8,128)(2,1)S(1)}, s16[65,32,128]{2,1,0:T(8,128)(2,1)S(1)}, u32[]{:S(2)}, u32[]{:S(2)}) collective-permute-start(s16[65,32,128]{2,1,0:T(8,128)(2,1)S(1)} %far_codes.3), channel_id=1, source_target_pairs={{0,2},{1,3},{2,0},{3,1},{4,6},{5,7},{6,4},{7,5},{8,10},{9,11},{10,... | collective-permute-start | bytes 1597448 | tf_op jit(solution)/shard_map/ppermute | solution.py:543
  130.7 12.0 %collective-permute-start.33 = (s16[25,16,128]{2,1,0:T(8,128)(2,1)S(1)}, s16[25,16,128]{2,1,0:T(8,128)(2,1)S(1)}, u32[]{:S(2)}, u32[]{:S(2)}) collective-permute-start(s16[25,16,128]{2,1,0:T(8,128)(2,1)S(1)} %get-tuple-element.160), channel_id=1, source_target_pairs={{0,4},{4,8},{8,12},{12,16},{16,20},{20,24},{24,28},{28,0},{1,5},{5... | collective-permute-start | bytes 307208 | tf_op jit(solution)/shard_map/ppermute | solution.py:546
  141.0 19.0 %collective-permute-start.26 = (s16[33,16,128]{2,1,0:T(8,128)(2,1)S(1)}, s16[33,16,128]{2,1,0:T(8,128)(2,1)S(1)}, u32[]{:S(2)}, u32[]{:S(2)}) collective-permute-start(s16[33,16,128]{2,1,0:T(8,128)(2,1)S(1)} %get-tuple-element.152), channel_id=1, source_target_pairs={{0,4},{4,8},{8,12},{12,16},{16,20},{20,24},{24,28},{28,0},{1,5},{5... | collective-permute-start | bytes 405512 | tf_op jit(solution)/shard_map/ppermute | solution.py:546
  142.7 17.4 %collective-permute-start.27 = (s16[33,16,128]{2,1,0:T(8,128)(2,1)S(1)}, s16[33,16,128]{2,1,0:T(8,128)(2,1)S(1)}, u32[]{:S(2)}, u32[]{:S(2)}) collective-permute-start(s16[33,16,128]{2,1,0:T(8,128)(2,1)S(1)} %get-tuple-element.153), channel_id=1, source_target_pairs={{0,8},{4,12},{8,16},{12,20},{16,24},{20,28},{24,0},{28,4},{1,9},{5... | collective-permute-start | bytes 405512 | tf_op jit(solution)/shard_map/ppermute | solution.py:546
  142.7 11.9 %collective-permute-start.37 = (s16[25,16,128]{2,1,0:T(8,128)(2,1)S(1)}, s16[25,16,128]{2,1,0:T(8,128)(2,1)S(1)}, u32[]{:S(2)}, u32[]{:S(2)}) collective-permute-start(s16[25,16,128]{2,1,0:T(8,128)(2,1)S(1)} %get-tuple-element.164), channel_id=1, source_target_pairs={{0,20},{4,24},{8,28},{12,0},{16,4},{20,8},{24,12},{28,16},{1,21},{... | collective-permute-start | bytes 307208 | tf_op jit(solution)/shard_map/ppermute | solution.py:546
  143.7 14.2 %collective-permute-start.38 = (s16[25,16,128]{2,1,0:T(8,128)(2,1)S(1)}, s16[25,16,128]{2,1,0:T(8,128)(2,1)S(1)}, u32[]{:S(2)}, u32[]{:S(2)}) collective-permute-start(s16[25,16,128]{2,1,0:T(8,128)(2,1)S(1)} %get-tuple-element.165), channel_id=1, source_target_pairs={{0,24},{4,28},{8,0},{12,4},{16,8},{20,12},{24,16},{28,20},{1,25},{... | collective-permute-start | bytes 307208 | tf_op jit(solution)/shard_map/ppermute | solution.py:546
  146.0 12.9 %collective-permute-start.39 = (s16[25,16,128]{2,1,0:T(8,128)(2,1)S(1)}, s16[25,16,128]{2,1,0:T(8,128)(2,1)S(1)}, u32[]{:S(2)}, u32[]{:S(2)}) collective-permute-start(s16[25,16,128]{2,1,0:T(8,128)(2,1)S(1)} %get-tuple-element.166), channel_id=1, source_target_pairs={{0,28},{4,0},{8,4},{12,8},{16,12},{20,16},{24,20},{28,24},{1,29},{... | collective-permute-start | bytes 307208 | tf_op jit(solution)/shard_map/ppermute | solution.py:546
  154.6 15.4 %collective-permute-start.28 = (s16[33,16,128]{2,1,0:T(8,128)(2,1)S(1)}, s16[33,16,128]{2,1,0:T(8,128)(2,1)S(1)}, u32[]{:S(2)}, u32[]{:S(2)}) collective-permute-start(s16[33,16,128]{2,1,0:T(8,128)(2,1)S(1)} %get-tuple-element.154), channel_id=1, source_target_pairs={{0,12},{4,16},{8,20},{12,24},{16,28},{20,0},{24,4},{28,8},{1,13},{... | collective-permute-start | bytes 405512 | tf_op jit(solution)/shard_map/ppermute | solution.py:546
  157.9 15.1 %collective-permute-start.29 = (s16[33,16,128]{2,1,0:T(8,128)(2,1)S(1)}, s16[33,16,128]{2,1,0:T(8,128)(2,1)S(1)}, u32[]{:S(2)}, u32[]{:S(2)}) collective-permute-start(s16[33,16,128]{2,1,0:T(8,128)(2,1)S(1)} %get-tuple-element.155), channel_id=1, source_target_pairs={{0,16},{4,20},{8,24},{12,28},{16,0},{20,4},{24,8},{28,12},{1,17},{... | collective-permute-start | bytes 405512 | tf_op jit(solution)/shard_map/ppermute | solution.py:546
  159.0 14.0 %collective-permute-start.30 = (s16[33,16,128]{2,1,0:T(8,128)(2,1)S(1)}, s16[33,16,128]{2,1,0:T(8,128)(2,1)S(1)}, u32[]{:S(2)}, u32[]{:S(2)}) collective-permute-start(s16[33,16,128]{2,1,0:T(8,128)(2,1)S(1)} %get-tuple-element.156), channel_id=1, source_target_pairs={{0,20},{4,24},{8,28},{12,0},{16,4},{20,8},{24,12},{28,16},{1,21},{... | collective-permute-start | bytes 405512 | tf_op jit(solution)/shard_map/ppermute | solution.py:546
  159.9 17.5 %collective-permute-start.31 = (s16[33,16,128]{2,1,0:T(8,128)(2,1)S(1)}, s16[33,16,128]{2,1,0:T(8,128)(2,1)S(1)}, u32[]{:S(2)}, u32[]{:S(2)}) collective-permute-start(s16[33,16,128]{2,1,0:T(8,128)(2,1)S(1)} %get-tuple-element.157), channel_id=1, source_target_pairs={{0,24},{4,28},{8,0},{12,4},{16,8},{20,12},{24,16},{28,20},{1,25},{... | collective-permute-start | bytes 405512 | tf_op jit(solution)/shard_map/ppermute | solution.py:546
  160.2 19.0 %collective-permute-start.32 = (s16[33,16,128]{2,1,0:T(8,128)(2,1)S(1)}, s16[33,16,128]{2,1,0:T(8,128)(2,1)S(1)}, u32[]{:S(2)}, u32[]{:S(2)}) collective-permute-start(s16[33,16,128]{2,1,0:T(8,128)(2,1)S(1)} %get-tuple-element.158), channel_id=1, source_target_pairs={{0,28},{4,0},{8,4},{12,8},{16,12},{20,16},{24,20},{28,24},{1,29},{... | collective-permute-start | bytes 405512 | tf_op jit(solution)/shard_map/ppermute | solution.py:546
  (31 other events, 325.4 us)

commit v14 on v13

--- a/solution.py
+++ b/solution.py
@@ -555,7 +555,7 @@
     asked = lax.psum(wanted, "dp")
 
     kvs, places = [], []
-    early = {}
+    early, pieces = {}, []
     sent = pack(me, asked, table, 0, share, cap)
     for c in range(n_chunks):
         rest = [d for d in farthest_first if d not in early]
@@ -566,25 +566,24 @@
             sent = pack(me, asked, table, c + 1, share, cap)
             early = to_all(sent, -1, farthest_first[:1])
             early, arrived = lax.optimization_barrier((early, arrived))
-        if kvs:
-            arrived, kvs = lax.optimization_barrier((arrived, kvs))
         mine = compact(request, arrived, n_requests)
-        near = [mine, over_core(mine)]
+        if pieces:
+            mine, pieces = lax.optimization_barrier((mine, pieces))
+            kvs = [project(pieces, key_weight, value_weight)]
         far = [over_x(mine, k) for k in range(1, n_x)]
         if c < n_chunks - 1:
-            early = {**early, **to_all(sent, -1, farthest_first[1:4])}
-            early, far = lax.optimization_barrier((early, far))
-            far = far + [over_core(x) for x in far]
-            kvs = kvs + [project(near + far, key_weight, value_weight)]
+            early = {**early, **to_all(sent, -1, farthest_first[1:5])}
+            early, far, mine = lax.optimization_barrier((early, far, mine))
+            pieces = [mine, over_core(mine)] + far + [over_core(x) for x in far]
         else:
-            near = project(near, key_weight, value_weight)
-            near, far = lax.optimization_barrier((near, far))
+            near = project([mine, over_core(mine)], key_weight, value_weight)
+            kvs, near, far = lax.optimization_barrier((kvs, near, far))
             late = far + [over_core(x) for x in far]
             kvs = kvs + [near]
         places += [(kind, 0, c) for kind in range(2)]
         places += [(kind, k, c) for kind in range(2) for k in range(1, n_x)]
 
-    split = 3 * LANES
+    split = 2 * LANES
     parts = ((0, split), (split, enc - split))
     attended, d_query, d_own, d_core, near, far, own, far_b = attend(
         kvs, late, key_weight, value_weight, places, 1, share, split, queries, cotangent
@@ -602,13 +601,16 @@
     sent = send_codes(request, own, near_got, codes, cuts, n_dp)
     sent, near_got_b = lax.optimization_barrier((sent, near_got_b))
     came = to_all(sent, 1)
-    arrived = [sent[0]] + [came[d] for d in range(1, n_dp)]
-    d_table = gather_grads(me, asked, arrived, n_slabs, share, enc, parts[0], None)
 
     cuts = (parts[1][1] // LANES,)
     far_got_b, _ = lax.optimization_barrier((far_got_b, codes))
     codes = far_codes(own_b, far_got_b, cuts)
     codes = [[over_x(x, n_x - k) for x in piece] for k, piece in enumerate(codes, 1)]
+    lead = {d: came[d] for d in range(1, n_dp - 1)}
+    codes, lead = lax.optimization_barrier((codes, lead))
+    came.update(lead)
+    arrived = [sent[0]] + [came[d] for d in range(1, n_dp)]
+    d_table = gather_grads(me, asked, arrived, n_slabs, share, enc, parts[0], None)
     sent = send_codes(request, own_b, near_got_b, codes, cuts, n_dp)
     came = to_all(sent, 1)
     arrived = [sent[0]] + [came[d] for d in range(1, n_dp)]

time: 183 us -> 188 us (1.027)
  waiting for transfers between devices: 46.1 us -> 60.5 us
  starting transfers between devices: 59.1 us -> 50.4 us
  Pallas kernels: 58.3 us -> 56.3 us
    ppermute x28, waiting for transfers between devices: 27.4 us -> 47.6 us  [over_dp(): return lax.ppermute(x, 'dp', [(i, (i + d) % n_dp) for i in range(n_dp)])]
    ppermute x8, starting transfers between devices: 14.3 us -> 4.51 us  [over_core(): return lax.ppermute(x, 'tensor', [(t, t ^ 1) for t in range(n_tp)])]
    ppermute x4, waiting for transfers between devices: 11.7 us -> 7.65 us  [over_x(): lax.ppermute(x, 'tensor', [(t, (t + 2 * d) % n_tp) for t in range(n_tp)])]
    pallas_call x1, Pallas kernels: 22.1 us -> 19.8 us  [attend(): pl.pallas_call(functools.partial(attend_body, places, len(kvs), len(late)...]
  transfers between devices with their start and end apart: 40 -> 40, of which waited for: 17 -> 18; matrix products, arithmetic and copies ran while one was open for 0% -> 0% of each run, Pallas kernels for 13% -> 14%
where the time goes in v14:
time: 188 us; the launch traced here: 187 us
  waiting for transfers between devices  60.5 us (32%)
  Pallas kernels  56.3 us (30%)
  starting transfers between devices  50.4 us (27%)
  local copies, waits for them, and re-layouts  10.1 us (5%)
  blocking collectives  8.59 us (5%)
    ppermute x28, waiting for transfers between devices, over_dp(): return lax.ppermute(x, 'dp', [(i, (i + d) % n_dp) for i in range(n_dp)])  47.6 us
    ppermute x28, starting transfers between devices, over_dp(): return lax.ppermute(x, 'dp', [(i, (i + d) % n_dp) for i in range(n_dp)])  42.8 us
    pallas_call x1, Pallas kernels, attend(): pl.pallas_call(functools.partial(attend_body, places, len(kvs), len(late)...  19.8 us
    unnamed x30, local copies, waits for them, and re-layouts  10.1 us
    pallas_call x2, Pallas kernels, project(): pl.pallas_call(functools.partial(project_body, n_in), out_shape=jax.Shape...  9.77 us
    psum x1, blocking collectives, on_device(): asked = lax.psum(wanted, 'dp')  8.59 us
    ppermute x4, waiting for transfers between devices, over_x(): lax.ppermute(x, 'tensor', [(t, (t + 2 * d) % n_tp) for t in range(n_tp)])  7.65 us
    pallas_call x2, Pallas kernels, pack(): pl.pallas_call(functools.partial(pack_body, n_dp, chunk, share), out_shap...  7.02 us
  transfers between devices with their start and end apart: 40, of which 18 were waited for; matrix products, arithmetic and copies ran while one was open for 0% of the time, Pallas kernels for 14%

profile of v14, /device:TPU:13, one launch (start us, length us, event | category | flops | bytes accessed | tf_op | source)
XLA Modules:
  0.0 187.0 jit_solution(2694625118236468678)
XLA Ops:
  2.2 8.6 %psum.7.asked = s32[8,32]{1,0:T(8,128)} all-reduce(s32[8,32]{1,0:T(8,128)} %get-tuple-element.93), channel_id=1, replica_groups=mesh['dp'=8,'tensor'=4] {'dp'}, use_global_device_ids=true, to_apply=%region_0.0 | all-reduce | flops 256 | bytes 2048 | tf_op jit(solution)/shard_map/psum | solution.py:555
  10.8 3.4 %pack_rows.3 = (bf16[4,16,896]{2,1,0:T(8,128)(2,1)}, bf16[4,16,896]{2,1,0:T(8,128)(2,1)}, bf16[4,16,896]{2,1,0:T(8,128)(2,1)}, bf16[4,16,896]{2,1,0:T(8,128)(2,1...) custom-call(s32[1]{0:T(128)} %get-tuple-element.92.me, ...), custom_call_target="tpu_custom_call" | custom-call | bytes 1835008 | tf_op jit(solution)/shard_map/pack_rows/pallas_call | solution.py:97
  19.3 3.6 %pack_rows.2 = (bf16[4,16,896]{2,1,0:T(8,128)(2,1)}, bf16[4,16,896]{2,1,0:T(8,128)(2,1)}, bf16[4,16,896]{2,1,0:T(8,128)(2,1)}, bf16[4,16,896]{2,1,0:T(8,128)(2,1...) custom-call(s32[1]{0:T(128)} %get-tuple-element.92.me, ...), custom_call_target="tpu_custom_call" | custom-call | bytes 1835008 | tf_op jit(solution)/shard_map/pack_rows/pallas_call | solution.py:97
  26.4 5.4 %collective-permute-start.3 = (bf16[4,16,896]{2,1,0:T(8,128)(2,1)}, bf16[4,16,896]{2,1,0:T(8,128)(2,1)S(1)}, u32[]{:S(2)}, u32[]{:S(2)}) collective-permute-start(bf16[4,16,896]{2,1,0:T(8,128)(2,1)} %get-tuple-element.98), channel_id=1, source_target_pairs={{0,16},{4,20},{8,24},{12,28},{16,0},{20,4},{24,8},{28,12},{1,17},{... | collective-permute-start | bytes 344072 | tf_op jit(solution)/shard_map/ppermute | solution.py:546
  31.9 2.4 %collective-permute-done.8.refs_5_ = bf16[4,16,896]{2,1,0:T(8,128)(2,1)S(1)} collective-permute-done((bf16[4,16,896]{2,1,0:T(8,128)(2,1)}, bf16[4,16,896]{2,1,0:T(8,128)(2,1)S(1)}, u32[]{:S(2)}, u32[]{:S(2)}) %collective-permute-start.8) | collective-permute-done | bytes 114720 | tf_op jit(solution)/shard_map/ppermute | solution.py:546
  34.2 2.4 %collective-permute-done.9.refs_6_ = bf16[4,16,896]{2,1,0:T(8,128)(2,1)S(1)} collective-permute-done((bf16[4,16,896]{2,1,0:T(8,128)(2,1)S(1)}, bf16[4,16,896]{2,1,0:T(8,128)(2,1)S(1)}, u32[]{:S(2)}, u32[]{:S(2)}) %collective-permute-start.9) | collective-permute-done | bytes 114720 | tf_op jit(solution)/shard_map/ppermute | solution.py:546
  38.4 2.6 %collective-permute-done.3.refs_4_ = bf16[4,16,896]{2,1,0:T(8,128)(2,1)S(1)} collective-permute-done((bf16[4,16,896]{2,1,0:T(8,128)(2,1)}, bf16[4,16,896]{2,1,0:T(8,128)(2,1)S(1)}, u32[]{:S(2)}, u32[]{:S(2)}) %collective-permute-start.3) | collective-permute-done | bytes 114720 | tf_op jit(solution)/shard_map/ppermute | solution.py:546
  52.0 6.7 %collective-permute-done.12.refs_6_ = bf16[4,16,896]{2,1,0:T(8,128)(2,1)S(1)} collective-permute-done((bf16[4,16,896]{2,1,0:T(8,128)(2,1)}, bf16[4,16,896]{2,1,0:T(8,128)(2,1)S(1)}, u32[]{:S(2)}, u32[]{:S(2)}) %collective-permute-start.12) | collective-permute-done | bytes 114720 | tf_op jit(solution)/shard_map/ppermute | solution.py:546
  60.8 2.4 %collective-permute-start.14 = (bf16[4,16,896]{2,1,0:T(8,128)(2,1)}, bf16[4,16,896]{2,1,0:T(8,128)(2,1)S(1)}, u32[]{:S(2)}, u32[]{:S(2)}) collective-permute-start(bf16[4,16,896]{2,1,0:T(8,128)(2,1)} %get-tuple-element.123), channel_id=1, source_target_pairs={{0,4},{4,8},{8,12},{12,16},{16,20},{20,24},{24,28},{28,0},{1,5},{5... | collective-permute-start | bytes 344072 | tf_op jit(solution)/shard_map/ppermute | solution.py:546
  63.2 2.9 %collective-permute-done.refs_1_ = bf16[4,16,896]{2,1,0:T(8,128)(2,1)S(1)} collective-permute-done((bf16[4,16,896]{2,1,0:T(8,128)(2,1)}, bf16[4,16,896]{2,1,0:T(8,128)(2,1)S(1)}, u32[]{:S(2)}, u32[]{:S(2)}) %collective-permute-start) | collective-permute-done | bytes 114720 | tf_op jit(solution)/shard_map/ppermute | solution.py:546
  66.1 3.3 %collective-permute-done.14.refs_7_ = bf16[4,16,896]{2,1,0:T(8,128)(2,1)S(1)} collective-permute-done((bf16[4,16,896]{2,1,0:T(8,128)(2,1)}, bf16[4,16,896]{2,1,0:T(8,128)(2,1)S(1)}, u32[]{:S(2)}, u32[]{:S(2)}) %collective-permute-start.14) | collective-permute-done | bytes 114720 | tf_op jit(solution)/shard_map/ppermute | solution.py:546
  74.5 6.2 %project.2.refs_0_ = bf16[4,16,16,2048]{3,2,1,0:T(8,128)(2,1)S(1)} custom-call(bf16[16,16,896]{2,1,0:T(8,128)(2,1)S(1)} %compact_rows.2.refs_0_, bf16[16,16,896]{2,1,0:T(8,128)(2,1)S(1)} %collective-permute-done.15.refs_1_, bf16[16,16,896]{2,1,0:T(8,128)(2,1)S(1)} %collective-permute-done.13.refs_2_, ...), custom_call_target="tpu_custom_call" | custom-call | flops 3758096384 | bytes 9699328 | tf_op jit(solution)/shard_map/project/pallas_call | solution.py:174
  82.7 3.6 %project.3.refs_1_ = bf16[2,16,16,2048]{3,2,1,0:T(8,128)(2,1)S(1)} custom-call(bf16[16,16,896]{2,1,0:T(8,128)(2,1)S(1)} %compact_rows.3.refs_0_, bf16[16,16,896]{2,1,0:T(8,128)(2,1)S(1)} %collective-permute-done.17.refs_1_, bf16[896,1024]{1,0:T(8,128)(2,1)S(1)} %copy-done.4, bf16[896,1024]{1,0:T(8,128)(2,1)S(1)} %copy-done.5), custom_call_target="tpu_custom_call" | custom-call | flops 1879048192 | bytes 6684672 | tf_op jit(solution)/shard_map/project/pallas_call | solution.py:174
  89.4 19.8 %attend.1 = (bf16[512,1024]{1,0:T(8,128)(2,1)}, bf16[512,1024]{1,0:T(8,128)(2,1)}, bf16[2,16,32,2048]{3,2,1,0:T(8,128)(2,1)}, bf16[2,16,32,2048]{3,2,1,0:T(8,128...) custom-call(bf16[4,16,16,2048]{3,2,1,0:T(8,128)(2,1)} %copy-done.10,, ...), custom_call_target="tpu_custom_call" | custom-call | flops 6174015488 | bytes 20971520 | tf_op jit(solution)/shard_map/attend/pallas_call | solution.py:293
  117.0 6.0 %grads.1 = (f32[1,16,32,640]{3,2,1,0:T(8,128)S(1)}, f32[2,16,32,640]{3,2,1,0:T(8,128)S(1)}) custom-call(bf16[2,16,32,2048]{3,2,1,0:T(8,128)(2,1)S(1)} %copy-done.12, bf16[2,16,32,2048]{3,2,1,0:T(8,128)(2,1)S(1)} %copy-done.11, bf16[896,1024]{1,0:T(8,128)(2,1)S(1)} %copy-done.4, bf16[896,1024]{1,0:T(8,128)(2,1)S(1)} %copy-done.6), custom_call_target="tpu_custom_call" | custom-call | flops 5368709120 | bytes 16252928 | tf_op jit(solution)/shard_map/grads/pallas_call | solution.py:366
  124.7 2.4 %collective-permute-done.20.got = f32[1,16,32,256]{3,2,1,0:T(8,128)S(1)} collective-permute-done((f32[1,16,32,256]{3,2,1,0:T(8,128)S(1)}, f32[1,16,32,256]{3,2,1,0:T(8,128)S(1)}, u32[]{:S(2)}, u32[]{:S(2)}) %collective-permute-start.20) | collective-permute-done | bytes 524320 | tf_op jit(solution)/shard_map/ppermute | solution.py:540
  133.1 7.6 %collective-permute-done.25.rest_0_ = s16[81,32,128]{2,1,0:T(8,128)(2,1)S(1)} collective-permute-done((s16[81,32,128]{2,1,0:T(8,128)(2,1)S(1)}, s16[81,32,128]{2,1,0:T(8,128)(2,1)S(1)}, u32[]{:S(2)}, u32[]{:S(2)}) %collective-permute-start.25) | collective-permute-done | bytes 663584 | tf_op jit(solution)/shard_map/ppermute | solution.py:543
  147.2 2.6 %collective-permute-start.32 = (s16[41,16,128]{2,1,0:T(8,128)(2,1)S(1)}, s16[41,16,128]{2,1,0:T(8,128)(2,1)S(1)}, u32[]{:S(2)}, u32[]{:S(2)}) collective-permute-start(s16[41,16,128]{2,1,0:T(8,128)(2,1)S(1)} %get-tuple-element.164), channel_id=1, source_target_pairs={{0,4},{4,8},{8,12},{12,16},{16,20},{20,24},{24,28},{28,0},{1,5},{5... | collective-permute-start | bytes 503816 | tf_op jit(solution)/shard_map/ppermute | solution.py:546
  156.4 2.6 %collective-permute-start.36 = (s16[41,16,128]{2,1,0:T(8,128)(2,1)S(1)}, s16[41,16,128]{2,1,0:T(8,128)(2,1)S(1)}, u32[]{:S(2)}, u32[]{:S(2)}) collective-permute-start(s16[41,16,128]{2,1,0:T(8,128)(2,1)S(1)} %get-tuple-element.168), channel_id=1, source_target_pairs={{0,20},{4,24},{8,28},{12,0},{16,4},{20,8},{24,12},{28,16},{1,21},{... | collective-permute-start | bytes 503816 | tf_op jit(solution)/shard_map/ppermute | solution.py:546
  159.0 3.2 %collective-permute-start.37 = (s16[41,16,128]{2,1,0:T(8,128)(2,1)S(1)}, s16[41,16,128]{2,1,0:T(8,128)(2,1)S(1)}, u32[]{:S(2)}, u32[]{:S(2)}) collective-permute-start(s16[41,16,128]{2,1,0:T(8,128)(2,1)S(1)} %get-tuple-element.169), channel_id=1, source_target_pairs={{0,24},{4,28},{8,0},{12,4},{16,8},{20,12},{24,16},{28,20},{1,25},{... | collective-permute-start | bytes 503816 | tf_op jit(solution)/shard_map/ppermute | solution.py:546
  162.3 2.6 %gather_grads.2.refs_8_ = f32[16,32,896]{2,1,0:T(8,128)} custom-call(s32[1]{0:T(128)} %get-tuple-element.92.me, s32[8,32]{1,0:T(8,128)S(1)} %copy-done.2, s16[17,16,128]{2,1,0:T(8,128)(2,1)S(1)} %get-tuple-element.171.refs_0_, s16[17,16,128]{2,1,0:T(8,128)(2,1)S(1)} %collective-permute-done.26.refs_1_, ...), custom_call_target="tpu_custom_call" | custom-call | bytes 1048576 | tf_op jit(solution)/shard_map/gather_grads/pallas_call | solution.py:515
  164.9 12.7 %collective-permute-done.35.refs_4_ = s16[41,16,128]{2,1,0:T(8,128)(2,1)S(1)} collective-permute-done((s16[41,16,128]{2,1,0:T(8,128)(2,1)S(1)}, s16[41,16,128]{2,1,0:T(8,128)(2,1)S(1)}, u32[]{:S(2)}, u32[]{:S(2)}) %collective-permute-start.35) | collective-permute-done | bytes 167968 | tf_op jit(solution)/shard_map/ppermute | solution.py:546
  177.5 4.3 %collective-permute-done.37.refs_6_ = s16[41,16,128]{2,1,0:T(8,128)(2,1)S(1)} collective-permute-done((s16[41,16,128]{2,1,0:T(8,128)(2,1)S(1)}, s16[41,16,128]{2,1,0:T(8,128)(2,1)S(1)}, u32[]{:S(2)}, u32[]{:S(2)}) %collective-permute-start.37) | collective-permute-done | bytes 167968 | tf_op jit(solution)/shard_map/ppermute | solution.py:546
  183.9 2.9 %gather_grads.3 = f32[16,32,896]{2,1,0:T(8,128)} custom-call(s32[1]{0:T(128)} %get-tuple-element.92.me, s32[8,32]{1,0:T(8,128)S(1)} %copy-done.2, s16[41,16,128]{2,1,0:T(8,128)(2,1)S(1)} %get-tuple-element.163.refs_0_, s16[41,16,128]{2,1,0:T(8,128)(2,1)S(1)} %collective-permute-done.32.refs_1_, ...), custom_call_target="tpu_custom_call", output_to_operand_aliasing={{}: (10, {})} | custom-call | bytes 2621440 | tf_op jit(solution)/shard_map/gather_grads/pallas_call | solution.py:515
  (102 shorter events, 65.8 us)
Async XLA Ops:
  17.6 14.2 %collective-permute-start.7 = (bf16[4,16,896]{2,1,0:T(8,128)(2,1)}, bf16[4,16,896]{2,1,0:T(8,128)(2,1)S(1)}, u32[]{:S(2)}, u32[]{:S(2)}) collective-permute-start(bf16[4,16,896]{2,1,0:T(8,128)(2,1)} %get-tuple-element.103), channel_id=1, source_target_pairs={{0,16},{4,20},{8,24},{12,28},{16,0},{20,4},{24,8},{28,12},{1,17},{... | collective-permute-start | bytes 344072 | tf_op jit(solution)/shard_map/ppermute | solution.py:546
  19.0 15.2 %collective-permute-start.8 = (bf16[4,16,896]{2,1,0:T(8,128)(2,1)}, bf16[4,16,896]{2,1,0:T(8,128)(2,1)S(1)}, u32[]{:S(2)}, u32[]{:S(2)}) collective-permute-start(bf16[4,16,896]{2,1,0:T(8,128)(2,1)} %get-tuple-element.104), channel_id=1, source_target_pairs={{0,12},{4,16},{8,20},{12,24},{16,28},{20,0},{24,4},{28,8},{1,13},{... | collective-permute-start | bytes 344072 | tf_op jit(solution)/shard_map/ppermute | solution.py:546
  22.9 13.7 %collective-permute-start.9 = (bf16[4,16,896]{2,1,0:T(8,128)(2,1)S(1)}, bf16[4,16,896]{2,1,0:T(8,128)(2,1)S(1)}, u32[]{:S(2)}, u32[]{:S(2)}) collective-permute-start(bf16[4,16,896]{2,1,0:T(8,128)(2,1)S(1)} %copy-done.14), channel_id=1, source_target_pairs={{0,8},{4,12},{8,16},{12,20},{16,24},{20,28},{24,0},{28,4},{1,9},{5... | collective-permute-start | bytes 344072 | tf_op jit(solution)/shard_map/ppermute | solution.py:546
  24.1 14.3 %collective-permute-start.10 = (bf16[4,16,896]{2,1,0:T(8,128)(2,1)S(1)}, bf16[4,16,896]{2,1,0:T(8,128)(2,1)S(1)}, u32[]{:S(2)}, u32[]{:S(2)}) collective-permute-start(bf16[4,16,896]{2,1,0:T(8,128)(2,1)S(1)} %copy-done.13), channel_id=1, source_target_pairs={{0,4},{4,8},{8,12},{12,16},{16,20},{20,24},{24,28},{28,0},{1,5},{5... | collective-permute-start | bytes 344072 | tf_op jit(solution)/shard_map/ppermute | solution.py:546
  26.4 14.5 %collective-permute-start.3 = (bf16[4,16,896]{2,1,0:T(8,128)(2,1)}, bf16[4,16,896]{2,1,0:T(8,128)(2,1)S(1)}, u32[]{:S(2)}, u32[]{:S(2)}) collective-permute-start(bf16[4,16,896]{2,1,0:T(8,128)(2,1)} %get-tuple-element.98), channel_id=1, source_target_pairs={{0,16},{4,20},{8,24},{12,28},{16,0},{20,4},{24,8},{28,12},{1,17},{... | collective-permute-start | bytes 344072 | tf_op jit(solution)/shard_map/ppermute | solution.py:546
  42.8 15.9 %collective-permute-start.13 = (bf16[16,16,896]{2,1,0:T(8,128)(2,1)S(1)}, bf16[16,16,896]{2,1,0:T(8,128)(2,1)S(1)}, u32[]{:S(2)}, u32[]{:S(2)}) collective-permute-start(bf16[16,16,896]{2,1,0:T(8,128)(2,1)S(1)} %compact_rows.2.refs_0_), channel_id=1, source_target_pairs={{0,2},{1,3},{2,0},{3,1},{4,6},{5,7},{6,4},{7,5},{8,10},{9,11},{10,... | collective-permute-start | bytes 1376264 | tf_op jit(solution)/shard_map/ppermute | solution.py:543
  47.3 11.4 %collective-permute-start.12 = (bf16[4,16,896]{2,1,0:T(8,128)(2,1)}, bf16[4,16,896]{2,1,0:T(8,128)(2,1)S(1)}, u32[]{:S(2)}, u32[]{:S(2)}) collective-permute-start(bf16[4,16,896]{2,1,0:T(8,128)(2,1)} %get-tuple-element.109), channel_id=1, source_target_pairs={{0,8},{4,12},{8,16},{12,20},{16,24},{20,28},{24,0},{28,4},{1,9},{5... | collective-permute-start | bytes 344072 | tf_op jit(solution)/shard_map/ppermute | solution.py:546
  58.7 13.5 %collective-permute-start.15 = (bf16[16,16,896]{2,1,0:T(8,128)(2,1)S(1)}, bf16[16,16,896]{2,1,0:T(8,128)(2,1)S(1)}, u32[]{:S(2)}, u32[]{:S(2)}) collective-permute-start(bf16[16,16,896]{2,1,0:T(8,128)(2,1)S(1)} %compact_rows.2.refs_0_), channel_id=1, source_target_pairs={{0,1},{1,0},{2,3},{3,2},{4,5},{5,4},{6,7},{7,6},{8,9},{9,8},{10,11... | collective-permute-start | bytes 1376264 | tf_op jit(solution)/shard_map/ppermute | solution.py:540
  60.8 11.4 %collective-permute-start.16 = (bf16[16,16,896]{2,1,0:T(8,128)(2,1)S(1)}, bf16[16,16,896]{2,1,0:T(8,128)(2,1)S(1)}, u32[]{:S(2)}, u32[]{:S(2)}) collective-permute-start(bf16[16,16,896]{2,1,0:T(8,128)(2,1)S(1)} %collective-permute-done.13.refs_2_), channel_id=1, source_target_pairs={{0,1},{1,0},{2,3},{3,2},{4,5},{5,4},{6,7},{7,6},{8,9},{9,8},{10,11... | collective-permute-start | bytes 1376264 | tf_op jit(solution)/shard_map/ppermute | solution.py:540
  72.7 14.9 %collective-permute-start.18 = (bf16[16,16,896]{2,1,0:T(8,128)(2,1)S(1)}, bf16[16,16,896]{2,1,0:T(8,128)(2,1)S(1)}, u32[]{:S(2)}, u32[]{:S(2)}) collective-permute-start(bf16[16,16,896]{2,1,0:T(8,128)(2,1)S(1)} %compact_rows.3.refs_0_), channel_id=1, source_target_pairs={{0,2},{1,3},{2,0},{3,1},{4,6},{5,7},{6,4},{7,5},{8,10},{9,11},{10,... | collective-permute-start | bytes 1376264 | tf_op jit(solution)/shard_map/ppermute | solution.py:543
  109.6 14.1 %collective-permute-start.24 = (f32[1,16,32,640]{3,2,1,0:T(8,128)S(1)}, f32[1,16,32,640]{3,2,1,0:T(8,128)S(1)}, u32[]{:S(2)}, u32[]{:S(2)}) collective-permute-start(f32[1,16,32,640]{3,2,1,0:T(8,128)S(1)} %get-tuple-element.154), channel_id=1, source_target_pairs={{0,1},{1,0},{2,3},{3,2},{4,5},{5,4},{6,7},{7,6},{8,9},{9,8},{10,11... | collective-permute-start | bytes 3932168 | tf_op jit(solution)/shard_map/ppermute | solution.py:540
  111.4 11.7 %collective-permute-start.22 = (s16[33,32,128]{2,1,0:T(8,128)(2,1)S(1)}, s16[33,32,128]{2,1,0:T(8,128)(2,1)S(1)}, u32[]{:S(2)}, u32[]{:S(2)}) collective-permute-start(s16[33,32,128]{2,1,0:T(8,128)(2,1)S(1)} %far_codes.2), channel_id=1, source_target_pairs={{0,2},{1,3},{2,0},{3,1},{4,6},{5,7},{6,4},{7,5},{8,10},{9,11},{10,... | collective-permute-start | bytes 811016 | tf_op jit(solution)/shard_map/ppermute | solution.py:543
  124.1 16.6 %collective-permute-start.25 = (s16[81,32,128]{2,1,0:T(8,128)(2,1)S(1)}, s16[81,32,128]{2,1,0:T(8,128)(2,1)S(1)}, u32[]{:S(2)}, u32[]{:S(2)}) collective-permute-start(s16[81,32,128]{2,1,0:T(8,128)(2,1)S(1)} %far_codes.3), channel_id=1, source_target_pairs={{0,2},{1,3},{2,0},{3,1},{4,6},{5,7},{6,4},{7,5},{8,10},{9,11},{10,... | collective-permute-start | bytes 1990664 | tf_op jit(solution)/shard_map/ppermute | solution.py:543
  128.3 13.7 %collective-permute-start.26 = (s16[17,16,128]{2,1,0:T(8,128)(2,1)S(1)}, s16[17,16,128]{2,1,0:T(8,128)(2,1)S(1)}, u32[]{:S(2)}, u32[]{:S(2)}) collective-permute-start(s16[17,16,128]{2,1,0:T(8,128)(2,1)S(1)} %get-tuple-element.156), channel_id=1, source_target_pairs={{0,4},{4,8},{8,12},{12,16},{16,20},{20,24},{24,28},{28,0},{1,5},{5... | collective-permute-start | bytes 208904 | tf_op jit(solution)/shard_map/ppermute | solution.py:546
  129.2 14.5 %collective-permute-start.27 = (s16[17,16,128]{2,1,0:T(8,128)(2,1)S(1)}, s16[17,16,128]{2,1,0:T(8,128)(2,1)S(1)}, u32[]{:S(2)}, u32[]{:S(2)}) collective-permute-start(s16[17,16,128]{2,1,0:T(8,128)(2,1)S(1)} %get-tuple-element.157), channel_id=1, source_target_pairs={{0,8},{4,12},{8,16},{12,20},{16,24},{20,28},{24,0},{28,4},{1,9},{5... | collective-permute-start | bytes 208904 | tf_op jit(solution)/shard_map/ppermute | solution.py:546
  130.4 13.3 %collective-permute-start.28 = (s16[17,16,128]{2,1,0:T(8,128)(2,1)S(1)}, s16[17,16,128]{2,1,0:T(8,128)(2,1)S(1)}, u32[]{:S(2)}, u32[]{:S(2)}) collective-permute-start(s16[17,16,128]{2,1,0:T(8,128)(2,1)S(1)} %get-tuple-element.158), channel_id=1, source_target_pairs={{0,12},{4,16},{8,20},{12,24},{16,28},{20,0},{24,4},{28,8},{1,13},{... | collective-permute-start | bytes 208904 | tf_op jit(solution)/shard_map/ppermute | solution.py:546
  132.6 11.1 %collective-permute-start.29 = (s16[17,16,128]{2,1,0:T(8,128)(2,1)S(1)}, s16[17,16,128]{2,1,0:T(8,128)(2,1)S(1)}, u32[]{:S(2)}, u32[]{:S(2)}) collective-permute-start(s16[17,16,128]{2,1,0:T(8,128)(2,1)S(1)} %get-tuple-element.159), channel_id=1, source_target_pairs={{0,16},{4,20},{8,24},{12,28},{16,0},{20,4},{24,8},{28,12},{1,17},{... | collective-permute-start | bytes 208904 | tf_op jit(solution)/shard_map/ppermute | solution.py:546
  147.2 11.9 %collective-permute-start.32 = (s16[41,16,128]{2,1,0:T(8,128)(2,1)S(1)}, s16[41,16,128]{2,1,0:T(8,128)(2,1)S(1)}, u32[]{:S(2)}, u32[]{:S(2)}) collective-permute-start(s16[41,16,128]{2,1,0:T(8,128)(2,1)S(1)} %get-tuple-element.164), channel_id=1, source_target_pairs={{0,4},{4,8},{8,12},{12,16},{16,20},{20,24},{24,28},{28,0},{1,5},{5... | collective-permute-start | bytes 503816 | tf_op jit(solution)/shard_map/ppermute | solution.py:546
  149.7 12.6 %collective-permute-start.33 = (s16[41,16,128]{2,1,0:T(8,128)(2,1)S(1)}, s16[41,16,128]{2,1,0:T(8,128)(2,1)S(1)}, u32[]{:S(2)}, u32[]{:S(2)}) collective-permute-start(s16[41,16,128]{2,1,0:T(8,128)(2,1)S(1)} %get-tuple-element.165), channel_id=1, source_target_pairs={{0,8},{4,12},{8,16},{12,20},{16,24},{20,28},{24,0},{28,4},{1,9},{5... | collective-permute-start | bytes 503816 | tf_op jit(solution)/shard_map/ppermute | solution.py:546
  151.6 13.3 %collective-permute-start.34 = (s16[41,16,128]{2,1,0:T(8,128)(2,1)S(1)}, s16[41,16,128]{2,1,0:T(8,128)(2,1)S(1)}, u32[]{:S(2)}, u32[]{:S(2)}) collective-permute-start(s16[41,16,128]{2,1,0:T(8,128)(2,1)S(1)} %get-tuple-element.166), channel_id=1, source_target_pairs={{0,12},{4,16},{8,20},{12,24},{16,28},{20,0},{24,4},{28,8},{1,13},{... | collective-permute-start | bytes 503816 | tf_op jit(solution)/shard_map/ppermute | solution.py:546
  153.7 23.8 %collective-permute-start.35 = (s16[41,16,128]{2,1,0:T(8,128)(2,1)S(1)}, s16[41,16,128]{2,1,0:T(8,128)(2,1)S(1)}, u32[]{:S(2)}, u32[]{:S(2)}) collective-permute-start(s16[41,16,128]{2,1,0:T(8,128)(2,1)S(1)} %get-tuple-element.167), channel_id=1, source_target_pairs={{0,16},{4,20},{8,24},{12,28},{16,0},{20,4},{24,8},{28,12},{1,17},{... | collective-permute-start | bytes 503816 | tf_op jit(solution)/shard_map/ppermute | solution.py:546
  156.4 21.1 %collective-permute-start.36 = (s16[41,16,128]{2,1,0:T(8,128)(2,1)S(1)}, s16[41,16,128]{2,1,0:T(8,128)(2,1)S(1)}, u32[]{:S(2)}, u32[]{:S(2)}) collective-permute-start(s16[41,16,128]{2,1,0:T(8,128)(2,1)S(1)} %get-tuple-element.168), channel_id=1, source_target_pairs={{0,20},{4,24},{8,28},{12,0},{16,4},{20,8},{24,12},{28,16},{1,21},{... | collective-permute-start | bytes 503816 | tf_op jit(solution)/shard_map/ppermute | solution.py:546
  159.0 22.8 %collective-permute-start.37 = (s16[41,16,128]{2,1,0:T(8,128)(2,1)S(1)}, s16[41,16,128]{2,1,0:T(8,128)(2,1)S(1)}, u32[]{:S(2)}, u32[]{:S(2)}) collective-permute-start(s16[41,16,128]{2,1,0:T(8,128)(2,1)S(1)} %get-tuple-element.169), channel_id=1, source_target_pairs={{0,24},{4,28},{8,0},{12,4},{16,8},{20,12},{24,16},{28,20},{1,25},{... | collective-permute-start | bytes 503816 | tf_op jit(solution)/shard_map/ppermute | solution.py:546
  162.3 21.6 %collective-permute-start.38 = (s16[41,16,128]{2,1,0:T(8,128)(2,1)S(1)}, s16[41,16,128]{2,1,0:T(8,128)(2,1)S(1)}, u32[]{:S(2)}, u32[]{:S(2)}) collective-permute-start(s16[41,16,128]{2,1,0:T(8,128)(2,1)S(1)} %get-tuple-element.170), channel_id=1, source_target_pairs={{0,28},{4,0},{8,4},{12,8},{16,12},{20,16},{24,20},{28,24},{1,29},{... | collective-permute-start | bytes 503816 | tf_op jit(solution)/shard_map/ppermute | solution.py:546
  (31 other events, 265.9 us)

commit v15 on v13

--- a/solution.py
+++ b/solution.py
@@ -13,7 +13,7 @@
 LANES = 128
 TILE = 16
 VMEM_LIMIT = 28 * 1024 * 1024
-VMEM_MORE = 44 * 1024 * 1024
+VMEM_MORE = 48 * 1024 * 1024
 VMEM_ALL = 60 * 1024 * 1024
 F32 = jnp.float32
 BF16 = jnp.bfloat16
@@ -196,6 +196,7 @@
     scale = 1.0 / math.sqrt(HD)
     heads = width // HD
     group = min(8, heads)
+    per = q_ref.shape[0] // SPAN
     last = (((1,), (1,)), ((), ()))
     first = (((0,), (0,)), ((), ()))
 
@@ -210,32 +211,32 @@
             late_kv[i, :, :, :width] = dot(rows, wk[...]).astype(BF16).reshape(shape)
             late_kv[i, :, :, width:] = dot(rows, wv[...]).astype(BF16).reshape(shape)
 
-    mine = pl.ds(2 * step, 2)
-
-    def rows_of(col):
+    def rows_of(u, col):
         cols = pl.ds(col, HD)
-        parts = [ref[:, :, :, cols].reshape(-1, HD) for ref in kvs]
-        parts.append(late_kv[:, mine, :, cols].reshape(-1, HD))
+        parts = [ref[:, 2 * u : 2 * u + 2, :, cols].reshape(-1, HD) for ref in kvs]
+        parts.append(late_kv[:, pl.ds(2 * (per * step + u), 2), :, cols].reshape(-1, HD))
         return jnp.concatenate(parts, axis=0)
 
-    def put(col, grad):
+    def put(u, col, grad):
         cols = pl.ds(col, HD)
         for at, (kind, k, c) in enumerate(places):
             block = grad[at * 2 * TILE : (at + 1) * 2 * TILE].reshape(2, TILE, HD)
             tokens = pl.ds(c * TILE, TILE)
-            grads[kind][k, :, tokens, cols] = block
-            (own_all, core_all)[kind][k, mine, tokens, cols] = block
+            if k < grads[kind].shape[0]:
+                grads[kind][k, 2 * u : 2 * u + 2, tokens, cols] = block
+            (own_all, core_all)[kind][k, pl.ds(2 * (per * step + u), 2), tokens, cols] = block
 
     zero = jnp.zeros((SPAN, HD), BF16)
-    for h0 in range(0, heads, group):
+    for u, h0 in [(u, h0) for u in range(per) for h0 in range(0, heads, group)]:
         hs = range(h0, h0 + group)
+        at = slice(u * SPAN, (u + 1) * SPAN)
         qg, kv = [], []
         for h in hs:
             cols = pl.ds(h * HD, HD)
-            top = jnp.concatenate([q_ref[:, cols], zero], axis=1)
-            low = jnp.concatenate([zero, g_ref[:, cols]], axis=1)
+            top = jnp.concatenate([q_ref[at, cols], zero], axis=1)
+            low = jnp.concatenate([zero, g_ref[at, cols]], axis=1)
             qg.append(jnp.concatenate([top, low], axis=0))
-            kv.append(jnp.concatenate([rows_of(h * HD), rows_of(width + h * HD)], axis=1))
+            kv.append(jnp.concatenate([rows_of(u, h * HD), rows_of(u, width + h * HD)], axis=1))
         both = [dot(a, b, last) for a, b in zip(qg, kv)]
         s = jnp.concatenate([x[:SPAN] for x in both], axis=0) * scale
         dw = jnp.concatenate([x[SPAN:] for x in both], axis=0)
@@ -249,10 +250,10 @@
         out = [dot(a, b).astype(BF16) for a, b in zip(dsw, kv)]
         back = [dot(a, b, first).astype(BF16) for a, b in zip(dsw, qg)]
         for i, h in enumerate(hs):
-            dq_ref[:, pl.ds(h * HD, HD)] = out[i][:SPAN, :HD]
-            att_ref[:, pl.ds(h * HD, HD)] = out[i][SPAN:, HD:]
-            put(h * HD, back[i][:, :HD])
-            put(width + h * HD, back[i][:, HD:])
+            dq_ref[at, pl.ds(h * HD, HD)] = out[i][:SPAN, :HD]
+            att_ref[at, pl.ds(h * HD, HD)] = out[i][SPAN:, HD:]
+            put(u, h * HD, back[i][:, :HD])
+            put(u, width + h * HD, back[i][:, HD:])
 
     @pl.when(step == pl.num_programs(0) - 1)
     def _():
@@ -275,11 +276,14 @@
     sub = share
     half = len(places) // (2 * (share // TILE))
     total = 2 * half
-    rows = pl.BlockSpec((SPAN, width), lambda i: (i, 0))
-    grads = pl.BlockSpec((half, 2, sub, 2 * width), lambda i: (0, i, 0, 0))
+    per = 2 if tokens % (2 * SPAN) == 0 else 1
+    rows = pl.BlockSpec((per * SPAN, width), lambda i: (i, 0))
+
+    def grads(pieces):
+        return pl.BlockSpec((pieces, 2 * per, sub, 2 * width), lambda i: (0, i, 0, 0))
 
     def kv_block(kv):
-        return pl.BlockSpec((kv.shape[0], 2, TILE, 2 * width), lambda i: (0, i, 0, 0))
+        return pl.BlockSpec((kv.shape[0], 2 * per, TILE, 2 * width), lambda i: (0, i, 0, 0))
 
     def once(shape):
         return pl.BlockSpec(shape, lambda i: (0,) * len(shape), pipeline_mode=pl.Buffered(1))
@@ -293,13 +297,13 @@
     return pl.pallas_call(
         functools.partial(attend_body, places, len(kvs), len(late), near),
         out_shape=[jax.ShapeDtypeStruct((tokens, width), BF16)] * 2
-        + [jax.ShapeDtypeStruct(every, BF16)] * 2
+        + [jax.ShapeDtypeStruct(every, BF16), jax.ShapeDtypeStruct((near, *every[1:]), BF16)]
         + [jax.ShapeDtypeStruct(part, F32) for part in parts],
-        grid=(tokens // SPAN,),
+        grid=(tokens // (per * SPAN),),
         in_specs=[kv_block(kv) for kv in kvs]
         + [once(x.shape) for x in late]
         + [once(wk.shape), once(wv.shape), rows, rows],
-        out_specs=[rows, rows, grads, grads] + [whole(part) for part in parts],
+        out_specs=[rows, rows, grads(half), grads(near)] + [whole(part) for part in parts],
         scratch_shapes=[
             pltpu.VMEM((len(late), n, TILE, 2 * width), BF16),
             pltpu.VMEM(every, BF16),

time: 183 us -> 184 us (level)
    unnamed x30 -> x36, local copies, waits for them, and re-layouts: 9.18 us -> 9.62 us
where the time goes in v15:
time: 184 us; the launch traced here: 183 us
  starting transfers between devices  59.3 us (32%)
  Pallas kernels  56.9 us (31%)
  waiting for transfers between devices  47.9 us (26%)
  local copies, waits for them, and re-layouts  9.62 us (5%)
  blocking collectives  8.6 us (5%)
    ppermute x28, starting transfers between devices, over_dp(): return lax.ppermute(x, 'dp', [(i, (i + d) % n_dp) for i in range(n_dp)])  43.2 us
    ppermute x28, waiting for transfers between devices, over_dp(): return lax.ppermute(x, 'dp', [(i, (i + d) % n_dp) for i in range(n_dp)])  27.8 us
    pallas_call x1, Pallas kernels, attend(): pl.pallas_call(functools.partial(attend_body, places, len(kvs), len(late)...  22 us
    ppermute x8, starting transfers between devices, over_core(): return lax.ppermute(x, 'tensor', [(t, t ^ 1) for t in range(n_tp)])  14.3 us
    ppermute x4, waiting for transfers between devices, over_x(): lax.ppermute(x, 'tensor', [(t, (t + 2 * d) % n_tp) for t in range(n_tp)])  12.6 us
    pallas_call x2, Pallas kernels, project(): pl.pallas_call(functools.partial(project_body, n_in), out_shape=jax.Shape...  9.74 us
    unnamed x36, local copies, waits for them, and re-layouts  9.62 us
    psum x1, blocking collectives, on_device(): asked = lax.psum(wanted, 'dp')  8.6 us
  transfers between devices with their start and end apart: 40, of which 17 were waited for; matrix products, arithmetic and copies ran while one was open for 0% of the time, Pallas kernels for 13%

profile of v15, /device:TPU:13, one launch (start us, length us, event | category | flops | bytes accessed | tf_op | source)
XLA Modules:
  0.0 183.5 jit_solution(12635091080792322053)
XLA Ops:
  2.2 8.6 %psum.7.asked = s32[8,32]{1,0:T(8,128)} all-reduce(s32[8,32]{1,0:T(8,128)} %get-tuple-element.86), channel_id=1, replica_groups=mesh['dp'=8,'tensor'=4] {'dp'}, use_global_device_ids=true, to_apply=%region_0.0 | all-reduce | flops 256 | bytes 2048 | tf_op jit(solution)/shard_map/psum | solution.py:559
  10.8 3.5 %pack_rows.3 = (bf16[4,16,896]{2,1,0:T(8,128)(2,1)}, bf16[4,16,896]{2,1,0:T(8,128)(2,1)}, bf16[4,16,896]{2,1,0:T(8,128)(2,1)}, bf16[4,16,896]{2,1,0:T(8,128)(2,1...) custom-call(s32[1]{0:T(128)} %get-tuple-element.85.me, ...), custom_call_target="tpu_custom_call" | custom-call | bytes 1835008 | tf_op jit(solution)/shard_map/pack_rows/pallas_call | solution.py:97
  19.0 3.7 %pack_rows.2 = (bf16[4,16,896]{2,1,0:T(8,128)(2,1)}, bf16[4,16,896]{2,1,0:T(8,128)(2,1)}, bf16[4,16,896]{2,1,0:T(8,128)(2,1)}, bf16[4,16,896]{2,1,0:T(8,128)(2,1...) custom-call(s32[1]{0:T(128)} %get-tuple-element.85.me, ...), custom_call_target="tpu_custom_call" | custom-call | bytes 1835008 | tf_op jit(solution)/shard_map/pack_rows/pallas_call | solution.py:97
  24.0 2.4 %collective-permute-start.10 = (bf16[4,16,896]{2,1,0:T(8,128)(2,1)S(1)}, bf16[4,16,896]{2,1,0:T(8,128)(2,1)S(1)}, u32[]{:S(2)}, u32[]{:S(2)}) collective-permute-start(bf16[4,16,896]{2,1,0:T(8,128)(2,1)S(1)} %copy-done.16), channel_id=1, source_target_pairs={{0,4},{4,8},{8,12},{12,16},{16,20},{20,24},{24,28},{28,0},{1,5},{5... | collective-permute-start | bytes 344072 | tf_op jit(solution)/shard_map/ppermute | solution.py:550
  26.4 5.5 %collective-permute-start.3 = (bf16[4,16,896]{2,1,0:T(8,128)(2,1)}, bf16[4,16,896]{2,1,0:T(8,128)(2,1)S(1)}, u32[]{:S(2)}, u32[]{:S(2)}) collective-permute-start(bf16[4,16,896]{2,1,0:T(8,128)(2,1)} %get-tuple-element.91), channel_id=1, source_target_pairs={{0,16},{4,20},{8,24},{12,28},{16,0},{20,4},{24,8},{28,12},{1,17},{... | collective-permute-start | bytes 344072 | tf_op jit(solution)/shard_map/ppermute | solution.py:550
  38.5 2.6 %collective-permute-done.3.refs_4_ = bf16[4,16,896]{2,1,0:T(8,128)(2,1)S(1)} collective-permute-done((bf16[4,16,896]{2,1,0:T(8,128)(2,1)}, bf16[4,16,896]{2,1,0:T(8,128)(2,1)S(1)}, u32[]{:S(2)}, u32[]{:S(2)}) %collective-permute-start.3) | collective-permute-done | bytes 114720 | tf_op jit(solution)/shard_map/ppermute | solution.py:550
  47.7 6.4 %collective-permute-start.15 = (bf16[16,16,896]{2,1,0:T(8,128)(2,1)S(1)}, bf16[16,16,896]{2,1,0:T(8,128)(2,1)S(1)}, u32[]{:S(2)}, u32[]{:S(2)}) collective-permute-start(bf16[16,16,896]{2,1,0:T(8,128)(2,1)S(1)} %compact_rows.2.refs_0_), channel_id=1, source_target_pairs={{0,1},{1,0},{2,3},{3,2},{4,5},{5,4},{6,7},{7,6},{8,9},{9,8},{10,11... | collective-permute-start | bytes 1376264 | tf_op jit(solution)/shard_map/ppermute | solution.py:544
  54.1 4.6 %collective-permute-start.16 = (bf16[16,16,896]{2,1,0:T(8,128)(2,1)S(1)}, bf16[16,16,896]{2,1,0:T(8,128)(2,1)S(1)}, u32[]{:S(2)}, u32[]{:S(2)}) collective-permute-start(bf16[16,16,896]{2,1,0:T(8,128)(2,1)S(1)} %collective-permute-done.12.refs_2_), channel_id=1, source_target_pairs={{0,1},{1,0},{2,3},{3,2},{4,5},{5,4},{6,7},{7,6},{8,9},{9,8},{10,11... | collective-permute-start | bytes 1376264 | tf_op jit(solution)/shard_map/ppermute | solution.py:544
  64.4 6.1 %project.2.refs_0_ = bf16[4,16,16,2048]{3,2,1,0:T(8,128)(2,1)S(1)} custom-call(bf16[16,16,896]{2,1,0:T(8,128)(2,1)S(1)} %compact_rows.2.refs_0_, bf16[16,16,896]{2,1,0:T(8,128)(2,1)S(1)} %collective-permute-done.15.refs_1_, bf16[16,16,896]{2,1,0:T(8,128)(2,1)S(1)} %collective-permute-done.12.refs_2_, ...), custom_call_target="tpu_custom_call" | custom-call | flops 3758096384 | bytes 9699328 | tf_op jit(solution)/shard_map/project/pallas_call | solution.py:174
  76.6 3.6 %project.3.refs_1_ = bf16[2,16,16,2048]{3,2,1,0:T(8,128)(2,1)S(1)} custom-call(bf16[16,16,896]{2,1,0:T(8,128)(2,1)S(1)} %compact_rows.3.refs_0_, bf16[16,16,896]{2,1,0:T(8,128)(2,1)S(1)} %collective-permute-done.17.refs_1_, bf16[896,1024]{1,0:T(8,128)(2,1)S(1)} %copy-done.6, bf16[896,1024]{1,0:T(8,128)(2,1)S(1)} %copy-done.8), custom_call_target="tpu_custom_call" | custom-call | flops 1879048192 | bytes 6684672 | tf_op jit(solution)/shard_map/project/pallas_call | solution.py:174
  81.5 5.7 %collective-permute-done.18.refs_2_ = bf16[16,16,896]{2,1,0:T(8,128)(2,1)S(1)} collective-permute-done((bf16[16,16,896]{2,1,0:T(8,128)(2,1)S(1)}, bf16[16,16,896]{2,1,0:T(8,128)(2,1)S(1)}, u32[]{:S(2)}, u32[]{:S(2)}) %collective-permute-start.18) | collective-permute-done | bytes 458784 | tf_op jit(solution)/shard_map/ppermute | solution.py:547
  89.5 22.0 %attend.1 = (bf16[512,1024]{1,0:T(8,128)(2,1)}, bf16[512,1024]{1,0:T(8,128)(2,1)}, bf16[2,16,32,2048]{3,2,1,0:T(8,128)(2,1)}, bf16[1,16,32,2048]{3,2,1,0:T(8,128...) custom-call(bf16[4,16,16,2048]{3,2,1,0:T(8,128)(2,1)} %copy-done.13,, ...), custom_call_target="tpu_custom_call" | custom-call | flops 7247757312 | bytes 20971520 | tf_op jit(solution)/shard_map/attend/pallas_call | solution.py:297
  119.0 4.1 %grads.1 = (f32[1,16,32,512]{3,2,1,0:T(8,128)S(1)}, f32[2,16,32,512]{3,2,1,0:T(8,128)S(1)}) custom-call(bf16[1,16,32,2048]{3,2,1,0:T(8,128)(2,1)S(1)} %copy-done.15, bf16[2,16,32,2048]{3,2,1,0:T(8,128)(2,1)S(1)} %copy-done.14, bf16[896,1024]{1,0:T(8,128)(2,1)S(1)} %copy-done.7, bf16[896,1024]{1,0:T(8,128)(2,1)S(1)} %copy-done.9), custom_call_target="tpu_custom_call" | custom-call | flops 4294967296 | bytes 14680064 | tf_op jit(solution)/shard_map/grads/pallas_call | solution.py:370
  123.2 2.9 %collective-permute-done.22.rest_0_ = s16[49,32,128]{2,1,0:T(8,128)(2,1)S(1)} collective-permute-done((s16[49,32,128]{2,1,0:T(8,128)(2,1)S(1)}, s16[49,32,128]{2,1,0:T(8,128)(2,1)S(1)}, u32[]{:S(2)}, u32[]{:S(2)}) %collective-permute-start.22) | collective-permute-done | bytes 401440 | tf_op jit(solution)/shard_map/ppermute | solution.py:547
  127.8 2.9 %collective-permute-done.20.got = f32[1,16,32,384]{3,2,1,0:T(8,128)S(1)} collective-permute-done((f32[1,16,32,384]{3,2,1,0:T(8,128)S(1)}, f32[1,16,32,384]{3,2,1,0:T(8,128)S(1)}, u32[]{:S(2)}, u32[]{:S(2)}) %collective-permute-start.20) | collective-permute-done | bytes 786464 | tf_op jit(solution)/shard_map/ppermute | solution.py:544
  136.9 4.0 %collective-permute-done.25.rest_0_ = s16[65,32,128]{2,1,0:T(8,128)(2,1)S(1)} collective-permute-done((s16[65,32,128]{2,1,0:T(8,128)(2,1)S(1)}, s16[65,32,128]{2,1,0:T(8,128)(2,1)S(1)}, u32[]{:S(2)}, u32[]{:S(2)}) %collective-permute-start.25) | collective-permute-done | bytes 532512 | tf_op jit(solution)/shard_map/ppermute | solution.py:547
  147.1 7.1 %collective-permute-start.39 = (s16[25,16,128]{2,1,0:T(8,128)(2,1)S(1)}, s16[25,16,128]{2,1,0:T(8,128)(2,1)S(1)}, u32[]{:S(2)}, u32[]{:S(2)}) collective-permute-start(s16[25,16,128]{2,1,0:T(8,128)(2,1)S(1)} %get-tuple-element.166), channel_id=1, source_target_pairs={{0,28},{4,0},{8,4},{12,8},{16,12},{20,16},{24,20},{28,24},{1,29},{... | collective-permute-start | bytes 307208 | tf_op jit(solution)/shard_map/ppermute | solution.py:550
  156.1 3.0 %collective-permute-done.38.refs_6_ = s16[25,16,128]{2,1,0:T(8,128)(2,1)S(1)} collective-permute-done((s16[25,16,128]{2,1,0:T(8,128)(2,1)S(1)}, s16[25,16,128]{2,1,0:T(8,128)(2,1)S(1)}, u32[]{:S(2)}, u32[]{:S(2)}) %collective-permute-start.38) | collective-permute-done | bytes 102432 | tf_op jit(solution)/shard_map/ppermute | solution.py:550
  161.5 2.4 %collective-permute-start.32 = (s16[33,16,128]{2,1,0:T(8,128)(2,1)S(1)}, s16[33,16,128]{2,1,0:T(8,128)(2,1)S(1)}, u32[]{:S(2)}, u32[]{:S(2)}) collective-permute-start(s16[33,16,128]{2,1,0:T(8,128)(2,1)S(1)} %get-tuple-element.158), channel_id=1, source_target_pairs={{0,28},{4,0},{8,4},{12,8},{16,12},{20,16},{24,20},{28,24},{1,29},{... | collective-permute-start | bytes 405512 | tf_op jit(solution)/shard_map/ppermute | solution.py:550
  163.9 2.7 %gather_grads.2.refs_8_ = f32[16,32,896]{2,1,0:T(8,128)} custom-call(s32[1]{0:T(128)} %get-tuple-element.85.me, s32[8,32]{1,0:T(8,128)S(1)} %copy-done.4, s16[25,16,128]{2,1,0:T(8,128)(2,1)S(1)} %get-tuple-element.159.refs_0_, s16[25,16,128]{2,1,0:T(8,128)(2,1)S(1)} %collective-permute-done.33.refs_1_, ...), custom_call_target="tpu_custom_call" | custom-call | bytes 1572864 | tf_op jit(solution)/shard_map/gather_grads/pallas_call | solution.py:519
  166.6 4.9 %collective-permute-done.28.refs_3_ = s16[33,16,128]{2,1,0:T(8,128)(2,1)S(1)} collective-permute-done((s16[33,16,128]{2,1,0:T(8,128)(2,1)S(1)}, s16[33,16,128]{2,1,0:T(8,128)(2,1)S(1)}, u32[]{:S(2)}, u32[]{:S(2)}) %collective-permute-start.28) | collective-permute-done | bytes 135200 | tf_op jit(solution)/shard_map/ppermute | solution.py:550
  171.5 2.9 %collective-permute-done.29.refs_4_ = s16[33,16,128]{2,1,0:T(8,128)(2,1)S(1)} collective-permute-done((s16[33,16,128]{2,1,0:T(8,128)(2,1)S(1)}, s16[33,16,128]{2,1,0:T(8,128)(2,1)S(1)}, u32[]{:S(2)}, u32[]{:S(2)}) %collective-permute-start.29) | collective-permute-done | bytes 135200 | tf_op jit(solution)/shard_map/ppermute | solution.py:550
  174.4 4.3 %collective-permute-done.31.refs_6_ = s16[33,16,128]{2,1,0:T(8,128)(2,1)S(1)} collective-permute-done((s16[33,16,128]{2,1,0:T(8,128)(2,1)S(1)}, s16[33,16,128]{2,1,0:T(8,128)(2,1)S(1)}, u32[]{:S(2)}, u32[]{:S(2)}) %collective-permute-start.31) | collective-permute-done | bytes 135200 | tf_op jit(solution)/shard_map/ppermute | solution.py:550
  180.5 2.8 %gather_grads.3 = f32[16,32,896]{2,1,0:T(8,128)} custom-call(s32[1]{0:T(128)} %get-tuple-element.85.me, s32[8,32]{1,0:T(8,128)S(1)} %copy-done.4, s16[33,16,128]{2,1,0:T(8,128)(2,1)S(1)} %get-tuple-element.151.refs_0_, s16[33,16,128]{2,1,0:T(8,128)(2,1)S(1)} %collective-permute-done.26.refs_1_, ...), custom_call_target="tpu_custom_call", output_to_operand_aliasing={{}: (10, {})} | custom-call | bytes 2097152 | tf_op jit(solution)/shard_map/gather_grads/pallas_call | solution.py:519
  (108 shorter events, 63.4 us)
Async XLA Ops:
  17.4 14.5 %collective-permute-start.7 = (bf16[4,16,896]{2,1,0:T(8,128)(2,1)}, bf16[4,16,896]{2,1,0:T(8,128)(2,1)S(1)}, u32[]{:S(2)}, u32[]{:S(2)}) collective-permute-start(bf16[4,16,896]{2,1,0:T(8,128)(2,1)} %get-tuple-element.96), channel_id=1, source_target_pairs={{0,16},{4,20},{8,24},{12,28},{16,0},{20,4},{24,8},{28,12},{1,17},{... | collective-permute-start | bytes 344072 | tf_op jit(solution)/shard_map/ppermute | solution.py:550
  19.0 15.4 %collective-permute-start.8 = (bf16[4,16,896]{2,1,0:T(8,128)(2,1)}, bf16[4,16,896]{2,1,0:T(8,128)(2,1)S(1)}, u32[]{:S(2)}, u32[]{:S(2)}) collective-permute-start(bf16[4,16,896]{2,1,0:T(8,128)(2,1)} %get-tuple-element.97), channel_id=1, source_target_pairs={{0,12},{4,16},{8,20},{12,24},{16,28},{20,0},{24,4},{28,8},{1,13},{... | collective-permute-start | bytes 344072 | tf_op jit(solution)/shard_map/ppermute | solution.py:550
  22.7 14.0 %collective-permute-start.9 = (bf16[4,16,896]{2,1,0:T(8,128)(2,1)S(1)}, bf16[4,16,896]{2,1,0:T(8,128)(2,1)S(1)}, u32[]{:S(2)}, u32[]{:S(2)}) collective-permute-start(bf16[4,16,896]{2,1,0:T(8,128)(2,1)S(1)} %copy-done.17), channel_id=1, source_target_pairs={{0,8},{4,12},{8,16},{12,20},{16,24},{20,28},{24,0},{28,4},{1,9},{5... | collective-permute-start | bytes 344072 | tf_op jit(solution)/shard_map/ppermute | solution.py:550
  24.0 14.4 %collective-permute-start.10 = (bf16[4,16,896]{2,1,0:T(8,128)(2,1)S(1)}, bf16[4,16,896]{2,1,0:T(8,128)(2,1)S(1)}, u32[]{:S(2)}, u32[]{:S(2)}) collective-permute-start(bf16[4,16,896]{2,1,0:T(8,128)(2,1)S(1)} %copy-done.16), channel_id=1, source_target_pairs={{0,4},{4,8},{8,12},{12,16},{16,20},{20,24},{24,28},{28,0},{1,5},{5... | collective-permute-start | bytes 344072 | tf_op jit(solution)/shard_map/ppermute | solution.py:550
  26.4 14.6 %collective-permute-start.3 = (bf16[4,16,896]{2,1,0:T(8,128)(2,1)}, bf16[4,16,896]{2,1,0:T(8,128)(2,1)S(1)}, u32[]{:S(2)}, u32[]{:S(2)}) collective-permute-start(bf16[4,16,896]{2,1,0:T(8,128)(2,1)} %get-tuple-element.91), channel_id=1, source_target_pairs={{0,16},{4,20},{8,24},{12,28},{16,0},{20,4},{24,8},{28,12},{1,17},{... | collective-permute-start | bytes 344072 | tf_op jit(solution)/shard_map/ppermute | solution.py:550
  42.8 11.3 %collective-permute-start.12 = (bf16[16,16,896]{2,1,0:T(8,128)(2,1)S(1)}, bf16[16,16,896]{2,1,0:T(8,128)(2,1)S(1)}, u32[]{:S(2)}, u32[]{:S(2)}) collective-permute-start(bf16[16,16,896]{2,1,0:T(8,128)(2,1)S(1)} %compact_rows.2.refs_0_), channel_id=1, source_target_pairs={{0,2},{1,3},{2,0},{3,1},{4,6},{5,7},{6,4},{7,5},{8,10},{9,11},{10,... | collective-permute-start | bytes 1376264 | tf_op jit(solution)/shard_map/ppermute | solution.py:547
  47.7 15.2 %collective-permute-start.15 = (bf16[16,16,896]{2,1,0:T(8,128)(2,1)S(1)}, bf16[16,16,896]{2,1,0:T(8,128)(2,1)S(1)}, u32[]{:S(2)}, u32[]{:S(2)}) collective-permute-start(bf16[16,16,896]{2,1,0:T(8,128)(2,1)S(1)} %compact_rows.2.refs_0_), channel_id=1, source_target_pairs={{0,1},{1,0},{2,3},{3,2},{4,5},{5,4},{6,7},{7,6},{8,9},{9,8},{10,11... | collective-permute-start | bytes 1376264 | tf_op jit(solution)/shard_map/ppermute | solution.py:544
  58.7 13.9 %collective-permute-start = (bf16[4,16,896]{2,1,0:T(8,128)(2,1)}, bf16[4,16,896]{2,1,0:T(8,128)(2,1)S(1)}, u32[]{:S(2)}, u32[]{:S(2)}) collective-permute-start(bf16[4,16,896]{2,1,0:T(8,128)(2,1)} %get-tuple-element.88), channel_id=1, source_target_pairs={{0,28},{4,0},{8,4},{12,8},{16,12},{20,16},{24,20},{28,24},{1,29},{... | collective-permute-start | bytes 344072 | tf_op jit(solution)/shard_map/ppermute | solution.py:550
  58.7 13.9 %collective-permute-start.13 = (bf16[4,16,896]{2,1,0:T(8,128)(2,1)}, bf16[4,16,896]{2,1,0:T(8,128)(2,1)S(1)}, u32[]{:S(2)}, u32[]{:S(2)}) collective-permute-start(bf16[4,16,896]{2,1,0:T(8,128)(2,1)} %get-tuple-element.115), channel_id=1, source_target_pairs={{0,8},{4,12},{8,16},{12,20},{16,24},{20,28},{24,0},{28,4},{1,9},{5... | collective-permute-start | bytes 344072 | tf_op jit(solution)/shard_map/ppermute | solution.py:550
  60.8 11.8 %collective-permute-start.14 = (bf16[4,16,896]{2,1,0:T(8,128)(2,1)}, bf16[4,16,896]{2,1,0:T(8,128)(2,1)S(1)}, u32[]{:S(2)}, u32[]{:S(2)}) collective-permute-start(bf16[4,16,896]{2,1,0:T(8,128)(2,1)} %get-tuple-element.116), channel_id=1, source_target_pairs={{0,4},{4,8},{8,12},{12,16},{16,20},{20,24},{24,28},{28,0},{1,5},{5... | collective-permute-start | bytes 344072 | tf_op jit(solution)/shard_map/ppermute | solution.py:550
  75.1 12.1 %collective-permute-start.18 = (bf16[16,16,896]{2,1,0:T(8,128)(2,1)S(1)}, bf16[16,16,896]{2,1,0:T(8,128)(2,1)S(1)}, u32[]{:S(2)}, u32[]{:S(2)}) collective-permute-start(bf16[16,16,896]{2,1,0:T(8,128)(2,1)S(1)} %compact_rows.3.refs_0_), channel_id=1, source_target_pairs={{0,2},{1,3},{2,0},{3,1},{4,6},{5,7},{6,4},{7,5},{8,10},{9,11},{10,... | collective-permute-start | bytes 1376264 | tf_op jit(solution)/shard_map/ppermute | solution.py:547
  111.9 15.4 %collective-permute-start.24 = (f32[1,16,32,512]{3,2,1,0:T(8,128)S(1)}, f32[1,16,32,512]{3,2,1,0:T(8,128)S(1)}, u32[]{:S(2)}, u32[]{:S(2)}) collective-permute-start(f32[1,16,32,512]{3,2,1,0:T(8,128)S(1)} %get-tuple-element.149), channel_id=1, source_target_pairs={{0,1},{1,0},{2,3},{3,2},{4,5},{5,4},{6,7},{7,6},{8,9},{9,8},{10,11... | collective-permute-start | bytes 3145736 | tf_op jit(solution)/shard_map/ppermute | solution.py:544
  127.6 13.2 %collective-permute-start.25 = (s16[65,32,128]{2,1,0:T(8,128)(2,1)S(1)}, s16[65,32,128]{2,1,0:T(8,128)(2,1)S(1)}, u32[]{:S(2)}, u32[]{:S(2)}) collective-permute-start(s16[65,32,128]{2,1,0:T(8,128)(2,1)S(1)} %far_codes.3), channel_id=1, source_target_pairs={{0,2},{1,3},{2,0},{3,1},{4,6},{5,7},{6,4},{7,5},{8,10},{9,11},{10,... | collective-permute-start | bytes 1597448 | tf_op jit(solution)/shard_map/ppermute | solution.py:547
  132.2 11.7 %collective-permute-start.33 = (s16[25,16,128]{2,1,0:T(8,128)(2,1)S(1)}, s16[25,16,128]{2,1,0:T(8,128)(2,1)S(1)}, u32[]{:S(2)}, u32[]{:S(2)}) collective-permute-start(s16[25,16,128]{2,1,0:T(8,128)(2,1)S(1)} %get-tuple-element.160), channel_id=1, source_target_pairs={{0,4},{4,8},{8,12},{12,16},{16,20},{20,24},{24,28},{28,0},{1,5},{5... | collective-permute-start | bytes 307208 | tf_op jit(solution)/shard_map/ppermute | solution.py:550
  142.1 19.1 %collective-permute-start.26 = (s16[33,16,128]{2,1,0:T(8,128)(2,1)S(1)}, s16[33,16,128]{2,1,0:T(8,128)(2,1)S(1)}, u32[]{:S(2)}, u32[]{:S(2)}) collective-permute-start(s16[33,16,128]{2,1,0:T(8,128)(2,1)S(1)} %get-tuple-element.152), channel_id=1, source_target_pairs={{0,4},{4,8},{8,12},{12,16},{16,20},{20,24},{24,28},{28,0},{1,5},{5... | collective-permute-start | bytes 405512 | tf_op jit(solution)/shard_map/ppermute | solution.py:550
  143.9 17.6 %collective-permute-start.27 = (s16[33,16,128]{2,1,0:T(8,128)(2,1)S(1)}, s16[33,16,128]{2,1,0:T(8,128)(2,1)S(1)}, u32[]{:S(2)}, u32[]{:S(2)}) collective-permute-start(s16[33,16,128]{2,1,0:T(8,128)(2,1)S(1)} %get-tuple-element.153), channel_id=1, source_target_pairs={{0,8},{4,12},{8,16},{12,20},{16,24},{20,28},{24,0},{28,4},{1,9},{5... | collective-permute-start | bytes 405512 | tf_op jit(solution)/shard_map/ppermute | solution.py:550
  143.9 12.0 %collective-permute-start.37 = (s16[25,16,128]{2,1,0:T(8,128)(2,1)S(1)}, s16[25,16,128]{2,1,0:T(8,128)(2,1)S(1)}, u32[]{:S(2)}, u32[]{:S(2)}) collective-permute-start(s16[25,16,128]{2,1,0:T(8,128)(2,1)S(1)} %get-tuple-element.164), channel_id=1, source_target_pairs={{0,20},{4,24},{8,28},{12,0},{16,4},{20,8},{24,12},{28,16},{1,21},{... | collective-permute-start | bytes 307208 | tf_op jit(solution)/shard_map/ppermute | solution.py:550
  144.9 14.3 %collective-permute-start.38 = (s16[25,16,128]{2,1,0:T(8,128)(2,1)S(1)}, s16[25,16,128]{2,1,0:T(8,128)(2,1)S(1)}, u32[]{:S(2)}, u32[]{:S(2)}) collective-permute-start(s16[25,16,128]{2,1,0:T(8,128)(2,1)S(1)} %get-tuple-element.165), channel_id=1, source_target_pairs={{0,24},{4,28},{8,0},{12,4},{16,8},{20,12},{24,16},{28,20},{1,25},{... | collective-permute-start | bytes 307208 | tf_op jit(solution)/shard_map/ppermute | solution.py:550
  147.1 13.2 %collective-permute-start.39 = (s16[25,16,128]{2,1,0:T(8,128)(2,1)S(1)}, s16[25,16,128]{2,1,0:T(8,128)(2,1)S(1)}, u32[]{:S(2)}, u32[]{:S(2)}) collective-permute-start(s16[25,16,128]{2,1,0:T(8,128)(2,1)S(1)} %get-tuple-element.166), channel_id=1, source_target_pairs={{0,28},{4,0},{8,4},{12,8},{16,12},{20,16},{24,20},{28,24},{1,29},{... | collective-permute-start | bytes 307208 | tf_op jit(solution)/shard_map/ppermute | solution.py:550
  155.9 15.6 %collective-permute-start.28 = (s16[33,16,128]{2,1,0:T(8,128)(2,1)S(1)}, s16[33,16,128]{2,1,0:T(8,128)(2,1)S(1)}, u32[]{:S(2)}, u32[]{:S(2)}) collective-permute-start(s16[33,16,128]{2,1,0:T(8,128)(2,1)S(1)} %get-tuple-element.154), channel_id=1, source_target_pairs={{0,12},{4,16},{8,20},{12,24},{16,28},{20,0},{24,4},{28,8},{1,13},{... | collective-permute-start | bytes 405512 | tf_op jit(solution)/shard_map/ppermute | solution.py:550
  159.2 15.2 %collective-permute-start.29 = (s16[33,16,128]{2,1,0:T(8,128)(2,1)S(1)}, s16[33,16,128]{2,1,0:T(8,128)(2,1)S(1)}, u32[]{:S(2)}, u32[]{:S(2)}) collective-permute-start(s16[33,16,128]{2,1,0:T(8,128)(2,1)S(1)} %get-tuple-element.155), channel_id=1, source_target_pairs={{0,16},{4,20},{8,24},{12,28},{16,0},{20,4},{24,8},{28,12},{1,17},{... | collective-permute-start | bytes 405512 | tf_op jit(solution)/shard_map/ppermute | solution.py:550
  160.2 14.1 %collective-permute-start.30 = (s16[33,16,128]{2,1,0:T(8,128)(2,1)S(1)}, s16[33,16,128]{2,1,0:T(8,128)(2,1)S(1)}, u32[]{:S(2)}, u32[]{:S(2)}) collective-permute-start(s16[33,16,128]{2,1,0:T(8,128)(2,1)S(1)} %get-tuple-element.156), channel_id=1, source_target_pairs={{0,20},{4,24},{8,28},{12,0},{16,4},{20,8},{24,12},{28,16},{1,21},{... | collective-permute-start | bytes 405512 | tf_op jit(solution)/shard_map/ppermute | solution.py:550
  161.2 17.5 %collective-permute-start.31 = (s16[33,16,128]{2,1,0:T(8,128)(2,1)S(1)}, s16[33,16,128]{2,1,0:T(8,128)(2,1)S(1)}, u32[]{:S(2)}, u32[]{:S(2)}) collective-permute-start(s16[33,16,128]{2,1,0:T(8,128)(2,1)S(1)} %get-tuple-element.157), channel_id=1, source_target_pairs={{0,24},{4,28},{8,0},{12,4},{16,8},{20,12},{24,16},{28,20},{1,25},{... | collective-permute-start | bytes 405512 | tf_op jit(solution)/shard_map/ppermute | solution.py:550
  161.5 19.0 %collective-permute-start.32 = (s16[33,16,128]{2,1,0:T(8,128)(2,1)S(1)}, s16[33,16,128]{2,1,0:T(8,128)(2,1)S(1)}, u32[]{:S(2)}, u32[]{:S(2)}) collective-permute-start(s16[33,16,128]{2,1,0:T(8,128)(2,1)S(1)} %get-tuple-element.158), channel_id=1, source_target_pairs={{0,28},{4,0},{8,4},{12,8},{16,12},{20,16},{24,20},{28,24},{1,29},{... | collective-permute-start | bytes 405512 | tf_op jit(solution)/shard_map/ppermute | solution.py:550
  (34 other events, 382.8 us)

commit v16 on v15

--- a/solution.py
+++ b/solution.py
@@ -13,7 +13,7 @@
 LANES = 128
 TILE = 16
 VMEM_LIMIT = 28 * 1024 * 1024
-VMEM_MORE = 48 * 1024 * 1024
+VMEM_MORE = 44 * 1024 * 1024
 VMEM_ALL = 60 * 1024 * 1024
 F32 = jnp.float32
 BF16 = jnp.bfloat16
@@ -189,7 +189,7 @@
 def attend_body(places, n_kv, n_late, near, *refs):
     kvs, late = refs[:n_kv], refs[n_kv : n_kv + n_late]
     wk, wv, q_ref, g_ref, att_ref, dq_ref = refs[n_kv + n_late : n_kv + n_late + 6]
-    *grads, near_out, far_out, own_out, rest_out, late_kv, own_all, core_all = refs[n_kv + n_late + 6 :]
+    *grads, far_out, own_out, rest_out, late_kv, own_all, core_all = refs[n_kv + n_late + 6 :]
     step = pl.program_id(0)
     width = q_ref.shape[1]
     enc = wk.shape[0]
@@ -259,15 +259,16 @@
     def _():
         count = own_out.shape[-1]
 
-        def part(ref, cols, out):
+        def part(ref, cols):
             rows = ref[...].reshape(-1, 2 * width)
             res = dot(rows[:, :width], wk[cols, :], last) + dot(rows[:, width:], wv[cols, :], last)
-            out[...] = res.reshape(out.shape)
-
-        part(core_all.at[near:], slice(0, count), far_out)
-        part(core_all.at[:near], slice(0, count), near_out)
-        part(own_all, slice(0, count), own_out)
-        part(core_all.at[near:], slice(count, enc), rest_out)
+            return res.reshape(ref.shape[:3] + (-1,))
+
+        far_out[...] = part(core_all.at[near:], slice(0, count))
+        own_out[...] = part(own_all, slice(0, count))
+        rest_out[:near] = jnp.zeros_like(rest_out[:near])
+        rest_out[:near, :, :, :count] = part(core_all.at[:near], slice(0, count))
+        rest_out[near:] = part(core_all.at[near:], slice(count, enc))
 
 
 def attend(kvs, late, wk, wv, places, near, share, count, queries, cotangent):
@@ -291,8 +292,7 @@
     def whole(shape):
         return pl.BlockSpec(shape, lambda i: (0,) * len(shape))
 
-    parts = [(near, n, sub, count), (half - near, n, sub, count), (half, n, sub, count)]
-    parts.append((half - near, n, sub, enc - count))
+    parts = [(half - near, n, sub, count), (half, n, sub, count), (half, n, sub, enc - count)]
     every = (half, n, sub, 2 * width)
     return pl.pallas_call(
         functools.partial(attend_body, places, len(kvs), len(late), near),
@@ -392,7 +392,7 @@
 
 
 def far_codes_body(cuts, mine, got, *codes):
-    far, n, sub, count = got.shape
+    far, n, sub, count = mine.shape
     row = lax.broadcasted_iota(jnp.int32, (sub, LANES), 0)
     for k in range(far):
         code, power = encode(mine[k] + got[k], (1, 2))
@@ -408,18 +408,22 @@
 
 
 def far_codes(own, got, cuts):
-    far, n, sub, count = got.shape
+    n_x, n, sub, count = own.shape
+    far = n_x - 1
     shapes = [(cut * n + (q == 0), sub, LANES) for q, cut in enumerate(cuts)] * far
+    block = tuple(pl.Element(size) for size in (far, n, sub, count))
 
     def whole(shape):
         return pl.BlockSpec(shape, lambda i: (0,) * len(shape))
 
-    mine = pl.BlockSpec(tuple(pl.Element(size) for size in got.shape), lambda i: (1, 0, 0, 0))
+    behind = got.shape[0] - far
+    mine = pl.BlockSpec(block, lambda i: (1, 0, 0, 0))
+    theirs = pl.BlockSpec(block, lambda i: (behind, 0, 0, 0))
     out = pl.pallas_call(
         functools.partial(far_codes_body, cuts),
         out_shape=[jax.ShapeDtypeStruct(shape, jnp.int16) for shape in shapes],
         grid=(1,),
-        in_specs=[mine, whole(got.shape)],
+        in_specs=[mine, theirs],
         out_specs=[whole(shape) for shape in shapes],
         compiler_params=params(),
         cost_estimate=cost(8 * got.size, 10 * got.size),
@@ -466,8 +470,8 @@
 
 
 def send_codes(request, own, got, codes, cuts, n_dp):
-    _, n, sub, count = got.shape
-    block = pl.BlockSpec(got.shape, lambda i: (0, 0, 0, 0))
+    _, n, sub, count = own.shape
+    block = pl.BlockSpec((1, n, sub, count), lambda i: (0, 0, 0, 0))
     size = count // LANES * (sub // TILE)
     cap = request.shape[0] // n_dp
     shape = (cap * size + 1, TILE, LANES)
@@ -590,12 +594,11 @@
 
     split = 3 * LANES
     parts = ((0, split), (split, enc - split))
-    attended, d_query, d_own, d_core, near, far, own, far_b = attend(
+    attended, d_query, d_own, d_core, far, own, rest = attend(
         kvs, late, key_weight, value_weight, places, 1, share, split, queries, cotangent
     )
     far_got = over_core(far)
-    near_got = over_core(near)
-    far_got_b = over_core(far_b)
+    near_got = far_got_b = over_core(rest)
     cuts = (parts[0][1] // LANES,)
     codes = far_codes(own, far_got, cuts)
     near_b, own_b = grads_of(d_core, d_own, key_weight, value_weight, parts[1])

time: 184 us -> 185 us (level)
  waiting for transfers between devices: 47.9 us -> 59.3 us
  starting transfers between devices: 59.3 us -> 52.5 us
  local copies, waits for them, and re-layouts: 9.62 us -> 7.03 us
    ppermute x28, waiting for transfers between devices: 27.8 us -> 35.2 us  [over_dp(): return lax.ppermute(x, 'dp', [(i, (i + d) % n_dp) for i in range(n_dp)])]
    ppermute x28, starting transfers between devices: 43.2 us -> 36.1 us  [over_dp(): return lax.ppermute(x, 'dp', [(i, (i + d) % n_dp) for i in range(n_dp)])]
    ppermute x4, waiting for transfers between devices: 12.6 us -> 16.6 us  [over_x(): lax.ppermute(x, 'tensor', [(t, (t + 2 * d) % n_tp) for t in range(n_tp)])]
    unnamed x36 -> x30, local copies, waits for them, and re-layouts: 9.62 us -> 7.03 us
    ppermute x8 -> x7, starting transfers between devices: 14.3 us -> 14.1 us  [over_core(): return lax.ppermute(x, 'tensor', [(t, t ^ 1) for t in range(n_tp)])]
    ppermute x8 -> x7, waiting for transfers between devices: 7.5 us -> 7.58 us  [over_core(): return lax.ppermute(x, 'tensor', [(t, t ^ 1) for t in range(n_tp)])]
  transfers between devices with their start and end apart: 40 -> 39, of which waited for: 17 -> 17; matrix products, arithmetic and copies ran while one was open for 0% -> 0% of each run, Pallas kernels for 13% -> 13%
where the time goes in v16:
time: 185 us; the launch traced here: 184 us
  waiting for transfers between devices  59.3 us (32%)
  Pallas kernels  55.5 us (30%)
  starting transfers between devices  52.5 us (28%)
  blocking collectives  8.59 us (5%)
  local copies, waits for them, and re-layouts  7.03 us (4%)
    ppermute x28, starting transfers between devices, over_dp(): return lax.ppermute(x, 'dp', [(i, (i + d) % n_dp) for i in range(n_dp)])  36.1 us
    ppermute x28, waiting for transfers between devices, over_dp(): return lax.ppermute(x, 'dp', [(i, (i + d) % n_dp) for i in range(n_dp)])  35.2 us
    pallas_call x1, Pallas kernels, attend(): pl.pallas_call(functools.partial(attend_body, places, len(kvs), len(late)...  20.8 us
    ppermute x4, waiting for transfers between devices, over_x(): lax.ppermute(x, 'tensor', [(t, (t + 2 * d) % n_tp) for t in range(n_tp)])  16.6 us
    ppermute x7, starting transfers between devices, over_core(): return lax.ppermute(x, 'tensor', [(t, t ^ 1) for t in range(n_tp)])  14.1 us
    pallas_call x2, Pallas kernels, project(): pl.pallas_call(functools.partial(project_body, n_in), out_shape=jax.Shape...  9.73 us
    psum x1, blocking collectives, on_device(): asked = lax.psum(wanted, 'dp')  8.59 us
    ppermute x7, waiting for transfers between devices, over_core(): return lax.ppermute(x, 'tensor', [(t, t ^ 1) for t in range(n_tp)])  7.58 us
  transfers between devices with their start and end apart: 39, of which 17 were waited for; matrix products, arithmetic and copies ran while one was open for 0% of the time, Pallas kernels for 13%

profile of v16, /device:TPU:13, one launch (start us, length us, event | category | flops | bytes accessed | tf_op | source)
XLA Modules:
  0.0 184.1 jit_solution(13257456913105632416)
XLA Ops:
  2.2 8.6 %psum.7.asked = s32[8,32]{1,0:T(8,128)} all-reduce(s32[8,32]{1,0:T(8,128)} %get-tuple-element.85), channel_id=1, replica_groups=mesh['dp'=8,'tensor'=4] {'dp'}, use_global_device_ids=true, to_apply=%region_0.0 | all-reduce | flops 256 | bytes 2048 | tf_op jit(solution)/shard_map/psum | solution.py:563
  10.8 3.4 %pack_rows.3 = (bf16[4,16,896]{2,1,0:T(8,128)(2,1)}, bf16[4,16,896]{2,1,0:T(8,128)(2,1)}, bf16[4,16,896]{2,1,0:T(8,128)(2,1)}, bf16[4,16,896]{2,1,0:T(8,128)(2,1...) custom-call(s32[1]{0:T(128)} %get-tuple-element.84.me, ...), custom_call_target="tpu_custom_call" | custom-call | bytes 1835008 | tf_op jit(solution)/shard_map/pack_rows/pallas_call | solution.py:97
  19.0 3.5 %pack_rows.2 = (bf16[4,16,896]{2,1,0:T(8,128)(2,1)}, bf16[4,16,896]{2,1,0:T(8,128)(2,1)}, bf16[4,16,896]{2,1,0:T(8,128)(2,1)}, bf16[4,16,896]{2,1,0:T(8,128)(2,1...) custom-call(s32[1]{0:T(128)} %get-tuple-element.84.me, ...), custom_call_target="tpu_custom_call" | custom-call | bytes 1835008 | tf_op jit(solution)/shard_map/pack_rows/pallas_call | solution.py:97
  25.9 6.0 %collective-permute-start.3 = (bf16[4,16,896]{2,1,0:T(8,128)(2,1)}, bf16[4,16,896]{2,1,0:T(8,128)(2,1)S(1)}, u32[]{:S(2)}, u32[]{:S(2)}) collective-permute-start(bf16[4,16,896]{2,1,0:T(8,128)(2,1)} %get-tuple-element.90), channel_id=1, source_target_pairs={{0,16},{4,20},{8,24},{12,28},{16,0},{20,4},{24,8},{28,12},{1,17},{... | collective-permute-start | bytes 344072 | tf_op jit(solution)/shard_map/ppermute | solution.py:554
  31.9 2.3 %collective-permute-done.8.refs_5_ = bf16[4,16,896]{2,1,0:T(8,128)(2,1)S(1)} collective-permute-done((bf16[4,16,896]{2,1,0:T(8,128)(2,1)}, bf16[4,16,896]{2,1,0:T(8,128)(2,1)S(1)}, u32[]{:S(2)}, u32[]{:S(2)}) %collective-permute-start.8) | collective-permute-done | bytes 114720 | tf_op jit(solution)/shard_map/ppermute | solution.py:554
  34.2 2.4 %collective-permute-done.9.refs_6_ = bf16[4,16,896]{2,1,0:T(8,128)(2,1)S(1)} collective-permute-done((bf16[4,16,896]{2,1,0:T(8,128)(2,1)S(1)}, bf16[4,16,896]{2,1,0:T(8,128)(2,1)S(1)}, u32[]{:S(2)}, u32[]{:S(2)}) %collective-permute-start.9) | collective-permute-done | bytes 114720 | tf_op jit(solution)/shard_map/ppermute | solution.py:554
  38.4 2.6 %collective-permute-done.3.refs_4_ = bf16[4,16,896]{2,1,0:T(8,128)(2,1)S(1)} collective-permute-done((bf16[4,16,896]{2,1,0:T(8,128)(2,1)}, bf16[4,16,896]{2,1,0:T(8,128)(2,1)S(1)}, u32[]{:S(2)}, u32[]{:S(2)}) %collective-permute-start.3) | collective-permute-done | bytes 114720 | tf_op jit(solution)/shard_map/ppermute | solution.py:554
  47.3 6.6 %collective-permute-start.15 = (bf16[16,16,896]{2,1,0:T(8,128)(2,1)S(1)}, bf16[16,16,896]{2,1,0:T(8,128)(2,1)S(1)}, u32[]{:S(2)}, u32[]{:S(2)}) collective-permute-start(bf16[16,16,896]{2,1,0:T(8,128)(2,1)S(1)} %compact_rows.2.refs_0_), channel_id=1, source_target_pairs={{0,1},{1,0},{2,3},{3,2},{4,5},{5,4},{6,7},{7,6},{8,9},{9,8},{10,11... | collective-permute-start | bytes 1376264 | tf_op jit(solution)/shard_map/ppermute | solution.py:548
  54.0 4.4 %collective-permute-start.16 = (bf16[16,16,896]{2,1,0:T(8,128)(2,1)S(1)}, bf16[16,16,896]{2,1,0:T(8,128)(2,1)S(1)}, u32[]{:S(2)}, u32[]{:S(2)}) collective-permute-start(bf16[16,16,896]{2,1,0:T(8,128)(2,1)S(1)} %collective-permute-done.12.refs_2_), channel_id=1, source_target_pairs={{0,1},{1,0},{2,3},{3,2},{4,5},{5,4},{6,7},{7,6},{8,9},{9,8},{10,11... | collective-permute-start | bytes 1376264 | tf_op jit(solution)/shard_map/ppermute | solution.py:548
  64.1 6.1 %project.2.refs_0_ = bf16[4,16,16,2048]{3,2,1,0:T(8,128)(2,1)S(1)} custom-call(bf16[16,16,896]{2,1,0:T(8,128)(2,1)S(1)} %compact_rows.2.refs_0_, bf16[16,16,896]{2,1,0:T(8,128)(2,1)S(1)} %collective-permute-done.15.refs_1_, bf16[16,16,896]{2,1,0:T(8,128)(2,1)S(1)} %collective-permute-done.12.refs_2_, ...), custom_call_target="tpu_custom_call" | custom-call | flops 3758096384 | bytes 9699328 | tf_op jit(solution)/shard_map/project/pallas_call | solution.py:174
  76.4 3.6 %project.3.refs_1_ = bf16[2,16,16,2048]{3,2,1,0:T(8,128)(2,1)S(1)} custom-call(bf16[16,16,896]{2,1,0:T(8,128)(2,1)S(1)} %compact_rows.3.refs_0_, bf16[16,16,896]{2,1,0:T(8,128)(2,1)S(1)} %collective-permute-done.17.refs_1_, bf16[896,1024]{1,0:T(8,128)(2,1)S(1)} %copy-done.4, bf16[896,1024]{1,0:T(8,128)(2,1)S(1)} %copy-done.5), custom_call_target="tpu_custom_call" | custom-call | flops 1879048192 | bytes 6684672 | tf_op jit(solution)/shard_map/project/pallas_call | solution.py:174
  81.3 5.7 %collective-permute-done.18.refs_2_ = bf16[16,16,896]{2,1,0:T(8,128)(2,1)S(1)} collective-permute-done((bf16[16,16,896]{2,1,0:T(8,128)(2,1)S(1)}, bf16[16,16,896]{2,1,0:T(8,128)(2,1)S(1)}, u32[]{:S(2)}, u32[]{:S(2)}) %collective-permute-start.18) | collective-permute-done | bytes 458784 | tf_op jit(solution)/shard_map/ppermute | solution.py:551
  89.4 20.8 %attend.1 = (bf16[512,1024]{1,0:T(8,128)(2,1)}, bf16[512,1024]{1,0:T(8,128)(2,1)}, bf16[2,16,32,2048]{3,2,1,0:T(8,128)(2,1)}, bf16[1,16,32,2048]{3,2,1,0:T(8,128...) custom-call(bf16[4,16,16,2048]{3,2,1,0:T(8,128)(2,1)} %copy-done.10, ...), custom_call_target="tpu_custom_call" | custom-call | flops 7247757312 | bytes 20971520 | tf_op jit(solution)/shard_map/attend/pallas_call | solution.py:297
  110.8 4.8 %collective-permute-done.21.got = f32[1,16,32,384]{3,2,1,0:T(8,128)S(1)} collective-permute-done((f32[1,16,32,384]{3,2,1,0:T(8,128)S(1)}, f32[1,16,32,384]{3,2,1,0:T(8,128)S(1)}, u32[]{:S(2)}, u32[]{:S(2)}) %collective-permute-start.21) | collective-permute-done | bytes 786464 | tf_op jit(solution)/shard_map/ppermute | solution.py:548
  118.4 4.1 %grads.1 = (f32[1,16,32,512]{3,2,1,0:T(8,128)S(1)}, f32[2,16,32,512]{3,2,1,0:T(8,128)S(1)}) custom-call(bf16[1,16,32,2048]{3,2,1,0:T(8,128)(2,1)S(1)} %copy-done.12, bf16[2,16,32,2048]{3,2,1,0:T(8,128)(2,1)S(1)} %copy-done.11, bf16[896,1024]{1,0:T(8,128)(2,1)S(1)} %copy-done.4, bf16[896,1024]{1,0:T(8,128)(2,1)S(1)} %copy-done.6), custom_call_target="tpu_custom_call" | custom-call | flops 4294967296 | bytes 14680064 | tf_op jit(solution)/shard_map/grads/pallas_call | solution.py:370
  122.5 4.1 %collective-permute-done.22.rest_0_ = s16[49,32,128]{2,1,0:T(8,128)(2,1)S(1)} collective-permute-done((s16[49,32,128]{2,1,0:T(8,128)(2,1)S(1)}, s16[49,32,128]{2,1,0:T(8,128)(2,1)S(1)}, u32[]{:S(2)}, u32[]{:S(2)}) %collective-permute-start.22) | collective-permute-done | bytes 401440 | tf_op jit(solution)/shard_map/ppermute | solution.py:551
  135.0 6.7 %collective-permute-done.24.rest_0_ = s16[65,32,128]{2,1,0:T(8,128)(2,1)S(1)} collective-permute-done((s16[65,32,128]{2,1,0:T(8,128)(2,1)S(1)}, s16[65,32,128]{2,1,0:T(8,128)(2,1)S(1)}, u32[]{:S(2)}, u32[]{:S(2)}) %collective-permute-start.24) | collective-permute-done | bytes 532512 | tf_op jit(solution)/shard_map/ppermute | solution.py:551
  145.7 2.6 %collective-permute-start.37 = (s16[25,16,128]{2,1,0:T(8,128)(2,1)S(1)}, s16[25,16,128]{2,1,0:T(8,128)(2,1)S(1)}, u32[]{:S(2)}, u32[]{:S(2)}) collective-permute-start(s16[25,16,128]{2,1,0:T(8,128)(2,1)S(1)} %get-tuple-element.163), channel_id=1, source_target_pairs={{0,24},{4,28},{8,0},{12,4},{16,8},{20,12},{24,16},{28,20},{1,25},{... | collective-permute-start | bytes 307208 | tf_op jit(solution)/shard_map/ppermute | solution.py:554
  148.6 5.4 %collective-permute-done.36.refs_5_ = s16[25,16,128]{2,1,0:T(8,128)(2,1)S(1)} collective-permute-done((s16[25,16,128]{2,1,0:T(8,128)(2,1)S(1)}, s16[25,16,128]{2,1,0:T(8,128)(2,1)S(1)}, u32[]{:S(2)}, u32[]{:S(2)}) %collective-permute-start.36) | collective-permute-done | bytes 102432 | tf_op jit(solution)/shard_map/ppermute | solution.py:554
  162.0 2.6 %gather_grads.2.refs_8_ = f32[16,32,896]{2,1,0:T(8,128)} custom-call(s32[1]{0:T(128)} %get-tuple-element.84.me, s32[8,32]{1,0:T(8,128)S(1)} %copy-done.2, s16[25,16,128]{2,1,0:T(8,128)(2,1)S(1)} %get-tuple-element.157.refs_0_, s16[25,16,128]{2,1,0:T(8,128)(2,1)S(1)} %collective-permute-done.32.refs_1_, ...), custom_call_target="tpu_custom_call" | custom-call | bytes 1572864 | tf_op jit(solution)/shard_map/gather_grads/pallas_call | solution.py:523
  164.7 7.8 %collective-permute-done.28.refs_4_ = s16[33,16,128]{2,1,0:T(8,128)(2,1)S(1)} collective-permute-done((s16[33,16,128]{2,1,0:T(8,128)(2,1)S(1)}, s16[33,16,128]{2,1,0:T(8,128)(2,1)S(1)}, u32[]{:S(2)}, u32[]{:S(2)}) %collective-permute-start.28) | collective-permute-done | bytes 135200 | tf_op jit(solution)/shard_map/ppermute | solution.py:554
  172.4 3.9 %collective-permute-done.30.refs_6_ = s16[33,16,128]{2,1,0:T(8,128)(2,1)S(1)} collective-permute-done((s16[33,16,128]{2,1,0:T(8,128)(2,1)S(1)}, s16[33,16,128]{2,1,0:T(8,128)(2,1)S(1)}, u32[]{:S(2)}, u32[]{:S(2)}) %collective-permute-start.30) | collective-permute-done | bytes 135200 | tf_op jit(solution)/shard_map/ppermute | solution.py:554
  176.3 4.8 %collective-permute-done.31.refs_7_ = s16[33,16,128]{2,1,0:T(8,128)(2,1)S(1)} collective-permute-done((s16[33,16,128]{2,1,0:T(8,128)(2,1)S(1)}, s16[33,16,128]{2,1,0:T(8,128)(2,1)S(1)}, u32[]{:S(2)}, u32[]{:S(2)}) %collective-permute-start.31) | collective-permute-done | bytes 135200 | tf_op jit(solution)/shard_map/ppermute | solution.py:554
  181.1 2.8 %gather_grads.3 = f32[16,32,896]{2,1,0:T(8,128)} custom-call(s32[1]{0:T(128)} %get-tuple-element.84.me, s32[8,32]{1,0:T(8,128)S(1)} %copy-done.2, s16[33,16,128]{2,1,0:T(8,128)(2,1)S(1)} %get-tuple-element.149.refs_0_, s16[33,16,128]{2,1,0:T(8,128)(2,1)S(1)} %collective-permute-done.25.refs_1_, ...), custom_call_target="tpu_custom_call", output_to_operand_aliasing={{}: (10, {})} | custom-call | bytes 2097152 | tf_op jit(solution)/shard_map/gather_grads/pallas_call | solution.py:523
  (100 shorter events, 57.3 us)
Async XLA Ops:
  17.5 14.4 %collective-permute-start.7 = (bf16[4,16,896]{2,1,0:T(8,128)(2,1)}, bf16[4,16,896]{2,1,0:T(8,128)(2,1)S(1)}, u32[]{:S(2)}, u32[]{:S(2)}) collective-permute-start(bf16[4,16,896]{2,1,0:T(8,128)(2,1)} %get-tuple-element.95), channel_id=1, source_target_pairs={{0,16},{4,20},{8,24},{12,28},{16,0},{20,4},{24,8},{28,12},{1,17},{... | collective-permute-start | bytes 344072 | tf_op jit(solution)/shard_map/ppermute | solution.py:554
  19.0 15.3 %collective-permute-start.8 = (bf16[4,16,896]{2,1,0:T(8,128)(2,1)}, bf16[4,16,896]{2,1,0:T(8,128)(2,1)S(1)}, u32[]{:S(2)}, u32[]{:S(2)}) collective-permute-start(bf16[4,16,896]{2,1,0:T(8,128)(2,1)} %get-tuple-element.96), channel_id=1, source_target_pairs={{0,12},{4,16},{8,20},{12,24},{16,28},{20,0},{24,4},{28,8},{1,13},{... | collective-permute-start | bytes 344072 | tf_op jit(solution)/shard_map/ppermute | solution.py:554
  22.5 14.1 %collective-permute-start.9 = (bf16[4,16,896]{2,1,0:T(8,128)(2,1)S(1)}, bf16[4,16,896]{2,1,0:T(8,128)(2,1)S(1)}, u32[]{:S(2)}, u32[]{:S(2)}) collective-permute-start(bf16[4,16,896]{2,1,0:T(8,128)(2,1)S(1)} %copy-done.14), channel_id=1, source_target_pairs={{0,8},{4,12},{8,16},{12,20},{16,24},{20,28},{24,0},{28,4},{1,9},{5... | collective-permute-start | bytes 344072 | tf_op jit(solution)/shard_map/ppermute | solution.py:554
  23.9 14.5 %collective-permute-start.10 = (bf16[4,16,896]{2,1,0:T(8,128)(2,1)S(1)}, bf16[4,16,896]{2,1,0:T(8,128)(2,1)S(1)}, u32[]{:S(2)}, u32[]{:S(2)}) collective-permute-start(bf16[4,16,896]{2,1,0:T(8,128)(2,1)S(1)} %copy-done.13), channel_id=1, source_target_pairs={{0,4},{4,8},{8,12},{12,16},{16,20},{20,24},{24,28},{28,0},{1,5},{5... | collective-permute-start | bytes 344072 | tf_op jit(solution)/shard_map/ppermute | solution.py:554
  25.9 15.0 %collective-permute-start.3 = (bf16[4,16,896]{2,1,0:T(8,128)(2,1)}, bf16[4,16,896]{2,1,0:T(8,128)(2,1)S(1)}, u32[]{:S(2)}, u32[]{:S(2)}) collective-permute-start(bf16[4,16,896]{2,1,0:T(8,128)(2,1)} %get-tuple-element.90), channel_id=1, source_target_pairs={{0,16},{4,20},{8,24},{12,28},{16,0},{20,4},{24,8},{28,12},{1,17},{... | collective-permute-start | bytes 344072 | tf_op jit(solution)/shard_map/ppermute | solution.py:554
  47.3 15.3 %collective-permute-start.15 = (bf16[16,16,896]{2,1,0:T(8,128)(2,1)S(1)}, bf16[16,16,896]{2,1,0:T(8,128)(2,1)S(1)}, u32[]{:S(2)}, u32[]{:S(2)}) collective-permute-start(bf16[16,16,896]{2,1,0:T(8,128)(2,1)S(1)} %compact_rows.2.refs_0_), channel_id=1, source_target_pairs={{0,1},{1,0},{2,3},{3,2},{4,5},{5,4},{6,7},{7,6},{8,9},{9,8},{10,11... | collective-permute-start | bytes 1376264 | tf_op jit(solution)/shard_map/ppermute | solution.py:548
  58.4 13.8 %collective-permute-start = (bf16[4,16,896]{2,1,0:T(8,128)(2,1)}, bf16[4,16,896]{2,1,0:T(8,128)(2,1)S(1)}, u32[]{:S(2)}, u32[]{:S(2)}) collective-permute-start(bf16[4,16,896]{2,1,0:T(8,128)(2,1)} %get-tuple-element.87), channel_id=1, source_target_pairs={{0,28},{4,0},{8,4},{12,8},{16,12},{20,16},{24,20},{28,24},{1,29},{... | collective-permute-start | bytes 344072 | tf_op jit(solution)/shard_map/ppermute | solution.py:554
  58.4 13.8 %collective-permute-start.13 = (bf16[4,16,896]{2,1,0:T(8,128)(2,1)}, bf16[4,16,896]{2,1,0:T(8,128)(2,1)S(1)}, u32[]{:S(2)}, u32[]{:S(2)}) collective-permute-start(bf16[4,16,896]{2,1,0:T(8,128)(2,1)} %get-tuple-element.114), channel_id=1, source_target_pairs={{0,8},{4,12},{8,16},{12,20},{16,24},{20,28},{24,0},{28,4},{1,9},{5... | collective-permute-start | bytes 344072 | tf_op jit(solution)/shard_map/ppermute | solution.py:554
  60.6 11.7 %collective-permute-start.14 = (bf16[4,16,896]{2,1,0:T(8,128)(2,1)}, bf16[4,16,896]{2,1,0:T(8,128)(2,1)S(1)}, u32[]{:S(2)}, u32[]{:S(2)}) collective-permute-start(bf16[4,16,896]{2,1,0:T(8,128)(2,1)} %get-tuple-element.115), channel_id=1, source_target_pairs={{0,4},{4,8},{8,12},{12,16},{16,20},{20,24},{24,28},{28,0},{1,5},{5... | collective-permute-start | bytes 344072 | tf_op jit(solution)/shard_map/ppermute | solution.py:554
  75.0 12.1 %collective-permute-start.18 = (bf16[16,16,896]{2,1,0:T(8,128)(2,1)S(1)}, bf16[16,16,896]{2,1,0:T(8,128)(2,1)S(1)}, u32[]{:S(2)}, u32[]{:S(2)}) collective-permute-start(bf16[16,16,896]{2,1,0:T(8,128)(2,1)S(1)} %compact_rows.3.refs_0_), channel_id=1, source_target_pairs={{0,2},{1,3},{2,0},{3,1},{4,6},{5,7},{6,4},{7,5},{8,10},{9,11},{10,... | collective-permute-start | bytes 1376264 | tf_op jit(solution)/shard_map/ppermute | solution.py:551
  110.2 17.4 %collective-permute-start.20 = (f32[2,16,32,512]{3,2,1,0:T(8,128)}, f32[2,16,32,512]{3,2,1,0:T(8,128)S(1)}, u32[]{:S(2)}, u32[]{:S(2)}) collective-permute-start(f32[2,16,32,512]{3,2,1,0:T(8,128)} %get-tuple-element.134), channel_id=1, source_target_pairs={{0,1},{1,0},{2,3},{3,2},{4,5},{5,4},{6,7},{7,6},{8,9},{9,8},{10,11... | collective-permute-start | bytes 6291464 | tf_op jit(solution)/shard_map/ppermute | solution.py:548
  127.9 13.8 %collective-permute-start.24 = (s16[65,32,128]{2,1,0:T(8,128)(2,1)S(1)}, s16[65,32,128]{2,1,0:T(8,128)(2,1)S(1)}, u32[]{:S(2)}, u32[]{:S(2)}) collective-permute-start(s16[65,32,128]{2,1,0:T(8,128)(2,1)S(1)} %far_codes.3), channel_id=1, source_target_pairs={{0,2},{1,3},{2,0},{3,1},{4,6},{5,7},{6,4},{7,5},{8,10},{9,11},{10,... | collective-permute-start | bytes 1597448 | tf_op jit(solution)/shard_map/ppermute | solution.py:551
  129.9 14.9 %collective-permute-start.32 = (s16[25,16,128]{2,1,0:T(8,128)(2,1)S(1)}, s16[25,16,128]{2,1,0:T(8,128)(2,1)S(1)}, u32[]{:S(2)}, u32[]{:S(2)}) collective-permute-start(s16[25,16,128]{2,1,0:T(8,128)(2,1)S(1)} %get-tuple-element.158), channel_id=1, source_target_pairs={{0,4},{4,8},{8,12},{12,16},{16,20},{20,24},{24,28},{28,0},{1,5},{5... | collective-permute-start | bytes 307208 | tf_op jit(solution)/shard_map/ppermute | solution.py:554
  131.6 13.2 %collective-permute-start.33 = (s16[25,16,128]{2,1,0:T(8,128)(2,1)S(1)}, s16[25,16,128]{2,1,0:T(8,128)(2,1)S(1)}, u32[]{:S(2)}, u32[]{:S(2)}) collective-permute-start(s16[25,16,128]{2,1,0:T(8,128)(2,1)S(1)} %get-tuple-element.159), channel_id=1, source_target_pairs={{0,8},{4,12},{8,16},{12,20},{16,24},{20,28},{24,0},{28,4},{1,9},{5... | collective-permute-start | bytes 307208 | tf_op jit(solution)/shard_map/ppermute | solution.py:554
  131.6 14.1 %collective-permute-start.34 = (s16[25,16,128]{2,1,0:T(8,128)(2,1)S(1)}, s16[25,16,128]{2,1,0:T(8,128)(2,1)S(1)}, u32[]{:S(2)}, u32[]{:S(2)}) collective-permute-start(s16[25,16,128]{2,1,0:T(8,128)(2,1)S(1)} %get-tuple-element.160), channel_id=1, source_target_pairs={{0,12},{4,16},{8,20},{12,24},{16,28},{20,0},{24,4},{28,8},{1,13},{... | collective-permute-start | bytes 307208 | tf_op jit(solution)/shard_map/ppermute | solution.py:554
  133.9 14.4 %collective-permute-start.35 = (s16[25,16,128]{2,1,0:T(8,128)(2,1)S(1)}, s16[25,16,128]{2,1,0:T(8,128)(2,1)S(1)}, u32[]{:S(2)}, u32[]{:S(2)}) collective-permute-start(s16[25,16,128]{2,1,0:T(8,128)(2,1)S(1)} %get-tuple-element.161), channel_id=1, source_target_pairs={{0,16},{4,20},{8,24},{12,28},{16,0},{20,4},{24,8},{28,12},{1,17},{... | collective-permute-start | bytes 307208 | tf_op jit(solution)/shard_map/ppermute | solution.py:554
  143.0 18.3 %collective-permute-start.25 = (s16[33,16,128]{2,1,0:T(8,128)(2,1)S(1)}, s16[33,16,128]{2,1,0:T(8,128)(2,1)S(1)}, u32[]{:S(2)}, u32[]{:S(2)}) collective-permute-start(s16[33,16,128]{2,1,0:T(8,128)(2,1)S(1)} %get-tuple-element.150), channel_id=1, source_target_pairs={{0,4},{4,8},{8,12},{12,16},{16,20},{20,24},{24,28},{28,0},{1,5},{5... | collective-permute-start | bytes 405512 | tf_op jit(solution)/shard_map/ppermute | solution.py:554
  144.8 16.5 %collective-permute-start.26 = (s16[33,16,128]{2,1,0:T(8,128)(2,1)S(1)}, s16[33,16,128]{2,1,0:T(8,128)(2,1)S(1)}, u32[]{:S(2)}, u32[]{:S(2)}) collective-permute-start(s16[33,16,128]{2,1,0:T(8,128)(2,1)S(1)} %get-tuple-element.151), channel_id=1, source_target_pairs={{0,8},{4,12},{8,16},{12,20},{16,24},{20,28},{24,0},{28,4},{1,9},{5... | collective-permute-start | bytes 405512 | tf_op jit(solution)/shard_map/ppermute | solution.py:554
  145.7 11.5 %collective-permute-start.37 = (s16[25,16,128]{2,1,0:T(8,128)(2,1)S(1)}, s16[25,16,128]{2,1,0:T(8,128)(2,1)S(1)}, u32[]{:S(2)}, u32[]{:S(2)}) collective-permute-start(s16[25,16,128]{2,1,0:T(8,128)(2,1)S(1)} %get-tuple-element.163), channel_id=1, source_target_pairs={{0,24},{4,28},{8,0},{12,4},{16,8},{20,12},{24,16},{28,20},{1,25},{... | collective-permute-start | bytes 307208 | tf_op jit(solution)/shard_map/ppermute | solution.py:554
  148.3 12.8 %collective-permute-start.38 = (s16[25,16,128]{2,1,0:T(8,128)(2,1)S(1)}, s16[25,16,128]{2,1,0:T(8,128)(2,1)S(1)}, u32[]{:S(2)}, u32[]{:S(2)}) collective-permute-start(s16[25,16,128]{2,1,0:T(8,128)(2,1)S(1)} %get-tuple-element.164), channel_id=1, source_target_pairs={{0,28},{4,0},{8,4},{12,8},{16,12},{20,16},{24,20},{28,24},{1,29},{... | collective-permute-start | bytes 307208 | tf_op jit(solution)/shard_map/ppermute | solution.py:554
  157.3 15.2 %collective-permute-start.28 = (s16[33,16,128]{2,1,0:T(8,128)(2,1)S(1)}, s16[33,16,128]{2,1,0:T(8,128)(2,1)S(1)}, u32[]{:S(2)}, u32[]{:S(2)}) collective-permute-start(s16[33,16,128]{2,1,0:T(8,128)(2,1)S(1)} %get-tuple-element.153), channel_id=1, source_target_pairs={{0,16},{4,20},{8,24},{12,28},{16,0},{20,4},{24,8},{28,12},{1,17},{... | collective-permute-start | bytes 405512 | tf_op jit(solution)/shard_map/ppermute | solution.py:554
  161.1 11.3 %collective-permute-start.29 = (s16[33,16,128]{2,1,0:T(8,128)(2,1)S(1)}, s16[33,16,128]{2,1,0:T(8,128)(2,1)S(1)}, u32[]{:S(2)}, u32[]{:S(2)}) collective-permute-start(s16[33,16,128]{2,1,0:T(8,128)(2,1)S(1)} %get-tuple-element.154), channel_id=1, source_target_pairs={{0,20},{4,24},{8,28},{12,0},{16,4},{20,8},{24,12},{28,16},{1,21},{... | collective-permute-start | bytes 405512 | tf_op jit(solution)/shard_map/ppermute | solution.py:554
  161.3 15.0 %collective-permute-start.30 = (s16[33,16,128]{2,1,0:T(8,128)(2,1)S(1)}, s16[33,16,128]{2,1,0:T(8,128)(2,1)S(1)}, u32[]{:S(2)}, u32[]{:S(2)}) collective-permute-start(s16[33,16,128]{2,1,0:T(8,128)(2,1)S(1)} %get-tuple-element.155), channel_id=1, source_target_pairs={{0,24},{4,28},{8,0},{12,4},{16,8},{20,12},{24,16},{28,20},{1,25},{... | collective-permute-start | bytes 405512 | tf_op jit(solution)/shard_map/ppermute | solution.py:554
  161.3 19.8 %collective-permute-start.31 = (s16[33,16,128]{2,1,0:T(8,128)(2,1)S(1)}, s16[33,16,128]{2,1,0:T(8,128)(2,1)S(1)}, u32[]{:S(2)}, u32[]{:S(2)}) collective-permute-start(s16[33,16,128]{2,1,0:T(8,128)(2,1)S(1)} %get-tuple-element.156), channel_id=1, source_target_pairs={{0,28},{4,0},{8,4},{12,8},{16,12},{20,16},{24,20},{28,24},{1,29},{... | collective-permute-start | bytes 405512 | tf_op jit(solution)/shard_map/ppermute | solution.py:554
  (30 other events, 335.8 us)

commit v17 on v15

--- a/solution.py
+++ b/solution.py
@@ -13,7 +13,7 @@
 LANES = 128
 TILE = 16
 VMEM_LIMIT = 28 * 1024 * 1024
-VMEM_MORE = 48 * 1024 * 1024
+VMEM_MORE = 44 * 1024 * 1024
 VMEM_ALL = 60 * 1024 * 1024
 F32 = jnp.float32
 BF16 = jnp.bfloat16

time: 184 us -> 181 us (0.984)
    unnamed x36 -> x30, local copies, waits for them, and re-layouts: 9.62 us -> 8.6 us
where the time goes in v17:
time: 181 us
  starting transfers between devices  59.7 us (33%)
  Pallas kernels  55.8 us (31%)
  waiting for transfers between devices  47.1 us (26%)
  local copies, waits for them, and re-layouts  8.6 us (5%)
  blocking collectives  8.59 us (5%)
    ppermute x28, starting transfers between devices, over_dp(): return lax.ppermute(x, 'dp', [(i, (i + d) % n_dp) for i in range(n_dp)])  43.2 us
    ppermute x28, waiting for transfers between devices, over_dp(): return lax.ppermute(x, 'dp', [(i, (i + d) % n_dp) for i in range(n_dp)])  28 us
    pallas_call x1, Pallas kernels, attend(): pl.pallas_call(functools.partial(attend_body, places, len(kvs), len(late)...  20.8 us
    ppermute x8, starting transfers between devices, over_core(): return lax.ppermute(x, 'tensor', [(t, t ^ 1) for t in range(n_tp)])  14.3 us
    ppermute x4, waiting for transfers between devices, over_x(): lax.ppermute(x, 'tensor', [(t, (t + 2 * d) % n_tp) for t in range(n_tp)])  12 us
    pallas_call x2, Pallas kernels, project(): pl.pallas_call(functools.partial(project_body, n_in), out_shape=jax.Shape...  9.74 us
    unnamed x30, local copies, waits for them, and re-layouts  8.6 us
    psum x1, blocking collectives, on_device(): asked = lax.psum(wanted, 'dp')  8.59 us
  transfers between devices with their start and end apart: 40, of which 17 were waited for; matrix products, arithmetic and copies ran while one was open for 0% of the time, Pallas kernels for 13%

profile of v17, /device:TPU:13, one launch (start us, length us, event | category | flops | bytes accessed | tf_op | source)
XLA Modules:
  0.0 180.9 jit_solution(14503052589085966855)
XLA Ops:
  2.2 8.6 %psum.7.asked = s32[8,32]{1,0:T(8,128)} all-reduce(s32[8,32]{1,0:T(8,128)} %get-tuple-element.86), channel_id=1, replica_groups=mesh['dp'=8,'tensor'=4] {'dp'}, use_global_device_ids=true, to_apply=%region_0.0 | all-reduce | flops 256 | bytes 2048 | tf_op jit(solution)/shard_map/psum | solution.py:559
  10.8 3.6 %pack_rows.3 = (bf16[4,16,896]{2,1,0:T(8,128)(2,1)}, bf16[4,16,896]{2,1,0:T(8,128)(2,1)}, bf16[4,16,896]{2,1,0:T(8,128)(2,1)}, bf16[4,16,896]{2,1,0:T(8,128)(2,1...) custom-call(s32[1]{0:T(128)} %get-tuple-element.85.me, ...), custom_call_target="tpu_custom_call" | custom-call | bytes 1835008 | tf_op jit(solution)/shard_map/pack_rows/pallas_call | solution.py:97
  19.1 3.7 %pack_rows.2 = (bf16[4,16,896]{2,1,0:T(8,128)(2,1)}, bf16[4,16,896]{2,1,0:T(8,128)(2,1)}, bf16[4,16,896]{2,1,0:T(8,128)(2,1)}, bf16[4,16,896]{2,1,0:T(8,128)(2,1...) custom-call(s32[1]{0:T(128)} %get-tuple-element.85.me, ...), custom_call_target="tpu_custom_call" | custom-call | bytes 1835008 | tf_op jit(solution)/shard_map/pack_rows/pallas_call | solution.py:97
  26.6 5.3 %collective-permute-start.3 = (bf16[4,16,896]{2,1,0:T(8,128)(2,1)}, bf16[4,16,896]{2,1,0:T(8,128)(2,1)S(1)}, u32[]{:S(2)}, u32[]{:S(2)}) collective-permute-start(bf16[4,16,896]{2,1,0:T(8,128)(2,1)} %get-tuple-element.91), channel_id=1, source_target_pairs={{0,16},{4,20},{8,24},{12,28},{16,0},{20,4},{24,8},{28,12},{1,17},{... | collective-permute-start | bytes 344072 | tf_op jit(solution)/shard_map/ppermute | solution.py:550
  31.9 2.6 %collective-permute-done.8.refs_5_ = bf16[4,16,896]{2,1,0:T(8,128)(2,1)S(1)} collective-permute-done((bf16[4,16,896]{2,1,0:T(8,128)(2,1)}, bf16[4,16,896]{2,1,0:T(8,128)(2,1)S(1)}, u32[]{:S(2)}, u32[]{:S(2)}) %collective-permute-start.8) | collective-permute-done | bytes 114720 | tf_op jit(solution)/shard_map/ppermute | solution.py:550
  34.4 2.3 %collective-permute-done.9.refs_6_ = bf16[4,16,896]{2,1,0:T(8,128)(2,1)S(1)} collective-permute-done((bf16[4,16,896]{2,1,0:T(8,128)(2,1)S(1)}, bf16[4,16,896]{2,1,0:T(8,128)(2,1)S(1)}, u32[]{:S(2)}, u32[]{:S(2)}) %collective-permute-start.9) | collective-permute-done | bytes 114720 | tf_op jit(solution)/shard_map/ppermute | solution.py:550
  38.6 2.6 %collective-permute-done.3.refs_4_ = bf16[4,16,896]{2,1,0:T(8,128)(2,1)S(1)} collective-permute-done((bf16[4,16,896]{2,1,0:T(8,128)(2,1)}, bf16[4,16,896]{2,1,0:T(8,128)(2,1)S(1)}, u32[]{:S(2)}, u32[]{:S(2)}) %collective-permute-start.3) | collective-permute-done | bytes 114720 | tf_op jit(solution)/shard_map/ppermute | solution.py:550
  47.5 6.6 %collective-permute-start.15 = (bf16[16,16,896]{2,1,0:T(8,128)(2,1)S(1)}, bf16[16,16,896]{2,1,0:T(8,128)(2,1)S(1)}, u32[]{:S(2)}, u32[]{:S(2)}) collective-permute-start(bf16[16,16,896]{2,1,0:T(8,128)(2,1)S(1)} %compact_rows.2.refs_0_), channel_id=1, source_target_pairs={{0,1},{1,0},{2,3},{3,2},{4,5},{5,4},{6,7},{7,6},{8,9},{9,8},{10,11... | collective-permute-start | bytes 1376264 | tf_op jit(solution)/shard_map/ppermute | solution.py:544
  54.1 4.5 %collective-permute-start.16 = (bf16[16,16,896]{2,1,0:T(8,128)(2,1)S(1)}, bf16[16,16,896]{2,1,0:T(8,128)(2,1)S(1)}, u32[]{:S(2)}, u32[]{:S(2)}) collective-permute-start(bf16[16,16,896]{2,1,0:T(8,128)(2,1)S(1)} %collective-permute-done.12.refs_2_), channel_id=1, source_target_pairs={{0,1},{1,0},{2,3},{3,2},{4,5},{5,4},{6,7},{7,6},{8,9},{9,8},{10,11... | collective-permute-start | bytes 1376264 | tf_op jit(solution)/shard_map/ppermute | solution.py:544
  64.3 6.1 %project.2.refs_0_ = bf16[4,16,16,2048]{3,2,1,0:T(8,128)(2,1)S(1)} custom-call(bf16[16,16,896]{2,1,0:T(8,128)(2,1)S(1)} %compact_rows.2.refs_0_, bf16[16,16,896]{2,1,0:T(8,128)(2,1)S(1)} %collective-permute-done.15.refs_1_, bf16[16,16,896]{2,1,0:T(8,128)(2,1)S(1)} %collective-permute-done.12.refs_2_, ...), custom_call_target="tpu_custom_call" | custom-call | flops 3758096384 | bytes 9699328 | tf_op jit(solution)/shard_map/project/pallas_call | solution.py:174
  76.4 3.6 %project.3.refs_1_ = bf16[2,16,16,2048]{3,2,1,0:T(8,128)(2,1)S(1)} custom-call(bf16[16,16,896]{2,1,0:T(8,128)(2,1)S(1)} %compact_rows.3.refs_0_, bf16[16,16,896]{2,1,0:T(8,128)(2,1)S(1)} %collective-permute-done.17.refs_1_, bf16[896,1024]{1,0:T(8,128)(2,1)S(1)} %copy-done.4, bf16[896,1024]{1,0:T(8,128)(2,1)S(1)} %copy-done.5), custom_call_target="tpu_custom_call" | custom-call | flops 1879048192 | bytes 6684672 | tf_op jit(solution)/shard_map/project/pallas_call | solution.py:174
  81.3 5.7 %collective-permute-done.18.refs_2_ = bf16[16,16,896]{2,1,0:T(8,128)(2,1)S(1)} collective-permute-done((bf16[16,16,896]{2,1,0:T(8,128)(2,1)S(1)}, bf16[16,16,896]{2,1,0:T(8,128)(2,1)S(1)}, u32[]{:S(2)}, u32[]{:S(2)}) %collective-permute-start.18) | collective-permute-done | bytes 458784 | tf_op jit(solution)/shard_map/ppermute | solution.py:547
  89.4 20.8 %attend.1 = (bf16[512,1024]{1,0:T(8,128)(2,1)}, bf16[512,1024]{1,0:T(8,128)(2,1)}, bf16[2,16,32,2048]{3,2,1,0:T(8,128)(2,1)}, bf16[1,16,32,2048]{3,2,1,0:T(8,128...) custom-call(bf16[4,16,16,2048]{3,2,1,0:T(8,128)(2,1)} %copy-done.10,, ...), custom_call_target="tpu_custom_call" | custom-call | flops 7247757312 | bytes 20971520 | tf_op jit(solution)/shard_map/attend/pallas_call | solution.py:297
  116.9 4.1 %grads.1 = (f32[1,16,32,512]{3,2,1,0:T(8,128)S(1)}, f32[2,16,32,512]{3,2,1,0:T(8,128)S(1)}) custom-call(bf16[1,16,32,2048]{3,2,1,0:T(8,128)(2,1)S(1)} %copy-done.12, bf16[2,16,32,2048]{3,2,1,0:T(8,128)(2,1)S(1)} %copy-done.11, bf16[896,1024]{1,0:T(8,128)(2,1)S(1)} %copy-done.4, bf16[896,1024]{1,0:T(8,128)(2,1)S(1)} %copy-done.6), custom_call_target="tpu_custom_call" | custom-call | flops 4294967296 | bytes 14680064 | tf_op jit(solution)/shard_map/grads/pallas_call | solution.py:370
  125.2 2.7 %collective-permute-done.20.got = f32[1,16,32,384]{3,2,1,0:T(8,128)S(1)} collective-permute-done((f32[1,16,32,384]{3,2,1,0:T(8,128)S(1)}, f32[1,16,32,384]{3,2,1,0:T(8,128)S(1)}, u32[]{:S(2)}, u32[]{:S(2)}) %collective-permute-start.20) | collective-permute-done | bytes 786464 | tf_op jit(solution)/shard_map/ppermute | solution.py:544
  134.2 3.9 %collective-permute-done.25.rest_0_ = s16[65,32,128]{2,1,0:T(8,128)(2,1)S(1)} collective-permute-done((s16[65,32,128]{2,1,0:T(8,128)(2,1)S(1)}, s16[65,32,128]{2,1,0:T(8,128)(2,1)S(1)}, u32[]{:S(2)}, u32[]{:S(2)}) %collective-permute-start.25) | collective-permute-done | bytes 532512 | tf_op jit(solution)/shard_map/ppermute | solution.py:547
  144.4 7.1 %collective-permute-start.39 = (s16[25,16,128]{2,1,0:T(8,128)(2,1)S(1)}, s16[25,16,128]{2,1,0:T(8,128)(2,1)S(1)}, u32[]{:S(2)}, u32[]{:S(2)}) collective-permute-start(s16[25,16,128]{2,1,0:T(8,128)(2,1)S(1)} %get-tuple-element.166), channel_id=1, source_target_pairs={{0,28},{4,0},{8,4},{12,8},{16,12},{20,16},{24,20},{28,24},{1,29},{... | collective-permute-start | bytes 307208 | tf_op jit(solution)/shard_map/ppermute | solution.py:550
  153.5 3.0 %collective-permute-done.38.refs_6_ = s16[25,16,128]{2,1,0:T(8,128)(2,1)S(1)} collective-permute-done((s16[25,16,128]{2,1,0:T(8,128)(2,1)S(1)}, s16[25,16,128]{2,1,0:T(8,128)(2,1)S(1)}, u32[]{:S(2)}, u32[]{:S(2)}) %collective-permute-start.38) | collective-permute-done | bytes 102432 | tf_op jit(solution)/shard_map/ppermute | solution.py:550
  158.8 2.4 %collective-permute-start.32 = (s16[33,16,128]{2,1,0:T(8,128)(2,1)S(1)}, s16[33,16,128]{2,1,0:T(8,128)(2,1)S(1)}, u32[]{:S(2)}, u32[]{:S(2)}) collective-permute-start(s16[33,16,128]{2,1,0:T(8,128)(2,1)S(1)} %get-tuple-element.158), channel_id=1, source_target_pairs={{0,28},{4,0},{8,4},{12,8},{16,12},{20,16},{24,20},{28,24},{1,29},{... | collective-permute-start | bytes 405512 | tf_op jit(solution)/shard_map/ppermute | solution.py:550
  161.2 2.7 %gather_grads.2.refs_8_ = f32[16,32,896]{2,1,0:T(8,128)} custom-call(s32[1]{0:T(128)} %get-tuple-element.85.me, s32[8,32]{1,0:T(8,128)S(1)} %copy-done.2, s16[25,16,128]{2,1,0:T(8,128)(2,1)S(1)} %get-tuple-element.159.refs_0_, s16[25,16,128]{2,1,0:T(8,128)(2,1)S(1)} %collective-permute-done.33.refs_1_, ...), custom_call_target="tpu_custom_call" | custom-call | bytes 1572864 | tf_op jit(solution)/shard_map/gather_grads/pallas_call | solution.py:519
  164.0 4.7 %collective-permute-done.28.refs_3_ = s16[33,16,128]{2,1,0:T(8,128)(2,1)S(1)} collective-permute-done((s16[33,16,128]{2,1,0:T(8,128)(2,1)S(1)}, s16[33,16,128]{2,1,0:T(8,128)(2,1)S(1)}, u32[]{:S(2)}, u32[]{:S(2)}) %collective-permute-start.28) | collective-permute-done | bytes 135200 | tf_op jit(solution)/shard_map/ppermute | solution.py:550
  168.7 2.9 %collective-permute-done.29.refs_4_ = s16[33,16,128]{2,1,0:T(8,128)(2,1)S(1)} collective-permute-done((s16[33,16,128]{2,1,0:T(8,128)(2,1)S(1)}, s16[33,16,128]{2,1,0:T(8,128)(2,1)S(1)}, u32[]{:S(2)}, u32[]{:S(2)}) %collective-permute-start.29) | collective-permute-done | bytes 135200 | tf_op jit(solution)/shard_map/ppermute | solution.py:550
  171.6 4.5 %collective-permute-done.31.refs_6_ = s16[33,16,128]{2,1,0:T(8,128)(2,1)S(1)} collective-permute-done((s16[33,16,128]{2,1,0:T(8,128)(2,1)S(1)}, s16[33,16,128]{2,1,0:T(8,128)(2,1)S(1)}, u32[]{:S(2)}, u32[]{:S(2)}) %collective-permute-start.31) | collective-permute-done | bytes 135200 | tf_op jit(solution)/shard_map/ppermute | solution.py:550
  177.8 2.9 %gather_grads.3 = f32[16,32,896]{2,1,0:T(8,128)} custom-call(s32[1]{0:T(128)} %get-tuple-element.85.me, s32[8,32]{1,0:T(8,128)S(1)} %copy-done.2, s16[33,16,128]{2,1,0:T(8,128)(2,1)S(1)} %get-tuple-element.151.refs_0_, s16[33,16,128]{2,1,0:T(8,128)(2,1)S(1)} %collective-permute-done.26.refs_1_, ...), custom_call_target="tpu_custom_call", output_to_operand_aliasing={{}: (10, {})} | custom-call | bytes 2097152 | tf_op jit(solution)/shard_map/gather_grads/pallas_call | solution.py:519
  (102 shorter events, 62.7 us)
Async XLA Ops:
  17.6 14.2 %collective-permute-start.7 = (bf16[4,16,896]{2,1,0:T(8,128)(2,1)}, bf16[4,16,896]{2,1,0:T(8,128)(2,1)S(1)}, u32[]{:S(2)}, u32[]{:S(2)}) collective-permute-start(bf16[4,16,896]{2,1,0:T(8,128)(2,1)} %get-tuple-element.96), channel_id=1, source_target_pairs={{0,16},{4,20},{8,24},{12,28},{16,0},{20,4},{24,8},{28,12},{1,17},{... | collective-permute-start | bytes 344072 | tf_op jit(solution)/shard_map/ppermute | solution.py:550
  19.1 15.4 %collective-permute-start.8 = (bf16[4,16,896]{2,1,0:T(8,128)(2,1)}, bf16[4,16,896]{2,1,0:T(8,128)(2,1)S(1)}, u32[]{:S(2)}, u32[]{:S(2)}) collective-permute-start(bf16[4,16,896]{2,1,0:T(8,128)(2,1)} %get-tuple-element.97), channel_id=1, source_target_pairs={{0,12},{4,16},{8,20},{12,24},{16,28},{20,0},{24,4},{28,8},{1,13},{... | collective-permute-start | bytes 344072 | tf_op jit(solution)/shard_map/ppermute | solution.py:550
  22.8 14.0 %collective-permute-start.9 = (bf16[4,16,896]{2,1,0:T(8,128)(2,1)S(1)}, bf16[4,16,896]{2,1,0:T(8,128)(2,1)S(1)}, u32[]{:S(2)}, u32[]{:S(2)}) collective-permute-start(bf16[4,16,896]{2,1,0:T(8,128)(2,1)S(1)} %copy-done.14), channel_id=1, source_target_pairs={{0,8},{4,12},{8,16},{12,20},{16,24},{20,28},{24,0},{28,4},{1,9},{5... | collective-permute-start | bytes 344072 | tf_op jit(solution)/shard_map/ppermute | solution.py:550
  24.2 14.4 %collective-permute-start.10 = (bf16[4,16,896]{2,1,0:T(8,128)(2,1)S(1)}, bf16[4,16,896]{2,1,0:T(8,128)(2,1)S(1)}, u32[]{:S(2)}, u32[]{:S(2)}) collective-permute-start(bf16[4,16,896]{2,1,0:T(8,128)(2,1)S(1)} %copy-done.13), channel_id=1, source_target_pairs={{0,4},{4,8},{8,12},{12,16},{16,20},{20,24},{24,28},{28,0},{1,5},{5... | collective-permute-start | bytes 344072 | tf_op jit(solution)/shard_map/ppermute | solution.py:550
  26.6 14.6 %collective-permute-start.3 = (bf16[4,16,896]{2,1,0:T(8,128)(2,1)}, bf16[4,16,896]{2,1,0:T(8,128)(2,1)S(1)}, u32[]{:S(2)}, u32[]{:S(2)}) collective-permute-start(bf16[4,16,896]{2,1,0:T(8,128)(2,1)} %get-tuple-element.91), channel_id=1, source_target_pairs={{0,16},{4,20},{8,24},{12,28},{16,0},{20,4},{24,8},{28,12},{1,17},{... | collective-permute-start | bytes 344072 | tf_op jit(solution)/shard_map/ppermute | solution.py:550
  47.5 15.3 %collective-permute-start.15 = (bf16[16,16,896]{2,1,0:T(8,128)(2,1)S(1)}, bf16[16,16,896]{2,1,0:T(8,128)(2,1)S(1)}, u32[]{:S(2)}, u32[]{:S(2)}) collective-permute-start(bf16[16,16,896]{2,1,0:T(8,128)(2,1)S(1)} %compact_rows.2.refs_0_), channel_id=1, source_target_pairs={{0,1},{1,0},{2,3},{3,2},{4,5},{5,4},{6,7},{7,6},{8,9},{9,8},{10,11... | collective-permute-start | bytes 1376264 | tf_op jit(solution)/shard_map/ppermute | solution.py:544
  58.6 13.8 %collective-permute-start = (bf16[4,16,896]{2,1,0:T(8,128)(2,1)}, bf16[4,16,896]{2,1,0:T(8,128)(2,1)S(1)}, u32[]{:S(2)}, u32[]{:S(2)}) collective-permute-start(bf16[4,16,896]{2,1,0:T(8,128)(2,1)} %get-tuple-element.88), channel_id=1, source_target_pairs={{0,28},{4,0},{8,4},{12,8},{16,12},{20,16},{24,20},{28,24},{1,29},{... | collective-permute-start | bytes 344072 | tf_op jit(solution)/shard_map/ppermute | solution.py:550
  58.6 13.8 %collective-permute-start.13 = (bf16[4,16,896]{2,1,0:T(8,128)(2,1)}, bf16[4,16,896]{2,1,0:T(8,128)(2,1)S(1)}, u32[]{:S(2)}, u32[]{:S(2)}) collective-permute-start(bf16[4,16,896]{2,1,0:T(8,128)(2,1)} %get-tuple-element.115), channel_id=1, source_target_pairs={{0,8},{4,12},{8,16},{12,20},{16,24},{20,28},{24,0},{28,4},{1,9},{5... | collective-permute-start | bytes 344072 | tf_op jit(solution)/shard_map/ppermute | solution.py:550
  60.8 11.7 %collective-permute-start.14 = (bf16[4,16,896]{2,1,0:T(8,128)(2,1)}, bf16[4,16,896]{2,1,0:T(8,128)(2,1)S(1)}, u32[]{:S(2)}, u32[]{:S(2)}) collective-permute-start(bf16[4,16,896]{2,1,0:T(8,128)(2,1)} %get-tuple-element.116), channel_id=1, source_target_pairs={{0,4},{4,8},{8,12},{12,16},{16,20},{20,24},{24,28},{28,0},{1,5},{5... | collective-permute-start | bytes 344072 | tf_op jit(solution)/shard_map/ppermute | solution.py:550
  75.0 12.1 %collective-permute-start.18 = (bf16[16,16,896]{2,1,0:T(8,128)(2,1)S(1)}, bf16[16,16,896]{2,1,0:T(8,128)(2,1)S(1)}, u32[]{:S(2)}, u32[]{:S(2)}) collective-permute-start(bf16[16,16,896]{2,1,0:T(8,128)(2,1)S(1)} %compact_rows.3.refs_0_), channel_id=1, source_target_pairs={{0,2},{1,3},{2,0},{3,1},{4,6},{5,7},{6,4},{7,5},{8,10},{9,11},{10,... | collective-permute-start | bytes 1376264 | tf_op jit(solution)/shard_map/ppermute | solution.py:547
  110.6 13.9 %collective-permute-start.24 = (f32[1,16,32,512]{3,2,1,0:T(8,128)S(1)}, f32[1,16,32,512]{3,2,1,0:T(8,128)S(1)}, u32[]{:S(2)}, u32[]{:S(2)}) collective-permute-start(f32[1,16,32,512]{3,2,1,0:T(8,128)S(1)} %get-tuple-element.149), channel_id=1, source_target_pairs={{0,1},{1,0},{2,3},{3,2},{4,5},{5,4},{6,7},{7,6},{8,9},{9,8},{10,11... | collective-permute-start | bytes 3145736 | tf_op jit(solution)/shard_map/ppermute | solution.py:544
  124.9 13.2 %collective-permute-start.25 = (s16[65,32,128]{2,1,0:T(8,128)(2,1)S(1)}, s16[65,32,128]{2,1,0:T(8,128)(2,1)S(1)}, u32[]{:S(2)}, u32[]{:S(2)}) collective-permute-start(s16[65,32,128]{2,1,0:T(8,128)(2,1)S(1)} %far_codes.3), channel_id=1, source_target_pairs={{0,2},{1,3},{2,0},{3,1},{4,6},{5,7},{6,4},{7,5},{8,10},{9,11},{10,... | collective-permute-start | bytes 1597448 | tf_op jit(solution)/shard_map/ppermute | solution.py:547
  129.1 12.0 %collective-permute-start.33 = (s16[25,16,128]{2,1,0:T(8,128)(2,1)S(1)}, s16[25,16,128]{2,1,0:T(8,128)(2,1)S(1)}, u32[]{:S(2)}, u32[]{:S(2)}) collective-permute-start(s16[25,16,128]{2,1,0:T(8,128)(2,1)S(1)} %get-tuple-element.160), channel_id=1, source_target_pairs={{0,4},{4,8},{8,12},{12,16},{16,20},{20,24},{24,28},{28,0},{1,5},{5... | collective-permute-start | bytes 307208 | tf_op jit(solution)/shard_map/ppermute | solution.py:550
  133.1 11.3 %collective-permute-start.36 = (s16[25,16,128]{2,1,0:T(8,128)(2,1)S(1)}, s16[25,16,128]{2,1,0:T(8,128)(2,1)S(1)}, u32[]{:S(2)}, u32[]{:S(2)}) collective-permute-start(s16[25,16,128]{2,1,0:T(8,128)(2,1)S(1)} %get-tuple-element.163), channel_id=1, source_target_pairs={{0,16},{4,20},{8,24},{12,28},{16,0},{20,4},{24,8},{28,12},{1,17},{... | collective-permute-start | bytes 307208 | tf_op jit(solution)/shard_map/ppermute | solution.py:550
  139.4 19.2 %collective-permute-start.26 = (s16[33,16,128]{2,1,0:T(8,128)(2,1)S(1)}, s16[33,16,128]{2,1,0:T(8,128)(2,1)S(1)}, u32[]{:S(2)}, u32[]{:S(2)}) collective-permute-start(s16[33,16,128]{2,1,0:T(8,128)(2,1)S(1)} %get-tuple-element.152), channel_id=1, source_target_pairs={{0,4},{4,8},{8,12},{12,16},{16,20},{20,24},{24,28},{28,0},{1,5},{5... | collective-permute-start | bytes 405512 | tf_op jit(solution)/shard_map/ppermute | solution.py:550
  141.1 17.7 %collective-permute-start.27 = (s16[33,16,128]{2,1,0:T(8,128)(2,1)S(1)}, s16[33,16,128]{2,1,0:T(8,128)(2,1)S(1)}, u32[]{:S(2)}, u32[]{:S(2)}) collective-permute-start(s16[33,16,128]{2,1,0:T(8,128)(2,1)S(1)} %get-tuple-element.153), channel_id=1, source_target_pairs={{0,8},{4,12},{8,16},{12,20},{16,24},{20,28},{24,0},{28,4},{1,9},{5... | collective-permute-start | bytes 405512 | tf_op jit(solution)/shard_map/ppermute | solution.py:550
  141.1 12.1 %collective-permute-start.37 = (s16[25,16,128]{2,1,0:T(8,128)(2,1)S(1)}, s16[25,16,128]{2,1,0:T(8,128)(2,1)S(1)}, u32[]{:S(2)}, u32[]{:S(2)}) collective-permute-start(s16[25,16,128]{2,1,0:T(8,128)(2,1)S(1)} %get-tuple-element.164), channel_id=1, source_target_pairs={{0,20},{4,24},{8,28},{12,0},{16,4},{20,8},{24,12},{28,16},{1,21},{... | collective-permute-start | bytes 307208 | tf_op jit(solution)/shard_map/ppermute | solution.py:550
  142.1 14.4 %collective-permute-start.38 = (s16[25,16,128]{2,1,0:T(8,128)(2,1)S(1)}, s16[25,16,128]{2,1,0:T(8,128)(2,1)S(1)}, u32[]{:S(2)}, u32[]{:S(2)}) collective-permute-start(s16[25,16,128]{2,1,0:T(8,128)(2,1)S(1)} %get-tuple-element.165), channel_id=1, source_target_pairs={{0,24},{4,28},{8,0},{12,4},{16,8},{20,12},{24,16},{28,20},{1,25},{... | collective-permute-start | bytes 307208 | tf_op jit(solution)/shard_map/ppermute | solution.py:550
  144.4 13.2 %collective-permute-start.39 = (s16[25,16,128]{2,1,0:T(8,128)(2,1)S(1)}, s16[25,16,128]{2,1,0:T(8,128)(2,1)S(1)}, u32[]{:S(2)}, u32[]{:S(2)}) collective-permute-start(s16[25,16,128]{2,1,0:T(8,128)(2,1)S(1)} %get-tuple-element.166), channel_id=1, source_target_pairs={{0,28},{4,0},{8,4},{12,8},{16,12},{20,16},{24,20},{28,24},{1,29},{... | collective-permute-start | bytes 307208 | tf_op jit(solution)/shard_map/ppermute | solution.py:550
  153.2 15.4 %collective-permute-start.28 = (s16[33,16,128]{2,1,0:T(8,128)(2,1)S(1)}, s16[33,16,128]{2,1,0:T(8,128)(2,1)S(1)}, u32[]{:S(2)}, u32[]{:S(2)}) collective-permute-start(s16[33,16,128]{2,1,0:T(8,128)(2,1)S(1)} %get-tuple-element.154), channel_id=1, source_target_pairs={{0,12},{4,16},{8,20},{12,24},{16,28},{20,0},{24,4},{28,8},{1,13},{... | collective-permute-start | bytes 405512 | tf_op jit(solution)/shard_map/ppermute | solution.py:550
  156.5 15.1 %collective-permute-start.29 = (s16[33,16,128]{2,1,0:T(8,128)(2,1)S(1)}, s16[33,16,128]{2,1,0:T(8,128)(2,1)S(1)}, u32[]{:S(2)}, u32[]{:S(2)}) collective-permute-start(s16[33,16,128]{2,1,0:T(8,128)(2,1)S(1)} %get-tuple-element.155), channel_id=1, source_target_pairs={{0,16},{4,20},{8,24},{12,28},{16,0},{20,4},{24,8},{28,12},{1,17},{... | collective-permute-start | bytes 405512 | tf_op jit(solution)/shard_map/ppermute | solution.py:550
  157.6 14.0 %collective-permute-start.30 = (s16[33,16,128]{2,1,0:T(8,128)(2,1)S(1)}, s16[33,16,128]{2,1,0:T(8,128)(2,1)S(1)}, u32[]{:S(2)}, u32[]{:S(2)}) collective-permute-start(s16[33,16,128]{2,1,0:T(8,128)(2,1)S(1)} %get-tuple-element.156), channel_id=1, source_target_pairs={{0,20},{4,24},{8,28},{12,0},{16,4},{20,8},{24,12},{28,16},{1,21},{... | collective-permute-start | bytes 405512 | tf_op jit(solution)/shard_map/ppermute | solution.py:550
  158.6 17.5 %collective-permute-start.31 = (s16[33,16,128]{2,1,0:T(8,128)(2,1)S(1)}, s16[33,16,128]{2,1,0:T(8,128)(2,1)S(1)}, u32[]{:S(2)}, u32[]{:S(2)}) collective-permute-start(s16[33,16,128]{2,1,0:T(8,128)(2,1)S(1)} %get-tuple-element.157), channel_id=1, source_target_pairs={{0,24},{4,28},{8,0},{12,4},{16,8},{20,12},{24,16},{28,20},{1,25},{... | collective-permute-start | bytes 405512 | tf_op jit(solution)/shard_map/ppermute | solution.py:550
  158.8 19.0 %collective-permute-start.32 = (s16[33,16,128]{2,1,0:T(8,128)(2,1)S(1)}, s16[33,16,128]{2,1,0:T(8,128)(2,1)S(1)}, u32[]{:S(2)}, u32[]{:S(2)}) collective-permute-start(s16[33,16,128]{2,1,0:T(8,128)(2,1)S(1)} %get-tuple-element.158), channel_id=1, source_target_pairs={{0,28},{4,0},{8,4},{12,8},{16,12},{20,16},{24,20},{28,24},{1,29},{... | collective-permute-start | bytes 405512 | tf_op jit(solution)/shard_map/ppermute | solution.py:550
  (31 other events, 325.1 us)
